TPU v7x, 32 devices: a whole 2x2x4 slice. The times are simulated.
32 devices in a mesh: segment: 4 (over x, core), fsdp: 2 (over y), dp: 4 (over z).
Axes of the slice: x: 2, y: 2, z: 4, core: 2. Of those that a mesh axis runs over, the one named last changes fastest.
Arguments:
- inputs: bfloat16 [3, 16, 49, 2880], P(None, ('fsdp', 'dp')), may hold values from -6 to 6
- cotangent: bfloat16 [3, 16, 49, 2880], P(None, ('fsdp', 'dp')), may hold values from -0.119628906 to 0.119628906
- plan: int32 [3], replicated, may hold values from 0 to 2, each once
- weight: bfloat16 [4, 2880, 2880], P('segment', 'fsdp'), may hold values from -0.109375 to 0.109375
- squeeze: bfloat16 [4, 2880, 360], P('segment', 'fsdp'), may hold values from -0.109375 to 0.109375
- excite: bfloat16 [4, 2880, 360], P('segment', 'fsdp'), may hold values from -0.3125 to 0.3125
Outputs:
- grad_weight: float32 [4, 2880, 2880], P('segment', ('fsdp', 'dp'))
- grad_squeeze: float32 [4, 2880, 360], P('segment', ('fsdp', 'dp'))
- grad_excite: float32 [4, 2880, 360], P('segment', ('fsdp', 'dp'))
Inputs may be any that keep to these rules, and one draw needn't show every extreme that they name: plan names each of the 3 microbatches exactly once.
All inputs are finite; a program needn't handle non-finite values.
Results may differ from a plain program's by a relative error of at most 0.024.
Values may be sent and summed in bfloat16 or wider, within the bound.
No kernel may reach another device: no remote copies, remote signals or barrier semaphores. Data moves between devices by JAX's collectives and lax.ppermute only.
A program may use at most 128 MiB of HBM per device.

v0:
```python
import jax
import jax.numpy as jnp
from jax import lax
from jax.sharding import PartitionSpec as P


def shifted(value, axis, steps):
    count = lax.axis_size(axis)
    leading, last = (max(0, -steps), min(count, count - steps))
    return lax.ppermute(value, axis, [(source, source + steps) for source in range(leading, last)])


def silu_slope(value):
    sigma = jax.nn.sigmoid(value)
    return sigma * (1.0 + value * (1.0 - sigma))


def contract_rows(left, right):
    return lax.dot_general(
        left, right, (((0,), (0,)), ((), ())), preferred_element_type=jnp.float32
    )


def contract_cols(left, right):
    return lax.dot_general(
        left, right, (((1,), (1,)), ((), ())), preferred_element_type=jnp.float32
    )


def project(images, matrix):
    flat = images.reshape(-1, images.shape[-1])
    result = jnp.dot(flat, matrix, preferred_element_type=jnp.float32)
    return result.reshape(images.shape[:-1] + (matrix.shape[1],))


def forward_block(images, matrix, squeeze_w, excite_w):
    pre = project(images, matrix)
    active_map = jax.nn.silu(pre).astype(jnp.bfloat16)
    pooled = jnp.mean(active_map.astype(jnp.float32), axis=1).astype(jnp.bfloat16)
    squeezed = jnp.dot(pooled, squeeze_w, preferred_element_type=jnp.float32)
    hidden = jax.nn.silu(squeezed).astype(jnp.bfloat16)
    gate = jax.nn.sigmoid(contract_cols(hidden, excite_w))
    output = (
        images.astype(jnp.float32) + active_map.astype(jnp.float32) * gate[:, None, :]
    ).astype(jnp.bfloat16)
    return (output, pre, pooled, squeezed, hidden, gate)


def backward_block(images, pre, squeezed, gate, upstream, matrix, squeeze_w, excite_w):
    active_map = jax.nn.silu(pre).astype(jnp.bfloat16)
    upper = upstream.astype(jnp.float32)
    d_act = upper * gate[:, None, :]
    d_gate = jnp.sum(upper * active_map.astype(jnp.float32), axis=1)
    d_excite = (d_gate * gate * (1.0 - gate)).astype(jnp.bfloat16)
    d_hidden = jnp.dot(d_excite, excite_w, preferred_element_type=jnp.float32)
    d_squeezed = (d_hidden * silu_slope(squeezed)).astype(jnp.bfloat16)
    d_pooled = contract_cols(d_squeezed, squeeze_w)
    d_act = d_act + d_pooled[:, None, :] / images.shape[1]
    d_pre = (d_act * silu_slope(pre)).astype(jnp.bfloat16)
    flat = d_pre.reshape(-1, d_pre.shape[-1])
    back = contract_cols(flat, matrix).reshape(images.shape)
    d_images = (upper + back).astype(jnp.bfloat16)
    return (d_excite, d_squeezed, d_pre, d_images)


def put_slot(store, position, value, active):
    current = lax.dynamic_index_in_dim(store, position, 0, keepdims=False)
    return lax.dynamic_update_index_in_dim(store, jnp.where(active, value, current), position, 0)


def take_slot(store, position):
    return lax.dynamic_index_in_dim(store, position, 0, keepdims=False)


def on_device(inputs, cotangent, plan, weight, squeeze, excite):
    full_w, full_s, full_e = (
        lax.all_gather(weight[0], "fsdp", axis=0, tiled=True),
        lax.all_gather(squeeze[0], "fsdp", axis=0, tiled=True),
        lax.all_gather(excite[0], "fsdp", axis=0, tiled=True),
    )
    sections = lax.axis_size("segment")
    segment_id = lax.axis_index("segment")
    ordered = inputs[plan]
    micro, images, pixels, width = ordered.shape
    hidden_width = full_s.shape[1]
    steps_total = micro + sections - 1
    store_in = jnp.zeros((micro, images, pixels, width), jnp.bfloat16)
    store_pre = jnp.zeros((micro, images, pixels, width), jnp.float32)
    store_pool = jnp.zeros((micro, images, width), jnp.bfloat16)
    store_sq = jnp.zeros((micro, images, hidden_width), jnp.float32)
    store_hid = jnp.zeros((micro, images, hidden_width), jnp.bfloat16)
    store_gate = jnp.zeros((micro, images, width), jnp.float32)
    incoming = jnp.zeros((images, pixels, width), jnp.bfloat16)
    for step in range(steps_total):
        slot_now = step - segment_id
        active = (slot_now >= 0) & (slot_now < micro)
        position = jnp.clip(slot_now, 0, micro - 1)
        first_in = ordered[min(step, micro - 1)]
        images_in = jnp.where(segment_id == 0, first_in, incoming)
        output, pre, pooled, squeezed, hidden, gate = forward_block(
            images_in, full_w, full_s, full_e
        )
        store_in = put_slot(store_in, position, images_in, active)
        store_pre = put_slot(store_pre, position, pre, active)
        store_pool = put_slot(store_pool, position, pooled, active)
        store_sq = put_slot(store_sq, position, squeezed, active)
        store_hid = put_slot(store_hid, position, hidden, active)
        store_gate = put_slot(store_gate, position, gate, active)
        if step < steps_total - 1:
            incoming = shifted(output, "segment", 1)
    store_dpre = jnp.zeros((micro, images, pixels, width), jnp.bfloat16)
    store_dsq = jnp.zeros((micro, images, hidden_width), jnp.bfloat16)
    store_dex = jnp.zeros((micro, images, width), jnp.bfloat16)
    incoming_grad = jnp.zeros((images, pixels, width), jnp.bfloat16)
    for step in range(steps_total):
        slot_now = micro - 1 - step + (sections - 1 - segment_id)
        active = (slot_now >= 0) & (slot_now < micro)
        position = jnp.clip(slot_now, 0, micro - 1)
        last_in = cotangent[max(micro - 1 - step, 0)]
        upstream = jnp.where(segment_id == sections - 1, last_in, incoming_grad)
        images_in = take_slot(store_in, position)
        pre = take_slot(store_pre, position)
        squeezed = take_slot(store_sq, position)
        gate = take_slot(store_gate, position)
        d_excite, d_squeezed, d_pre, d_images = backward_block(
            images_in, pre, squeezed, gate, upstream, full_w, full_s, full_e
        )
        store_dpre = put_slot(store_dpre, position, d_pre, active)
        store_dsq = put_slot(store_dsq, position, d_squeezed, active)
        store_dex = put_slot(store_dex, position, d_excite, active)
        if step < steps_total - 1:
            incoming_grad = shifted(d_images, "segment", -1)
    flat_in = store_in.reshape(-1, width)
    flat_dpre = store_dpre.reshape(-1, width)
    grad_s = contract_rows(store_pool.reshape(-1, width), store_dsq.reshape(-1, hidden_width))
    grad_e = contract_rows(store_dex.reshape(-1, width), store_hid.reshape(-1, hidden_width))
    grad_w = contract_rows(flat_in, flat_dpre)
    shard_w, shard_s, shard_e = (
        lax.psum_scatter(
            grad_w.astype(jnp.bfloat16), ("fsdp", "dp"), scatter_dimension=0, tiled=True
        ).astype(jnp.float32),
        lax.psum_scatter(
            grad_s.astype(jnp.bfloat16), ("fsdp", "dp"), scatter_dimension=0, tiled=True
        ).astype(jnp.float32),
        lax.psum_scatter(
            grad_e.astype(jnp.bfloat16), ("fsdp", "dp"), scatter_dimension=0, tiled=True
        ).astype(jnp.float32),
    )
    return (shard_w[None], shard_s[None], shard_e[None])


def solution(mesh):
    placed = (
        P(None, ("fsdp", "dp"), None, None),
        P(None, ("fsdp", "dp"), None, None),
        P(),
        P("segment", "fsdp", None),
        P("segment", "fsdp", None),
        P("segment", "fsdp", None),
    )
    return jax.shard_map(
        on_device,
        mesh=mesh,
        in_specs=placed,
        out_specs=(
            P("segment", ("fsdp", "dp"), None),
            P("segment", ("fsdp", "dp"), None),
            P("segment", ("fsdp", "dp"), None),
        ),
        check_vma=False,
    )
```

profile of v0, /device:TPU:10, one launch (start us, length us, event | category | flops | bytes accessed | tf_op | source)
XLA Modules:
  0.0 1012.3 jit_solution(11532854117454839898)
XLA Ops:
  9.5 6.0 gather_fusion
  15.5 3.5 fusion.350
  19.0 4.3 fusion.349
  25.7 2.1 constant_dynamic-slice_fusion.56
  27.8 186.3 %all-gather.7.cloned.1.call-done = bf16[1,2880,2880]{2,1,0:T(8,128)(2,1)} async-done(((bf16[1,1440,2880]{2,1,0:T(8,128)(2,1)}), bf16[1,2880,2880]{2,1,0:T(8,128)(2,1)}) %all-gather.7.cloned.1.call-update) | async-done | bytes 16588816 | tf_op jit(solution)/shard_map/all_gather | solution.py:77
  214.1 9.7 convert_reduce_fusion.4
  223.8 26.3 %all-gather.9.cloned.1.call-done = bf16[1,2880,360]{2,1,0:T(8,128)(2,1)} async-done(((bf16[1,1440,360]{2,1,0:T(8,128)(2,1)}), bf16[1,2880,360]{2,1,0:T(8,128)(2,1)}) %all-gather.9.cloned.1.call-update) | async-done | bytes 2073616 | tf_op jit(solution)/shard_map/all_gather | solution.py:78
  250.1 2.0 constant_dynamic-update-slice_fusion.29
  252.1 34.0 %all-gather.11.cloned.1.call-done = bf16[1,2880,360]{2,1,0:T(8,128)(2,1)} async-done(((bf16[1,1440,360]{2,1,0:T(8,128)(2,1)}), bf16[1,2880,360]{2,1,0:T(8,128)(2,1)}) %all-gather.11.cloned.1.call-update) | async-done | bytes 2073616 | tf_op jit(solution)/shard_map/all_gather | solution.py:79
  286.1 2.3 constant_dynamic-update-slice_fusion.34
  289.1 2.1 collective-permute-start
  292.9 7.3 collective-permute-done
  300.2 8.8 convert_reduce_fusion.3
  312.4 1.9 collective-permute-start.1
  317.9 5.6 collective-permute-done.1
  323.5 3.9 convert_reduce_fusion.2
  329.3 2.3 collective-permute-start.2
  334.2 6.1 collective-permute-done.2
  340.4 3.9 convert_reduce_fusion.1
  346.2 1.9 collective-permute-start.3
  350.7 6.6 collective-permute-done.3
  357.3 2.9 convert_reduce_fusion
  362.4 2.1 collective-permute-start.4
  365.6 2.1 constant_dynamic-slice_fusion.52
  367.7 5.9 collective-permute-done.4
  373.6 4.9 bitcast_dynamic-update-slice_fusion
  378.5 3.2 fusion.123
  386.5 12.4 %fusion.51 = bf16[2,49,2880]{2,1,0:T(8,128)(2,1)} fusion(bf16[1,2880,2880]{2,1,0:T(8,128)(2,1)} %all-gather.7.cloned.1.call-done, f32[3,2,49,2880]{3,2,1,0:T(8,128)} %copy-done.9, s32[]{:T(128)S(6)} %min.30, f32[2,2880]{1,0:T(2,128)} %convolution_multiply_fusion.5, f32[2,2880]{1,0:T(2,128)} %copy-done.34, bf16[1,2,49,2880]{3,1,2,0:T(2,128)(2,1)} %get-tuple-element.15, ...), kind=kOutput, calls=%fused_computation.37 | convolution fusion | flops 1630500480 | bytes 20043520 | tf_op jit(solution)/shard_map/dot_general | solution.py:25
  398.9 1.6 copy.51
  400.5 2.1 collective-permute-start.5
  403.5 2.0 select_dynamic-update-slice_fusion
  406.8 2.2 bitcast_dynamic-update-slice_fusion.11
  409.7 2.0 fusion.137
  414.0 12.5 %fusion.48 = bf16[2,49,2880]{2,1,0:T(8,128)(2,1)} fusion(bf16[1,2880,2880]{2,1,0:T(8,128)(2,1)} %all-gather.7.cloned.1.call-done, bf16[2,49,2880]{2,0,1:T(2,128)(2,1)} %copy-done.20, bf16[1,2,49,2880]{3,1,2,0:T(2,128)(2,1)S(1)} %copy-done.14, pred[]{:T(512)S(6)} %eq.5, f32[3,2,49,2880]{3,2,1,0:T(8,128)} %copy-done.9, s32[]{:T(128)S(6)} %min.29, ...), kind=kOutput, calls=%fused_computation.36 | convolution fusion | flops 1630500480 | bytes 21197568 | tf_op jit(solution)/shard_map/dot_general | solution.py:25
  428.0 4.3 collective-permute-start.6
  433.1 6.1 collective-permute-done.6
  439.2 2.0 fusion.141
  443.5 12.4 %fusion.45 = bf16[2,49,2880]{2,1,0:T(8,128)(2,1)} fusion(bf16[1,2880,2880]{2,1,0:T(8,128)(2,1)} %all-gather.7.cloned.1.call-done, bf16[2,49,2880]{2,0,1:T(2,128)(2,1)} %copy-done.22, bf16[1,2,49,2880]{3,1,2,0:T(2,128)(2,1)S(1)} %get-tuple-element.13, pred[]{:T(512)S(6)} %eq.5, f32[3,2,49,2880]{3,2,1,0:T(8,128)} %copy-done.9, s32[]{:T(128)S(6)} %min.28, ...), kind=kOutput, calls=%fused_computation.35 | convolution fusion | flops 1630500480 | bytes 21197568 | tf_op jit(solution)/shard_map/dot_general | solution.py:25
  457.5 3.9 collective-permute-start.7
  462.1 6.5 collective-permute-done.7
  468.6 2.0 fusion.145
  472.9 12.4 %fusion.42 = bf16[2,49,2880]{2,1,0:T(8,128)(2,1)} fusion(bf16[1,2880,2880]{2,1,0:T(8,128)(2,1)} %all-gather.7.cloned.1.call-done, bf16[2,49,2880]{2,0,1:T(2,128)(2,1)} %copy-done.26, bf16[1,2,49,2880]{3,1,2,0:T(2,128)(2,1)S(1)} %get-tuple-element.13, pred[]{:T(512)S(6)} %eq.5, f32[3,2,49,2880]{3,2,1,0:T(8,128)} %copy-done.9, s32[]{:T(128)S(6)} %min.27, ...), kind=kOutput, calls=%fused_computation.34 | convolution fusion | flops 1630500480 | bytes 21197568 | tf_op jit(solution)/shard_map/dot_general | solution.py:25
  486.9 4.1 collective-permute-start.8
  491.7 6.4 collective-permute-done.8
  498.1 2.0 fusion.149
  502.4 12.4 %fusion.39 = bf16[2,49,2880]{2,1,0:T(8,128)(2,1)} fusion(bf16[1,2880,2880]{2,1,0:T(8,128)(2,1)} %all-gather.7.cloned.1.call-done, bf16[2,49,2880]{2,0,1:T(2,128)(2,1)} %copy-done.24, bf16[1,2,49,2880]{3,1,2,0:T(2,128)(2,1)S(1)} %get-tuple-element.13, pred[]{:T(512)S(6)} %eq.5, f32[3,2,49,2880]{3,2,1,0:T(8,128)} %copy-done.9, s32[]{:T(128)S(6)} %min.26, ...), kind=kOutput, calls=%fused_computation.33 | convolution fusion | flops 1630500480 | bytes 21197568 | tf_op jit(solution)/shard_map/dot_general | solution.py:25
  516.4 3.8 collective-permute-start.9
  520.2 7.2 collective-permute-done.9
  527.5 2.0 fusion.133
  529.5 2.2 fusion.23
  533.1 3.0 bitcast_dynamic-update-slice_fusion.10
  537.4 1.6 bitcast_dynamic-update-slice_fusion.9
  540.4 1.6 bitcast_dynamic-update-slice_fusion.8
  542.0 2.0 constant_dynamic-slice_fusion.23
  545.7 2.9 fusion.22
  549.6 3.1 bitcast_dynamic-update-slice_fusion.7
  555.6 2.1 bitcast_dynamic-update-slice_fusion.6
  557.7 13.8 %bitcast_convert_fusion = bf16[2880,2880]{1,0:T(8,128)(2,1)} fusion(bf16[3,2,49,2880]{3,2,1,0:T(8,128)(2,1)} %bitcast_dynamic-update-slice_fusion.11, bf16[3,2,49,2880]{3,2,1,0:T(8,128)(2,1)S(1)} %bitcast_dynamic-update-slice_fusion.6), kind=kOutput, calls=%fused_computation.1 | convolution fusion | flops 4885401600 | bytes 19975680 | tf_op jit(solution)/shard_map/dot_general | solution.py:19
  571.5 28.2 %reduce-scatter.15.cloned.1.call-done = bf16[360,360]{1,0:T(8,128)(2,1)} async-done(((bf16[2880,360]{1,0:T(8,128)(2,1)}), bf16[360,360]{1,0:T(8,128)(2,1)}) %reduce-scatter.15.cloned.1.call-update) | async-done | bytes 259216
  599.6 1.8 bitcast_convert_fusion.2
  601.4 69.5 %reduce-scatter.13.cloned.1.call-done = bf16[360,360]{1,0:T(8,128)(2,1)} async-done(((bf16[2880,360]{1,0:T(8,128)(2,1)}), bf16[360,360]{1,0:T(8,128)(2,1)}) %reduce-scatter.13.cloned.1.call-update) | async-done | bytes 259216
  670.9 1.8 bitcast_convert_fusion.3
  672.7 328.5 %reduce-scatter.11.cloned.1.call-done = bf16[360,2880]{1,0:T(8,128)(2,1)} async-done(((bf16[2880,2880]{1,0:T(8,128)(2,1)}), bf16[360,2880]{1,0:T(8,128)(2,1)}) %reduce-scatter.11.cloned.1.call-update) | async-done | bytes 2073616
  1001.2 4.0 bitcast_convert_fusion.1
  (219 shorter events, 60.5 us)
Async XLA Ops:
  7.2 2.3 copy-start
  7.2 206.9 %all-gather.7.cloned.1.call-start = ((), (), s32[]{:S(2)}) async-start(), calls=%async_computation.3 | async-start | bytes 25436160 | tf_op jit(solution)/shard_map/all_gather | solution.py:77
  7.9 1.6 copy-start.47
  7.9 242.1 %all-gather.9.cloned.1.call-start = ((), (), s32[]{:S(2)}) async-start(), calls=%async_computation.4 | async-start | bytes 3317760 | tf_op jit(solution)/shard_map/all_gather | solution.py:78
  8.7 277.4 %all-gather.11.cloned.1.call-start = ((), (), s32[]{:S(2)}) async-start(), calls=%async_computation.5 | async-start | bytes 3317760 | tf_op jit(solution)/shard_map/all_gather | solution.py:79
  9.4 590.2 %reduce-scatter.15.cloned.1.call-start = ((), (), s32[]{:S(2)}) async-start(), calls=%async_computation.8 | async-start | bytes 2488320
  289.1 11.1 %collective-permute-start = (bf16[2,49,2880]{2,0,1:T(2,128)(2,1)S(1)}, bf16[2,49,2880]{2,0,1:T(2,128)(2,1)S(1)}, u32[]{:S(2)}, u32[]{:S(2)}) collective-permute-start(bf16[2,49,2880]{2,0,1:T(2,128)(2,1)S(1)} %copy.38), channel_id=1, source_target_pairs={{0,8},{8,16},{16,24},{1,9},{9,17},{17,25},{2,10},{10,18},{18,26},{... | collective-permute-start | bytes 1693448 | tf_op jit(solution)/shard_map/ppermute | solution.py:10
  291.3 1.3 copy-start.30
  292.8 7.5 copy-start.17
  300.2 8.9 copy-start.2
  300.2 23.2 %slice-start = ((s8[16957440]{0:T(1024)(128)(4,1)}), s8[4194304]{0:T(1024)(128)(4,1)S(1)}, s32[]{:S(2)}) async-start(s8[16957440]{0:T(1024)(128)(4,1)} %bitcast.877), calls=%async_computation.9 | async-start | bytes 8388608
  300.2 23.2 %slice-start.1 = ((s8[16957440]{0:T(1024)(128)(4,1)}), s8[4194304]{0:T(1024)(128)(4,1)S(1)}, s32[]{:S(2)}) async-start(s8[16957440]{0:T(1024)(128)(4,1)} %bitcast.877), calls=%async_computation.10 | async-start | bytes 8388608
  300.2 23.2 %slice-start.2 = ((s8[16957440]{0:T(1024)(128)(4,1)}), s8[4194304]{0:T(1024)(128)(4,1)S(1)}, s32[]{:S(2)}) async-start(s8[16957440]{0:T(1024)(128)(4,1)} %bitcast.877), calls=%async_computation.11 | async-start | bytes 8388608
  309.0 1.9 copy-start.3
  309.1 14.4 %slice-start.3 = ((s8[16957440]{0:T(1024)(128)(4,1)}), s8[4194304]{0:T(1024)(128)(4,1)S(1)}, s32[]{:S(2)}) async-start(s8[16957440]{0:T(1024)(128)(4,1)} %bitcast.877), calls=%async_computation.12 | async-start | bytes 8388608
  312.4 11.1 %collective-permute-start.1 = (bf16[2,49,2880]{2,0,1:T(2,128)(2,1)S(1)}, bf16[2,49,2880]{2,0,1:T(2,128)(2,1)S(1)}, u32[]{:S(2)}, u32[]{:S(2)}) collective-permute-start(bf16[2,49,2880]{2,0,1:T(2,128)(2,1)S(1)} %copy.41), channel_id=1, source_target_pairs={{0,8},{8,16},{16,24},{1,9},{9,17},{17,25},{2,10},{10,18},{18,26},{... | collective-permute-start | bytes 1693448 | tf_op jit(solution)/shard_map/ppermute | solution.py:10
  314.3 9.1 slice-start.4
  328.5 3.1 copy-start.31
  329.3 11.1 %collective-permute-start.2 = (bf16[2,49,2880]{2,0,1:T(2,128)(2,1)S(1)}, bf16[2,49,2880]{2,0,1:T(2,128)(2,1)S(1)}, u32[]{:S(2)}, u32[]{:S(2)}) collective-permute-start(bf16[2,49,2880]{2,0,1:T(2,128)(2,1)S(1)} %copy.43), channel_id=1, source_target_pairs={{0,8},{8,16},{16,24},{1,9},{9,17},{17,25},{2,10},{10,18},{18,26},{... | collective-permute-start | bytes 1693448 | tf_op jit(solution)/shard_map/ppermute | solution.py:10
  345.4 2.7 copy-start.32
  346.2 11.1 %collective-permute-start.3 = (bf16[2,49,2880]{2,0,1:T(2,128)(2,1)S(1)}, bf16[2,49,2880]{2,0,1:T(2,128)(2,1)S(1)}, u32[]{:S(2)}, u32[]{:S(2)}) collective-permute-start(bf16[2,49,2880]{2,0,1:T(2,128)(2,1)S(1)} %copy.45), channel_id=1, source_target_pairs={{0,8},{8,16},{16,24},{1,9},{9,17},{17,25},{2,10},{10,18},{18,26},{... | collective-permute-start | bytes 1693448 | tf_op jit(solution)/shard_map/ppermute | solution.py:10
  362.4 11.2 %collective-permute-start.4 = (bf16[2,49,2880]{2,0,1:T(2,128)(2,1)S(1)}, bf16[2,49,2880]{2,0,1:T(2,128)(2,1)}, u32[]{:S(2)}, u32[]{:S(2)}) collective-permute-start(bf16[2,49,2880]{2,0,1:T(2,128)(2,1)S(1)} %copy.47), channel_id=1, source_target_pairs={{0,8},{8,16},{16,24},{1,9},{9,17},{17,25},{2,10},{10,18},{18,26},{... | collective-permute-start | bytes 1693448 | tf_op jit(solution)/shard_map/ppermute | solution.py:10
  367.7 10.8 %copy-start.15 = (bf16[1,2,49,2880]{3,1,2,0:T(2,128)(2,1)S(1)}, bf16[1,2,49,2880]{3,1,2,0:T(2,128)(2,1)}, u32[]{:S(2)}) copy-start(bf16[1,2,49,2880]{3,1,2,0:T(2,128)(2,1)} %get-tuple-element.15) | copy-start | bytes 1693444
  378.5 5.1 copy-start.9
  382.2 1.4 copy-start.45
  383.5 1.6 copy-start.34
  398.9 4.5 copy-start.16
  398.9 4.5 copy-start.35
  398.9 4.6 copy-start.36
  400.5 9.2 collective-permute-start.5
  403.4 3.4 copy-start.19
  405.5 1.3 copy-start.11
  406.8 2.9 copy-start.13
  409.0 2.7 copy-start.4
  409.7 3.0 copy-start.20
  412.7 1.3 copy-start.14
  428.0 13.2 %copy-start.5 = (bf16[1,2880,360]{2,1,0:T(8,128)(2,1)S(1)}, bf16[1,2880,360]{2,1,0:T(8,128)(2,1)}, u32[]{:S(2)}) copy-start(bf16[1,2880,360]{2,1,0:T(8,128)(2,1)} %all-gather.11.cloned.1.call-done) | copy-start | bytes 6220804
  428.0 11.2 %collective-permute-start.6 = (bf16[2,49,2880]{2,0,1:T(2,128)(2,1)S(1)}, bf16[2,49,2880]{2,0,1:T(2,128)(2,1)S(1)}, u32[]{:S(2)}, u32[]{:S(2)}) collective-permute-start(bf16[2,49,2880]{2,0,1:T(2,128)(2,1)S(1)} %copy.54), channel_id=1, source_target_pairs={{8,0},{16,8},{24,16},{9,1},{17,9},{25,17},{10,2},{18,10},{26,18},{... | collective-permute-start | bytes 1693448 | tf_op jit(solution)/shard_map/ppermute | solution.py:10
  439.2 3.0 copy-start.22
  457.5 13.2 %copy-start.6 = (bf16[1,2880,360]{2,1,0:T(8,128)(2,1)S(1)}, bf16[1,2880,360]{2,1,0:T(8,128)(2,1)}, u32[]{:S(2)}) copy-start(bf16[1,2880,360]{2,1,0:T(8,128)(2,1)} %all-gather.11.cloned.1.call-done) | copy-start | bytes 6220804
  457.5 11.2 %collective-permute-start.7 = (bf16[2,49,2880]{2,0,1:T(2,128)(2,1)S(1)}, bf16[2,49,2880]{2,0,1:T(2,128)(2,1)S(1)}, u32[]{:S(2)}, u32[]{:S(2)}) collective-permute-start(bf16[2,49,2880]{2,0,1:T(2,128)(2,1)S(1)} %copy.56), channel_id=1, source_target_pairs={{8,0},{16,8},{24,16},{9,1},{17,9},{25,17},{10,2},{18,10},{26,18},{... | collective-permute-start | bytes 1693448 | tf_op jit(solution)/shard_map/ppermute | solution.py:10
  468.6 3.0 copy-start.26
  486.9 13.2 %copy-start.7 = (bf16[1,2880,360]{2,1,0:T(8,128)(2,1)S(1)}, bf16[1,2880,360]{2,1,0:T(8,128)(2,1)}, u32[]{:S(2)}) copy-start(bf16[1,2880,360]{2,1,0:T(8,128)(2,1)} %all-gather.11.cloned.1.call-done) | copy-start | bytes 6220804
  486.9 11.2 %collective-permute-start.8 = (bf16[2,49,2880]{2,0,1:T(2,128)(2,1)S(1)}, bf16[2,49,2880]{2,0,1:T(2,128)(2,1)S(1)}, u32[]{:S(2)}, u32[]{:S(2)}) collective-permute-start(bf16[2,49,2880]{2,0,1:T(2,128)(2,1)S(1)} %copy.58), channel_id=1, source_target_pairs={{8,0},{16,8},{24,16},{9,1},{17,9},{25,17},{10,2},{18,10},{26,18},{... | collective-permute-start | bytes 1693448 | tf_op jit(solution)/shard_map/ppermute | solution.py:10
  498.1 3.0 copy-start.24
  516.4 13.2 %copy-start.46 = (bf16[3,2,360]{2,1,0:T(2,128)(2,1)S(1)}, bf16[3,2,360]{2,1,0:T(2,128)(2,1)}, u32[]{:S(2)}) copy-start(bf16[3,2,360]{2,1,0:T(2,128)(2,1)} %copy-done.45) | copy-start | bytes 12964
  516.4 11.1 %collective-permute-start.9 = (bf16[2,49,2880]{2,0,1:T(2,128)(2,1)S(1)}, bf16[2,49,2880]{2,0,1:T(2,128)(2,1)S(1)}, u32[]{:S(2)}, u32[]{:S(2)}) collective-permute-start(bf16[2,49,2880]{2,0,1:T(2,128)(2,1)S(1)} %copy.60), channel_id=1, source_target_pairs={{8,0},{16,8},{24,16},{9,1},{17,9},{25,17},{10,2},{18,10},{26,18},{... | collective-permute-start | bytes 1693448 | tf_op jit(solution)/shard_map/ppermute | solution.py:10
  527.4 2.1 copy-start.28
  531.7 1.3 copy-start.37
  531.7 1.3 copy-start.44
  531.8 139.1 %reduce-scatter.13.cloned.1.call-start = ((), (), s32[]{:S(2)}) async-start(), calls=%async_computation.7 | async-start | bytes 2488320
  531.8 1.3 copy-start.21
  533.1 4.2 copy-start.10
  536.1 1.3 copy-start.38
  536.1 1.3 copy-start.43
  539.0 1.4 copy-start.27
  539.0 1.4 copy-start.40
  539.0 1.4 copy-start.42
  540.4 4.3 copy-start.8
  542.0 2.7 copy-start.33
  548.6 452.6 %reduce-scatter.11.cloned.1.call-start = ((), (), s32[]{:S(2)}) async-start(), calls=%async_computation.6 | async-start | bytes 19077120
  552.8 1.9 copy-start.29
  554.0 1.6 copy-start.12
  1001.2 4.0 copy-start.1
  (5 other events, 5.5 us)
Sparse Core Ops, SparseCore 0:
  9.6 204.4 all-gather.6
  215.6 34.4 all-gather.8
  251.6 34.3 all-gather.10
  531.9 67.7 reduce-scatter.14
  603.5 67.3 reduce-scatter.12
  673.1 328.0 reduce-scatter.10
where the time goes:
time: 1020 us; the launch traced here: 1010 us
  waiting for transfers between devices  733 us (72%)
  matrix products  138 us (14%)
  local copies, waits for them, and re-layouts  52 us (5%)
  other arithmetic  44.8 us (4%)
  starting transfers between devices  29.2 us (3%)
  between operations  15.2 us (1%)
    unnamed x9, waiting for transfers between devices  428 us
    all_gather x1, waiting for transfers between devices, on_device(): lax.all_gather(weight[0], 'fsdp', axis=0, tiled=True)  186 us
    dot_general x17, matrix products, contract_cols(): lax.dot_general(left, right, (((1,), (1,)), ((), ())), preferred_element_...  75.2 us
    ppermute x10, waiting for transfers between devices, shifted(): lax.ppermute(value, axis, [(source, source + steps) for source in range(l...  58.2 us
    dot_general x6, matrix products, project(): result = jnp.dot(flat, matrix, preferred_element_type=jnp.float32)  34.1 us
    all_gather x1, waiting for transfers between devices, on_device(): lax.all_gather(excite[0], 'fsdp', axis=0, tiled=True)  34 us
    ppermute x10, starting transfers between devices, shifted(): lax.ppermute(value, axis, [(source, source + steps) for source in range(l...  28.7 us
    all_gather x1, waiting for transfers between devices, on_device(): lax.all_gather(squeeze[0], 'fsdp', axis=0, tiled=True)  26.3 us
  transfers between devices with their start and end apart: 16, of which 16 were waited for; matrix products, arithmetic and copies ran while one was open for 9% of the time, Pallas kernels for 0%

commit v1 on v0

v1 whole, which is shorter than its diff:
```python
import functools

import jax
import jax.numpy as jnp
from jax import lax
from jax.experimental import pallas as pl
from jax.experimental.pallas import tpu as pltpu
from jax.sharding import PartitionSpec as P

BF = jnp.bfloat16
F32 = jnp.float32
SUB = 8
PIECES = 3
VMEM_LIMIT = 62 * 1024 * 1024


def up(value, step):
    return -(-value // step) * step


def silu_slope(value):
    sigma = jax.nn.sigmoid(value)
    return sigma * (1.0 + value * (1.0 - sigma))


def nn(left, right):
    return lax.dot_general(left, right, (((1,), (0,)), ((), ())), preferred_element_type=F32)


def nt(left, right):
    return lax.dot_general(left, right, (((1,), (1,)), ((), ())), preferred_element_type=F32)


def tn(left, right):
    return lax.dot_general(left, right, (((0,), (0,)), ((), ())), preferred_element_type=F32)


class Loader:
    def __init__(self, meta, own, other, bufs, sems):
        self.meta, self.own, self.other, self.bufs, self.sems = meta, own, other, bufs, sems

    def copies(self, block, refs):
        w_pieces, s_pieces = refs
        w_buf, s_buf, e_buf = self.bufs
        slot = 0
        for index, piece in enumerate(w_pieces):
            rows = piece.shape[0]
            at = pl.ds(pl.multiple_of(self.meta[1 + index], 16), rows)
            yield pltpu.make_async_copy(piece, w_buf.at[block, at], self.sems.at[block, slot])
            slot += 1
        for index, piece in enumerate(s_pieces):
            rows = piece.shape[0] // 2
            at = pl.ds(pl.multiple_of(self.meta[1 + len(w_pieces) + index], 16), rows)
            for half, buf in enumerate((s_buf, e_buf)):
                source = piece.at[pl.ds(half * rows, rows)]
                yield pltpu.make_async_copy(source, buf.at[block, at], self.sems.at[block, slot])
                slot += 1

    def start(self, block):
        @pl.when(self.meta[0] == block)
        def _():
            for copy in self.copies(block, self.own):
                copy.start()

        @pl.when(self.meta[0] != block)
        def _():
            for copy in self.copies(block, self.other):
                copy.start()

    def wait(self, block):
        for copy in self.copies(block, self.own):
            copy.wait()


def image_masks(rows, images, pixels):
    row = lax.broadcasted_iota(jnp.int32, (rows, 1), 0)
    return [(row >= i * pixels) & (row < (i + 1) * pixels) for i in range(images)]


def per_image(value, masks):
    slot = lax.broadcasted_iota(jnp.int32, (SUB, 1), 0)
    total = jnp.zeros((SUB, value.shape[1]), F32)
    for i, mask in enumerate(masks):
        summed = jnp.sum(jnp.where(mask, value, 0.0), axis=0, keepdims=True)
        total = jnp.where(slot == i, summed, total)
    return total


def per_row(value, masks):
    spread = jnp.zeros((masks[0].shape[0], value.shape[1]), F32)
    for i, mask in enumerate(masks):
        spread = jnp.where(mask, value[i : i + 1, :], spread)
    return spread


def forward_kernel(cfg, meta, h_ref, *refs):
    n_w, n_s, images, pixels, tiles = cfg
    pieces, refs = refs[: 2 * (n_w + n_s)], refs[2 * (n_w + n_s) :]
    own = (pieces[:n_w], pieces[n_w : n_w + n_s])
    other = (pieces[n_w + n_s : 2 * n_w + n_s], pieces[2 * n_w + n_s :])
    mid_ref, out_ref, pre_ref, gate_ref, sq_ref, pool_ref, hid_ref = refs[:7]
    w_buf, s_buf, e_buf, act_ref, sems = refs[7:]
    loader = Loader(meta, own, other, (w_buf, s_buf, e_buf), sems)
    loader.start(0)
    loader.start(1)
    masks = image_masks(h_ref.shape[0], images, pixels)
    for block, (src, dst) in enumerate(((h_ref, mid_ref), (mid_ref, out_ref))):
        loader.wait(block)
        squeezed = jnp.zeros(sq_ref.shape[1:], F32)
        for low, width in tiles:
            cols = slice(low, low + width)
            pre = nn(src[...], w_buf[block, :, cols])
            pre_ref[block, :, cols] = pre
            active = (pre * jax.nn.sigmoid(pre)).astype(BF)
            act_ref[:, cols] = active
            pooled = (per_image(active.astype(F32), masks) / pixels).astype(BF)
            pool_ref[block, :, cols] = pooled.astype(F32)
            squeezed = squeezed + nn(pooled, s_buf[block, cols, :])
        sq_ref[block] = squeezed
        hidden = (squeezed * jax.nn.sigmoid(squeezed)).astype(BF)
        hid_ref[block] = hidden.astype(F32)
        for low, width in tiles:
            cols = slice(low, low + width)
            gate = jax.nn.sigmoid(nt(hidden, e_buf[block, cols, :]))
            gate_ref[block, :, cols] = gate
            gated = act_ref[:, cols].astype(F32) * per_row(gate, masks)
            dst[:, cols] = (src[:, cols].astype(F32) + gated).astype(BF)


def backward_kernel(cfg, meta, up_ref, pre_ref, gate_ref, sq_ref, *refs):
    n_w, n_s, images, pixels, tiles = cfg
    pieces, refs = refs[: 2 * (n_w + n_s)], refs[2 * (n_w + n_s) :]
    own = (pieces[:n_w], pieces[n_w : n_w + n_s])
    other = (pieces[n_w + n_s : 2 * n_w + n_s], pieces[2 * n_w + n_s :])
    out_ref, dpre_ref, dsq_ref, dex_ref = refs[:4]
    w_buf, s_buf, e_buf, mid_ref, flat_ref, sems = refs[4:]
    loader = Loader(meta, own, other, (w_buf, s_buf, e_buf), sems)
    loader.start(1)
    loader.start(0)
    masks = image_masks(up_ref.shape[0], images, pixels)
    for block, src, dst in ((1, up_ref, mid_ref), (0, mid_ref, out_ref)):
        loader.wait(block)
        d_hidden = jnp.zeros(dsq_ref.shape[1:], F32)
        for low, width in tiles:
            cols = slice(low, low + width)
            pre = pre_ref[block, :, cols]
            active = (pre * jax.nn.sigmoid(pre)).astype(BF).astype(F32)
            d_gate = per_image(src[:, cols].astype(F32) * active, masks)
            gate = gate_ref[block, :, cols]
            d_excite = (d_gate * gate * (1.0 - gate)).astype(BF)
            dex_ref[block, :, cols] = d_excite.astype(F32)
            d_hidden = d_hidden + nn(d_excite, e_buf[block, cols, :])
        d_squeezed = (d_hidden * silu_slope(sq_ref[block])).astype(BF)
        dsq_ref[block] = d_squeezed.astype(F32)
        for tile, (low, width) in enumerate(tiles):
            cols = slice(low, low + width)
            pre = pre_ref[block, :, cols]
            d_pool = nt(d_squeezed, s_buf[block, cols, :]) / pixels
            d_act = src[:, cols].astype(F32) * per_row(gate_ref[block, :, cols], masks)
            d_act = d_act + per_row(d_pool, masks)
            d_pre = (d_act * silu_slope(pre)).astype(BF)
            flat_ref[:, cols] = d_pre
            if width < dpre_ref.shape[3]:
                dpre_ref[block, tile] = jnp.zeros(dpre_ref.shape[2:], BF)
            dpre_ref[block, tile, :, :width] = d_pre
        for low, width in tiles:
            cols = slice(low, low + width)
            back = nt(flat_ref[...], w_buf[block, cols, :])
            dst[:, cols] = (src[:, cols].astype(F32) + back).astype(BF)


def run_pass(kernel, cfg, meta, dense, sets, outs, scratch, channels, hidden, flops):
    own, other = sets
    pieces = [*own[0], *own[1], *other[0], *other[1]]
    copies = len(own[0]) + 2 * len(own[1])
    vmem = pl.BlockSpec(memory_space=pltpu.VMEM)
    return pl.pallas_call(
        functools.partial(kernel, cfg),
        out_shape=[jax.ShapeDtypeStruct(shape, dtype) for shape, dtype in outs],
        in_specs=[pl.BlockSpec(memory_space=pltpu.SMEM)]
        + [vmem] * len(dense)
        + [pl.BlockSpec(memory_space=pl.ANY)] * len(pieces),
        out_specs=[vmem] * len(outs),
        scratch_shapes=[
            pltpu.VMEM((2, channels, channels), BF),
            pltpu.VMEM((2, channels, hidden), BF),
            pltpu.VMEM((2, channels, hidden), BF),
            *scratch,
            pltpu.SemaphoreType.DMA((2, copies)),
        ],
        compiler_params=pltpu.CompilerParams(vmem_limit_bytes=VMEM_LIMIT),
        cost_estimate=pl.CostEstimate(
            flops=flops, bytes_accessed=2 * 2 * channels * (channels + 2 * hidden), transcendentals=0
        ),
    )(meta, *dense, *pieces)


def swap(value, axis, stride=1):
    count = lax.axis_size(axis)
    return lax.ppermute(value, axis, [(i, i ^ stride) for i in range(count)])


def rotate(value, axis, steps):
    count = lax.axis_size(axis)
    return lax.ppermute(value, axis, [(i, (i + steps) % count) for i in range(count)])


def over_fsdp(value):
    count = lax.axis_size("fsdp")
    return [value] + [rotate(value, "fsdp", -step) for step in range(1, count)]


def gather_weights(weight, squeeze, excite):
    fsdp, dp = lax.axis_size("fsdp"), lax.axis_size("dp")
    rows = weight.shape[0]
    pair = jnp.concatenate([squeeze, excite], axis=0)
    if fsdp != 2 or dp % 2 or rows % (2 * 16 * PIECES):
        whole = lax.all_gather(weight, "fsdp", axis=0, tiled=True)
        both = [lax.all_gather(part, "fsdp", axis=0, tiled=True) for part in (squeeze, excite)]
        zero = jnp.int32(0)
        return [whole], [jnp.concatenate(both, axis=0)], [zero], [zero]
    mine = lax.axis_index("fsdp") * rows
    far = rows - mine
    parity = lax.axis_index("dp") % 2
    half = rows // 2
    step = half // PIECES
    near_at = far + parity * half
    cross_at = far + (1 - parity) * half
    near_s = swap(
        jnp.concatenate(
            [lax.dynamic_slice_in_dim(part, parity * half, half, 0) for part in (squeeze, excite)], 0
        ),
        "fsdp",
    )
    near = [
        swap(lax.dynamic_slice_in_dim(weight, parity * half + i * step, step, 0), "fsdp")
        for i in range(PIECES)
    ]
    cross_s = swap(near_s, "dp")
    cross = [swap(part, "dp") for part in near]
    w_at = [mine] + [near_at + i * step for i in range(PIECES)]
    w_at += [cross_at + i * step for i in range(PIECES)]
    return [weight, *near, *cross], [pair, near_s, cross_s], w_at, [mine, near_at, cross_at]


def shifted(value, axis, steps):
    count = lax.axis_size(axis)
    leading, last = (max(0, -steps), min(count, count - steps))
    return lax.ppermute(value, axis, [(source, source + steps) for source in range(leading, last)])


def on_device(inputs, cotangent, plan, weight, squeeze, excite):
    fsdp, dp = lax.axis_size("fsdp"), lax.axis_size("dp")
    sections = lax.axis_size("segment")
    section = lax.axis_index("segment")
    core = section % 2
    mesh_f, mesh_z = lax.axis_index("fsdp"), lax.axis_index("dp")
    micro, images_dev, pixels, channels = inputs.shape
    hidden = squeeze.shape[2]
    per_core = images_dev // 2
    images = micro * per_core
    rows = up(images * pixels, 16)
    group = up(-(-channels // dp), 128)
    tiles = [(low, min(group, channels - low)) for low in range(0, channels, group)]

    w_own, s_own, w_at, s_at = gather_weights(weight[0], squeeze[0], excite[0])
    w_other = [swap(part, "segment") for part in w_own]
    s_other = [swap(part, "segment") for part in s_own]
    sets = ((w_own, s_own), (w_other, s_other))
    meta = jnp.stack([core, *w_at, *s_at]).astype(jnp.int32)
    cfg = (len(w_own), len(s_own), images, pixels, tiles)

    def flat(maps):
        mine = lax.dynamic_slice_in_dim(maps, core * per_core, per_core, 1)
        mine = mine.reshape(images * pixels, channels)
        return jnp.pad(mine, ((0, rows - images * pixels), (0, 0)))

    def forward_pass(h_in):
        outs = [
            ((rows, channels), BF),
            ((rows, channels), BF),
            ((2, rows, channels), F32),
            ((2, SUB, channels), F32),
            ((2, SUB, hidden), F32),
            ((2, SUB, channels), F32),
            ((2, SUB, hidden), F32),
        ]
        scratch = [pltpu.VMEM((rows, channels), BF)]
        flops = 4 * rows * channels * channels
        return run_pass(
            forward_kernel, cfg, meta, [h_in], sets, outs, scratch, channels, hidden, flops
        )

    def backward_pass(d_out, pre, gate, sq):
        outs = [
            ((rows, channels), BF),
            ((2, len(tiles), rows, group), BF),
            ((2, SUB, hidden), F32),
            ((2, SUB, channels), F32),
        ]
        scratch = [pltpu.VMEM((rows, channels), BF), pltpu.VMEM((rows, channels), BF)]
        flops = 4 * rows * channels * channels
        return run_pass(
            backward_kernel,
            cfg,
            meta,
            [d_out, pre, gate, sq],
            sets,
            outs,
            scratch,
            channels,
            hidden,
            flops,
        )

    stages = sections // 2
    stage = section // 2
    h_in = flat(inputs[plan])
    d_in = flat(cotangent)
    kept = None
    for step in range(stages):
        mid, out, pre, gate, sq, pool, hid = forward_pass(h_in)
        new = (h_in, mid, pre, gate, sq, pool, hid)
        last = new
        if step == 0:
            kept = new
        elif step < stages - 1:
            kept = [jnp.where(stage == step, a, b) for a, b in zip(new, kept)]
        if step < stages - 1:
            h_in = shifted(out, "segment", 2)
    final = stage == stages - 1
    h_a, h_b, pool, hid = [
        jnp.where(final, last[i], kept[i]) for i in (0, 1, 5, 6)
    ]

    def swap_blocks(first, second):
        keep = jnp.where(core == 0, first, second)
        give = jnp.where(core == 0, second, first)
        return keep, swap(give, "segment")

    part = channels // fsdp

    def channel_part(value, owner):
        return lax.dynamic_slice_in_dim(value, owner * part, part, 1)

    h_pair = jnp.concatenate(swap_blocks(h_a, h_b), axis=0)
    h_mine = [channel_part(h_pair, mesh_f)]
    for step in range(1, fsdp):
        h_mine.append(rotate(channel_part(h_pair, (mesh_f - step) % fsdp), "fsdp", -step))
    h_mine = jnp.concatenate(h_mine, axis=0)
    h_all = lax.all_gather(h_mine, "dp", axis=0, tiled=False)
    early = jnp.concatenate([pool, hid], axis=2).astype(BF)
    early = jnp.concatenate(swap_blocks(early[0], early[1]), axis=0)
    early = lax.all_gather(early, ("fsdp", "dp"), axis=0, tiled=True)

    result = backward_pass(d_in, *last[2:5])
    for step in range(1, stages):
        d_out = shifted(result[0], "segment", -2)
        saved = kept[2:5]
        new = backward_pass(d_out, *saved)
        here = stage == stages - 1 - step
        result = [new[0]] + [jnp.where(here, a, b) for a, b in zip(new[1:], result[1:])]
    d_pre, d_sq, d_ex = result[1:]

    late = jnp.concatenate([d_ex, d_sq], axis=2).astype(BF)
    late = jnp.concatenate(swap_blocks(late[0], late[1]), axis=0)
    late = lax.all_gather(late, ("fsdp", "dp"), axis=0, tiled=True)

    d_pair = jnp.concatenate(swap_blocks(d_pre[0], d_pre[1]), axis=1)
    total = None
    for step in range(dp):
        piece = lax.dynamic_index_in_dim(d_pair, (mesh_z + step) % dp, 0, keepdims=False)
        if step:
            piece = rotate(piece, "dp", step)
        piece = jnp.concatenate(over_fsdp(piece), axis=0)
        source = lax.dynamic_index_in_dim(h_all, (mesh_z - step) % dp, 0, keepdims=False)
        term = tn(source, piece)
        total = term if total is None else total + term
    total = total.astype(BF)
    own_rows = part // dp
    gathered = jnp.zeros((dp, own_rows, group), BF)
    for step in range(dp):
        block = lax.dynamic_slice_in_dim(total, ((mesh_z + step) % dp) * own_rows, own_rows, 0)
        if step:
            block = rotate(block, "dp", step)
        gathered = lax.dynamic_update_index_in_dim(gathered, block, (mesh_z - step) % dp, 0)
    grad_w = jnp.concatenate([gathered[i, :, :w] for i, (_, w) in enumerate(tiles)], axis=1)

    first = mesh_f * part + mesh_z * own_rows
    pool_rows = lax.dynamic_slice_in_dim(early[:, :channels], first, own_rows, 1)
    dex_rows = lax.dynamic_slice_in_dim(late[:, :channels], first, own_rows, 1)
    grad_s = tn(pool_rows, late[:, channels:])
    grad_e = tn(dex_rows, early[:, channels:])
    return (grad_w.astype(F32)[None], grad_s[None], grad_e[None])


def solution(mesh):
    placed = (
        P(None, ("fsdp", "dp"), None, None),
        P(None, ("fsdp", "dp"), None, None),
        P(),
        P("segment", "fsdp", None),
        P("segment", "fsdp", None),
        P("segment", "fsdp", None),
    )
    return jax.shard_map(
        on_device,
        mesh=mesh,
        in_specs=placed,
        out_specs=(
            P("segment", ("fsdp", "dp"), None),
            P("segment", ("fsdp", "dp"), None),
            P("segment", ("fsdp", "dp"), None),
        ),
        check_vma=False,
    )
```

time: 1020 us -> 652 us (0.64)
  waiting for transfers between devices: 733 us -> 271 us
  blocking collectives: 0 us -> 160 us
  matrix products: 138 us -> 14.3 us
  Pallas kernels: 0 us -> 93.5 us
  other arithmetic: 44.8 us -> 14.7 us
    unnamed x9 -> x1, waiting for transfers between devices: 428 us -> 0.02 us
    all_gather x3 -> x1, waiting for transfers between devices: 247 us -> 0.01 us  [on_device(): h_all = lax.all_gather(h_mine, 'dp', axis=0, tiled=False)]
    ppermute x0 -> x33, waiting for transfers between devices: none -> 227 us  [the longest x22 172 us: swap(): return lax.ppermute(value, axis, [(i, i ^ stride) for i in range(count)])]
    all_gather x0 -> x2, blocking collectives: none -> 160 us  [the longest x1 114 us: on_device(): early = lax.all_gather(early, ('fsdp', 'dp'), axis=0, tiled=True)]
    dot_general x38 -> x6, matrix products: 138 us -> 14.3 us  [tn(): lax.dot_general(left, right, (((0,), (0,)), ((), ())), preferred_element_...]
    pallas_call x0 -> x4, Pallas kernels: none -> 93.5 us  [run_pass(): pl.pallas_call(functools.partial(kernel, cfg), out_shape=[jax.ShapeDtypeS...]
    ppermute x0 -> x33, starting transfers between devices: none -> 26 us  [the longest x11 18.4 us: rotate(): lax.ppermute(value, axis, [(i, (i + steps) % count) for i in range(count)])]
    ppermute x10 -> x2, starting transfers between devices: 28.7 us -> 3.17 us  [shifted(): lax.ppermute(value, axis, [(source, source + steps) for source in range(l...]
  transfers between devices with their start and end apart: 16 -> 36, of which waited for: 16 -> 16; matrix products, arithmetic and copies ran while one was open for 9% -> 9% of each run, Pallas kernels for 0% -> 8%
where the time goes in v1:
time: 652 us; the launch traced here: 642 us
  waiting for transfers between devices  271 us (42%)
  blocking collectives  160 us (25%)
  Pallas kernels  93.5 us (14%)
  local copies, waits for them, and re-layouts  44.2 us (7%)
  starting transfers between devices  29.2 us (4%)
  between operations  14.9 us (2%)
  other arithmetic  14.7 us (2%)
  matrix products  14.3 us (2%)
    ppermute x22, waiting for transfers between devices, swap(): return lax.ppermute(value, axis, [(i, i ^ stride) for i in range(count)])  172 us
    all_gather x1, blocking collectives, on_device(): early = lax.all_gather(early, ('fsdp', 'dp'), axis=0, tiled=True)  114 us
    pallas_call x4, Pallas kernels, run_pass(): pl.pallas_call(functools.partial(kernel, cfg), out_shape=[jax.ShapeDtypeS...  93.5 us
    ppermute x11, waiting for transfers between devices, rotate(): lax.ppermute(value, axis, [(i, (i + steps) % count) for i in range(count)])  55.1 us
    all_gather x1, blocking collectives, on_device(): late = lax.all_gather(late, ('fsdp', 'dp'), axis=0, tiled=True)  46.8 us
    ppermute x2, waiting for transfers between devices, shifted(): lax.ppermute(value, axis, [(source, source + steps) for source in range(l...  43.3 us
    ppermute x11, starting transfers between devices, rotate(): lax.ppermute(value, axis, [(i, (i + steps) % count) for i in range(count)])  18.4 us
    dot_general x6, matrix products, tn(): lax.dot_general(left, right, (((0,), (0,)), ((), ())), preferred_element_...  14.3 us
  transfers between devices with their start and end apart: 36, of which 16 were waited for; matrix products, arithmetic and copies ran while one was open for 9% of the time, Pallas kernels for 8%

profile of v1, /device:TPU:10, one launch (start us, length us, event | category | flops | bytes accessed | tf_op | source)
XLA Modules:
  0.0 641.9 jit_solution(1304174346648816863)
XLA Ops:
  7.4 4.5 dynamic-slice_bitcast_fusion
  11.8 1.5 collective-permute-start
  13.5 1.1 pad_maximum_fusion.2
  15.2 1.5 collective-permute-start.1
  17.2 1.6 pad_maximum_fusion.refs_7_
  18.8 4.1 copy.9
  22.9 46.7 %collective-permute-done.6.refs_8_ = bf16[1440,360]{1,0:T(8,128)(2,1)} collective-permute-done((bf16[1440,360]{1,0:T(8,128)(2,1)}, bf16[1440,360]{1,0:T(8,128)(2,1)}, u32[]{:S(2)}, u32[]{:S(2)}) %collective-permute-start.6) | collective-permute-done | bytes 1036832 | tf_op jit(solution)/shard_map/ppermute | solution.py:200
  70.1 29.8 %collective-permute-done.1.refs_2_ = bf16[240,2880]{1,0:T(8,128)(2,1)} collective-permute-done((bf16[240,2880]{1,0:T(8,128)(2,1)}, bf16[240,2880]{1,0:T(8,128)(2,1)}, u32[]{:S(2)}, u32[]{:S(2)}) %collective-permute-start.1) | collective-permute-done | bytes 1382432 | tf_op jit(solution)/shard_map/ppermute | solution.py:200
  100.4 29.4 %collective-permute-done.2.refs_3_ = bf16[240,2880]{1,0:T(8,128)(2,1)} collective-permute-done((bf16[240,2880]{1,0:T(8,128)(2,1)}, bf16[240,2880]{1,0:T(8,128)(2,1)}, u32[]{:S(2)}, u32[]{:S(2)}) %collective-permute-start.2) | collective-permute-done | bytes 1382432 | tf_op jit(solution)/shard_map/ppermute | solution.py:200
  130.2 2.5 collective-permute-done.16.refs_18_
  134.2 29.6 %collective-permute-done.4.refs_5_ = bf16[240,2880]{1,0:T(8,128)(2,1)} collective-permute-done((bf16[240,2880]{1,0:T(8,128)(2,1)}, bf16[240,2880]{1,0:T(8,128)(2,1)}, u32[]{:S(2)}, u32[]{:S(2)}) %collective-permute-start.4) | collective-permute-done | bytes 1382432 | tf_op jit(solution)/shard_map/ppermute | solution.py:200
  163.8 29.9 %collective-permute-done.5.refs_6_ = bf16[240,2880]{1,0:T(8,128)(2,1)} collective-permute-done((bf16[240,2880]{1,0:T(8,128)(2,1)}, bf16[240,2880]{1,0:T(8,128)(2,1)}, u32[]{:S(2)}, u32[]{:S(2)}) %collective-permute-start.5) | collective-permute-done | bytes 1382432 | tf_op jit(solution)/shard_map/ppermute | solution.py:200
  194.8 0.6 copy-done.4
  195.4 1.1 copy-done.5
  196.9 6.0 gather_fusion
  202.9 7.6 %dynamic-slice_reduce_fusion.1 = bf16[3,49,2880]{2,1,0:T(8,128)(2,1)} fusion(bf16[3,2,49,2880]{3,1,2,0:T(2,128)(2,1)} %gather_fusion, s32[]{:T(128)S(6)} %select_n.248), kind=kLoop, calls=%fused_computation.31 | loop fusion | bytes 1693444 | tf_op jit(solution)/shard_map/dynamic_slice | solution.py:274
  210.5 1.6 reshape.76
  212.1 1.0 pad.7.h_ref
  213.1 0.7 stack.38.meta
  213.8 4.4 copy.10.refs_17_
  218.2 21.8 %shard_map.85 = (bf16[160,2880]{1,0:T(8,128)(2,1)}, bf16[160,2880]{1,0:T(8,128)(2,1)}, f32[2,160,2880]{2,1,0:T(8,128)}, f32[2,8,2880]{2,1,0:T(8,128)}, f32[2,8,3...) custom-call(s32[11]{0:T(128)} %stack.38.meta, bf16[160,2880]{1,0:T(8,128)(2,1)} %pad.7.h_ref, ...), custom_call_target="tpu_custom_call" | custom-call | flops 5308416000 | bytes 41472000 | tf_op jit(solution)/shard_map/pallas_call | solution.py:177
  240.0 1.7 collective-permute-start.18
  241.7 23.4 %collective-permute-done.18.h_ref = bf16[160,2880]{1,0:T(8,128)(2,1)} collective-permute-done((bf16[160,2880]{1,0:T(8,128)(2,1)}, bf16[160,2880]{1,0:T(8,128)(2,1)}, u32[]{:S(2)}, u32[]{:S(2)}) %collective-permute-start.18) | collective-permute-done | bytes 921632 | tf_op jit(solution)/shard_map/ppermute | solution.py:249
  265.1 21.6 %shard_map.86 = (bf16[160,2880]{1,0:T(8,128)(2,1)}, bf16[160,2880]{1,0:T(8,128)(2,1)}, f32[2,160,2880]{2,1,0:T(8,128)}, f32[2,8,2880]{2,1,0:T(8,128)}, f32[2,8,3...) custom-call(s32[11]{0:T(128)} %stack.38.meta, bf16[160,2880]{1,0:T(8,128)(2,1)} %collective-permute-done.18.h_ref, ...), custom_call_target="tpu_custom_call" | custom-call | flops 5308416000 | bytes 41472000 | tf_op jit(solution)/shard_map/pallas_call | solution.py:177
  286.7 3.0 broadcast_select_fusion.3
  289.8 2.7 collective-permute-done.19
  292.5 1.0 copy-done.10
  293.5 2.3 fusion.15
  295.7 1.6 collective-permute-start.20
  297.3 22.3 %collective-permute-done.20 = bf16[320,1440]{1,0:T(8,128)(2,1)S(1)} collective-permute-done((bf16[320,1440]{1,0:T(8,128)(2,1)S(1)}, bf16[320,1440]{1,0:T(8,128)(2,1)S(1)}, u32[]{:S(2)}, u32[]{:S(2)}) %collective-permute-start.20) | collective-permute-done | bytes 921632 | tf_op jit(solution)/shard_map/ppermute | solution.py:205
  319.6 1.5 pad_maximum_fusion.1
  321.2 1.3 copy-done.9
  322.5 5.3 dynamic-slice_reduce_fusion
  328.2 1.0 pad.8.up_ref
  329.2 26.0 %shard_map.87 = (bf16[160,2880]{1,0:T(8,128)(2,1)}, bf16[2,4,160,768]{3,2,1,0:T(8,128)(2,1)}, f32[2,8,360]{2,1,0:T(8,128)}, f32[2,8,2880]{2,1,0:T(8,128)}) custom-call(s32[11]{0:T(128)} %stack.38.meta, bf16[160,2880]{1,0:T(8,128)(2,1)} %pad.8.up_ref, f32[2,160,2880]{2,1,0:T(8,128)} %get-tuple-element.26.pre_ref, f32[2,8,2880]{2,1,0:T(8,128)} %get-tuple-element.27.gate_ref, ...), custom_call_target="tpu_custom_call" | custom-call | flops 5308416000 | bytes 41472000 | tf_op jit(solution)/shard_map/pallas_call | solution.py:177
  355.2 1.5 collective-permute-start.21
  356.9 19.9 %collective-permute-done.21.up_ref = bf16[160,2880]{1,0:T(8,128)(2,1)S(1)} collective-permute-done((bf16[160,2880]{1,0:T(8,128)(2,1)}, bf16[160,2880]{1,0:T(8,128)(2,1)S(1)}, u32[]{:S(2)}, u32[]{:S(2)}) %collective-permute-start.21) | collective-permute-done | bytes 921632 | tf_op jit(solution)/shard_map/ppermute | solution.py:249
  376.8 1.0 copy-done.11
  377.8 24.1 %shard_map.88 = (bf16[160,2880]{1,0:T(8,128)(2,1)}, bf16[2,4,160,768]{3,2,1,0:T(8,128)(2,1)}, f32[2,8,360]{2,1,0:T(8,128)}, f32[2,8,2880]{2,1,0:T(8,128)}) custom-call(s32[11]{0:T(128)} %stack.38.meta, bf16[160,2880]{1,0:T(8,128)(2,1)} %copy-done.11, f32[2,160,2880]{2,1,0:T(8,128)} %get-tuple-element.30.pre_ref, f32[2,8,2880]{2,1,0:T(8,128)} %get-tuple-element.31.gate_ref, ...), custom_call_target="tpu_custom_call" | custom-call | flops 5308416000 | bytes 41472000 | tf_op jit(solution)/shard_map/pallas_call | solution.py:177
  401.9 1.8 broadcast_select_fusion
  404.7 1.7 collective-permute-done.22
  406.6 1.6 collective-permute-start.24
  408.2 1.3 collective-permute-start.26
  409.7 1.6 collective-permute-start.23
  411.2 1.7 collective-permute-start.28
  413.0 113.6 %all_gather.14 = bf16[128,3240]{1,0:T(8,128)(2,1)S(1)} all-gather(bf16[16,3240]{1,0:T(8,128)(2,1)S(1)} %pad_maximum_fusion.3), channel_id=1, replica_groups=mesh['segment'=4,'fsdp'=2,'dp'=4] {'fsdp','dp'}, dimensions={0}, use_global_device_ids=true | all-gather | bytes 933120 | tf_op jit(solution)/shard_map/all_gather | solution.py:354
  526.6 2.0 collective-permute-start.25
  528.7 0.7 pad_maximum_fusion.4
  529.4 1.9 collective-permute-start.29
  531.3 3.7 fusion.8
  535.0 6.2 collective-permute-done.25
  541.2 3.1 fusion.6
  544.3 7.4 %collective-permute-done.27 = bf16[320,768]{1,0:T(8,128)(2,1)} collective-permute-done((bf16[320,768]{1,0:T(8,128)(2,1)}, bf16[320,768]{1,0:T(8,128)(2,1)}, u32[]{:S(2)}, u32[]{:S(2)}) %collective-permute-start.27) | collective-permute-done | bytes 491552 | tf_op jit(solution)/shard_map/ppermute | solution.py:205
  551.7 3.1 fusion.4
  554.8 2.0 collective-permute-done.29
  556.9 2.1 add_convert_fusion
  559.1 2.4 collective-permute-start.30
  561.5 46.8 %all_gather.15 = bf16[128,3240]{1,0:T(8,128)(2,1)S(1)} all-gather(bf16[16,3240]{1,0:T(8,128)(2,1)S(1)} %copy-done.13), channel_id=1, replica_groups=mesh['segment'=4,'fsdp'=2,'dp'=4] {'fsdp','dp'}, dimensions={0}, use_global_device_ids=true | all-gather | bytes 933120 | tf_op jit(solution)/shard_map/all_gather | solution.py:367
  608.5 1.2 convolution_bitcast_fusion
  609.6 1.2 convolution_bitcast_fusion.1
  610.8 4.1 collective-permute-start.32
  615.1 15.8 %collective-permute-done.31 = bf16[360,768]{1,0:T(8,128)(2,1)S(1)} collective-permute-done((bf16[360,768]{1,0:T(8,128)(2,1)S(1)}, bf16[360,768]{1,0:T(8,128)(2,1)S(1)}, u32[]{:S(2)}, u32[]{:S(2)}) %collective-permute-start.31) | collective-permute-done | bytes 552992 | tf_op jit(solution)/shard_map/ppermute | solution.py:205
  631.0 1.4 collective-permute-done.32
  632.6 2.3 maximum_convert_fusion
  (108 shorter events, 8.5 us)
Async XLA Ops:
  7.2 189.8 %copy-start = (bf16[3,2,49,2880]{3,1,2,0:T(2,128)(2,1)S(1)}, bf16[3,2,49,2880]{3,1,2,0:T(2,128)(2,1)}, u32[]{:S(2)}) copy-start(bf16[3,2,49,2880]{3,1,2,0:T(2,128)(2,1)} %param.6) | copy-start | bytes 5080324
  7.2 524.1 %all-gather.3.cloned.1.call-start = ((), (), s32[]{:S(2)}) async-start(), calls=%async_computation | async-start | bytes 9830400 | tf_op jit(solution)/shard_map/all_gather | solution.py:351
  7.2 211.0 %collective-permute-start.8 = (bf16[1440,2880]{1,0:T(8,128)(2,1)}, bf16[1440,2880]{1,0:T(8,128)(2,1)}, u32[]{:S(2)}, u32[]{:S(2)}) collective-permute-start(bf16[1440,2880]{1,0:T(8,128)(2,1)} %bitcast.68), channel_id=1, source_target_pairs={{0,8},{8,0},{16,24},{24,16},{1,9},{9,1},{17,25},{25,17},{2,10},{10... | collective-permute-start | bytes 24883208 | tf_op jit(solution)/shard_map/ppermute | solution.py:200
  7.3 6.0 copy-start.7
  7.4 6.0 copy-start.8
  11.8 58.2 %collective-permute-start = (bf16[240,2880]{1,0:T(8,128)(2,1)}, bf16[240,2880]{1,0:T(8,128)(2,1)S(1)}, u32[]{:S(2)}, u32[]{:S(2)}) collective-permute-start(bf16[240,2880]{1,0:T(8,128)(2,1)} %get-tuple-element.44), channel_id=1, source_target_pairs={{0,4},{4,0},{1,5},{5,1},{2,6},{6,2},{3,7},{7,3},{8,12},{12,8},{9,1... | collective-permute-start | bytes 4147208 | tf_op jit(solution)/shard_map/ppermute | solution.py:200
  14.7 55.0 %collective-permute-start.6 = (bf16[1440,360]{1,0:T(8,128)(2,1)}, bf16[1440,360]{1,0:T(8,128)(2,1)}, u32[]{:S(2)}, u32[]{:S(2)}) collective-permute-start(bf16[1440,360]{1,0:T(8,128)(2,1)} %pad_maximum_fusion.2), channel_id=1, source_target_pairs={{0,4},{4,0},{1,5},{5,1},{2,6},{6,2},{3,7},{7,3},{8,12},{12,8},{9,1... | collective-permute-start | bytes 3110408 | tf_op jit(solution)/shard_map/ppermute | solution.py:200
  15.2 84.8 %collective-permute-start.1 = (bf16[240,2880]{1,0:T(8,128)(2,1)}, bf16[240,2880]{1,0:T(8,128)(2,1)}, u32[]{:S(2)}, u32[]{:S(2)}) collective-permute-start(bf16[240,2880]{1,0:T(8,128)(2,1)} %get-tuple-element.45), channel_id=1, source_target_pairs={{0,4},{4,0},{1,5},{5,1},{2,6},{6,2},{3,7},{7,3},{8,12},{12,8},{9,1... | collective-permute-start | bytes 4147208 | tf_op jit(solution)/shard_map/ppermute | solution.py:200
  16.7 113.0 %collective-permute-start.2 = (bf16[240,2880]{1,0:T(8,128)(2,1)}, bf16[240,2880]{1,0:T(8,128)(2,1)}, u32[]{:S(2)}, u32[]{:S(2)}) collective-permute-start(bf16[240,2880]{1,0:T(8,128)(2,1)} %get-tuple-element.43), channel_id=1, source_target_pairs={{0,4},{4,0},{1,5},{5,1},{2,6},{6,2},{3,7},{7,3},{8,12},{12,8},{9,1... | collective-permute-start | bytes 4147208 | tf_op jit(solution)/shard_map/ppermute | solution.py:200
  18.8 178.1 %copy-start.22 = (s32[3]{0:T(128)S(1)}, s32[3]{0:T(128)}, u32[]{:S(2)}) copy-start(s32[3]{0:T(128)} %param.8) | copy-start | bytes 40
  69.6 60.1 %collective-permute-start.7 = (bf16[1440,360]{1,0:T(8,128)(2,1)}, bf16[1440,360]{1,0:T(8,128)(2,1)}, u32[]{:S(2)}, u32[]{:S(2)}) collective-permute-start(bf16[1440,360]{1,0:T(8,128)(2,1)} %collective-permute-done.6.refs_8_), channel_id=1, source_target_pairs={{0,1},{1,0},{2,3},{3,2},{4,5},{5,4},{6,7},{7,6},{8,9},{9,8},{10,11... | collective-permute-start | bytes 3110408 | tf_op jit(solution)/shard_map/ppermute | solution.py:200
  70.1 132.8 %copy-start.2 = (bf16[240,2880]{1,0:T(8,128)(2,1)}, bf16[240,2880]{1,0:T(8,128)(2,1)S(1)}, u32[]{:S(2)}) copy-start(bf16[240,2880]{1,0:T(8,128)(2,1)S(1)} %collective-permute-done.refs_1_) | copy-start | bytes 4147204
  70.1 63.6 %collective-permute-start.15 = (bf16[2880,360]{0,1:T(8,128)(2,1)}, bf16[2880,360]{0,1:T(8,128)(2,1)}, u32[]{:S(2)}, u32[]{:S(2)}) collective-permute-start(bf16[2880,360]{0,1:T(8,128)(2,1)} %copy.9), channel_id=1, source_target_pairs={{0,8},{8,0},{16,24},{24,16},{1,9},{9,1},{17,25},{25,17},{2,10},{10... | collective-permute-start | bytes 6220808 | tf_op jit(solution)/shard_map/ppermute | solution.py:200
  99.9 33.9 %collective-permute-start.3 = (bf16[240,2880]{1,0:T(8,128)(2,1)S(1)}, bf16[240,2880]{1,0:T(8,128)(2,1)}, u32[]{:S(2)}, u32[]{:S(2)}) collective-permute-start(bf16[240,2880]{1,0:T(8,128)(2,1)S(1)} %collective-permute-done.refs_1_), channel_id=1, source_target_pairs={{0,1},{1,0},{2,3},{3,2},{4,5},{5,4},{6,7},{7,6},{8,9},{9,8},{10,11... | collective-permute-start | bytes 4147208 | tf_op jit(solution)/shard_map/ppermute | solution.py:200
  129.7 3.0 collective-permute-start.16
  129.7 34.1 %collective-permute-start.4 = (bf16[240,2880]{1,0:T(8,128)(2,1)}, bf16[240,2880]{1,0:T(8,128)(2,1)}, u32[]{:S(2)}, u32[]{:S(2)}) collective-permute-start(bf16[240,2880]{1,0:T(8,128)(2,1)} %collective-permute-done.1.refs_2_), channel_id=1, source_target_pairs={{0,1},{1,0},{2,3},{3,2},{4,5},{5,4},{6,7},{7,6},{8,9},{9,8},{10,11... | collective-permute-start | bytes 4147208 | tf_op jit(solution)/shard_map/ppermute | solution.py:200
  132.7 1.0 copy-start.6
  132.7 61.0 %collective-permute-start.5 = (bf16[240,2880]{1,0:T(8,128)(2,1)}, bf16[240,2880]{1,0:T(8,128)(2,1)}, u32[]{:S(2)}, u32[]{:S(2)}) collective-permute-start(bf16[240,2880]{1,0:T(8,128)(2,1)} %collective-permute-done.2.refs_3_), channel_id=1, source_target_pairs={{0,1},{1,0},{2,3},{3,2},{4,5},{5,4},{6,7},{7,6},{8,9},{9,8},{10,11... | collective-permute-start | bytes 4147208 | tf_op jit(solution)/shard_map/ppermute | solution.py:200
  133.7 60.0 %collective-permute-start.10 = (bf16[240,2880]{1,0:T(8,128)(2,1)}, bf16[240,2880]{1,0:T(8,128)(2,1)S(1)}, u32[]{:S(2)}, u32[]{:S(2)}) collective-permute-start(bf16[240,2880]{1,0:T(8,128)(2,1)} %collective-permute-done.1.refs_2_), channel_id=1, source_target_pairs={{0,8},{8,0},{16,24},{24,16},{1,9},{9,1},{17,25},{25,17},{2,10},{10... | collective-permute-start | bytes 4147208 | tf_op jit(solution)/shard_map/ppermute | solution.py:200
  133.9 60.4 %collective-permute-start.11 = (bf16[240,2880]{1,0:T(8,128)(2,1)}, bf16[240,2880]{1,0:T(8,128)(2,1)S(1)}, u32[]{:S(2)}, u32[]{:S(2)}) collective-permute-start(bf16[240,2880]{1,0:T(8,128)(2,1)} %collective-permute-done.2.refs_3_), channel_id=1, source_target_pairs={{0,8},{8,0},{16,24},{24,16},{1,9},{9,1},{17,25},{25,17},{2,10},{10... | collective-permute-start | bytes 4147208 | tf_op jit(solution)/shard_map/ppermute | solution.py:200
  163.8 30.5 %collective-permute-start.9 = (bf16[240,2880]{1,0:T(8,128)(2,1)S(1)}, bf16[240,2880]{1,0:T(8,128)(2,1)S(1)}, u32[]{:S(2)}, u32[]{:S(2)}) collective-permute-start(bf16[240,2880]{1,0:T(8,128)(2,1)S(1)} %collective-permute-done.refs_1_), channel_id=1, source_target_pairs={{0,8},{8,0},{16,24},{24,16},{1,9},{9,1},{17,25},{25,17},{2,10},{10... | collective-permute-start | bytes 4147208 | tf_op jit(solution)/shard_map/ppermute | solution.py:200
  193.7 24.4 %collective-permute-start.12 = (bf16[240,2880]{1,0:T(8,128)(2,1)}, bf16[240,2880]{1,0:T(8,128)(2,1)}, u32[]{:S(2)}, u32[]{:S(2)}) collective-permute-start(bf16[240,2880]{1,0:T(8,128)(2,1)} %collective-permute-done.3.refs_4_), channel_id=1, source_target_pairs={{0,8},{8,0},{16,24},{24,16},{1,9},{9,1},{17,25},{25,17},{2,10},{10... | collective-permute-start | bytes 4147208 | tf_op jit(solution)/shard_map/ppermute | solution.py:200
  193.7 1.1 copy-start.3
  193.7 24.4 %collective-permute-start.13 = (bf16[240,2880]{1,0:T(8,128)(2,1)}, bf16[240,2880]{1,0:T(8,128)(2,1)}, u32[]{:S(2)}, u32[]{:S(2)}) collective-permute-start(bf16[240,2880]{1,0:T(8,128)(2,1)} %collective-permute-done.4.refs_5_), channel_id=1, source_target_pairs={{0,8},{8,0},{16,24},{24,16},{1,9},{9,1},{17,25},{25,17},{2,10},{10... | collective-permute-start | bytes 4147208 | tf_op jit(solution)/shard_map/ppermute | solution.py:200
  194.2 1.2 copy-start.4
  194.2 23.9 %collective-permute-start.14 = (bf16[240,2880]{1,0:T(8,128)(2,1)}, bf16[240,2880]{1,0:T(8,128)(2,1)}, u32[]{:S(2)}, u32[]{:S(2)}) collective-permute-start(bf16[240,2880]{1,0:T(8,128)(2,1)} %collective-permute-done.5.refs_6_), channel_id=1, source_target_pairs={{0,8},{8,0},{16,24},{24,16},{1,9},{9,1},{17,25},{25,17},{2,10},{10... | collective-permute-start | bytes 4147208 | tf_op jit(solution)/shard_map/ppermute | solution.py:200
  195.4 1.1 copy-start.5
  196.5 21.7 %collective-permute-start.17 = (bf16[1440,360]{1,0:T(8,128)(2,1)}, bf16[1440,360]{1,0:T(8,128)(2,1)}, u32[]{:S(2)}, u32[]{:S(2)}) collective-permute-start(bf16[1440,360]{1,0:T(8,128)(2,1)} %collective-permute-done.7.refs_9_), channel_id=1, source_target_pairs={{0,8},{8,0},{16,24},{24,16},{1,9},{9,1},{17,25},{25,17},{2,10},{10... | collective-permute-start | bytes 3110408 | tf_op jit(solution)/shard_map/ppermute | solution.py:200
  240.0 25.1 %collective-permute-start.18 = (bf16[160,2880]{1,0:T(8,128)(2,1)}, bf16[160,2880]{1,0:T(8,128)(2,1)}, u32[]{:S(2)}, u32[]{:S(2)}) collective-permute-start(bf16[160,2880]{1,0:T(8,128)(2,1)} %get-tuple-element.23), channel_id=1, source_target_pairs={{0,16},{8,24},{1,17},{9,25},{2,18},{10,26},{3,19},{11,27},{4,20},{... | collective-permute-start | bytes 2764808 | tf_op jit(solution)/shard_map/ppermute | solution.py:249
  289.7 2.7 collective-permute-start.19
  292.5 1.0 copy-start.10
  295.7 23.9 %collective-permute-start.20 = (bf16[320,1440]{1,0:T(8,128)(2,1)S(1)}, bf16[320,1440]{1,0:T(8,128)(2,1)S(1)}, u32[]{:S(2)}, u32[]{:S(2)}) collective-permute-start(bf16[320,1440]{1,0:T(8,128)(2,1)S(1)} %get-tuple-element.61), channel_id=1, source_target_pairs={{0,4},{4,0},{1,5},{5,1},{2,6},{6,2},{3,7},{7,3},{8,12},{12,8},{9,1... | collective-permute-start | bytes 2764808 | tf_op jit(solution)/shard_map/ppermute | solution.py:205
  321.1 1.5 copy-start.9
  329.2 27.5 %copy-start.18 = (f32[2,8,360]{2,1,0:T(8,128)S(1)}, f32[2,8,360]{2,1,0:T(8,128)}, u32[]{:S(2)}) copy-start(f32[2,8,360]{2,1,0:T(8,128)} %get-tuple-element.38) | copy-start | bytes 69124
  329.2 27.5 %copy-start.19 = (f32[2,8,360]{2,1,0:T(8,128)S(1)}, f32[2,8,360]{2,1,0:T(8,128)}, u32[]{:S(2)}) copy-start(f32[2,8,360]{2,1,0:T(8,128)} %get-tuple-element.37) | copy-start | bytes 69124
  329.2 27.5 %copy-start.14 = (f32[2,8,2880]{2,1,0:T(8,128)S(1)}, f32[2,8,2880]{2,1,0:T(8,128)}, u32[]{:S(2)}) copy-start(f32[2,8,2880]{2,1,0:T(8,128)} %get-tuple-element.36) | copy-start | bytes 552964
  329.2 27.5 %copy-start.15 = (f32[2,8,2880]{2,1,0:T(8,128)S(1)}, f32[2,8,2880]{2,1,0:T(8,128)}, u32[]{:S(2)}) copy-start(f32[2,8,2880]{2,1,0:T(8,128)} %get-tuple-element.35) | copy-start | bytes 552964
  355.2 21.6 %collective-permute-start.21 = (bf16[160,2880]{1,0:T(8,128)(2,1)}, bf16[160,2880]{1,0:T(8,128)(2,1)S(1)}, u32[]{:S(2)}, u32[]{:S(2)}) collective-permute-start(bf16[160,2880]{1,0:T(8,128)(2,1)} %get-tuple-element.29), channel_id=1, source_target_pairs={{16,0},{24,8},{17,1},{25,9},{18,2},{26,10},{19,3},{27,11},{20,4},{... | collective-permute-start | bytes 2764808 | tf_op jit(solution)/shard_map/ppermute | solution.py:249
  356.9 47.1 %collective-permute-start.33 = (bf16[8,3240]{1,0:T(8,128)(2,1)S(1)}, bf16[8,3240]{1,0:T(8,128)(2,1)S(1)}, u32[]{:S(2)}, u32[]{:S(2)}) collective-permute-start(bf16[8,3240]{1,0:T(8,128)(2,1)S(1)} %get-tuple-element.63), channel_id=1, source_target_pairs={{0,8},{8,0},{16,24},{24,16},{1,9},{9,1},{17,25},{25,17},{2,10},{10... | collective-permute-start | bytes 155528 | tf_op jit(solution)/shard_map/ppermute | solution.py:200
  376.8 1.0 copy-start.11
  403.7 0.7 copy-start.20
  403.7 0.7 copy-start.21
  403.7 0.9 copy-start.16
  403.7 1.0 copy-start.17
  403.9 2.6 collective-permute-start.22
  406.6 120.0 %collective-permute-start.24 = (bf16[320,768]{1,0:T(8,128)(2,1)S(1)}, bf16[320,768]{1,0:T(8,128)(2,1)}, u32[]{:S(2)}, u32[]{:S(2)}) collective-permute-start(bf16[320,768]{1,0:T(8,128)(2,1)S(1)} %get-tuple-element.56), channel_id=1, source_target_pairs={{0,1},{1,2},{2,3},{3,0},{4,5},{5,6},{6,7},{7,4},{8,9},{9,10},{10,1... | collective-permute-start | bytes 1474568 | tf_op jit(solution)/shard_map/ppermute | solution.py:205
  408.2 120.4 %collective-permute-start.26 = (bf16[320,768]{1,0:T(8,128)(2,1)S(1)}, bf16[320,768]{1,0:T(8,128)(2,1)}, u32[]{:S(2)}, u32[]{:S(2)}) collective-permute-start(bf16[320,768]{1,0:T(8,128)(2,1)S(1)} %get-tuple-element.57), channel_id=1, source_target_pairs={{0,2},{1,3},{2,0},{3,1},{4,6},{5,7},{6,4},{7,5},{8,10},{9,11},{10,... | collective-permute-start | bytes 1474568 | tf_op jit(solution)/shard_map/ppermute | solution.py:205
  409.6 119.1 %collective-permute-start.34 = (bf16[8,3240]{1,0:T(8,128)(2,1)S(1)}, bf16[8,3240]{1,0:T(8,128)(2,1)S(1)}, u32[]{:S(2)}, u32[]{:S(2)}) collective-permute-start(bf16[8,3240]{1,0:T(8,128)(2,1)S(1)} %get-tuple-element.65), channel_id=1, source_target_pairs={{0,8},{8,0},{16,24},{24,16},{1,9},{9,1},{17,25},{25,17},{2,10},{10... | collective-permute-start | bytes 155528 | tf_op jit(solution)/shard_map/ppermute | solution.py:200
  409.7 121.6 %collective-permute-start.23 = (bf16[320,768]{1,0:T(8,128)(2,1)S(1)}, bf16[320,768]{1,0:T(8,128)(2,1)}, u32[]{:S(2)}, u32[]{:S(2)}) collective-permute-start(bf16[320,768]{1,0:T(8,128)(2,1)S(1)} %get-tuple-element.55), channel_id=1, source_target_pairs={{0,4},{4,0},{1,5},{5,1},{2,6},{6,2},{3,7},{7,3},{8,12},{12,8},{9,1... | collective-permute-start | bytes 1474568 | tf_op jit(solution)/shard_map/ppermute | solution.py:205
  411.2 118.1 %collective-permute-start.28 = (bf16[320,768]{1,0:T(8,128)(2,1)S(1)}, bf16[320,768]{1,0:T(8,128)(2,1)S(1)}, u32[]{:S(2)}, u32[]{:S(2)}) collective-permute-start(bf16[320,768]{1,0:T(8,128)(2,1)S(1)} %get-tuple-element.54), channel_id=1, source_target_pairs={{0,3},{1,0},{2,1},{3,2},{4,7},{5,4},{6,5},{7,6},{8,11},{9,8},{10,9... | collective-permute-start | bytes 1474568 | tf_op jit(solution)/shard_map/ppermute | solution.py:205
  526.6 14.5 %collective-permute-start.25 = (bf16[320,768]{1,0:T(8,128)(2,1)}, bf16[320,768]{1,0:T(8,128)(2,1)}, u32[]{:S(2)}, u32[]{:S(2)}) collective-permute-start(bf16[320,768]{1,0:T(8,128)(2,1)} %collective-permute-done.24), channel_id=1, source_target_pairs={{0,4},{4,0},{1,5},{5,1},{2,6},{6,2},{3,7},{7,3},{8,12},{12,8},{9,1... | collective-permute-start | bytes 1474568 | tf_op jit(solution)/shard_map/ppermute | solution.py:205
  528.6 23.1 %collective-permute-start.27 = (bf16[320,768]{1,0:T(8,128)(2,1)}, bf16[320,768]{1,0:T(8,128)(2,1)}, u32[]{:S(2)}, u32[]{:S(2)}) collective-permute-start(bf16[320,768]{1,0:T(8,128)(2,1)} %collective-permute-done.26), channel_id=1, source_target_pairs={{0,4},{4,0},{1,5},{5,1},{2,6},{6,2},{3,7},{7,3},{8,12},{12,8},{9,1... | collective-permute-start | bytes 1474568 | tf_op jit(solution)/shard_map/ppermute | solution.py:205
  529.4 27.5 %collective-permute-start.29 = (bf16[320,768]{1,0:T(8,128)(2,1)S(1)}, bf16[320,768]{1,0:T(8,128)(2,1)S(1)}, u32[]{:S(2)}, u32[]{:S(2)}) collective-permute-start(bf16[320,768]{1,0:T(8,128)(2,1)S(1)} %collective-permute-done.28), channel_id=1, source_target_pairs={{0,4},{4,0},{1,5},{5,1},{2,6},{6,2},{3,7},{7,3},{8,12},{12,8},{9,1... | collective-permute-start | bytes 1474568 | tf_op jit(solution)/shard_map/ppermute | solution.py:205
  531.3 9.9 %copy-start.12 = (bf16[2560,1440]{1,0:T(8,128)(2,1)S(1)}, bf16[2560,1440]{1,0:T(8,128)(2,1)}, u32[]{:S(2)}) copy-start(bf16[2560,1440]{1,0:T(8,128)(2,1)} %all-gather.3.cloned.1.call-done) | copy-start | bytes 22118404
  559.0 2.6 copy-start.13
  559.1 56.0 %collective-permute-start.30 = (bf16[360,768]{1,0:T(8,128)(2,1)S(1)}, bf16[360,768]{1,0:T(8,128)(2,1)S(1)}, u32[]{:S(2)}, u32[]{:S(2)}) collective-permute-start(bf16[360,768]{1,0:T(8,128)(2,1)S(1)} %get-tuple-element.53), channel_id=1, source_target_pairs={{0,1},{1,2},{2,3},{3,0},{4,5},{5,6},{6,7},{7,4},{8,9},{9,10},{10,1... | collective-permute-start | bytes 1658888 | tf_op jit(solution)/shard_map/ppermute | solution.py:205
  608.4 22.5 %collective-permute-start.31 = (bf16[360,768]{1,0:T(8,128)(2,1)S(1)}, bf16[360,768]{1,0:T(8,128)(2,1)S(1)}, u32[]{:S(2)}, u32[]{:S(2)}) collective-permute-start(bf16[360,768]{1,0:T(8,128)(2,1)S(1)} %get-tuple-element.52), channel_id=1, source_target_pairs={{0,2},{1,3},{2,0},{3,1},{4,6},{5,7},{6,4},{7,5},{8,10},{9,11},{10,... | collective-permute-start | bytes 1658888 | tf_op jit(solution)/shard_map/ppermute | solution.py:205
  610.8 21.6 %collective-permute-start.32 = (bf16[360,768]{1,0:T(8,128)(2,1)S(1)}, bf16[360,768]{1,0:T(8,128)(2,1)S(1)}, u32[]{:S(2)}, u32[]{:S(2)}) collective-permute-start(bf16[360,768]{1,0:T(8,128)(2,1)S(1)} %get-tuple-element.51), channel_id=1, source_target_pairs={{0,3},{1,0},{2,1},{3,2},{4,7},{5,4},{6,5},{7,6},{8,11},{9,8},{10,9... | collective-permute-start | bytes 1658888 | tf_op jit(solution)/shard_map/ppermute | solution.py:205
  632.6 2.3 copy-start.1
Sparse Core Ops, SparseCore 0:
  321.2 186.1 all-gather.2

commit v2 on v0

v2 whole, which is shorter than its diff:
```python
import functools
import itertools

import jax
import jax.numpy as jnp
from jax import lax
from jax.experimental import pallas as pl
from jax.experimental.pallas import tpu as pltpu
from jax.sharding import PartitionSpec as P

BF = jnp.bfloat16
F32 = jnp.float32
SUB = 8
PIECES = 3
VMEM_LIMIT = 62 * 1024 * 1024


def up(value, step):
    return -(-value // step) * step


def silu_slope(value):
    sigma = jax.nn.sigmoid(value)
    return sigma * (1.0 + value * (1.0 - sigma))


def nn(left, right):
    return lax.dot_general(left, right, (((1,), (0,)), ((), ())), preferred_element_type=F32)


def nt(left, right):
    return lax.dot_general(left, right, (((1,), (1,)), ((), ())), preferred_element_type=F32)


def tn(left, right):
    return lax.dot_general(left, right, (((0,), (0,)), ((), ())), preferred_element_type=F32)


class Loader:
    def __init__(self, meta, own, other, n_w, tiles):
        self.core, self.at, self.own, self.other = meta[0], meta, own, other
        self.n_w, self.tiles = n_w, tiles

    def place(self, index, rows):
        return pl.ds(pl.multiple_of(self.at[3 + index], 16), rows)

    def weight(self, refs, buf, sems, tile):
        low, width = self.tiles[tile]
        cols = pl.ds(low, width)
        for index, piece in enumerate(refs[: self.n_w]):
            target = buf.at[self.place(index, piece.shape[0]), cols]
            yield pltpu.make_async_copy(piece.at[:, cols], target, sems.at[tile, index])

    def pair(self, refs, bufs, sems):
        for index, piece in enumerate(refs[self.n_w :]):
            rows = piece.shape[0] // 2
            at = self.place(self.n_w + index, rows)
            for half, buf in enumerate(bufs):
                source = piece.at[pl.ds(half * rows, rows)]
                yield pltpu.make_async_copy(source, buf.at[at], sems.at[half, index])

    def start(self, block, kind, *args):
        for mine, refs in ((True, self.own), (False, self.other)):

            @pl.when((self.core == block) == mine)
            def _():
                for copy in kind(refs, *args):
                    copy.start()

    def wait(self, kind, *args):
        for copy in kind(self.own, *args):
            copy.wait()


def halves(value_ref, mine_ref, give_ref, index):
    part = mine_ref.shape[1]
    for here in range(value_ref.shape[1] // part):

        @pl.when(index == here)
        def _():
            mine_ref[...] = value_ref[:, here * part : (here + 1) * part]
            there = 1 - here
            give_ref[...] = value_ref[:, there * part : (there + 1) * part]


def pick_kernel(cfg, meta, order, all_ref, *refs):
    images, pixels, images_dev = cfg
    out_ref = refs[0]
    rows, count = out_ref.shape[0], all_ref.shape[0]
    per_core = images_dev // 2
    row = lax.broadcasted_iota(jnp.int32, (rows, 1), 0)
    target = jnp.full((rows, 1), -1, jnp.int32)
    for i in range(images):
        micro, slot = divmod(i, per_core)
        first = order[micro] * (pixels * images_dev) + meta[0] * per_core + slot
        inside = (row >= i * pixels) & (row < (i + 1) * pixels)
        target = jnp.where(inside, first + (row - i * pixels) * images_dev, target)
    chosen = lax.broadcasted_iota(jnp.int32, (rows, count), 1) == target
    chosen = jnp.where(chosen, 1.0, 0.0).astype(BF)
    out_ref[...] = nn(chosen, all_ref[...]).astype(BF)
    if len(refs) > 1:
        halves(out_ref, refs[1], refs[2], meta[2])


def partial_kernel(cfg, block, meta, mine_ref, recv_ref, own, other, keep_ref, give_ref, *scratch):
    (tiles,) = cfg
    x_buf, w_buf, sems = scratch
    rows = mine_ref.shape[0]

    def copy(ref, tile):
        cols = pl.ds(*tiles[tile])
        return pltpu.make_async_copy(ref.at[:, cols], w_buf.at[:, cols], sems.at[tile])

    @pl.when(meta[1] == 1)
    def _():
        for here, ref in ((True, own), (False, other)):

            @pl.when((meta[0] == block) == here)
            def _():
                for tile in range(len(tiles)):
                    copy(ref, tile).start()

        x_buf[:rows] = mine_ref[...]
        x_buf[rows:] = recv_ref[...]
        for tile, (low, width) in enumerate(tiles):
            cols = slice(low, low + width)
            copy(own, tile).wait()
            both = nn(x_buf[...], w_buf[:, cols])
            keep_ref[:, cols] = both[:rows]
            give_ref[:, cols] = both[rows:].astype(BF)


def image_masks(rows, images, pixels):
    row = lax.broadcasted_iota(jnp.int32, (rows, 1), 0)
    return [(row >= i * pixels) & (row < (i + 1) * pixels) for i in range(images)]


def per_image(value, masks):
    slot = lax.broadcasted_iota(jnp.int32, (SUB, 1), 0)
    total = jnp.zeros((SUB, value.shape[1]), F32)
    for i, mask in enumerate(masks):
        summed = jnp.sum(jnp.where(mask, value, 0.0), axis=0, keepdims=True)
        total = jnp.where(slot == i, summed, total)
    return total


def per_row(value, masks):
    spread = jnp.zeros((masks[0].shape[0], value.shape[1]), F32)
    for i, mask in enumerate(masks):
        spread = jnp.where(mask, value[i : i + 1, :], spread)
    return spread


def gated_block(tiles, masks, pixels, pre_of, src, dst, s_buf, e_buf, act_ref, outs):
    pre_ref, gate_ref, sq_ref, pool_ref, hid_ref = outs
    squeezed = jnp.zeros(sq_ref.shape, F32)
    for tile, (low, width) in enumerate(tiles):
        cols = slice(low, low + width)
        pre = pre_of(tile, cols)
        pre_ref[:, cols] = pre
        active = (pre * jax.nn.sigmoid(pre)).astype(BF)
        act_ref[:, cols] = active
        pooled = (per_image(active.astype(F32), masks) / pixels).astype(BF)
        pool_ref[:, cols] = pooled.astype(F32)
        squeezed = squeezed + nn(pooled, s_buf[cols, :])
    sq_ref[...] = squeezed
    hidden = (squeezed * jax.nn.sigmoid(squeezed)).astype(BF)
    hid_ref[...] = hidden.astype(F32)
    for low, width in tiles:
        cols = slice(low, low + width)
        gate = jax.nn.sigmoid(nt(hidden, e_buf[cols, :]))
        gate_ref[:, cols] = gate
        gated = act_ref[:, cols].astype(F32) * per_row(gate, masks)
        dst[:, cols] = (src[:, cols].astype(F32) + gated).astype(BF)


def split_pieces(refs, n_w, n_s):
    count = n_w + n_s
    return refs[:count], refs[count : 2 * count], refs[2 * count :]


def gate_kernel(cfg, block, meta, h_ref, keep_ref, recv_ref, *refs):
    n_s, images, pixels, tiles, send = cfg
    own, other, refs = split_pieces(refs, 0, n_s)
    out_ref, outs, refs = refs[0], refs[1:6], refs[6:]
    sends, refs = refs[: 2 * send], refs[2 * send :]
    s_buf, e_buf, act_ref, sems = refs
    loader = Loader(meta, own, other, 0, tiles)

    @pl.when(meta[1] == 1)
    def _():
        loader.start(block, loader.pair, (s_buf, e_buf), sems)
        masks = image_masks(h_ref.shape[0], images, pixels)
        waited = []

        def pre_of(tile, cols):
            if not waited:
                waited.append(True)
                loader.wait(loader.pair, (s_buf, e_buf), sems)
            return keep_ref[:, cols] + recv_ref[:, cols].astype(F32)

        gated_block(
            tiles, masks, pixels, pre_of, h_ref, out_ref, s_buf, e_buf, act_ref, outs
        )
        if send:
            halves(out_ref, sends[0], sends[1], meta[2])


def forward_kernel(cfg, meta, h_ref, *refs):
    n_w, n_s, images, pixels, tiles = cfg
    own, other, refs = split_pieces(refs, n_w, n_s)
    mid_ref, out_ref = refs[:2]
    outs = (refs[2:7], refs[7:12])
    w_buf, s_buf, e_buf, act_ref, w_sems, s_sems = refs[12:]
    loader = Loader(meta, own, other, n_w, tiles)

    @pl.when(meta[1] == 1)
    def _():
        for block in range(2):
            loader.start(block, loader.weight, w_buf.at[block], w_sems.at[block], 0)
            pair = (s_buf.at[block], e_buf.at[block])
            loader.start(block, loader.pair, pair, s_sems.at[block])
            for tile in range(1, len(tiles)):
                loader.start(block, loader.weight, w_buf.at[block], w_sems.at[block], tile)
        masks = image_masks(h_ref.shape[0], images, pixels)
        for block, (src, dst) in enumerate(((h_ref, mid_ref), (mid_ref, out_ref))):

            def pre_of(tile, cols):
                loader.wait(loader.weight, w_buf.at[block], w_sems.at[block], tile)
                if tile == 0:
                    pair = (s_buf.at[block], e_buf.at[block])
                    loader.wait(loader.pair, pair, s_sems.at[block])
                return nn(src[...], w_buf[block, :, cols])

            gated_block(
                tiles,
                masks,
                pixels,
                pre_of,
                src,
                dst,
                s_buf.at[block],
                e_buf.at[block],
                act_ref,
                outs[block],
            )


def backward_kernel(cfg, meta, up_ref, *refs):
    n_w, n_s, images, pixels, tiles, through = cfg
    saved, refs = (refs[:3], refs[3:6]), refs[6:]
    own, other, refs = split_pieces(refs, n_w, n_s)
    outs, refs = (refs[:3], refs[3:6]), refs[6:]
    if through:
        end_ref, refs = refs[0], refs[1:]
    w_buf, s_buf, e_buf, mid_ref, flat_ref, w_sems, s_sems = refs
    loader = Loader(meta, own, other, n_w, tiles)
    weighted = (0, 1) if through else (1,)
    slot = {block: place for place, block in enumerate(weighted)}

    @pl.when(meta[1] == 1)
    def _():
        for block in (1, 0):
            pair = (s_buf.at[block], e_buf.at[block])
            loader.start(block, loader.pair, pair, s_sems.at[block])
        for block in reversed(weighted):
            for tile in range(len(tiles)):
                at = slot[block]
                loader.start(block, loader.weight, w_buf.at[at], w_sems.at[at], tile)
        masks = image_masks(up_ref.shape[0], images, pixels)
        for block, src in ((1, up_ref), (0, mid_ref)):
            pre_ref, gate_ref, sq_ref = saved[block]
            dpre_ref, dsq_ref, dex_ref = outs[block]
            pair = (s_buf.at[block], e_buf.at[block])
            loader.wait(loader.pair, pair, s_sems.at[block])
            d_hidden = jnp.zeros(dsq_ref.shape, F32)
            for low, width in tiles:
                cols = slice(low, low + width)
                pre = pre_ref[:, cols]
                active = (pre * jax.nn.sigmoid(pre)).astype(BF).astype(F32)
                d_gate = per_image(src[:, cols].astype(F32) * active, masks)
                gate = gate_ref[:, cols]
                d_excite = (d_gate * gate * (1.0 - gate)).astype(BF)
                dex_ref[:, cols] = d_excite.astype(F32)
                d_hidden = d_hidden + nn(d_excite, e_buf[block, cols, :])
            d_squeezed = (d_hidden * silu_slope(sq_ref[...])).astype(BF)
            dsq_ref[...] = d_squeezed.astype(F32)
            for tile, (low, width) in enumerate(tiles):
                cols = slice(low, low + width)
                pre = pre_ref[:, cols]
                d_pool = nt(d_squeezed, s_buf[block, cols, :]) / pixels
                d_act = src[:, cols].astype(F32) * per_row(gate_ref[:, cols], masks)
                d_act = d_act + per_row(d_pool, masks)
                d_pre = (d_act * silu_slope(pre)).astype(BF)
                flat_ref[:, cols] = d_pre
                if width < dpre_ref.shape[2]:
                    dpre_ref[tile] = jnp.zeros(dpre_ref.shape[1:], BF)
                dpre_ref[tile, :, :width] = d_pre
            if block not in slot:
                continue
            at = slot[block]
            for tile in range(len(tiles)):
                loader.wait(loader.weight, w_buf.at[at], w_sems.at[at], tile)
            dst = mid_ref if block else end_ref
            for low, width in tiles:
                cols = slice(low, low + width)
                back = nt(flat_ref[...], w_buf[at, cols, :])
                dst[:, cols] = (src[:, cols].astype(F32) + back).astype(BF)


def call(kernel, smem, dense, pieces, outs, scratch, flops, moved):
    vmem = pl.BlockSpec(memory_space=pltpu.VMEM)
    return pl.pallas_call(
        kernel,
        out_shape=[jax.ShapeDtypeStruct(shape, dtype) for shape, dtype in outs],
        in_specs=[pl.BlockSpec(memory_space=pltpu.SMEM)] * len(smem)
        + [vmem] * len(dense)
        + [pl.BlockSpec(memory_space=pl.ANY)] * len(pieces),
        out_specs=[vmem] * len(outs),
        scratch_shapes=scratch,
        compiler_params=pltpu.CompilerParams(vmem_limit_bytes=VMEM_LIMIT),
        cost_estimate=pl.CostEstimate(flops=flops, bytes_accessed=moved, transcendentals=0),
    )(*smem, *dense, *pieces)


def move(value, axes, target):
    sizes = [lax.axis_size(axis) for axis in axes]
    pairs = []
    for index in itertools.product(*[range(size) for size in sizes]):
        goal = target(*index)
        if goal is not None:
            flat = [0, 0]
            for size, a, b in zip(sizes, index, goal):
                flat = [flat[0] * size + a, flat[1] * size + b]
            pairs.append(tuple(flat))
    return lax.ppermute(value, axes, pairs)


def swap(value, axis, stride=1):
    count = lax.axis_size(axis)
    return lax.ppermute(value, axis, [(i, i ^ stride) for i in range(count)])


def rotate(value, axis, steps):
    count = lax.axis_size(axis)
    return lax.ppermute(value, axis, [(i, (i + steps) % count) for i in range(count)])


def over_fsdp(value):
    count = lax.axis_size("fsdp")
    return [value] + [rotate(value, "fsdp", -step) for step in range(1, count)]


def parity_half(value, parity, low, rows):
    return lax.dynamic_slice_in_dim(value, parity * (value.shape[0] // 2) + low, rows, 0)


def far_half(weight, parity, chosen):
    step = weight.shape[0] // 2 // PIECES
    cuts = [parity_half(weight, parity, i * step, step) for i in range(PIECES)]
    near = [
        move(cut, ("segment", "fsdp"), lambda s, f: (s, 1 - f) if s in chosen else None)
        for cut in cuts
    ]
    cross = [
        move(cut, ("segment", "dp"), lambda s, z: (s, z ^ 1) if s in chosen else None)
        for cut in near
    ]
    return near + cross


def to_other_core(values, chosen):
    return [
        move(value, ("segment",), lambda s: (s ^ 1,) if s in chosen else None) for value in values
    ]


def small_exchange(wide, narrow, mesh_f, mesh_z):
    fsdp, dp = lax.axis_size("fsdp"), lax.axis_size("dp")
    rows, channels = wide.shape
    cut = channels // (fsdp * dp)
    wide = wide.reshape(rows, fsdp, dp, cut).transpose(1, 2, 0, 3)
    narrow = jnp.broadcast_to(narrow, (fsdp, dp) + narrow.shape)
    packed = jnp.concatenate([wide, narrow], axis=3).astype(BF)
    parts = []
    for step in range(fsdp):
        part = lax.dynamic_index_in_dim(packed, (mesh_f - step) % fsdp, 0, keepdims=False)
        parts.append(rotate(part, "fsdp", -step) if step else part)
    parts = jnp.stack(parts, axis=1)
    found = []
    for step in range(dp):
        part = lax.dynamic_index_in_dim(parts, mesh_z ^ step, 0, keepdims=False)
        found.append(swap(part, "dp", step) if step else part)
    found = jnp.stack(found).reshape(-1, cut + narrow.shape[3])
    return found[:, :cut], found[:, cut:]


def on_device(inputs, cotangent, plan, weight, squeeze, excite):
    fsdp, dp = lax.axis_size("fsdp"), lax.axis_size("dp")
    sections = lax.axis_size("segment")
    section = lax.axis_index("segment")
    core, stage = section % 2, section // 2
    mesh_f, mesh_z = lax.axis_index("fsdp"), lax.axis_index("dp")
    micro, images_dev, pixels, channels = inputs.shape
    hidden = squeeze.shape[2]
    images = micro * images_dev // 2
    rows = up(images * pixels, 16)
    group = up(-(-channels // dp), 128)
    part = channels // fsdp
    tiles = [(low, min(group, channels - low)) for low in range(0, channels, group)]
    weight, squeeze, excite = weight[0], squeeze[0], excite[0]
    assert sections == 4 and dp & (dp - 1) == 0 and len(tiles) == dp
    fast = fsdp == 2 and dp % 2 == 0 and part % (2 * 16 * PIECES) == 0
    first_stage, last_stage = (0, 1), (2, 3)
    barrier = lax.optimization_barrier

    if fast:
        mine_at = mesh_f * part
        far_at = part - mine_at
        parity = mesh_z % 2
        half = part // 2
        near_at = far_at + parity * half
        cross_at = far_at + (1 - parity) * half
        pair = jnp.concatenate([squeeze, excite], axis=0)
        near_s = [parity_half(side, parity, 0, half) for side in (squeeze, excite)]
        near_s = swap(jnp.concatenate(near_s, axis=0), "fsdp")
        cross_s = swap(near_s, "dp")
        s_own = [pair, near_s, cross_s]
        s_at = [mine_at, near_at, cross_at]
        step = half // PIECES
        w_at = [mine_at] + [near_at + i * step for i in range(PIECES)]
        w_at += [cross_at + i * step for i in range(PIECES)]
    else:
        both = [lax.all_gather(side, "fsdp", axis=0, tiled=True) for side in (squeeze, excite)]
        s_own = [jnp.concatenate(both, axis=0)]
        s_at = w_at = [jnp.int32(0)]
    s_other = [swap(piece, "segment") for piece in s_own]
    n_w, n_s = len(w_at), len(s_at)

    def meta_for(at, where):
        fields = [core, (stage == where).astype(jnp.int32), mesh_f, *at]
        return jnp.stack([jnp.asarray(field, jnp.int32) for field in fields])

    slots = jnp.arange(micro, dtype=jnp.int32)
    back_order = jnp.sum(jnp.where(plan[None, :] == slots[:, None], slots[None, :], 0), axis=1)

    def flat(maps, order, send):
        maps = maps.transpose(0, 2, 1, 3).reshape(-1, channels)
        shape = ((rows, channels), BF)
        outs = [shape] + [((rows, part), BF)] * (2 * send)
        kernel = functools.partial(pick_kernel, (images, pixels, images_dev))
        smem = [meta_for([], 0), order.astype(jnp.int32)]
        return call(kernel, smem, [maps], [], outs, [], rows * channels, 4 * rows * channels)

    picked = flat(inputs, slots, fast)
    h_first = picked[0]

    saved_shapes = [
        ((rows, channels), F32),
        ((SUB, channels), F32),
        ((SUB, hidden), F32),
        ((SUB, channels), F32),
        ((SUB, hidden), F32),
    ]
    act_shape = pltpu.VMEM((rows, channels), BF)

    def weight_bufs(count, w_count):
        return [
            pltpu.VMEM((count, channels, channels), BF),
            pltpu.VMEM((2, channels, hidden), BF),
            pltpu.VMEM((2, channels, hidden), BF),
        ], [
            pltpu.SemaphoreType.DMA((count, len(tiles), w_count)),
            pltpu.SemaphoreType.DMA((2, 2, n_s)),
        ]

    def forward_pass(h_in, where, pieces):
        bufs, sems = weight_bufs(2, n_w)
        return call(
            functools.partial(forward_kernel, (n_w, n_s, images, pixels, tiles)),
            [meta_for([*w_at, *s_at], where)],
            [h_in],
            pieces,
            [((rows, channels), BF)] * 2 + saved_shapes * 2,
            [*bufs, act_shape, *sems],
            4 * rows * channels * channels,
            4 * channels * channels,
        )

    def backward_pass(d_out, saved, where, pieces, through):
        bufs, sems = weight_bufs(1 + through, n_w)
        outs = [((dp, rows, group), BF), ((SUB, hidden), F32), ((SUB, channels), F32)] * 2
        outs += [((rows, channels), BF)] * through
        return call(
            functools.partial(backward_kernel, (n_w, n_s, images, pixels, tiles, through)),
            [meta_for([*w_at, *s_at], where)],
            [d_out, *saved[0][:3], *saved[1][:3]],
            pieces,
            outs,
            [*bufs, act_shape, act_shape, *sems],
            4 * rows * channels * channels,
            4 * channels * channels,
        )

    if fast:
        w_swapped = swap(weight, "segment")
        meta_s = meta_for(s_at, 0)
        mine, give = picked[1:]
        later_weight, give = barrier((weight, give))
        far_early = far_half(later_weight, parity, last_stage)

        def share(block, mine, give):
            recv = move(
                give, ("segment", "fsdp"), lambda s, f: (s, 1 - f) if s in first_stage else None
            )
            shapes = [((rows, channels), F32), ((rows, channels), BF)]
            return recv, call(
                functools.partial(share_kernel, block),
                [meta_s],
                [mine, recv],
                [weight, w_swapped],
                shapes,
                [
                    pltpu.VMEM((2 * rows, part), BF),
                    pltpu.VMEM((part, channels), BF),
                    pltpu.SemaphoreType.DMA((len(tiles),)),
                ],
                4 * rows * part * channels,
                2 * part * channels,
            )

        def share_kernel(block, meta, mine_ref, recv_ref, own, other, *refs):
            partial_kernel((tiles,), block, meta, mine_ref, recv_ref, own, other, *refs)

        def finish(block, h_row, keep, give):
            recv = move(
                give, ("segment", "fsdp"), lambda s, f: (s, 1 - f) if s in first_stage else None
            )
            send = block == 0
            outs = [((rows, channels), BF), *saved_shapes]
            outs += [((rows, part), BF)] * (2 * send)
            return call(
                functools.partial(gate_kernel, (n_s, images, pixels, tiles, send), block),
                [meta_s],
                [h_row, keep, recv],
                [*s_own, *s_other],
                outs,
                [
                    pltpu.VMEM((channels, hidden), BF),
                    pltpu.VMEM((channels, hidden), BF),
                    act_shape,
                    pltpu.SemaphoreType.DMA((2, n_s)),
                ],
                rows * channels * 64,
                4 * channels * hidden,
            )

        d_last = flat(cotangent, back_order, False)[0]
        recv = None
        _, (keep, give) = share(0, mine, give)
        give, d_last = barrier((give, d_last))
        result = finish(0, h_first, keep, give)
        h_mid, saved_a = result[0], result[1:6]
        _, (keep, give) = share(1, *result[6:])
        late_weight, give = barrier((weight, give))
        result = finish(1, h_mid, keep, give)
        h_out, saved_b = result[0], result[1:6]
        far_late = far_half(late_weight, parity, (1,))
        late_other = to_other_core(far_late, (1,))
        early = [weight, *far_early, *s_own]
        early += [w_swapped, *to_other_core(far_early, last_stage), *s_other]
        late = [weight, *far_late, *s_own, w_swapped, *late_other, *s_other]
    else:
        d_last = flat(cotangent, back_order, False)[0]
        whole = lax.all_gather(weight, "fsdp", axis=0, tiled=True)
        early = late = [whole, *s_own, swap(whole, "segment"), *s_other]
        result = forward_pass(h_first, 0, early)
        h_mid, h_out, saved_a, saved_b = result[0], result[1], result[2:7], result[7:12]
    first = (saved_a, saved_b)

    final = stage == 1
    h_in = move(h_out, ("segment",), lambda s: (s + 2,) if s < 2 else None)
    result = forward_pass(h_in, 1, early)
    last = (result[2:7], result[7:12])
    h_a = jnp.where(final, h_in, h_first)
    h_b = jnp.where(final, result[0], h_mid)

    def swap_blocks(first, second):
        keep = jnp.where(core == 0, first, second)
        give = jnp.where(core == 0, second, first)
        return jnp.concatenate([keep, swap(give, "segment")], axis=-2)

    def of_stage(ours, theirs):
        return jnp.where(final, ours, theirs)

    h_pair = swap_blocks(h_a, h_b)
    h_mine = []
    for step in range(fsdp):
        cut = lax.dynamic_slice_in_dim(h_pair, ((mesh_f - step) % fsdp) * part, part, 1)
        h_mine.append(rotate(cut, "fsdp", -step) if step else cut)

    ended = backward_pass(d_last, last, 1, early, True)
    h_mine, ended = barrier((h_mine, ended))
    h_mine = jnp.concatenate(h_mine, axis=0)
    h_all = [h_mine] + [None] * (dp - 1)
    if dp == 4:
        h_all[1] = swap(h_mine, "dp", 1)
        h_all[2] = swap(h_mine, "dp", 2)
        inner = lax.ppermute(h_mine, "dp", [(1, 2), (2, 1)])
        outer = lax.ppermute(h_all[2], "dp", [(2, 3), (1, 0)])
        h_all[3] = jnp.where((mesh_z == 1) | (mesh_z == 2), inner, outer)
    else:
        for step in range(1, dp):
            h_all[step] = swap(h_mine, "dp", step)
    pool = swap_blocks(*[of_stage(last[b][3], first[b][3]) for b in range(2)])
    hid = swap_blocks(*[of_stage(last[b][4], first[b][4]) for b in range(2)])
    pool, hid = small_exchange(pool, hid, mesh_f, mesh_z)

    d_out = move(ended[6], ("segment",), lambda s: (s - 2,) if s > 1 else None)
    begun = backward_pass(d_out, first, 0, late, False)
    d_pre, d_sq, d_ex = [
        swap_blocks(*[of_stage(ended[3 * b + i], begun[3 * b + i]) for b in range(2)])
        for i in range(3)
    ]

    total = None
    for step in range(dp):
        piece = lax.dynamic_index_in_dim(d_pre, mesh_z ^ step, 0, keepdims=False)
        if step:
            piece = swap(piece, "dp", step)
        piece = jnp.concatenate(over_fsdp(piece), axis=0)
        term = tn(h_all[step], piece)
        total = term if total is None else total + term
    total = total.astype(BF)
    d_ex, d_sq = small_exchange(d_ex, d_sq, mesh_f, mesh_z)
    own_rows = part // dp
    gathered = jnp.zeros((dp, own_rows, group), BF)
    for step in range(dp):
        block = lax.dynamic_slice_in_dim(total, (mesh_z ^ step) * own_rows, own_rows, 0)
        if step:
            block = swap(block, "dp", step)
        gathered = lax.dynamic_update_index_in_dim(gathered, block, mesh_z ^ step, 0)
    grad_w = jnp.concatenate([gathered[i, :, :w] for i, (_, w) in enumerate(tiles)], axis=1)
    return (grad_w.astype(F32)[None], tn(pool, d_sq)[None], tn(d_ex, hid)[None])


def solution(mesh):
    placed = (
        P(None, ("fsdp", "dp"), None, None),
        P(None, ("fsdp", "dp"), None, None),
        P(),
        P("segment", "fsdp", None),
        P("segment", "fsdp", None),
        P("segment", "fsdp", None),
    )
    return jax.shard_map(
        on_device,
        mesh=mesh,
        in_specs=placed,
        out_specs=(
            P("segment", ("fsdp", "dp"), None),
            P("segment", ("fsdp", "dp"), None),
            P("segment", ("fsdp", "dp"), None),
        ),
        check_vma=False,
    )
```

time: 1020 us -> 589 us (0.58)
  waiting for transfers between devices: 733 us -> 325 us
  matrix products: 138 us -> 16.2 us
  Pallas kernels: 0 us -> 75.5 us
  starting transfers between devices: 29.2 us -> 103 us
  other arithmetic: 44.8 us -> 18.6 us
  local copies, waits for them, and re-layouts: 52 us -> 37.9 us
  between operations: 15.2 us -> 1.98 us
    unnamed x9 -> x0, waiting for transfers between devices: 428 us -> none
    ppermute x10 -> x65, waiting for transfers between devices: 58.2 us -> 325 us  [the longest x26 160 us: swap(): return lax.ppermute(value, axis, [(i, i ^ stride) for i in range(count)])]
    all_gather x3 -> x0, waiting for transfers between devices: 247 us -> none  [the longest x1 186 us: on_device(): lax.all_gather(weight[0], 'fsdp', axis=0, tiled=True)]
    dot_general x38 -> x6, matrix products: 138 us -> 16.2 us  [tn(): lax.dot_general(left, right, (((0,), (0,)), ((), ())), preferred_element_...]
    pallas_call x0 -> x9, Pallas kernels: none -> 75.5 us  [call(): pl.pallas_call(kernel, out_shape=[jax.ShapeDtypeStruct(shape, dtype) for...]
    ppermute x10 -> x65, starting transfers between devices: 28.7 us -> 103 us  [the longest x30 59.1 us: move(): return lax.ppermute(value, axes, pairs)]
    dynamic_update_slice x35 -> x0, other arithmetic: 22.5 us -> none  [put_slot(): lax.dynamic_update_index_in_dim(store, jnp.where(active, value, current),...]
    reduce_sum x6 -> x1, other arithmetic: 13.3 us -> 0.63 us  [on_device(): jnp.sum(jnp.where(plan[None, :] == slots[:, None], slots[None, :], 0), ax...]
  transfers between devices with their start and end apart: 16 -> 65, of which waited for: 16 -> 21; matrix products, arithmetic and copies ran while one was open for 9% -> 12% of each run, Pallas kernels for 0% -> 13%
where the time goes in v2:
time: 589 us; the launch traced here: 578 us
  waiting for transfers between devices  325 us (55%)
  starting transfers between devices  103 us (17%)
  Pallas kernels  75.5 us (13%)
  local copies, waits for them, and re-layouts  37.9 us (6%)
  other arithmetic  18.6 us (3%)
  matrix products  16.2 us (3%)
    ppermute x26, waiting for transfers between devices, swap(): return lax.ppermute(value, axis, [(i, i ^ stride) for i in range(count)])  160 us
    ppermute x30, waiting for transfers between devices, move(): return lax.ppermute(value, axes, pairs)  135 us
    pallas_call x9, Pallas kernels, call(): pl.pallas_call(kernel, out_shape=[jax.ShapeDtypeStruct(shape, dtype) for...  75.5 us
    ppermute x30, starting transfers between devices, move(): return lax.ppermute(value, axes, pairs)  59.1 us
    ppermute x7, waiting for transfers between devices, rotate(): lax.ppermute(value, axis, [(i, (i + steps) % count) for i in range(count)])  30 us
    ppermute x26, starting transfers between devices, swap(): return lax.ppermute(value, axis, [(i, i ^ stride) for i in range(count)])  27.7 us
    dot_general x6, matrix products, tn(): lax.dot_general(left, right, (((0,), (0,)), ((), ())), preferred_element_...  16.2 us
  transfers between devices with their start and end apart: 65, of which 21 were waited for; matrix products, arithmetic and copies ran while one was open for 12% of the time, Pallas kernels for 13%

profile of v2, /device:TPU:10, one launch (start us, length us, event | category | flops | bytes accessed | tf_op | source)
XLA Modules:
  0.0 578.1 jit_solution(18427276877858978343)
XLA Ops:
  4.9 3.7 reshape.78.all_ref
  9.7 3.6 shard_map.85
  14.8 4.4 constant_dynamic-slice_fusion.6
  19.2 2.4 collective-permute-start.11
  21.9 2.7 copy.32
  24.6 6.2 %collective-permute-done.3.refs_1_.refs_8_.refs_14_ = bf16[1440,360]{1,0:T(8,128)(2,1)S(1)} collective-permute-done((bf16[1440,360]{1,0:T(8,128)(2,1)}, bf16[1440,360]{1,0:T(8,128)(2,1)S(1)}, u32[]{:S(2)}, u32[]{:S(2)}) %collective-permute-start.3) | collective-permute-done | bytes 1036832 | tf_op jit(solution)/shard_map/ppermute | solution.py:341
  31.2 3.4 collective-permute-start.12
  34.7 26.5 %collective-permute-done.11.refs_1_.refs_7_ = bf16[240,2880]{1,0:T(8,128)(2,1)} collective-permute-done((bf16[240,2880]{1,0:T(8,128)(2,1)}, bf16[240,2880]{1,0:T(8,128)(2,1)}, u32[]{:S(2)}, u32[]{:S(2)}) %collective-permute-start.11) | collective-permute-done | bytes 1382432 | tf_op jit(solution)/shard_map/ppermute | solution.py:336
  61.2 3.4 collective-permute-start.13
  65.2 4.9 reshape.79.all_ref
  70.1 3.1 shard_map.87.up_ref
  74.0 2.9 shard_map.86
  76.9 14.6 %collective-permute-done.12.refs_2_.refs_8_ = bf16[240,2880]{1,0:T(8,128)(2,1)} collective-permute-done((bf16[240,2880]{1,0:T(8,128)(2,1)}, bf16[240,2880]{1,0:T(8,128)(2,1)}, u32[]{:S(2)}, u32[]{:S(2)}) %collective-permute-start.12) | collective-permute-done | bytes 1382432 | tf_op jit(solution)/shard_map/ppermute | solution.py:336
  93.1 2.3 collective-permute-start.14
  95.4 3.5 collective-permute-start.15
  98.9 4.1 copy.33.refs_3_.refs_17_.refs_23_
  103.0 4.3 shard_map.88
  108.0 13.3 %collective-permute-done.13.refs_3_.refs_9_ = bf16[240,2880]{1,0:T(8,128)(2,1)} collective-permute-done((bf16[240,2880]{1,0:T(8,128)(2,1)}, bf16[240,2880]{1,0:T(8,128)(2,1)}, u32[]{:S(2)}, u32[]{:S(2)}) %collective-permute-start.13) | collective-permute-done | bytes 1382432 | tf_op jit(solution)/shard_map/ppermute | solution.py:336
  121.3 2.3 collective-permute-start.16
  123.7 1.9 collective-permute-start.17
  125.6 2.4 collective-permute-start.18
  128.0 2.8 shard_map.89
  130.9 1.9 collective-permute-start.19
  132.8 26.6 %collective-permute-done.15.refs_5_.refs_11_ = bf16[240,2880]{1,0:T(8,128)(2,1)} collective-permute-done((bf16[240,2880]{1,0:T(8,128)(2,1)}, bf16[240,2880]{1,0:T(8,128)(2,1)}, u32[]{:S(2)}, u32[]{:S(2)}) %collective-permute-start.15) | collective-permute-done | bytes 1382432 | tf_op jit(solution)/shard_map/ppermute | solution.py:336
  161.0 26.9 %collective-permute-done.16.refs_6_.refs_12_ = bf16[240,2880]{1,0:T(8,128)(2,1)} collective-permute-done((bf16[240,2880]{1,0:T(8,128)(2,1)}, bf16[240,2880]{1,0:T(8,128)(2,1)}, u32[]{:S(2)}, u32[]{:S(2)}) %collective-permute-start.16) | collective-permute-done | bytes 1382432 | tf_op jit(solution)/shard_map/ppermute | solution.py:336
  187.9 1.9 collective-permute-start.20
  189.9 4.3 constant_dynamic-slice_fusion.3
  194.2 2.4 collective-permute-start.21
  198.3 1.9 collective-permute-start.22
  200.3 3.7 shard_map.90
  207.7 1.9 collective-permute-start.28
  211.4 18.1 %collective-permute-done.10.h_ref = bf16[160,2880]{1,0:T(8,128)(2,1)} collective-permute-done((bf16[160,2880]{1,0:T(8,128)(2,1)}, bf16[160,2880]{1,0:T(8,128)(2,1)}, u32[]{:S(2)}, u32[]{:S(2)}) %collective-permute-start.10) | collective-permute-done | bytes 921632 | tf_op jit(solution)/shard_map/ppermute | solution.py:336
  229.5 24.2 %shard_map.91 = (bf16[160,2880]{1,0:T(8,128)(2,1)}, bf16[160,2880]{1,0:T(8,128)(2,1)}, f32[160,2880]{1,0:T(8,128)}, f32[8,2880]{1,0:T(8,128)}, f32[8,360]{1,0:T(...) custom-call(s32[13]{0:T(128)} %stack.152.meta, ...), custom_call_target="tpu_custom_call" | custom-call | flops 5308416000 | bytes 33177600 | tf_op jit(solution)/shard_map/pallas_call | solution.py:313
  253.8 2.7 broadcast_select_fusion.6
  257.1 1.8 collective-permute-start.32
  263.6 2.4 fusion.2
  274.3 16.1 %collective-permute-done.24 = bf16[320,1440]{1,0:T(8,128)(2,1)} collective-permute-done((bf16[320,1440]{1,0:T(8,128)(2,1)}, bf16[320,1440]{1,0:T(8,128)(2,1)}, u32[]{:S(2)}, u32[]{:S(2)}) %collective-permute-start.24) | collective-permute-done | bytes 921632 | tf_op jit(solution)/shard_map/ppermute | solution.py:346
  292.2 26.8 %shard_map.92 = (bf16[4,160,768]{2,1,0:T(8,128)(2,1)}, f32[8,360]{1,0:T(8,128)}, f32[8,2880]{1,0:T(8,128)}, bf16[4,160,768]{2,1,0:T(8,128)(2,1)}, f32[8,360]{1,0...) custom-call(s32[13]{0:T(128)} %stack.152.meta, bf16[160,2880]{1,0:T(8,128)(2,1)} %shard_map.87.up_ref, ...), custom_call_target="tpu_custom_call" | custom-call | flops 5308416000 | bytes 33177600 | tf_op jit(solution)/shard_map/pallas_call | solution.py:313
  319.0 2.2 collective-permute-start.25
  325.4 2.2 copy.38
  329.7 2.6 collective-permute-start.43
  332.3 8.6 %collective-permute-done.25.up_ref = bf16[160,2880]{1,0:T(8,128)(2,1)} collective-permute-done((bf16[160,2880]{1,0:T(8,128)(2,1)}, bf16[160,2880]{1,0:T(8,128)(2,1)}, u32[]{:S(2)}, u32[]{:S(2)}) %collective-permute-start.25) | collective-permute-done | bytes 921632 | tf_op jit(solution)/shard_map/ppermute | solution.py:336
  340.8 4.2 shard_map.93
  347.7 1.9 collective-permute-done.60
  357.2 9.2 %collective-permute-done.61 = bf16[4,16,720]{2,1,0:T(8,128)(2,1)S(1)} collective-permute-done((bf16[4,16,720]{2,1,0:T(8,128)(2,1)S(1)}, bf16[4,16,720]{2,1,0:T(8,128)(2,1)S(1)}, u32[]{:S(2)}, u32[]{:S(2)}) %collective-permute-start.61) | collective-permute-done | bytes 92192 | tf_op jit(solution)/shard_map/ppermute | solution.py:346
  366.4 4.6 collective-permute-start.46
  371.0 42.2 %collective-permute-done.43 = bf16[640,1440]{0,1:T(8,128)(2,1)} collective-permute-done((bf16[640,1440]{0,1:T(8,128)(2,1)}, bf16[640,1440]{0,1:T(8,128)(2,1)}, u32[]{:S(2)}, u32[]{:S(2)}) %collective-permute-start.43) | collective-permute-done | bytes 1843232 | tf_op jit(solution)/shard_map/ppermute | solution.py:341
  413.2 4.3 collective-permute-start.47
  417.5 3.5 collective-permute-done.41
  421.1 3.8 collective-permute-start.44
  427.5 56.1 %collective-permute-done.44 = bf16[320,768]{1,0:T(8,128)(2,1)} collective-permute-done((bf16[320,768]{1,0:T(8,128)(2,1)}, bf16[320,768]{1,0:T(8,128)(2,1)}, u32[]{:S(2)}, u32[]{:S(2)}) %collective-permute-start.44) | collective-permute-done | bytes 491552 | tf_op jit(solution)/shard_map/ppermute | solution.py:341
  484.4 8.8 %collective-permute-done.48 = bf16[320,768]{1,0:T(8,128)(2,1)S(1)} collective-permute-done((bf16[320,768]{1,0:T(8,128)(2,1)S(1)}, bf16[320,768]{1,0:T(8,128)(2,1)S(1)}, u32[]{:S(2)}, u32[]{:S(2)}) %collective-permute-start.48) | collective-permute-done | bytes 491552 | tf_op jit(solution)/shard_map/ppermute | solution.py:341
  493.8 3.0 fusion.4
  498.4 3.5 fusion.12
  503.5 4.1 collective-permute-done.42
  507.6 4.3 collective-permute-start.57
  511.9 3.5 fusion.8
  519.0 3.9 add_convert_fusion
  523.6 2.5 collective-permute-start.50
  527.6 3.7 collective-permute-start.51
  534.8 8.7 %collective-permute-done.50 = bf16[360,768]{1,0:T(8,128)(2,1)S(1)} collective-permute-done((bf16[360,768]{1,0:T(8,128)(2,1)S(1)}, bf16[360,768]{1,0:T(8,128)(2,1)S(1)}, u32[]{:S(2)}, u32[]{:S(2)}) %collective-permute-start.50) | collective-permute-done | bytes 552992 | tf_op jit(solution)/shard_map/ppermute | solution.py:341
  543.5 23.2 %collective-permute-done.51 = bf16[360,768]{1,0:T(8,128)(2,1)S(1)} collective-permute-done((bf16[360,768]{1,0:T(8,128)(2,1)S(1)}, bf16[360,768]{1,0:T(8,128)(2,1)S(1)}, u32[]{:S(2)}, u32[]{:S(2)}) %collective-permute-start.51) | collective-permute-done | bytes 552992 | tf_op jit(solution)/shard_map/ppermute | solution.py:341
  566.8 8.4 %collective-permute-done.52 = bf16[360,768]{1,0:T(8,128)(2,1)S(1)} collective-permute-done((bf16[360,768]{1,0:T(8,128)(2,1)S(1)}, bf16[360,768]{1,0:T(8,128)(2,1)S(1)}, u32[]{:S(2)}, u32[]{:S(2)}) %collective-permute-start.52) | collective-permute-done | bytes 552992 | tf_op jit(solution)/shard_map/ppermute | solution.py:341
  575.4 2.3 maximum_convert_fusion
  (184 shorter events, 68.4 us)
Async XLA Ops:
  0.6 73.2 %collective-permute-start.1 = (bf16[1440,2880]{1,0:T(8,128)(2,1)}, bf16[1440,2880]{1,0:T(8,128)(2,1)}, u32[]{:S(2)}, u32[]{:S(2)}) collective-permute-start(bf16[1440,2880]{1,0:T(8,128)(2,1)} %bitcast.79), channel_id=1, source_target_pairs={{0,8},{8,0},{16,24},{24,16},{1,9},{9,1},{17,25},{25,17},{2,10},{10... | collective-permute-start | bytes 24883208 | tf_op jit(solution)/shard_map/ppermute | solution.py:341
  3.4 27.4 %collective-permute-start.3 = (bf16[1440,360]{1,0:T(8,128)(2,1)}, bf16[1440,360]{1,0:T(8,128)(2,1)S(1)}, u32[]{:S(2)}, u32[]{:S(2)}) collective-permute-start(bf16[1440,360]{1,0:T(8,128)(2,1)} %pad_maximum_fusion.1), channel_id=1, source_target_pairs={{0,4},{4,0},{1,5},{5,1},{2,6},{6,2},{3,7},{7,3},{8,12},{12,8},{9,1... | collective-permute-start | bytes 3110408 | tf_op jit(solution)/shard_map/ppermute | solution.py:341
  13.3 17.9 %collective-permute-start = (bf16[160,1440]{1,0:T(8,128)(2,1)}, bf16[160,1440]{1,0:T(8,128)(2,1)}, u32[]{:S(2)}, u32[]{:S(2)}) collective-permute-start(bf16[160,1440]{1,0:T(8,128)(2,1)} %get-tuple-element.66), channel_id=1, source_target_pairs={{0,4},{4,0},{8,12},{12,8},{1,5},{5,1},{9,13},{13,9},{2,6},{6,2},{1... | collective-permute-start | bytes 1382408 | tf_op jit(solution)/shard_map/ppermute | solution.py:336
  19.2 42.0 %collective-permute-start.11 = (bf16[240,2880]{1,0:T(8,128)(2,1)}, bf16[240,2880]{1,0:T(8,128)(2,1)}, u32[]{:S(2)}, u32[]{:S(2)}) collective-permute-start(bf16[240,2880]{1,0:T(8,128)(2,1)} %get-tuple-element.128), channel_id=1, source_target_pairs={{16,20},{20,16},{24,28},{28,24},{17,21},{21,17},{25,29},{29,25},{1... | collective-permute-start | bytes 4147208 | tf_op jit(solution)/shard_map/ppermute | solution.py:336
  24.6 70.8 %collective-permute-start.5 = (bf16[2880,360]{0,1:T(8,128)(2,1)}, bf16[2880,360]{0,1:T(8,128)(2,1)}, u32[]{:S(2)}, u32[]{:S(2)}) collective-permute-start(bf16[2880,360]{0,1:T(8,128)(2,1)} %copy.32), channel_id=1, source_target_pairs={{0,8},{8,0},{16,24},{24,16},{1,9},{9,1},{17,25},{25,17},{2,10},{10... | collective-permute-start | bytes 6220808 | tf_op jit(solution)/shard_map/ppermute | solution.py:341
  30.8 30.4 %collective-permute-start.4 = (bf16[1440,360]{1,0:T(8,128)(2,1)S(1)}, bf16[1440,360]{1,0:T(8,128)(2,1)}, u32[]{:S(2)}, u32[]{:S(2)}) collective-permute-start(bf16[1440,360]{1,0:T(8,128)(2,1)S(1)} %collective-permute-done.3.refs_1_.refs_8_.refs_14_), channel_id=1, source_target_pairs={{0,1},{1,0},{2,3},{3,2},{4,5},{5,4},{6,7},{7,6},{8,9},{9,8},{10,11... | collective-permute-start | bytes 3110408 | tf_op jit(solution)/shard_map/ppermute | solution.py:341
  31.2 60.2 %collective-permute-start.12 = (bf16[240,2880]{1,0:T(8,128)(2,1)}, bf16[240,2880]{1,0:T(8,128)(2,1)}, u32[]{:S(2)}, u32[]{:S(2)}) collective-permute-start(bf16[240,2880]{1,0:T(8,128)(2,1)} %get-tuple-element.127), channel_id=1, source_target_pairs={{16,20},{20,16},{24,28},{28,24},{17,21},{21,17},{25,29},{29,25},{1... | collective-permute-start | bytes 4147208 | tf_op jit(solution)/shard_map/ppermute | solution.py:336
  61.2 31.9 %collective-permute-start.6 = (bf16[1440,360]{1,0:T(8,128)(2,1)S(1)}, bf16[1440,360]{1,0:T(8,128)(2,1)}, u32[]{:S(2)}, u32[]{:S(2)}) collective-permute-start(bf16[1440,360]{1,0:T(8,128)(2,1)S(1)} %collective-permute-done.3.refs_1_.refs_8_.refs_14_), channel_id=1, source_target_pairs={{0,8},{8,0},{16,24},{24,16},{1,9},{9,1},{17,25},{25,17},{2,10},{10... | collective-permute-start | bytes 3110408 | tf_op jit(solution)/shard_map/ppermute | solution.py:341
  61.2 60.1 %collective-permute-start.13 = (bf16[240,2880]{1,0:T(8,128)(2,1)}, bf16[240,2880]{1,0:T(8,128)(2,1)}, u32[]{:S(2)}, u32[]{:S(2)}) collective-permute-start(bf16[240,2880]{1,0:T(8,128)(2,1)} %get-tuple-element.126), channel_id=1, source_target_pairs={{16,20},{20,16},{24,28},{28,24},{17,21},{21,17},{25,29},{29,25},{1... | collective-permute-start | bytes 4147208 | tf_op jit(solution)/shard_map/ppermute | solution.py:336
  73.8 29.2 %collective-permute-start.7 = (bf16[1440,360]{1,0:T(8,128)(2,1)}, bf16[1440,360]{1,0:T(8,128)(2,1)}, u32[]{:S(2)}, u32[]{:S(2)}) collective-permute-start(bf16[1440,360]{1,0:T(8,128)(2,1)} %collective-permute-done.4.refs_2_.refs_9_.refs_15_), channel_id=1, source_target_pairs={{0,8},{8,0},{16,24},{24,16},{1,9},{9,1},{17,25},{25,17},{2,10},{10... | collective-permute-start | bytes 3110408 | tf_op jit(solution)/shard_map/ppermute | solution.py:341
  91.5 11.5 %collective-permute-start.2 = (bf16[160,2880]{1,0:T(8,128)(2,1)}, bf16[160,2880]{1,0:T(8,128)(2,1)}, u32[]{:S(2)}, u32[]{:S(2)}) collective-permute-start(bf16[160,2880]{1,0:T(8,128)(2,1)} %get-tuple-element.69), channel_id=1, source_target_pairs={{0,4},{4,0},{8,12},{12,8},{1,5},{5,1},{9,13},{13,9},{2,6},{6,2},{1... | collective-permute-start | bytes 2764808 | tf_op jit(solution)/shard_map/ppermute | solution.py:336
  93.1 37.8 %collective-permute-start.14 = (bf16[240,2880]{1,0:T(8,128)(2,1)}, bf16[240,2880]{1,0:T(8,128)(2,1)S(1)}, u32[]{:S(2)}, u32[]{:S(2)}) collective-permute-start(bf16[240,2880]{1,0:T(8,128)(2,1)} %collective-permute-done.11.refs_1_.refs_7_), channel_id=1, source_target_pairs={{16,17},{17,16},{18,19},{19,18},{24,25},{25,24},{26,27},{27,26},{2... | collective-permute-start | bytes 4147208 | tf_op jit(solution)/shard_map/ppermute | solution.py:336
  95.4 64.0 %collective-permute-start.15 = (bf16[240,2880]{1,0:T(8,128)(2,1)}, bf16[240,2880]{1,0:T(8,128)(2,1)}, u32[]{:S(2)}, u32[]{:S(2)}) collective-permute-start(bf16[240,2880]{1,0:T(8,128)(2,1)} %collective-permute-done.12.refs_2_.refs_8_), channel_id=1, source_target_pairs={{16,17},{17,16},{18,19},{19,18},{24,25},{25,24},{26,27},{27,26},{2... | collective-permute-start | bytes 4147208 | tf_op jit(solution)/shard_map/ppermute | solution.py:336
  107.3 18.3 %collective-permute-start.8 = (bf16[160,1440]{1,0:T(8,128)(2,1)}, bf16[160,1440]{1,0:T(8,128)(2,1)S(1)}, u32[]{:S(2)}, u32[]{:S(2)}) collective-permute-start(bf16[160,1440]{1,0:T(8,128)(2,1)} %get-tuple-element.72), channel_id=1, source_target_pairs={{0,4},{4,0},{8,12},{12,8},{1,5},{5,1},{9,13},{13,9},{2,6},{6,2},{1... | collective-permute-start | bytes 1382408 | tf_op jit(solution)/shard_map/ppermute | solution.py:336
  121.3 66.6 %collective-permute-start.16 = (bf16[240,2880]{1,0:T(8,128)(2,1)}, bf16[240,2880]{1,0:T(8,128)(2,1)}, u32[]{:S(2)}, u32[]{:S(2)}) collective-permute-start(bf16[240,2880]{1,0:T(8,128)(2,1)} %collective-permute-done.13.refs_3_.refs_9_), channel_id=1, source_target_pairs={{16,17},{17,16},{18,19},{19,18},{24,25},{25,24},{26,27},{27,26},{2... | collective-permute-start | bytes 4147208 | tf_op jit(solution)/shard_map/ppermute | solution.py:336
  123.7 70.5 %collective-permute-start.17 = (bf16[240,2880]{1,0:T(8,128)(2,1)}, bf16[240,2880]{1,0:T(8,128)(2,1)}, u32[]{:S(2)}, u32[]{:S(2)}) collective-permute-start(bf16[240,2880]{1,0:T(8,128)(2,1)} %collective-permute-done.11.refs_1_.refs_7_), channel_id=1, source_target_pairs={{16,24},{24,16},{17,25},{25,17},{18,26},{26,18},{19,27},{27,19},{2... | collective-permute-start | bytes 4147208 | tf_op jit(solution)/shard_map/ppermute | solution.py:336
  125.6 71.0 %collective-permute-start.18 = (bf16[240,2880]{1,0:T(8,128)(2,1)}, bf16[240,2880]{1,0:T(8,128)(2,1)}, u32[]{:S(2)}, u32[]{:S(2)}) collective-permute-start(bf16[240,2880]{1,0:T(8,128)(2,1)} %collective-permute-done.12.refs_2_.refs_8_), channel_id=1, source_target_pairs={{16,24},{24,16},{17,25},{25,17},{18,26},{26,18},{19,27},{27,19},{2... | collective-permute-start | bytes 4147208 | tf_op jit(solution)/shard_map/ppermute | solution.py:336
  130.9 73.1 %collective-permute-start.19 = (bf16[240,2880]{1,0:T(8,128)(2,1)}, bf16[240,2880]{1,0:T(8,128)(2,1)}, u32[]{:S(2)}, u32[]{:S(2)}) collective-permute-start(bf16[240,2880]{1,0:T(8,128)(2,1)} %collective-permute-done.13.refs_3_.refs_9_), channel_id=1, source_target_pairs={{16,24},{24,16},{17,25},{25,17},{18,26},{26,18},{19,27},{27,19},{2... | collective-permute-start | bytes 4147208 | tf_op jit(solution)/shard_map/ppermute | solution.py:336
  159.4 38.9 %collective-permute-start.9 = (bf16[160,2880]{1,0:T(8,128)(2,1)}, bf16[160,2880]{1,0:T(8,128)(2,1)}, u32[]{:S(2)}, u32[]{:S(2)}) collective-permute-start(bf16[160,2880]{1,0:T(8,128)(2,1)} %get-tuple-element.75), channel_id=1, source_target_pairs={{0,4},{4,0},{8,12},{12,8},{1,5},{5,1},{9,13},{13,9},{2,6},{6,2},{1... | collective-permute-start | bytes 2764808 | tf_op jit(solution)/shard_map/ppermute | solution.py:336
  187.9 18.0 %collective-permute-start.20 = (bf16[240,2880]{1,0:T(8,128)(2,1)S(1)}, bf16[240,2880]{1,0:T(8,128)(2,1)}, u32[]{:S(2)}, u32[]{:S(2)}) collective-permute-start(bf16[240,2880]{1,0:T(8,128)(2,1)S(1)} %collective-permute-done.14.refs_4_.refs_10_), channel_id=1, source_target_pairs={{16,24},{24,16},{17,25},{25,17},{18,26},{26,18},{19,27},{27,19},{2... | collective-permute-start | bytes 4147208 | tf_op jit(solution)/shard_map/ppermute | solution.py:336
  194.2 13.6 %collective-permute-start.21 = (bf16[240,2880]{1,0:T(8,128)(2,1)}, bf16[240,2880]{1,0:T(8,128)(2,1)}, u32[]{:S(2)}, u32[]{:S(2)}) collective-permute-start(bf16[240,2880]{1,0:T(8,128)(2,1)} %collective-permute-done.15.refs_5_.refs_11_), channel_id=1, source_target_pairs={{16,24},{24,16},{17,25},{25,17},{18,26},{26,18},{19,27},{27,19},{2... | collective-permute-start | bytes 4147208 | tf_op jit(solution)/shard_map/ppermute | solution.py:336
  196.6 13.1 %collective-permute-start.26 = (bf16[240,2880]{1,0:T(8,128)(2,1)}, bf16[240,2880]{1,0:T(8,128)(2,1)}, u32[]{:S(2)}, u32[]{:S(2)}) collective-permute-start(bf16[240,2880]{1,0:T(8,128)(2,1)} %get-tuple-element.125), channel_id=1, source_target_pairs={{8,12},{12,8},{9,13},{13,9},{10,14},{14,10},{11,15},{15,11}} | collective-permute-start | bytes 4147208 | tf_op jit(solution)/shard_map/ppermute | solution.py:336
  198.3 13.0 %collective-permute-start.22 = (bf16[240,2880]{1,0:T(8,128)(2,1)}, bf16[240,2880]{1,0:T(8,128)(2,1)}, u32[]{:S(2)}, u32[]{:S(2)}) collective-permute-start(bf16[240,2880]{1,0:T(8,128)(2,1)} %collective-permute-done.16.refs_6_.refs_12_), channel_id=1, source_target_pairs={{16,24},{24,16},{17,25},{25,17},{18,26},{26,18},{19,27},{27,19},{2... | collective-permute-start | bytes 4147208 | tf_op jit(solution)/shard_map/ppermute | solution.py:336
  204.0 25.5 %collective-permute-start.10 = (bf16[160,2880]{1,0:T(8,128)(2,1)}, bf16[160,2880]{1,0:T(8,128)(2,1)}, u32[]{:S(2)}, u32[]{:S(2)}) collective-permute-start(bf16[160,2880]{1,0:T(8,128)(2,1)} %get-tuple-element.76), channel_id=1, source_target_pairs={{0,16},{8,24},{1,17},{9,25},{2,18},{10,26},{3,19},{11,27},{4,20},{... | collective-permute-start | bytes 2764808 | tf_op jit(solution)/shard_map/ppermute | solution.py:336
  205.9 51.2 %collective-permute-start.27 = (bf16[240,2880]{1,0:T(8,128)(2,1)}, bf16[240,2880]{1,0:T(8,128)(2,1)}, u32[]{:S(2)}, u32[]{:S(2)}) collective-permute-start(bf16[240,2880]{1,0:T(8,128)(2,1)} %get-tuple-element.124), channel_id=1, source_target_pairs={{8,12},{12,8},{9,13},{13,9},{10,14},{14,10},{11,15},{15,11}} | collective-permute-start | bytes 4147208 | tf_op jit(solution)/shard_map/ppermute | solution.py:336
  207.7 51.2 %collective-permute-start.28 = (bf16[240,2880]{1,0:T(8,128)(2,1)}, bf16[240,2880]{1,0:T(8,128)(2,1)}, u32[]{:S(2)}, u32[]{:S(2)}) collective-permute-start(bf16[240,2880]{1,0:T(8,128)(2,1)} %get-tuple-element.123), channel_id=1, source_target_pairs={{8,12},{12,8},{9,13},{13,9},{10,14},{14,10},{11,15},{15,11}} | collective-permute-start | bytes 4147208 | tf_op jit(solution)/shard_map/ppermute | solution.py:336
  209.6 57.9 %collective-permute-start.29 = (bf16[240,2880]{1,0:T(8,128)(2,1)}, bf16[240,2880]{1,0:T(8,128)(2,1)}, u32[]{:S(2)}, u32[]{:S(2)}) collective-permute-start(bf16[240,2880]{1,0:T(8,128)(2,1)} %collective-permute-done.26.refs_7_), channel_id=1, source_target_pairs={{8,9},{9,8},{10,11},{11,10},{12,13},{13,12},{14,15},{15,14}} | collective-permute-start | bytes 4147208 | tf_op jit(solution)/shard_map/ppermute | solution.py:336
  256.5 6.9 %collective-permute-start.23 = (bf16[160,2880]{1,0:T(8,128)(2,1)}, bf16[160,2880]{1,0:T(8,128)(2,1)S(1)}, u32[]{:S(2)}, u32[]{:S(2)}) collective-permute-start(bf16[160,2880]{1,0:T(8,128)(2,1)} %get-tuple-element.131), channel_id=1, source_target_pairs={{0,8},{8,0},{16,24},{24,16},{1,9},{9,1},{17,25},{25,17},{2,10},{10... | collective-permute-start | bytes 2764808 | tf_op jit(solution)/shard_map/ppermute | solution.py:341
  256.5 4.1 collective-permute-start.54
  257.1 15.4 %collective-permute-start.32 = (bf16[240,2880]{1,0:T(8,128)(2,1)}, bf16[240,2880]{1,0:T(8,128)(2,1)}, u32[]{:S(2)}, u32[]{:S(2)}) collective-permute-start(bf16[240,2880]{1,0:T(8,128)(2,1)} %collective-permute-done.26.refs_7_), channel_id=1, source_target_pairs={{8,0},{9,1},{10,2},{11,3},{12,4},{13,5},{14,6},{15,7}} | collective-permute-start | bytes 4147208 | tf_op jit(solution)/shard_map/ppermute | solution.py:336
  258.9 10.1 %collective-permute-start.30 = (bf16[240,2880]{1,0:T(8,128)(2,1)}, bf16[240,2880]{1,0:T(8,128)(2,1)}, u32[]{:S(2)}, u32[]{:S(2)}) collective-permute-start(bf16[240,2880]{1,0:T(8,128)(2,1)} %collective-permute-done.27.refs_8_), channel_id=1, source_target_pairs={{8,9},{9,8},{10,11},{11,10},{12,13},{13,12},{14,15},{15,14}} | collective-permute-start | bytes 4147208 | tf_op jit(solution)/shard_map/ppermute | solution.py:336
  260.7 10.1 %collective-permute-start.31 = (bf16[240,2880]{1,0:T(8,128)(2,1)}, bf16[240,2880]{1,0:T(8,128)(2,1)}, u32[]{:S(2)}, u32[]{:S(2)}) collective-permute-start(bf16[240,2880]{1,0:T(8,128)(2,1)} %collective-permute-done.28.refs_9_), channel_id=1, source_target_pairs={{8,9},{9,8},{10,11},{11,10},{12,13},{13,12},{14,15},{15,14}} | collective-permute-start | bytes 4147208 | tf_op jit(solution)/shard_map/ppermute | solution.py:336
  263.4 2.6 collective-permute-start.53
  266.0 24.4 %collective-permute-start.24 = (bf16[320,1440]{1,0:T(8,128)(2,1)}, bf16[320,1440]{1,0:T(8,128)(2,1)}, u32[]{:S(2)}, u32[]{:S(2)}) collective-permute-start(bf16[320,1440]{1,0:T(8,128)(2,1)} %get-tuple-element.143), channel_id=1, source_target_pairs={{0,4},{4,0},{1,5},{5,1},{2,6},{6,2},{3,7},{7,3},{8,12},{12,8},{9,1... | collective-permute-start | bytes 2764808 | tf_op jit(solution)/shard_map/ppermute | solution.py:346
  267.5 51.5 %collective-permute-start.33 = (bf16[240,2880]{1,0:T(8,128)(2,1)}, bf16[240,2880]{1,0:T(8,128)(2,1)S(1)}, u32[]{:S(2)}, u32[]{:S(2)}) collective-permute-start(bf16[240,2880]{1,0:T(8,128)(2,1)} %collective-permute-done.27.refs_8_), channel_id=1, source_target_pairs={{8,0},{9,1},{10,2},{11,3},{12,4},{13,5},{14,6},{15,7}} | collective-permute-start | bytes 4147208 | tf_op jit(solution)/shard_map/ppermute | solution.py:336
  269.0 58.7 %collective-permute-start.34 = (bf16[240,2880]{1,0:T(8,128)(2,1)}, bf16[240,2880]{1,0:T(8,128)(2,1)}, u32[]{:S(2)}, u32[]{:S(2)}) collective-permute-start(bf16[240,2880]{1,0:T(8,128)(2,1)} %collective-permute-done.28.refs_9_), channel_id=1, source_target_pairs={{8,0},{9,1},{10,2},{11,3},{12,4},{13,5},{14,6},{15,7}} | collective-permute-start | bytes 4147208 | tf_op jit(solution)/shard_map/ppermute | solution.py:336
  270.8 58.4 %collective-permute-start.35 = (bf16[240,2880]{1,0:T(8,128)(2,1)}, bf16[240,2880]{1,0:T(8,128)(2,1)}, u32[]{:S(2)}, u32[]{:S(2)}) collective-permute-start(bf16[240,2880]{1,0:T(8,128)(2,1)} %collective-permute-done.29.refs_10_), channel_id=1, source_target_pairs={{8,0},{9,1},{10,2},{11,3},{12,4},{13,5},{14,6},{15,7}} | collective-permute-start | bytes 4147208 | tf_op jit(solution)/shard_map/ppermute | solution.py:336
  272.5 57.1 %collective-permute-start.36 = (bf16[240,2880]{1,0:T(8,128)(2,1)}, bf16[240,2880]{1,0:T(8,128)(2,1)}, u32[]{:S(2)}, u32[]{:S(2)}) collective-permute-start(bf16[240,2880]{1,0:T(8,128)(2,1)} %collective-permute-done.30.refs_11_), channel_id=1, source_target_pairs={{8,0},{9,1},{10,2},{11,3},{12,4},{13,5},{14,6},{15,7}} | collective-permute-start | bytes 4147208 | tf_op jit(solution)/shard_map/ppermute | solution.py:336
  290.4 41.8 %collective-permute-start.37 = (bf16[240,2880]{1,0:T(8,128)(2,1)}, bf16[240,2880]{1,0:T(8,128)(2,1)}, u32[]{:S(2)}, u32[]{:S(2)}) collective-permute-start(bf16[240,2880]{1,0:T(8,128)(2,1)} %collective-permute-done.31.refs_12_), channel_id=1, source_target_pairs={{8,0},{9,1},{10,2},{11,3},{12,4},{13,5},{14,6},{15,7}} | collective-permute-start | bytes 4147208 | tf_op jit(solution)/shard_map/ppermute | solution.py:336
  319.0 21.8 %collective-permute-start.25 = (bf16[160,2880]{1,0:T(8,128)(2,1)}, bf16[160,2880]{1,0:T(8,128)(2,1)}, u32[]{:S(2)}, u32[]{:S(2)}) collective-permute-start(bf16[160,2880]{1,0:T(8,128)(2,1)} %get-tuple-element.96), channel_id=1, source_target_pairs={{16,0},{24,8},{17,1},{25,9},{18,2},{26,10},{19,3},{27,11},{20,4},{... | collective-permute-start | bytes 2764808 | tf_op jit(solution)/shard_map/ppermute | solution.py:336
  327.7 29.0 %collective-permute-start.55 = (bf16[4,16,720]{2,1,0:T(8,128)(2,1)}, bf16[4,16,720]{2,1,0:T(8,128)(2,1)}, u32[]{:S(2)}, u32[]{:S(2)}) collective-permute-start(bf16[4,16,720]{2,1,0:T(8,128)(2,1)} %bitcast.77), channel_id=1, source_target_pairs={{0,4},{4,0},{1,5},{5,1},{2,6},{6,2},{3,7},{7,3},{8,12},{12,8},{9,1... | collective-permute-start | bytes 276488 | tf_op jit(solution)/shard_map/ppermute | solution.py:346
  329.2 172.7 %collective-permute-start.40 = (bf16[640,1440]{0,1:T(8,128)(2,1)}, bf16[640,1440]{0,1:T(8,128)(2,1)}, u32[]{:S(2)}, u32[]{:S(2)}) collective-permute-start(bf16[640,1440]{0,1:T(8,128)(2,1)} %copy.38), channel_id=1, source_target_pairs={{0,1},{1,0},{2,3},{3,2},{4,5},{5,4},{6,7},{7,6},{8,9},{9,8},{10,11... | collective-permute-start | bytes 5529608 | tf_op jit(solution)/shard_map/ppermute | solution.py:341
  329.7 83.5 %collective-permute-start.43 = (bf16[640,1440]{0,1:T(8,128)(2,1)}, bf16[640,1440]{0,1:T(8,128)(2,1)}, u32[]{:S(2)}, u32[]{:S(2)}) collective-permute-start(bf16[640,1440]{0,1:T(8,128)(2,1)} %copy.38), channel_id=1, source_target_pairs={{0,2},{1,3},{2,0},{3,1},{4,6},{5,7},{6,4},{7,5},{8,10},{9,11},{10,... | collective-permute-start | bytes 5529608 | tf_op jit(solution)/shard_map/ppermute | solution.py:341
  346.9 2.8 collective-permute-start.38
  347.1 2.5 collective-permute-start.60
  350.7 70.4 %collective-permute-start.41 = (bf16[320,768]{1,0:T(8,128)(2,1)S(1)}, bf16[320,768]{1,0:T(8,128)(2,1)}, u32[]{:S(2)}, u32[]{:S(2)}) collective-permute-start(bf16[320,768]{1,0:T(8,128)(2,1)S(1)} %get-tuple-element.141), channel_id=1, source_target_pairs={{0,1},{1,0},{2,3},{3,2},{4,5},{5,4},{6,7},{7,6},{8,9},{9,8},{10,11... | collective-permute-start | bytes 1474568 | tf_op jit(solution)/shard_map/ppermute | solution.py:341
  351.1 73.7 %collective-permute-start.39 = (bf16[320,768]{1,0:T(8,128)(2,1)S(1)}, bf16[320,768]{1,0:T(8,128)(2,1)}, u32[]{:S(2)}, u32[]{:S(2)}) collective-permute-start(bf16[320,768]{1,0:T(8,128)(2,1)S(1)} %get-tuple-element.140), channel_id=1, source_target_pairs={{0,4},{4,0},{1,5},{5,1},{2,6},{6,2},{3,7},{7,3},{8,12},{12,8},{9,1... | collective-permute-start | bytes 1474568 | tf_op jit(solution)/shard_map/ppermute | solution.py:346
  356.7 9.8 %collective-permute-start.61 = (bf16[4,16,720]{2,1,0:T(8,128)(2,1)S(1)}, bf16[4,16,720]{2,1,0:T(8,128)(2,1)S(1)}, u32[]{:S(2)}, u32[]{:S(2)}) collective-permute-start(bf16[4,16,720]{2,1,0:T(8,128)(2,1)S(1)} %bitcast.99), channel_id=1, source_target_pairs={{0,4},{4,0},{1,5},{5,1},{2,6},{6,2},{3,7},{7,3},{8,12},{12,8},{9,1... | collective-permute-start | bytes 276488 | tf_op jit(solution)/shard_map/ppermute | solution.py:346
  366.4 149.0 %collective-permute-start.46 = (bf16[640,1440]{0,1:T(8,128)(2,1)}, bf16[640,1440]{0,1:T(8,128)(2,1)}, u32[]{:S(2)}, u32[]{:S(2)}) collective-permute-start(bf16[640,1440]{0,1:T(8,128)(2,1)} %copy.38), channel_id=1, source_target_pairs={{1,2},{2,1},{5,6},{6,5},{9,10},{10,9},{13,14},{14,13},{17,18},{18,... | collective-permute-start | bytes 5529608 | tf_op jit(solution)/shard_map/ppermute | solution.py:609
  413.2 104.4 %collective-permute-start.47 = (bf16[640,1440]{0,1:T(8,128)(2,1)}, bf16[640,1440]{0,1:T(8,128)(2,1)}, u32[]{:S(2)}, u32[]{:S(2)}) collective-permute-start(bf16[640,1440]{0,1:T(8,128)(2,1)} %collective-permute-done.43), channel_id=1, source_target_pairs={{2,3},{1,0},{6,7},{5,4},{10,11},{9,8},{14,15},{13,12},{18,19},{17,... | collective-permute-start | bytes 5529608 | tf_op jit(solution)/shard_map/ppermute | solution.py:610
  421.1 62.5 %collective-permute-start.44 = (bf16[320,768]{1,0:T(8,128)(2,1)}, bf16[320,768]{1,0:T(8,128)(2,1)}, u32[]{:S(2)}, u32[]{:S(2)}) collective-permute-start(bf16[320,768]{1,0:T(8,128)(2,1)} %get-tuple-element.142), channel_id=1, source_target_pairs={{0,2},{1,3},{2,0},{3,1},{4,6},{5,7},{6,4},{7,5},{8,10},{9,11},{10,... | collective-permute-start | bytes 1474568 | tf_op jit(solution)/shard_map/ppermute | solution.py:341
  424.8 68.4 %collective-permute-start.48 = (bf16[320,768]{1,0:T(8,128)(2,1)S(1)}, bf16[320,768]{1,0:T(8,128)(2,1)S(1)}, u32[]{:S(2)}, u32[]{:S(2)}) collective-permute-start(bf16[320,768]{1,0:T(8,128)(2,1)S(1)} %get-tuple-element.139), channel_id=1, source_target_pairs={{0,3},{1,2},{2,1},{3,0},{4,7},{5,6},{6,5},{7,4},{8,11},{9,10},{10,... | collective-permute-start | bytes 1474568 | tf_op jit(solution)/shard_map/ppermute | solution.py:341
  483.6 13.2 %collective-permute-start.45 = (bf16[320,768]{1,0:T(8,128)(2,1)}, bf16[320,768]{1,0:T(8,128)(2,1)S(1)}, u32[]{:S(2)}, u32[]{:S(2)}) collective-permute-start(bf16[320,768]{1,0:T(8,128)(2,1)} %collective-permute-done.44), channel_id=1, source_target_pairs={{0,4},{4,0},{1,5},{5,1},{2,6},{6,2},{3,7},{7,3},{8,12},{12,8},{9,1... | collective-permute-start | bytes 1474568 | tf_op jit(solution)/shard_map/ppermute | solution.py:346
  493.3 14.4 %collective-permute-start.42 = (bf16[320,768]{1,0:T(8,128)(2,1)}, bf16[320,768]{1,0:T(8,128)(2,1)S(1)}, u32[]{:S(2)}, u32[]{:S(2)}) collective-permute-start(bf16[320,768]{1,0:T(8,128)(2,1)} %collective-permute-done.41), channel_id=1, source_target_pairs={{0,4},{4,0},{1,5},{5,1},{2,6},{6,2},{3,7},{7,3},{8,12},{12,8},{9,1... | collective-permute-start | bytes 1474568 | tf_op jit(solution)/shard_map/ppermute | solution.py:346
  496.8 19.2 %collective-permute-start.49 = (bf16[320,768]{1,0:T(8,128)(2,1)S(1)}, bf16[320,768]{1,0:T(8,128)(2,1)S(1)}, u32[]{:S(2)}, u32[]{:S(2)}) collective-permute-start(bf16[320,768]{1,0:T(8,128)(2,1)S(1)} %collective-permute-done.48), channel_id=1, source_target_pairs={{0,4},{4,0},{1,5},{5,1},{2,6},{6,2},{3,7},{7,3},{8,12},{12,8},{9,1... | collective-permute-start | bytes 1474568 | tf_op jit(solution)/shard_map/ppermute | solution.py:346
  501.9 21.1 %collective-permute-start.56 = (bf16[2,16,720]{2,1,0:T(8,128)(2,1)S(1)}, bf16[2,16,720]{2,1,0:T(8,128)(2,1)S(1)}, u32[]{:S(2)}, u32[]{:S(2)}) collective-permute-start(bf16[2,16,720]{2,1,0:T(8,128)(2,1)S(1)} %get-tuple-element.150), channel_id=1, source_target_pairs={{0,1},{1,0},{2,3},{3,2},{4,5},{5,4},{6,7},{7,6},{8,9},{9,8},{10,11... | collective-permute-start | bytes 138248 | tf_op jit(solution)/shard_map/ppermute | solution.py:341
  507.6 16.0 %collective-permute-start.57 = (bf16[2,16,720]{2,1,0:T(8,128)(2,1)S(1)}, bf16[2,16,720]{2,1,0:T(8,128)(2,1)S(1)}, u32[]{:S(2)}, u32[]{:S(2)}) collective-permute-start(bf16[2,16,720]{2,1,0:T(8,128)(2,1)S(1)} %get-tuple-element.151), channel_id=1, source_target_pairs={{0,2},{1,3},{2,0},{3,1},{4,6},{5,7},{6,4},{7,5},{8,10},{9,11},{10,... | collective-permute-start | bytes 138248 | tf_op jit(solution)/shard_map/ppermute | solution.py:341
  515.4 10.7 %collective-permute-start.58 = (bf16[2,16,720]{2,1,0:T(8,128)(2,1)S(1)}, bf16[2,16,720]{2,1,0:T(8,128)(2,1)S(1)}, u32[]{:S(2)}, u32[]{:S(2)}) collective-permute-start(bf16[2,16,720]{2,1,0:T(8,128)(2,1)S(1)} %get-tuple-element.152), channel_id=1, source_target_pairs={{0,3},{1,2},{2,1},{3,0},{4,7},{5,6},{6,5},{7,4},{8,11},{9,10},{10,... | collective-permute-start | bytes 138248 | tf_op jit(solution)/shard_map/ppermute | solution.py:341
  516.0 10.1 %collective-permute-start.62 = (bf16[2,16,720]{2,1,0:T(8,128)(2,1)S(1)}, bf16[2,16,720]{2,1,0:T(8,128)(2,1)S(1)}, u32[]{:S(2)}, u32[]{:S(2)}) collective-permute-start(bf16[2,16,720]{2,1,0:T(8,128)(2,1)S(1)} %get-tuple-element.156), channel_id=1, source_target_pairs={{0,1},{1,0},{2,3},{3,2},{4,5},{5,4},{6,7},{7,6},{8,9},{9,8},{10,11... | collective-permute-start | bytes 138248 | tf_op jit(solution)/shard_map/ppermute | solution.py:341
  517.6 8.6 %collective-permute-start.63 = (bf16[2,16,720]{2,1,0:T(8,128)(2,1)S(1)}, bf16[2,16,720]{2,1,0:T(8,128)(2,1)S(1)}, u32[]{:S(2)}, u32[]{:S(2)}) collective-permute-start(bf16[2,16,720]{2,1,0:T(8,128)(2,1)S(1)} %get-tuple-element.157), channel_id=1, source_target_pairs={{0,2},{1,3},{2,0},{3,1},{4,6},{5,7},{6,4},{7,5},{8,10},{9,11},{10,... | collective-permute-start | bytes 138248 | tf_op jit(solution)/shard_map/ppermute | solution.py:341
  523.1 4.5 collective-permute-start.64
  523.6 19.9 %collective-permute-start.50 = (bf16[360,768]{1,0:T(8,128)(2,1)S(1)}, bf16[360,768]{1,0:T(8,128)(2,1)S(1)}, u32[]{:S(2)}, u32[]{:S(2)}) collective-permute-start(bf16[360,768]{1,0:T(8,128)(2,1)S(1)} %get-tuple-element.138), channel_id=1, source_target_pairs={{0,1},{1,0},{2,3},{3,2},{4,5},{5,4},{6,7},{7,6},{8,9},{9,8},{10,11... | collective-permute-start | bytes 1658888 | tf_op jit(solution)/shard_map/ppermute | solution.py:341
  527.6 39.1 %collective-permute-start.51 = (bf16[360,768]{1,0:T(8,128)(2,1)S(1)}, bf16[360,768]{1,0:T(8,128)(2,1)S(1)}, u32[]{:S(2)}, u32[]{:S(2)}) collective-permute-start(bf16[360,768]{1,0:T(8,128)(2,1)S(1)} %get-tuple-element.137), channel_id=1, source_target_pairs={{0,2},{1,3},{2,0},{3,1},{4,6},{5,7},{6,4},{7,5},{8,10},{9,11},{10,... | collective-permute-start | bytes 1658888 | tf_op jit(solution)/shard_map/ppermute | solution.py:341
  533.5 41.7 %collective-permute-start.52 = (bf16[360,768]{1,0:T(8,128)(2,1)S(1)}, bf16[360,768]{1,0:T(8,128)(2,1)S(1)}, u32[]{:S(2)}, u32[]{:S(2)}) collective-permute-start(bf16[360,768]{1,0:T(8,128)(2,1)S(1)} %get-tuple-element.136), channel_id=1, source_target_pairs={{0,3},{1,2},{2,1},{3,0},{4,7},{5,6},{6,5},{7,4},{8,11},{9,10},{10,... | collective-permute-start | bytes 1658888 | tf_op jit(solution)/shard_map/ppermute | solution.py:341
  (26 other events, 364.4 us)

commit v3 on v2

--- a/solution.py
+++ b/solution.py
@@ -355,20 +355,6 @@
     return lax.dynamic_slice_in_dim(value, parity * (value.shape[0] // 2) + low, rows, 0)
 
 
-def far_half(weight, parity, chosen):
-    step = weight.shape[0] // 2 // PIECES
-    cuts = [parity_half(weight, parity, i * step, step) for i in range(PIECES)]
-    near = [
-        move(cut, ("segment", "fsdp"), lambda s, f: (s, 1 - f) if s in chosen else None)
-        for cut in cuts
-    ]
-    cross = [
-        move(cut, ("segment", "dp"), lambda s, z: (s, z ^ 1) if s in chosen else None)
-        for cut in near
-    ]
-    return near + cross
-
-
 def to_other_core(values, chosen):
     return [
         move(value, ("segment",), lambda s: (s ^ 1,) if s in chosen else None) for value in values
@@ -409,7 +395,7 @@
     part = channels // fsdp
     tiles = [(low, min(group, channels - low)) for low in range(0, channels, group)]
     weight, squeeze, excite = weight[0], squeeze[0], excite[0]
-    assert sections == 4 and dp & (dp - 1) == 0 and len(tiles) == dp
+    assert PIECES == 3 and sections == 4 and dp & (dp - 1) == 0 and len(tiles) == dp
     fast = fsdp == 2 and dp % 2 == 0 and part % (2 * 16 * PIECES) == 0
     first_stage, last_stage = (0, 1), (2, 3)
     barrier = lax.optimization_barrier
@@ -487,13 +473,13 @@
             4 * channels * channels,
         )
 
-    def backward_pass(d_out, saved, where, pieces, through):
-        bufs, sems = weight_bufs(1 + through, n_w)
+    def backward_pass(d_out, saved, where, pieces, at, through):
+        bufs, sems = weight_bufs(1 + through, len(at))
         outs = [((dp, rows, group), BF), ((SUB, hidden), F32), ((SUB, channels), F32)] * 2
         outs += [((rows, channels), BF)] * through
         return call(
-            functools.partial(backward_kernel, (n_w, n_s, images, pixels, tiles, through)),
-            [meta_for([*w_at, *s_at], where)],
+            functools.partial(backward_kernel, (len(at), n_s, images, pixels, tiles, through)),
+            [meta_for([*at, *s_at], where)],
             [d_out, *saved[0][:3], *saved[1][:3]],
             pieces,
             outs,
@@ -507,7 +493,15 @@
         meta_s = meta_for(s_at, 0)
         mine, give = picked[1:]
         later_weight, give = barrier((weight, give))
-        far_early = far_half(later_weight, parity, last_stage)
+
+        def near(index):
+            cut = parity_half(later_weight, parity, index * step, step)
+            return move(cut, ("segment", "fsdp"), lambda s, f: (s, 1 - f) if s > 1 else None)
+
+        def cross(cut):
+            return move(cut, ("segment", "dp"), lambda s, z: (s, z ^ 1) if s > 1 else None)
+
+        near_w = [near(index) for index in range(PIECES)]
 
         def share(block, mine, give):
             recv = move(
@@ -556,72 +550,119 @@
             )
 
         d_last = flat(cotangent, back_order, False)[0]
-        recv = None
-        _, (keep, give) = share(0, mine, give)
+        mine, near_w[0] = barrier((mine, near_w[0]))
+        recv_a, (keep, give) = share(0, mine, give)
         give, d_last = barrier((give, d_last))
+        cross_w = [cross(near_w[0])]
+        keep, cross_w[0], near_w[1] = barrier((keep, cross_w[0], near_w[1]))
         result = finish(0, h_first, keep, give)
         h_mid, saved_a = result[0], result[1:6]
-        _, (keep, give) = share(1, *result[6:])
+        mid_mine, mid_give = result[6:]
+        cross_w.append(cross(near_w[1]))
+        mid_mine, cross_w[1], near_w[2] = barrier((mid_mine, cross_w[1], near_w[2]))
+        recv_b, (keep, give) = share(1, mid_mine, mid_give)
         late_weight, give = barrier((weight, give))
         result = finish(1, h_mid, keep, give)
         h_out, saved_b = result[0], result[1:6]
-        far_late = far_half(late_weight, parity, (1,))
+        cross_w.append(cross(near_w[2]))
+        far_early = near_w + cross_w
+        far_late = [
+            move(cut, ("segment", "fsdp"), lambda s, f: (s, 1 - f) if s == 1 else None)
+            for cut in (late_weight[:half], late_weight[half:])
+        ]
         late_other = to_other_core(far_late, (1,))
+        late_at = [mine_at, far_at, far_at + half]
         early = [weight, *far_early, *s_own]
         early += [w_swapped, *to_other_core(far_early, last_stage), *s_other]
         late = [weight, *far_late, *s_own, w_swapped, *late_other, *s_other]
+        first_units = [jnp.concatenate(pair, axis=0) for pair in ((mine, recv_a), (mid_mine, recv_b))]
     else:
         d_last = flat(cotangent, back_order, False)[0]
         whole = lax.all_gather(weight, "fsdp", axis=0, tiled=True)
+        late_at = w_at
         early = late = [whole, *s_own, swap(whole, "segment"), *s_other]
         result = forward_pass(h_first, 0, early)
         h_mid, h_out, saved_a, saved_b = result[0], result[1], result[2:7], result[7:12]
+        first_units = None
     first = (saved_a, saved_b)
 
     final = stage == 1
-    h_in = move(h_out, ("segment",), lambda s: (s + 2,) if s < 2 else None)
-    result = forward_pass(h_in, 1, early)
-    last = (result[2:7], result[7:12])
-    h_a = jnp.where(final, h_in, h_first)
-    h_b = jnp.where(final, result[0], h_mid)
+
+    def of_stage(ours, theirs):
+        return jnp.where(final, ours, theirs)
+
+    def fsdp_unit(value):
+        found = []
+        for step in range(fsdp):
+            cut = lax.dynamic_slice_in_dim(value, ((mesh_f - step) % fsdp) * part, part, 1)
+            if step and first_units is not None:
+                cut = move(
+                    cut,
+                    ("segment", "fsdp"),
+                    lambda s, f: (s, (f - step) % fsdp) if s > 1 else None,
+                )
+            elif step:
+                cut = rotate(cut, "fsdp", -step)
+            found.append(cut)
+        return found
+
+    def dp_slots(unit):
+        found = [unit] + [swap(unit, "dp", step) for step in range(1, dp if dp != 4 else 3)]
+        if dp == 4:
+            inner = lax.ppermute(unit, "dp", [(1, 2), (2, 1)])
+            found.append(inner)
+        return found
+
+    def forwarded(slots):
+        if dp != 4:
+            return slots
+        outer = lax.ppermute(slots[2], "dp", [(2, 3), (1, 0)])
+        return slots[:3] + [jnp.where((mesh_z == 1) | (mesh_z == 2), slots[3], outer)]
 
     def swap_blocks(first, second):
         keep = jnp.where(core == 0, first, second)
         give = jnp.where(core == 0, second, first)
-        return jnp.concatenate([keep, swap(give, "segment")], axis=-2)
-
-    def of_stage(ours, theirs):
-        return jnp.where(final, ours, theirs)
-
-    h_pair = swap_blocks(h_a, h_b)
-    h_mine = []
-    for step in range(fsdp):
-        cut = lax.dynamic_slice_in_dim(h_pair, ((mesh_f - step) % fsdp) * part, part, 1)
-        h_mine.append(rotate(cut, "fsdp", -step) if step else cut)
-
-    ended = backward_pass(d_last, last, 1, early, True)
-    h_mine, ended = barrier((h_mine, ended))
-    h_mine = jnp.concatenate(h_mine, axis=0)
-    h_all = [h_mine] + [None] * (dp - 1)
+        return keep, swap(give, "segment")
+
+    def both_cores(first, second):
+        return jnp.concatenate(swap_blocks(first, second), axis=-2)
+
+    h_in = move(h_out, ("segment",), lambda s: (s + 2,) if s < 2 else None)
+    unit_a = fsdp_unit(h_in)
+    if first_units is not None:
+        h_in, far_late[0] = barrier((h_in, far_late[0]))
+    result = forward_pass(h_in, 1, early)
+    last = (result[2:7], result[7:12])
+    unit_b = fsdp_unit(result[0])
+    unit_a, mid = barrier((unit_a, result[0]))
+    if first_units is None:
+        theirs = [jnp.concatenate(fsdp_unit(h), axis=0) for h in (h_first, h_mid)]
+    else:
+        theirs = first_units
+    slots_a = dp_slots(of_stage(jnp.concatenate(unit_a, axis=0), theirs[0]))
+
+    ended = backward_pass(d_last, last, 1, early, w_at, True)
+    unit_b, ended = barrier((unit_b, ended))
+    slots_b = dp_slots(of_stage(jnp.concatenate(unit_b, axis=0), theirs[1]))
+    pool = both_cores(*[of_stage(last[b][3], first[b][3]) for b in range(2)])
+    hid = both_cores(*[of_stage(last[b][4], first[b][4]) for b in range(2)])
+    pool, hid = small_exchange(pool, hid, mesh_f, mesh_z)
+
+    d_out = move(ended[6], ("segment",), lambda s: (s - 2,) if s > 1 else None)
     if dp == 4:
-        h_all[1] = swap(h_mine, "dp", 1)
-        h_all[2] = swap(h_mine, "dp", 2)
-        inner = lax.ppermute(h_mine, "dp", [(1, 2), (2, 1)])
-        outer = lax.ppermute(h_all[2], "dp", [(2, 3), (1, 0)])
-        h_all[3] = jnp.where((mesh_z == 1) | (mesh_z == 2), inner, outer)
-    else:
-        for step in range(1, dp):
-            h_all[step] = swap(h_mine, "dp", step)
-    pool = swap_blocks(*[of_stage(last[b][3], first[b][3]) for b in range(2)])
-    hid = swap_blocks(*[of_stage(last[b][4], first[b][4]) for b in range(2)])
-    pool, hid = small_exchange(pool, hid, mesh_f, mesh_z)
-
-    d_out = move(ended[6], ("segment",), lambda s: (s - 2,) if s > 1 else None)
-    begun = backward_pass(d_out, first, 0, late, False)
+        d_out, slots_a[2] = barrier((d_out, slots_a[2]))
+    begun = backward_pass(d_out, first, 0, late, late_at, False)
     d_pre, d_sq, d_ex = [
-        swap_blocks(*[of_stage(ended[3 * b + i], begun[3 * b + i]) for b in range(2)])
+        both_cores(*[of_stage(ended[3 * b + i], begun[3 * b + i]) for b in range(2)])
         for i in range(3)
     ]
+    h_all = []
+    for slot_a, slot_b in zip(forwarded(slots_a), forwarded(slots_b)):
+        keep, other = swap_blocks(slot_a, slot_b)
+        cuts = []
+        for step in range(fsdp):
+            cuts += [side[step * rows : (step + 1) * rows] for side in (keep, other)]
+        h_all.append(jnp.concatenate(cuts, axis=0))
 
     total = None
     for step in range(dp):

time: 589 us -> 632 us (1.073)
  starting transfers between devices: 103 us -> 136 us
  local copies, waits for them, and re-layouts: 37.9 us -> 47.3 us
  waiting for transfers between devices: 325 us -> 333 us
    ppermute x30 -> x24, waiting for transfers between devices: 135 us -> 74.5 us  [move(): return lax.ppermute(value, axes, pairs)]
    ppermute x2 -> x4, waiting for transfers between devices: 0.01 us -> 55.2 us  [the longest x2 33.3 us: dp_slots(): inner = lax.ppermute(unit, 'dp', [(1, 2), (2, 1)])]
    ppermute x26 -> x31, waiting for transfers between devices: 160 us -> 197 us  [swap(): return lax.ppermute(value, axis, [(i, i ^ stride) for i in range(count)])]
    ppermute x30 -> x24, starting transfers between devices: 59.1 us -> 90.9 us  [move(): return lax.ppermute(value, axes, pairs)]
    ppermute x7 -> x6, waiting for transfers between devices: 30 us -> 5.52 us  [rotate(): lax.ppermute(value, axis, [(i, (i + steps) % count) for i in range(count)])]
    slice x0 -> x9, local copies, waits for them, and re-layouts: none -> 14.7 us  [the longest x8 8.71 us: on_device(): cuts += [side[step * rows:(step + 1) * rows] for side in (keep, other)]]
    ppermute x26 -> x31, starting transfers between devices: 27.7 us -> 33.2 us  [swap(): return lax.ppermute(value, axis, [(i, i ^ stride) for i in range(count)])]
  transfers between devices with their start and end apart: 65 -> 65, of which waited for: 21 -> 20; matrix products, arithmetic and copies ran while one was open for 12% -> 11% of each run, Pallas kernels for 13% -> 12%
where the time goes in v3:
time: 632 us; the launch traced here: 623 us
  waiting for transfers between devices  333 us (53%)
  starting transfers between devices  136 us (22%)
  Pallas kernels  76.2 us (12%)
  local copies, waits for them, and re-layouts  47.3 us (7%)
  other arithmetic  17 us (3%)
  matrix products  11.7 us (2%)
    ppermute x31, waiting for transfers between devices, swap(): return lax.ppermute(value, axis, [(i, i ^ stride) for i in range(count)])  197 us
    ppermute x24, starting transfers between devices, move(): return lax.ppermute(value, axes, pairs)  90.9 us
    pallas_call x9, Pallas kernels, call(): pl.pallas_call(kernel, out_shape=[jax.ShapeDtypeStruct(shape, dtype) for...  76.2 us
    ppermute x24, waiting for transfers between devices, move(): return lax.ppermute(value, axes, pairs)  74.5 us
    ppermute x2, waiting for transfers between devices, dp_slots(): inner = lax.ppermute(unit, 'dp', [(1, 2), (2, 1)])  33.3 us
    ppermute x31, starting transfers between devices, swap(): return lax.ppermute(value, axis, [(i, i ^ stride) for i in range(count)])  33.2 us
    ppermute x2, waiting for transfers between devices, forwarded(): outer = lax.ppermute(slots[2], 'dp', [(2, 3), (1, 0)])  21.9 us
  transfers between devices with their start and end apart: 65, of which 20 were waited for; matrix products, arithmetic and copies ran while one was open for 11% of the time, Pallas kernels for 12%

profile of v3, /device:TPU:10, one launch (start us, length us, event | category | flops | bytes accessed | tf_op | source)
XLA Modules:
  0.0 622.8 jit_solution(6256614579197745276)
XLA Ops:
  0.7 4.8 reshape.78.all_ref
  6.6 3.6 shard_map.85
  10.2 4.4 constant_dynamic-slice_fusion.7
  14.7 3.4 collective-permute-start
  20.2 2.7 copy.29
  23.5 27.1 %collective-permute-done.refs_1_.refs_7_ = bf16[240,2880]{1,0:T(8,128)(2,1)} collective-permute-done((bf16[240,2880]{1,0:T(8,128)(2,1)}, bf16[240,2880]{1,0:T(8,128)(2,1)}, u32[]{:S(2)}, u32[]{:S(2)}) %collective-permute-start) | collective-permute-done | bytes 1382432 | tf_op jit(solution)/shard_map/ppermute | solution.py:336
  50.6 3.4 collective-permute-start.4
  54.1 2.4 collective-permute-start.3
  56.5 17.8 %collective-permute-done.6.refs_1_.refs_8_.refs_14_.refs_10_ = bf16[1440,360]{1,0:T(8,128)(2,1)S(1)} collective-permute-done((bf16[1440,360]{1,0:T(8,128)(2,1)}, bf16[1440,360]{1,0:T(8,128)(2,1)S(1)}, u32[]{:S(2)}, u32[]{:S(2)}) %collective-permute-start.6) | collective-permute-done | bytes 1036832 | tf_op jit(solution)/shard_map/ppermute | solution.py:341
  75.4 4.9 reshape.79.all_ref
  80.2 3.1 shard_map.87.up_ref
  84.0 27.9 %collective-permute-done.7.refs_2_.refs_9_.refs_15_.refs_11_ = bf16[1440,360]{1,0:T(8,128)(2,1)} collective-permute-done((bf16[1440,360]{1,0:T(8,128)(2,1)S(1)}, bf16[1440,360]{1,0:T(8,128)(2,1)}, u32[]{:S(2)}, u32[]{:S(2)}) %collective-permute-start.7) | collective-permute-done | bytes 1036832 | tf_op jit(solution)/shard_map/ppermute | solution.py:341
  112.4 2.9 shard_map.86
  116.9 2.4 collective-permute-start.12
  119.3 2.4 collective-permute-start.11
  121.6 4.1 copy.30.refs_3_.refs_17_.refs_23_.refs_15_
  125.8 4.1 shard_map.88
  130.5 21.5 %collective-permute-done.12.refs_3_.refs_9_ = bf16[240,2880]{1,0:T(8,128)(2,1)} collective-permute-done((bf16[240,2880]{1,0:T(8,128)(2,1)}, bf16[240,2880]{1,0:T(8,128)(2,1)}, u32[]{:S(2)}, u32[]{:S(2)}) %collective-permute-start.12) | collective-permute-done | bytes 1382432 | tf_op jit(solution)/shard_map/ppermute | solution.py:336
  152.0 2.1 collective-permute-done.11.refs_5_.refs_11_
  154.9 3.2 shard_map.89
  158.1 6.0 fusion.80
  164.1 2.7 collective-permute-start.17
  170.3 2.4 collective-permute-start.18
  172.7 3.8 shard_map.90
  179.9 2.2 collective-permute-start.22
  182.1 23.8 %collective-permute-done.18.refs_6_.refs_12_ = bf16[240,2880]{1,0:T(8,128)(2,1)} collective-permute-done((bf16[240,2880]{1,0:T(8,128)(2,1)}, bf16[240,2880]{1,0:T(8,128)(2,1)}, u32[]{:S(2)}, u32[]{:S(2)}) %collective-permute-start.18) | collective-permute-done | bytes 1382432 | tf_op jit(solution)/shard_map/ppermute | solution.py:336
  207.8 39.5 %collective-permute-start.23 = (bf16[240,2880]{1,0:T(8,128)(2,1)}, bf16[240,2880]{1,0:T(8,128)(2,1)}, u32[]{:S(2)}, u32[]{:S(2)}) collective-permute-start(bf16[240,2880]{1,0:T(8,128)(2,1)} %collective-permute-done.11.refs_5_.refs_11_), channel_id=1, source_target_pairs={{16,24},{24,16},{17,25},{25,17},{18,26},{26,18},{19,27},{27,19},{2... | collective-permute-start | bytes 4147208 | tf_op jit(solution)/shard_map/ppermute | solution.py:336
  252.1 2.7 collective-permute-start.29
  254.9 3.6 collective-permute-start.16
  258.5 24.1 %shard_map.91 = (bf16[160,2880]{1,0:T(8,128)(2,1)}, bf16[160,2880]{1,0:T(8,128)(2,1)}, f32[160,2880]{1,0:T(8,128)}, f32[8,2880]{1,0:T(8,128)}, f32[8,360]{1,0:T(...) custom-call(s32[13]{0:T(128)} %stack.152.meta, ...), custom_call_target="tpu_custom_call" | custom-call | flops 5308416000 | bytes 33177600 | tf_op jit(solution)/shard_map/pallas_call | solution.py:313
  285.0 2.6 constant_dynamic-slice_fusion.3
  287.5 2.4 collective-permute-start.25
  293.2 27.1 %shard_map.92 = (bf16[4,160,768]{2,1,0:T(8,128)(2,1)}, f32[8,360]{1,0:T(8,128)}, f32[8,2880]{1,0:T(8,128)}, bf16[4,160,768]{2,1,0:T(8,128)(2,1)}, f32[8,360]{1,0...) custom-call(s32[13]{0:T(128)} %stack.152.meta, bf16[160,2880]{1,0:T(8,128)(2,1)} %shard_map.87.up_ref, ...), custom_call_target="tpu_custom_call" | custom-call | flops 5308416000 | bytes 33177600 | tf_op jit(solution)/shard_map/pallas_call | solution.py:313
  322.7 2.1 broadcast_select_fusion.13
  324.9 2.7 collective-permute-start.28
  328.0 2.2 collective-permute-start.27
  332.9 2.8 collective-permute-start.30
  335.7 34.0 %collective-permute-done.28 = bf16[320,1440]{1,0:T(8,128)(2,1)S(1)} collective-permute-done((bf16[320,1440]{1,0:T(8,128)(2,1)S(1)}, bf16[320,1440]{1,0:T(8,128)(2,1)S(1)}, u32[]{:S(2)}, u32[]{:S(2)}) %collective-permute-start.28) | collective-permute-done | bytes 921632 | tf_op jit(solution)/shard_map/ppermute | solution.py:341
  369.8 2.6 collective-permute-start.31
  372.4 3.4 collective-permute-start.39
  377.7 29.0 %collective-permute-done.35 = bf16[320,1440]{1,0:T(8,128)(2,1)S(1)} collective-permute-done((bf16[320,1440]{1,0:T(8,128)(2,1)S(1)}, bf16[320,1440]{1,0:T(8,128)(2,1)S(1)}, u32[]{:S(2)}, u32[]{:S(2)}) %collective-permute-start.35) | collective-permute-done | bytes 921632 | tf_op jit(solution)/shard_map/ppermute | solution.py:341
  408.0 11.1 %collective-permute-done.39 = bf16[320,1440]{1,0:T(8,128)(2,1)S(1)} collective-permute-done((bf16[320,1440]{1,0:T(8,128)(2,1)S(1)}, bf16[320,1440]{1,0:T(8,128)(2,1)S(1)}, u32[]{:S(2)}, u32[]{:S(2)}) %collective-permute-start.39) | collective-permute-done | bytes 921632 | tf_op jit(solution)/shard_map/ppermute | solution.py:341
  422.0 18.1 %collective-permute-done.43 = bf16[320,1440]{1,0:T(8,128)(2,1)S(1)} collective-permute-done((bf16[320,1440]{1,0:T(8,128)(2,1)S(1)}, bf16[320,1440]{1,0:T(8,128)(2,1)S(1)}, u32[]{:S(2)}, u32[]{:S(2)}) %collective-permute-start.43) | collective-permute-done | bytes 921632 | tf_op jit(solution)/shard_map/ppermute | solution.py:612
  445.0 15.3 %collective-permute-done.45 = bf16[320,1440]{1,0:T(8,128)(2,1)S(1)} collective-permute-done((bf16[320,1440]{1,0:T(8,128)(2,1)S(1)}, bf16[320,1440]{1,0:T(8,128)(2,1)S(1)}, u32[]{:S(2)}, u32[]{:S(2)}) %collective-permute-start.45) | collective-permute-done | bytes 921632 | tf_op jit(solution)/shard_map/ppermute | solution.py:612
  460.2 3.4 collective-permute-done.44
  463.6 18.5 %collective-permute-done.46 = bf16[320,1440]{1,0:T(8,128)(2,1)S(1)} collective-permute-done((bf16[320,1440]{1,0:T(8,128)(2,1)S(1)}, bf16[320,1440]{1,0:T(8,128)(2,1)S(1)}, u32[]{:S(2)}, u32[]{:S(2)}) %collective-permute-start.46) | collective-permute-done | bytes 921632 | tf_op jit(solution)/shard_map/ppermute | solution.py:619
  484.4 4.4 shard_map.93
  490.9 2.2 fusion.89
  493.9 2.5 collective-permute-start.37
  502.1 2.5 collective-permute-start.41
  504.6 7.9 %collective-permute-done.37 = bf16[320,768]{1,0:T(8,128)(2,1)} collective-permute-done((bf16[320,768]{1,0:T(8,128)(2,1)S(1)}, bf16[320,768]{1,0:T(8,128)(2,1)}, u32[]{:S(2)}, u32[]{:S(2)}) %collective-permute-start.37) | collective-permute-done | bytes 491552 | tf_op jit(solution)/shard_map/ppermute | solution.py:341
  514.3 2.7 collective-permute-start.56
  518.7 19.6 %collective-permute-done.41 = bf16[320,768]{1,0:T(8,128)(2,1)S(1)} collective-permute-done((bf16[320,768]{1,0:T(8,128)(2,1)S(1)}, bf16[320,768]{1,0:T(8,128)(2,1)S(1)}, u32[]{:S(2)}, u32[]{:S(2)}) %collective-permute-start.41) | collective-permute-done | bytes 491552 | tf_op jit(solution)/shard_map/ppermute | solution.py:341
  540.9 8.6 %collective-permute-done.48 = bf16[320,768]{1,0:T(8,128)(2,1)S(1)} collective-permute-done((bf16[320,768]{1,0:T(8,128)(2,1)S(1)}, bf16[320,768]{1,0:T(8,128)(2,1)S(1)}, u32[]{:S(2)}, u32[]{:S(2)}) %collective-permute-start.48) | collective-permute-done | bytes 491552 | tf_op jit(solution)/shard_map/ppermute | solution.py:341
  549.5 2.3 collective-permute-start.58
  552.4 3.1 fusion.8
  557.6 5.5 collective-permute-done.49
  563.2 2.5 add_convert_fusion
  566.1 4.0 collective-permute-start.50
  570.3 5.1 collective-permute-start.51
  578.2 9.4 %collective-permute-done.50 = bf16[360,768]{1,0:T(8,128)(2,1)S(1)} collective-permute-done((bf16[360,768]{1,0:T(8,128)(2,1)S(1)}, bf16[360,768]{1,0:T(8,128)(2,1)S(1)}, u32[]{:S(2)}, u32[]{:S(2)}) %collective-permute-start.50) | collective-permute-done | bytes 552992 | tf_op jit(solution)/shard_map/ppermute | solution.py:341
  587.6 24.0 %collective-permute-done.51 = bf16[360,768]{1,0:T(8,128)(2,1)S(1)} collective-permute-done((bf16[360,768]{1,0:T(8,128)(2,1)S(1)}, bf16[360,768]{1,0:T(8,128)(2,1)S(1)}, u32[]{:S(2)}, u32[]{:S(2)}) %collective-permute-start.51) | collective-permute-done | bytes 552992 | tf_op jit(solution)/shard_map/ppermute | solution.py:341
  611.6 8.2 %collective-permute-done.52 = bf16[360,768]{1,0:T(8,128)(2,1)S(1)} collective-permute-done((bf16[360,768]{1,0:T(8,128)(2,1)S(1)}, bf16[360,768]{1,0:T(8,128)(2,1)S(1)}, u32[]{:S(2)}, u32[]{:S(2)}) %collective-permute-start.52) | collective-permute-done | bytes 552992 | tf_op jit(solution)/shard_map/ppermute | solution.py:341
  620.0 2.3 maximum_convert_fusion
  (226 shorter events, 67.8 us)
Async XLA Ops:
  0.6 111.2 %collective-permute-start.2 = (bf16[1440,2880]{1,0:T(8,128)(2,1)}, bf16[1440,2880]{1,0:T(8,128)(2,1)}, u32[]{:S(2)}, u32[]{:S(2)}) collective-permute-start(bf16[1440,2880]{1,0:T(8,128)(2,1)} %bitcast.78), channel_id=1, source_target_pairs={{0,8},{8,0},{16,24},{24,16},{1,9},{9,1},{17,25},{25,17},{2,10},{10... | collective-permute-start | bytes 24883208 | tf_op jit(solution)/shard_map/ppermute | solution.py:341
  14.7 36.0 %collective-permute-start = (bf16[240,2880]{1,0:T(8,128)(2,1)}, bf16[240,2880]{1,0:T(8,128)(2,1)}, u32[]{:S(2)}, u32[]{:S(2)}) collective-permute-start(bf16[240,2880]{1,0:T(8,128)(2,1)} %get-tuple-element.156), channel_id=1, source_target_pairs={{16,20},{20,16},{24,28},{28,24},{17,21},{21,17},{25,29},{29,25},{1... | collective-permute-start | bytes 4147208 | tf_op jit(solution)/shard_map/ppermute | solution.py:336
  19.4 54.8 %collective-permute-start.6 = (bf16[1440,360]{1,0:T(8,128)(2,1)}, bf16[1440,360]{1,0:T(8,128)(2,1)S(1)}, u32[]{:S(2)}, u32[]{:S(2)}) collective-permute-start(bf16[1440,360]{1,0:T(8,128)(2,1)} %pad_maximum_fusion.1), channel_id=1, source_target_pairs={{0,4},{4,0},{1,5},{5,1},{2,6},{6,2},{3,7},{7,3},{8,12},{12,8},{9,1... | collective-permute-start | bytes 3110408 | tf_op jit(solution)/shard_map/ppermute | solution.py:341
  22.8 96.4 %collective-permute-start.8 = (bf16[2880,360]{0,1:T(8,128)(2,1)}, bf16[2880,360]{0,1:T(8,128)(2,1)}, u32[]{:S(2)}, u32[]{:S(2)}) collective-permute-start(bf16[2880,360]{0,1:T(8,128)(2,1)} %copy.29), channel_id=1, source_target_pairs={{0,8},{8,0},{16,24},{24,16},{1,9},{9,1},{17,25},{25,17},{2,10},{10... | collective-permute-start | bytes 6220808 | tf_op jit(solution)/shard_map/ppermute | solution.py:341
  22.8 31.2 %collective-permute-start.1 = (bf16[160,1440]{1,0:T(8,128)(2,1)}, bf16[160,1440]{1,0:T(8,128)(2,1)S(1)}, u32[]{:S(2)}, u32[]{:S(2)}) collective-permute-start(bf16[160,1440]{1,0:T(8,128)(2,1)} %get-tuple-element.81), channel_id=1, source_target_pairs={{0,4},{4,0},{8,12},{12,8},{1,5},{5,1},{9,13},{13,9},{2,6},{6,2},{1... | collective-permute-start | bytes 1382408 | tf_op jit(solution)/shard_map/ppermute | solution.py:336
  50.6 64.6 %collective-permute-start.4 = (bf16[240,2880]{1,0:T(8,128)(2,1)}, bf16[240,2880]{1,0:T(8,128)(2,1)}, u32[]{:S(2)}, u32[]{:S(2)}) collective-permute-start(bf16[240,2880]{1,0:T(8,128)(2,1)} %get-tuple-element.155), channel_id=1, source_target_pairs={{16,20},{20,16},{24,28},{28,24},{17,21},{21,17},{25,29},{29,25},{1... | collective-permute-start | bytes 4147208 | tf_op jit(solution)/shard_map/ppermute | solution.py:336
  54.1 62.8 %collective-permute-start.3 = (bf16[240,2880]{1,0:T(8,128)(2,1)}, bf16[240,2880]{1,0:T(8,128)(2,1)}, u32[]{:S(2)}, u32[]{:S(2)}) collective-permute-start(bf16[240,2880]{1,0:T(8,128)(2,1)} %collective-permute-done.refs_1_.refs_7_), channel_id=1, source_target_pairs={{16,17},{17,16},{18,19},{19,18},{24,25},{25,24},{26,27},{27,26},{2... | collective-permute-start | bytes 4147208 | tf_op jit(solution)/shard_map/ppermute | solution.py:336
  74.2 37.6 %collective-permute-start.7 = (bf16[1440,360]{1,0:T(8,128)(2,1)S(1)}, bf16[1440,360]{1,0:T(8,128)(2,1)}, u32[]{:S(2)}, u32[]{:S(2)}) collective-permute-start(bf16[1440,360]{1,0:T(8,128)(2,1)S(1)} %collective-permute-done.6.refs_1_.refs_8_.refs_14_.refs_10_), channel_id=1, source_target_pairs={{0,1},{1,0},{2,3},{3,2},{4,5},{5,4},{6,7},{7,6},{8,9},{9,8},{10,11... | collective-permute-start | bytes 3110408 | tf_op jit(solution)/shard_map/ppermute | solution.py:341
  111.8 13.9 %collective-permute-start.9 = (bf16[1440,360]{1,0:T(8,128)(2,1)S(1)}, bf16[1440,360]{1,0:T(8,128)(2,1)}, u32[]{:S(2)}, u32[]{:S(2)}) collective-permute-start(bf16[1440,360]{1,0:T(8,128)(2,1)S(1)} %collective-permute-done.6.refs_1_.refs_8_.refs_14_.refs_10_), channel_id=1, source_target_pairs={{0,8},{8,0},{16,24},{24,16},{1,9},{9,1},{17,25},{25,17},{2,10},{10... | collective-permute-start | bytes 3110408 | tf_op jit(solution)/shard_map/ppermute | solution.py:341
  111.8 13.9 %collective-permute-start.10 = (bf16[1440,360]{1,0:T(8,128)(2,1)}, bf16[1440,360]{1,0:T(8,128)(2,1)}, u32[]{:S(2)}, u32[]{:S(2)}) collective-permute-start(bf16[1440,360]{1,0:T(8,128)(2,1)} %collective-permute-done.7.refs_2_.refs_9_.refs_15_.refs_11_), channel_id=1, source_target_pairs={{0,8},{8,0},{16,24},{24,16},{1,9},{9,1},{17,25},{25,17},{2,10},{10... | collective-permute-start | bytes 3110408 | tf_op jit(solution)/shard_map/ppermute | solution.py:341
  115.2 10.5 %collective-permute-start.5 = (bf16[160,2880]{1,0:T(8,128)(2,1)}, bf16[160,2880]{1,0:T(8,128)(2,1)}, u32[]{:S(2)}, u32[]{:S(2)}) collective-permute-start(bf16[160,2880]{1,0:T(8,128)(2,1)} %get-tuple-element.86), channel_id=1, source_target_pairs={{0,4},{4,0},{8,12},{12,8},{1,5},{5,1},{9,13},{13,9},{2,6},{6,2},{1... | collective-permute-start | bytes 2764808 | tf_op jit(solution)/shard_map/ppermute | solution.py:336
  116.9 35.1 %collective-permute-start.12 = (bf16[240,2880]{1,0:T(8,128)(2,1)}, bf16[240,2880]{1,0:T(8,128)(2,1)}, u32[]{:S(2)}, u32[]{:S(2)}) collective-permute-start(bf16[240,2880]{1,0:T(8,128)(2,1)} %get-tuple-element.154), channel_id=1, source_target_pairs={{16,20},{20,16},{24,28},{28,24},{17,21},{21,17},{25,29},{29,25},{1... | collective-permute-start | bytes 4147208 | tf_op jit(solution)/shard_map/ppermute | solution.py:336
  119.3 34.9 %collective-permute-start.11 = (bf16[240,2880]{1,0:T(8,128)(2,1)}, bf16[240,2880]{1,0:T(8,128)(2,1)}, u32[]{:S(2)}, u32[]{:S(2)}) collective-permute-start(bf16[240,2880]{1,0:T(8,128)(2,1)} %collective-permute-done.4.refs_2_.refs_8_), channel_id=1, source_target_pairs={{16,17},{17,16},{18,19},{19,18},{24,25},{25,24},{26,27},{27,26},{2... | collective-permute-start | bytes 4147208 | tf_op jit(solution)/shard_map/ppermute | solution.py:336
  129.8 24.3 %collective-permute-start.13 = (bf16[160,1440]{1,0:T(8,128)(2,1)}, bf16[160,1440]{1,0:T(8,128)(2,1)S(1)}, u32[]{:S(2)}, u32[]{:S(2)}) collective-permute-start(bf16[160,1440]{1,0:T(8,128)(2,1)} %get-tuple-element.91), channel_id=1, source_target_pairs={{0,4},{4,0},{8,12},{12,8},{1,5},{5,1},{9,13},{13,9},{2,6},{6,2},{1... | collective-permute-start | bytes 1382408 | tf_op jit(solution)/shard_map/ppermute | solution.py:336
  164.1 83.3 %collective-permute-start.17 = (bf16[720,2880]{1,0:T(8,128)(2,1)}, bf16[720,2880]{1,0:T(8,128)(2,1)}, u32[]{:S(2)}, u32[]{:S(2)}) collective-permute-start(bf16[720,2880]{1,0:T(8,128)(2,1)} %get-tuple-element.153), channel_id=1, source_target_pairs={{8,12},{12,8},{9,13},{13,9},{10,14},{14,10},{11,15},{15,11}} | collective-permute-start | bytes 12441608 | tf_op jit(solution)/shard_map/ppermute | solution.py:336
  166.8 5.9 collective-permute-start.14
  168.4 11.5 %collective-permute-start.19 = (bf16[240,2880]{1,0:T(8,128)(2,1)}, bf16[240,2880]{1,0:T(8,128)(2,1)S(1)}, u32[]{:S(2)}, u32[]{:S(2)}) collective-permute-start(bf16[240,2880]{1,0:T(8,128)(2,1)} %collective-permute-done.refs_1_.refs_7_), channel_id=1, source_target_pairs={{16,24},{24,16},{17,25},{25,17},{18,26},{26,18},{19,27},{27,19},{2... | collective-permute-start | bytes 4147208 | tf_op jit(solution)/shard_map/ppermute | solution.py:336
  170.3 35.6 %collective-permute-start.18 = (bf16[240,2880]{1,0:T(8,128)(2,1)}, bf16[240,2880]{1,0:T(8,128)(2,1)}, u32[]{:S(2)}, u32[]{:S(2)}) collective-permute-start(bf16[240,2880]{1,0:T(8,128)(2,1)} %collective-permute-done.12.refs_3_.refs_9_), channel_id=1, source_target_pairs={{16,17},{17,16},{18,19},{19,18},{24,25},{25,24},{26,27},{27,26},{2... | collective-permute-start | bytes 4147208 | tf_op jit(solution)/shard_map/ppermute | solution.py:336
  176.5 31.3 %collective-permute-start.15 = (bf16[160,2880]{1,0:T(8,128)(2,1)}, bf16[160,2880]{1,0:T(8,128)(2,1)S(1)}, u32[]{:S(2)}, u32[]{:S(2)}) collective-permute-start(bf16[160,2880]{1,0:T(8,128)(2,1)} %get-tuple-element.95), channel_id=1, source_target_pairs={{0,16},{8,24},{1,17},{9,25},{2,18},{10,26},{3,19},{11,27},{4,20},{... | collective-permute-start | bytes 2764808 | tf_op jit(solution)/shard_map/ppermute | solution.py:336
  177.8 74.4 %collective-permute-start.20 = (bf16[240,2880]{1,0:T(8,128)(2,1)}, bf16[240,2880]{1,0:T(8,128)(2,1)}, u32[]{:S(2)}, u32[]{:S(2)}) collective-permute-start(bf16[240,2880]{1,0:T(8,128)(2,1)} %collective-permute-done.4.refs_2_.refs_8_), channel_id=1, source_target_pairs={{16,24},{24,16},{17,25},{25,17},{18,26},{26,18},{19,27},{27,19},{2... | collective-permute-start | bytes 4147208 | tf_op jit(solution)/shard_map/ppermute | solution.py:336
  179.9 75.0 %collective-permute-start.22 = (bf16[240,2880]{1,0:T(8,128)(2,1)}, bf16[240,2880]{1,0:T(8,128)(2,1)}, u32[]{:S(2)}, u32[]{:S(2)}) collective-permute-start(bf16[240,2880]{1,0:T(8,128)(2,1)} %collective-permute-done.3.refs_4_.refs_10_), channel_id=1, source_target_pairs={{16,24},{24,16},{17,25},{25,17},{18,26},{26,18},{19,27},{27,19},{2... | collective-permute-start | bytes 4147208 | tf_op jit(solution)/shard_map/ppermute | solution.py:336
  205.9 52.6 %collective-permute-start.21 = (bf16[240,2880]{1,0:T(8,128)(2,1)}, bf16[240,2880]{1,0:T(8,128)(2,1)}, u32[]{:S(2)}, u32[]{:S(2)}) collective-permute-start(bf16[240,2880]{1,0:T(8,128)(2,1)} %collective-permute-done.12.refs_3_.refs_9_), channel_id=1, source_target_pairs={{16,24},{24,16},{17,25},{25,17},{18,26},{26,18},{19,27},{27,19},{2... | collective-permute-start | bytes 4147208 | tf_op jit(solution)/shard_map/ppermute | solution.py:336
  207.8 50.7 %collective-permute-start.23 = (bf16[240,2880]{1,0:T(8,128)(2,1)}, bf16[240,2880]{1,0:T(8,128)(2,1)}, u32[]{:S(2)}, u32[]{:S(2)}) collective-permute-start(bf16[240,2880]{1,0:T(8,128)(2,1)} %collective-permute-done.11.refs_5_.refs_11_), channel_id=1, source_target_pairs={{16,24},{24,16},{17,25},{25,17},{18,26},{26,18},{19,27},{27,19},{2... | collective-permute-start | bytes 4147208 | tf_op jit(solution)/shard_map/ppermute | solution.py:336
  247.4 11.1 %collective-permute-start.24 = (bf16[240,2880]{1,0:T(8,128)(2,1)}, bf16[240,2880]{1,0:T(8,128)(2,1)}, u32[]{:S(2)}, u32[]{:S(2)}) collective-permute-start(bf16[240,2880]{1,0:T(8,128)(2,1)} %collective-permute-done.18.refs_6_.refs_12_), channel_id=1, source_target_pairs={{16,24},{24,16},{17,25},{25,17},{18,26},{26,18},{19,27},{27,19},{2... | collective-permute-start | bytes 4147208 | tf_op jit(solution)/shard_map/ppermute | solution.py:336
  252.1 80.8 %collective-permute-start.29 = (bf16[720,2880]{1,0:T(8,128)(2,1)}, bf16[720,2880]{1,0:T(8,128)(2,1)}, u32[]{:S(2)}, u32[]{:S(2)}) collective-permute-start(bf16[720,2880]{1,0:T(8,128)(2,1)} %get-tuple-element.152), channel_id=1, source_target_pairs={{8,12},{12,8},{9,13},{13,9},{10,14},{14,10},{11,15},{15,11}} | collective-permute-start | bytes 12441608 | tf_op jit(solution)/shard_map/ppermute | solution.py:336
  254.9 65.4 %collective-permute-start.16 = (bf16[160,1440]{1,0:T(8,128)(2,1)}, bf16[160,1440]{1,0:T(8,128)(2,1)}, u32[]{:S(2)}, u32[]{:S(2)}) collective-permute-start(bf16[160,1440]{1,0:T(8,128)(2,1)} %get-tuple-element.193), channel_id=1, source_target_pairs={{16,20},{20,16},{24,28},{28,24},{17,21},{21,17},{25,29},{29,25},{1... | collective-permute-start | bytes 1382408 | tf_op jit(solution)/shard_map/ppermute | solution.py:336
  283.7 6.3 %collective-permute-start.53 = (bf16[8,2880]{1,0:T(8,128)(2,1)S(1)}, bf16[8,2880]{1,0:T(8,128)(2,1)S(1)}, u32[]{:S(2)}, u32[]{:S(2)}) collective-permute-start(bf16[8,2880]{1,0:T(8,128)(2,1)S(1)} %get-tuple-element.196), channel_id=1, source_target_pairs={{0,8},{8,0},{16,24},{24,16},{1,9},{9,1},{17,25},{25,17},{2,10},{10... | collective-permute-start | bytes 138248 | tf_op jit(solution)/shard_map/ppermute | solution.py:341
  284.6 5.3 collective-permute-start.54
  287.5 35.2 %collective-permute-start.25 = (bf16[160,1440]{1,0:T(8,128)(2,1)}, bf16[160,1440]{1,0:T(8,128)(2,1)}, u32[]{:S(2)}, u32[]{:S(2)}) collective-permute-start(bf16[160,1440]{1,0:T(8,128)(2,1)} %get-tuple-element.191), channel_id=1, source_target_pairs={{16,20},{20,16},{24,28},{28,24},{17,21},{21,17},{25,29},{29,25},{1... | collective-permute-start | bytes 1382408 | tf_op jit(solution)/shard_map/ppermute | solution.py:336
  291.6 29.6 %collective-permute-start.55 = (bf16[4,16,720]{2,1,0:T(8,128)(2,1)}, bf16[4,16,720]{2,1,0:T(8,128)(2,1)}, u32[]{:S(2)}, u32[]{:S(2)}) collective-permute-start(bf16[4,16,720]{2,1,0:T(8,128)(2,1)} %bitcast.76), channel_id=1, source_target_pairs={{0,4},{4,0},{1,5},{5,1},{2,6},{6,2},{3,7},{7,3},{8,12},{12,8},{9,1... | collective-permute-start | bytes 276488 | tf_op jit(solution)/shard_map/ppermute | solution.py:346
  324.9 44.9 %collective-permute-start.28 = (bf16[320,1440]{1,0:T(8,128)(2,1)S(1)}, bf16[320,1440]{1,0:T(8,128)(2,1)S(1)}, u32[]{:S(2)}, u32[]{:S(2)}) collective-permute-start(bf16[320,1440]{1,0:T(8,128)(2,1)S(1)} %get-tuple-element.150), channel_id=1, source_target_pairs={{0,2},{1,3},{2,0},{3,1},{4,6},{5,7},{6,4},{7,5},{8,10},{9,11},{10,... | collective-permute-start | bytes 2764808 | tf_op jit(solution)/shard_map/ppermute | solution.py:341
  327.6 48.3 %collective-permute-start.34 = (bf16[320,1440]{1,0:T(8,128)(2,1)S(1)}, bf16[320,1440]{1,0:T(8,128)(2,1)S(1)}, u32[]{:S(2)}, u32[]{:S(2)}) collective-permute-start(bf16[320,1440]{1,0:T(8,128)(2,1)S(1)} %get-tuple-element.150), channel_id=1, source_target_pairs={{0,1},{1,0},{2,3},{3,2},{4,5},{5,4},{6,7},{7,6},{8,9},{9,8},{10,11... | collective-permute-start | bytes 2764808 | tf_op jit(solution)/shard_map/ppermute | solution.py:341
  328.0 44.4 %collective-permute-start.27 = (bf16[160,2880]{1,0:T(8,128)(2,1)S(1)}, bf16[160,2880]{1,0:T(8,128)(2,1)}, u32[]{:S(2)}, u32[]{:S(2)}) collective-permute-start(bf16[160,2880]{1,0:T(8,128)(2,1)S(1)} %copy-done.38), channel_id=1, source_target_pairs={{16,0},{24,8},{17,1},{25,9},{18,2},{26,10},{19,3},{27,11},{20,4},{... | collective-permute-start | bytes 2764808 | tf_op jit(solution)/shard_map/ppermute | solution.py:336
  330.2 76.5 %collective-permute-start.35 = (bf16[320,1440]{1,0:T(8,128)(2,1)S(1)}, bf16[320,1440]{1,0:T(8,128)(2,1)S(1)}, u32[]{:S(2)}, u32[]{:S(2)}) collective-permute-start(bf16[320,1440]{1,0:T(8,128)(2,1)S(1)} %get-tuple-element.151), channel_id=1, source_target_pairs={{0,1},{1,0},{2,3},{3,2},{4,5},{5,4},{6,7},{7,6},{8,9},{9,8},{10,11... | collective-permute-start | bytes 2764808 | tf_op jit(solution)/shard_map/ppermute | solution.py:341
  332.9 151.4 %collective-permute-start.30 = (bf16[720,2880]{1,0:T(8,128)(2,1)}, bf16[720,2880]{1,0:T(8,128)(2,1)}, u32[]{:S(2)}, u32[]{:S(2)}) collective-permute-start(bf16[720,2880]{1,0:T(8,128)(2,1)} %collective-permute-done.17.refs_7_), channel_id=1, source_target_pairs={{8,0},{9,1},{10,2},{11,3},{12,4},{13,5},{14,6},{15,7}} | collective-permute-start | bytes 12441608 | tf_op jit(solution)/shard_map/ppermute | solution.py:336
  369.8 114.6 %collective-permute-start.31 = (bf16[720,2880]{1,0:T(8,128)(2,1)}, bf16[720,2880]{1,0:T(8,128)(2,1)}, u32[]{:S(2)}, u32[]{:S(2)}) collective-permute-start(bf16[720,2880]{1,0:T(8,128)(2,1)} %collective-permute-done.29.refs_8_), channel_id=1, source_target_pairs={{8,0},{9,1},{10,2},{11,3},{12,4},{13,5},{14,6},{15,7}} | collective-permute-start | bytes 12441608 | tf_op jit(solution)/shard_map/ppermute | solution.py:336
  372.4 46.7 %collective-permute-start.39 = (bf16[320,1440]{1,0:T(8,128)(2,1)S(1)}, bf16[320,1440]{1,0:T(8,128)(2,1)S(1)}, u32[]{:S(2)}, u32[]{:S(2)}) collective-permute-start(bf16[320,1440]{1,0:T(8,128)(2,1)S(1)} %get-tuple-element.151), channel_id=1, source_target_pairs={{0,2},{1,3},{2,0},{3,1},{4,6},{5,7},{6,4},{7,5},{8,10},{9,11},{10,... | collective-permute-start | bytes 2764808 | tf_op jit(solution)/shard_map/ppermute | solution.py:341
  375.8 64.3 %collective-permute-start.43 = (bf16[320,1440]{1,0:T(8,128)(2,1)S(1)}, bf16[320,1440]{1,0:T(8,128)(2,1)S(1)}, u32[]{:S(2)}, u32[]{:S(2)}) collective-permute-start(bf16[320,1440]{1,0:T(8,128)(2,1)S(1)} %get-tuple-element.150), channel_id=1, source_target_pairs={{1,2},{2,1},{5,6},{6,5},{9,10},{10,9},{13,14},{14,13},{17,18},{18,... | collective-permute-start | bytes 2764808 | tf_op jit(solution)/shard_map/ppermute | solution.py:612
  406.8 34.7 %collective-permute-start.26 = (bf16[320,1440]{1,0:T(8,128)(2,1)S(1)}, bf16[320,1440]{1,0:T(8,128)(2,1)S(1)}, u32[]{:S(2)}, u32[]{:S(2)}) collective-permute-start(bf16[320,1440]{1,0:T(8,128)(2,1)S(1)} %broadcast_select_fusion.12), channel_id=1, source_target_pairs={{0,8},{8,0},{16,24},{24,16},{1,9},{9,1},{17,25},{25,17},{2,10},{10... | collective-permute-start | bytes 2764808 | tf_op jit(solution)/shard_map/ppermute | solution.py:341
  419.0 41.2 %collective-permute-start.45 = (bf16[320,1440]{1,0:T(8,128)(2,1)S(1)}, bf16[320,1440]{1,0:T(8,128)(2,1)S(1)}, u32[]{:S(2)}, u32[]{:S(2)}) collective-permute-start(bf16[320,1440]{1,0:T(8,128)(2,1)S(1)} %get-tuple-element.151), channel_id=1, source_target_pairs={{1,2},{2,1},{5,6},{6,5},{9,10},{10,9},{13,14},{14,13},{17,18},{18,... | collective-permute-start | bytes 2764808 | tf_op jit(solution)/shard_map/ppermute | solution.py:612
  440.1 23.5 %collective-permute-start.44 = (bf16[320,1440]{1,0:T(8,128)(2,1)S(1)}, bf16[320,1440]{1,0:T(8,128)(2,1)S(1)}, u32[]{:S(2)}, u32[]{:S(2)}) collective-permute-start(bf16[320,1440]{1,0:T(8,128)(2,1)S(1)} %collective-permute-done.28), channel_id=1, source_target_pairs={{2,3},{1,0},{6,7},{5,4},{10,11},{9,8},{14,15},{13,12},{18,19},{17,... | collective-permute-start | bytes 2764808 | tf_op jit(solution)/shard_map/ppermute | solution.py:619
  441.5 40.6 %collective-permute-start.46 = (bf16[320,1440]{1,0:T(8,128)(2,1)S(1)}, bf16[320,1440]{1,0:T(8,128)(2,1)S(1)}, u32[]{:S(2)}, u32[]{:S(2)}) collective-permute-start(bf16[320,1440]{1,0:T(8,128)(2,1)S(1)} %collective-permute-done.39), channel_id=1, source_target_pairs={{2,3},{1,0},{6,7},{5,4},{10,11},{9,8},{14,15},{13,12},{18,19},{17,... | collective-permute-start | bytes 2764808 | tf_op jit(solution)/shard_map/ppermute | solution.py:619
  460.2 23.1 %collective-permute-start.36 = (bf16[320,1440]{1,0:T(8,128)(2,1)S(1)}, bf16[320,1440]{1,0:T(8,128)(2,1)S(1)}, u32[]{:S(2)}, u32[]{:S(2)}) collective-permute-start(bf16[320,1440]{1,0:T(8,128)(2,1)S(1)} %get-tuple-element.172), channel_id=1, source_target_pairs={{0,8},{8,0},{16,24},{24,16},{1,9},{9,1},{17,25},{25,17},{2,10},{10... | collective-permute-start | bytes 2764808 | tf_op jit(solution)/shard_map/ppermute | solution.py:341
  463.6 27.3 %collective-permute-start.40 = (bf16[320,1440]{1,0:T(8,128)(2,1)}, bf16[320,1440]{1,0:T(8,128)(2,1)}, u32[]{:S(2)}, u32[]{:S(2)}) collective-permute-start(bf16[320,1440]{1,0:T(8,128)(2,1)} %get-tuple-element.174), channel_id=1, source_target_pairs={{0,8},{8,0},{16,24},{24,16},{1,9},{9,1},{17,25},{25,17},{2,10},{10... | collective-permute-start | bytes 2764808 | tf_op jit(solution)/shard_map/ppermute | solution.py:341
  483.3 21.3 %collective-permute-start.47 = (bf16[320,1440]{1,0:T(8,128)(2,1)}, bf16[320,1440]{1,0:T(8,128)(2,1)}, u32[]{:S(2)}, u32[]{:S(2)}) collective-permute-start(bf16[320,1440]{1,0:T(8,128)(2,1)} %get-tuple-element.158), channel_id=1, source_target_pairs={{0,8},{8,0},{16,24},{24,16},{1,9},{9,1},{17,25},{25,17},{2,10},{10... | collective-permute-start | bytes 2764808 | tf_op jit(solution)/shard_map/ppermute | solution.py:341
  490.3 3.5 collective-permute-start.32
  493.1 3.4 collective-permute-start.59
  493.9 18.5 %collective-permute-start.37 = (bf16[320,768]{1,0:T(8,128)(2,1)S(1)}, bf16[320,768]{1,0:T(8,128)(2,1)}, u32[]{:S(2)}, u32[]{:S(2)}) collective-permute-start(bf16[320,768]{1,0:T(8,128)(2,1)S(1)} %get-tuple-element.169), channel_id=1, source_target_pairs={{0,1},{1,0},{2,3},{3,2},{4,5},{5,4},{6,7},{7,6},{8,9},{9,8},{10,11... | collective-permute-start | bytes 1474568 | tf_op jit(solution)/shard_map/ppermute | solution.py:341
  500.0 14.3 %collective-permute-start.61 = (bf16[4,16,720]{2,1,0:T(8,128)(2,1)S(1)}, bf16[4,16,720]{2,1,0:T(8,128)(2,1)S(1)}, u32[]{:S(2)}, u32[]{:S(2)}) collective-permute-start(bf16[4,16,720]{2,1,0:T(8,128)(2,1)S(1)} %bitcast.98), channel_id=1, source_target_pairs={{0,4},{4,0},{1,5},{5,1},{2,6},{6,2},{3,7},{7,3},{8,12},{12,8},{9,1... | collective-permute-start | bytes 276488 | tf_op jit(solution)/shard_map/ppermute | solution.py:346
  500.6 16.4 %collective-permute-start.33 = (bf16[320,768]{1,0:T(8,128)(2,1)S(1)}, bf16[320,768]{1,0:T(8,128)(2,1)S(1)}, u32[]{:S(2)}, u32[]{:S(2)}) collective-permute-start(bf16[320,768]{1,0:T(8,128)(2,1)S(1)} %get-tuple-element.168), channel_id=1, source_target_pairs={{0,4},{4,0},{1,5},{5,1},{2,6},{6,2},{3,7},{7,3},{8,12},{12,8},{9,1... | collective-permute-start | bytes 1474568 | tf_op jit(solution)/shard_map/ppermute | solution.py:346
  502.1 36.3 %collective-permute-start.41 = (bf16[320,768]{1,0:T(8,128)(2,1)S(1)}, bf16[320,768]{1,0:T(8,128)(2,1)S(1)}, u32[]{:S(2)}, u32[]{:S(2)}) collective-permute-start(bf16[320,768]{1,0:T(8,128)(2,1)S(1)} %get-tuple-element.170), channel_id=1, source_target_pairs={{0,2},{1,3},{2,0},{3,1},{4,6},{5,7},{6,4},{7,5},{8,10},{9,11},{10,... | collective-permute-start | bytes 1474568 | tf_op jit(solution)/shard_map/ppermute | solution.py:341
  504.6 44.9 %collective-permute-start.48 = (bf16[320,768]{1,0:T(8,128)(2,1)S(1)}, bf16[320,768]{1,0:T(8,128)(2,1)S(1)}, u32[]{:S(2)}, u32[]{:S(2)}) collective-permute-start(bf16[320,768]{1,0:T(8,128)(2,1)S(1)} %get-tuple-element.167), channel_id=1, source_target_pairs={{0,3},{1,2},{2,1},{3,0},{4,7},{5,6},{6,5},{7,4},{8,11},{9,10},{10,... | collective-permute-start | bytes 1474568 | tf_op jit(solution)/shard_map/ppermute | solution.py:341
  512.5 39.3 %collective-permute-start.38 = (bf16[320,768]{1,0:T(8,128)(2,1)}, bf16[320,768]{1,0:T(8,128)(2,1)S(1)}, u32[]{:S(2)}, u32[]{:S(2)}) collective-permute-start(bf16[320,768]{1,0:T(8,128)(2,1)} %collective-permute-done.37), channel_id=1, source_target_pairs={{0,4},{4,0},{1,5},{5,1},{2,6},{6,2},{3,7},{7,3},{8,12},{12,8},{9,1... | collective-permute-start | bytes 1474568 | tf_op jit(solution)/shard_map/ppermute | solution.py:346
  514.3 51.6 %collective-permute-start.56 = (bf16[2,16,720]{2,1,0:T(8,128)(2,1)}, bf16[2,16,720]{2,1,0:T(8,128)(2,1)S(1)}, u32[]{:S(2)}, u32[]{:S(2)}) collective-permute-start(bf16[2,16,720]{2,1,0:T(8,128)(2,1)} %get-tuple-element.200), channel_id=1, source_target_pairs={{0,1},{1,0},{2,3},{3,2},{4,5},{5,4},{6,7},{7,6},{8,9},{9,8},{10,11... | collective-permute-start | bytes 138248 | tf_op jit(solution)/shard_map/ppermute | solution.py:341
  517.0 49.2 %collective-permute-start.57 = (bf16[2,16,720]{2,1,0:T(8,128)(2,1)}, bf16[2,16,720]{2,1,0:T(8,128)(2,1)S(1)}, u32[]{:S(2)}, u32[]{:S(2)}) collective-permute-start(bf16[2,16,720]{2,1,0:T(8,128)(2,1)} %get-tuple-element.201), channel_id=1, source_target_pairs={{0,2},{1,3},{2,0},{3,1},{4,6},{5,7},{6,4},{7,5},{8,10},{9,11},{10,... | collective-permute-start | bytes 138248 | tf_op jit(solution)/shard_map/ppermute | solution.py:341
  538.4 17.1 %collective-permute-start.42 = (bf16[320,768]{1,0:T(8,128)(2,1)S(1)}, bf16[320,768]{1,0:T(8,128)(2,1)S(1)}, u32[]{:S(2)}, u32[]{:S(2)}) collective-permute-start(bf16[320,768]{1,0:T(8,128)(2,1)S(1)} %collective-permute-done.41), channel_id=1, source_target_pairs={{0,4},{4,0},{1,5},{5,1},{2,6},{6,2},{3,7},{7,3},{8,12},{12,8},{9,1... | collective-permute-start | bytes 1474568 | tf_op jit(solution)/shard_map/ppermute | solution.py:346
  549.5 20.7 %collective-permute-start.58 = (bf16[2,16,720]{2,1,0:T(8,128)(2,1)S(1)}, bf16[2,16,720]{2,1,0:T(8,128)(2,1)S(1)}, u32[]{:S(2)}, u32[]{:S(2)}) collective-permute-start(bf16[2,16,720]{2,1,0:T(8,128)(2,1)S(1)} %copy-done.31), channel_id=1, source_target_pairs={{0,3},{1,2},{2,1},{3,0},{4,7},{5,6},{6,5},{7,4},{8,11},{9,10},{10,... | collective-permute-start | bytes 138248 | tf_op jit(solution)/shard_map/ppermute | solution.py:341
  551.8 11.3 %collective-permute-start.49 = (bf16[320,768]{1,0:T(8,128)(2,1)S(1)}, bf16[320,768]{1,0:T(8,128)(2,1)S(1)}, u32[]{:S(2)}, u32[]{:S(2)}) collective-permute-start(bf16[320,768]{1,0:T(8,128)(2,1)S(1)} %collective-permute-done.48), channel_id=1, source_target_pairs={{0,4},{4,0},{1,5},{5,1},{2,6},{6,2},{3,7},{7,3},{8,12},{12,8},{9,1... | collective-permute-start | bytes 1474568 | tf_op jit(solution)/shard_map/ppermute | solution.py:346
  555.5 14.7 %collective-permute-start.62 = (bf16[2,16,720]{2,1,0:T(8,128)(2,1)S(1)}, bf16[2,16,720]{2,1,0:T(8,128)(2,1)S(1)}, u32[]{:S(2)}, u32[]{:S(2)}) collective-permute-start(bf16[2,16,720]{2,1,0:T(8,128)(2,1)S(1)} %get-tuple-element.206), channel_id=1, source_target_pairs={{0,1},{1,0},{2,3},{3,2},{4,5},{5,4},{6,7},{7,6},{8,9},{9,8},{10,11... | collective-permute-start | bytes 138248 | tf_op jit(solution)/shard_map/ppermute | solution.py:341
  563.1 7.1 %collective-permute-start.63 = (bf16[2,16,720]{2,1,0:T(8,128)(2,1)S(1)}, bf16[2,16,720]{2,1,0:T(8,128)(2,1)S(1)}, u32[]{:S(2)}, u32[]{:S(2)}) collective-permute-start(bf16[2,16,720]{2,1,0:T(8,128)(2,1)S(1)} %get-tuple-element.207), channel_id=1, source_target_pairs={{0,2},{1,3},{2,0},{3,1},{4,6},{5,7},{6,4},{7,5},{8,10},{9,11},{10,... | collective-permute-start | bytes 138248 | tf_op jit(solution)/shard_map/ppermute | solution.py:341
  565.8 4.4 collective-permute-start.64
  566.1 21.4 %collective-permute-start.50 = (bf16[360,768]{1,0:T(8,128)(2,1)S(1)}, bf16[360,768]{1,0:T(8,128)(2,1)S(1)}, u32[]{:S(2)}, u32[]{:S(2)}) collective-permute-start(bf16[360,768]{1,0:T(8,128)(2,1)S(1)} %get-tuple-element.166), channel_id=1, source_target_pairs={{0,1},{1,0},{2,3},{3,2},{4,5},{5,4},{6,7},{7,6},{8,9},{9,8},{10,11... | collective-permute-start | bytes 1658888 | tf_op jit(solution)/shard_map/ppermute | solution.py:341
  570.3 41.3 %collective-permute-start.51 = (bf16[360,768]{1,0:T(8,128)(2,1)S(1)}, bf16[360,768]{1,0:T(8,128)(2,1)S(1)}, u32[]{:S(2)}, u32[]{:S(2)}) collective-permute-start(bf16[360,768]{1,0:T(8,128)(2,1)S(1)} %get-tuple-element.165), channel_id=1, source_target_pairs={{0,2},{1,3},{2,0},{3,1},{4,6},{5,7},{6,4},{7,5},{8,10},{9,11},{10,... | collective-permute-start | bytes 1658888 | tf_op jit(solution)/shard_map/ppermute | solution.py:341
  577.7 42.1 %collective-permute-start.52 = (bf16[360,768]{1,0:T(8,128)(2,1)S(1)}, bf16[360,768]{1,0:T(8,128)(2,1)S(1)}, u32[]{:S(2)}, u32[]{:S(2)}) collective-permute-start(bf16[360,768]{1,0:T(8,128)(2,1)S(1)} %get-tuple-element.164), channel_id=1, source_target_pairs={{0,3},{1,2},{2,1},{3,0},{4,7},{5,6},{6,5},{7,4},{8,11},{9,10},{10,... | collective-permute-start | bytes 1658888 | tf_op jit(solution)/shard_map/ppermute | solution.py:341
  (42 other events, 781.1 us)

commit v4 on v3

--- a/solution.py
+++ b/solution.py
@@ -207,11 +207,12 @@
 
 
 def forward_kernel(cfg, meta, h_ref, *refs):
-    n_w, n_s, images, pixels, tiles = cfg
+    n_w, n_s, images, pixels, tiles, send = cfg
     own, other, refs = split_pieces(refs, n_w, n_s)
     mid_ref, out_ref = refs[:2]
-    outs = (refs[2:7], refs[7:12])
-    w_buf, s_buf, e_buf, act_ref, w_sems, s_sems = refs[12:]
+    outs, refs = (refs[2:7], refs[7:12]), refs[12:]
+    sends, refs = refs[: 2 * send], refs[2 * send :]
+    w_buf, s_buf, e_buf, act_ref, w_sems, s_sems = refs
     loader = Loader(meta, own, other, n_w, tiles)
 
     @pl.when(meta[1] == 1)
@@ -244,6 +245,8 @@
                 act_ref,
                 outs[block],
             )
+            if send:
+                halves(src, sends[0].at[block], sends[1].at[block], meta[2])
 
 
 def backward_kernel(cfg, meta, up_ref, *refs):
@@ -308,7 +311,7 @@
                 dst[:, cols] = (src[:, cols].astype(F32) + back).astype(BF)
 
 
-def call(kernel, smem, dense, pieces, outs, scratch, flops, moved):
+def call(kernel, smem, dense, pieces, outs, scratch):
     vmem = pl.BlockSpec(memory_space=pltpu.VMEM)
     return pl.pallas_call(
         kernel,
@@ -319,7 +322,7 @@
         out_specs=[vmem] * len(outs),
         scratch_shapes=scratch,
         compiler_params=pltpu.CompilerParams(vmem_limit_bytes=VMEM_LIMIT),
-        cost_estimate=pl.CostEstimate(flops=flops, bytes_accessed=moved, transcendentals=0),
+        cost_estimate=pl.CostEstimate(flops=1024, bytes_accessed=1024, transcendentals=0),
     )(*smem, *dense, *pieces)
 
 
@@ -361,13 +364,13 @@
     ]
 
 
-def small_exchange(wide, narrow, mesh_f, mesh_z):
+def small_exchange(wides, narrow, mesh_f, mesh_z):
     fsdp, dp = lax.axis_size("fsdp"), lax.axis_size("dp")
-    rows, channels = wide.shape
+    rows, channels = wides[0].shape
     cut = channels // (fsdp * dp)
-    wide = wide.reshape(rows, fsdp, dp, cut).transpose(1, 2, 0, 3)
+    wides = [wide.reshape(rows, fsdp, dp, cut).transpose(1, 2, 0, 3) for wide in wides]
     narrow = jnp.broadcast_to(narrow, (fsdp, dp) + narrow.shape)
-    packed = jnp.concatenate([wide, narrow], axis=3).astype(BF)
+    packed = jnp.concatenate([*wides, narrow], axis=3)
     parts = []
     for step in range(fsdp):
         part = lax.dynamic_index_in_dim(packed, (mesh_f - step) % fsdp, 0, keepdims=False)
@@ -377,8 +380,8 @@
     for step in range(dp):
         part = lax.dynamic_index_in_dim(parts, mesh_z ^ step, 0, keepdims=False)
         found.append(swap(part, "dp", step) if step else part)
-    found = jnp.stack(found).reshape(-1, cut + narrow.shape[3])
-    return found[:, :cut], found[:, cut:]
+    found = jnp.stack(found).reshape(-1, packed.shape[3])
+    return found[:, : len(wides) * cut], found[:, len(wides) * cut :]
 
 
 def on_device(inputs, cotangent, plan, weight, squeeze, excite):
@@ -407,11 +410,9 @@
         half = part // 2
         near_at = far_at + parity * half
         cross_at = far_at + (1 - parity) * half
-        pair = jnp.concatenate([squeeze, excite], axis=0)
         near_s = [parity_half(side, parity, 0, half) for side in (squeeze, excite)]
-        near_s = swap(jnp.concatenate(near_s, axis=0), "fsdp")
-        cross_s = swap(near_s, "dp")
-        s_own = [pair, near_s, cross_s]
+        near_s, inputs = barrier((jnp.concatenate(near_s, axis=0), inputs))
+        near_s = swap(near_s, "fsdp")
         s_at = [mine_at, near_at, cross_at]
         step = half // PIECES
         w_at = [mine_at] + [near_at + i * step for i in range(PIECES)]
@@ -419,8 +420,8 @@
     else:
         both = [lax.all_gather(side, "fsdp", axis=0, tiled=True) for side in (squeeze, excite)]
         s_own = [jnp.concatenate(both, axis=0)]
+        s_other = [swap(s_own[0], "segment")]
         s_at = w_at = [jnp.int32(0)]
-    s_other = [swap(piece, "segment") for piece in s_own]
     n_w, n_s = len(w_at), len(s_at)
 
     def meta_for(at, where):
@@ -436,7 +437,7 @@
         outs = [shape] + [((rows, part), BF)] * (2 * send)
         kernel = functools.partial(pick_kernel, (images, pixels, images_dev))
         smem = [meta_for([], 0), order.astype(jnp.int32)]
-        return call(kernel, smem, [maps], [], outs, [], rows * channels, 4 * rows * channels)
+        return call(kernel, smem, [maps], [], outs, [])
 
     picked = flat(inputs, slots, fast)
     h_first = picked[0]
@@ -463,14 +464,14 @@
     def forward_pass(h_in, where, pieces):
         bufs, sems = weight_bufs(2, n_w)
         return call(
-            functools.partial(forward_kernel, (n_w, n_s, images, pixels, tiles)),
+            functools.partial(forward_kernel, (n_w, n_s, images, pixels, tiles, fast)),
             [meta_for([*w_at, *s_at], where)],
             [h_in],
             pieces,
-            [((rows, channels), BF)] * 2 + saved_shapes * 2,
+            [((rows, channels), BF)] * 2
+            + saved_shapes * 2
+            + [((2, rows, part), BF)] * (2 * fast),
             [*bufs, act_shape, *sems],
-            4 * rows * channels * channels,
-            4 * channels * channels,
         )
 
     def backward_pass(d_out, saved, where, pieces, at, through):
@@ -484,8 +485,6 @@
             pieces,
             outs,
             [*bufs, act_shape, act_shape, *sems],
-            4 * rows * channels * channels,
-            4 * channels * channels,
         )
 
     if fast:
@@ -519,17 +518,17 @@
                     pltpu.VMEM((part, channels), BF),
                     pltpu.SemaphoreType.DMA((len(tiles),)),
                 ],
-                4 * rows * part * channels,
-                2 * part * channels,
             )
 
         def share_kernel(block, meta, mine_ref, recv_ref, own, other, *refs):
             partial_kernel((tiles,), block, meta, mine_ref, recv_ref, own, other, *refs)
 
-        def finish(block, h_row, keep, give):
-            recv = move(
+        def meet(give):
+            return move(
                 give, ("segment", "fsdp"), lambda s, f: (s, 1 - f) if s in first_stage else None
             )
+
+        def finish(block, h_row, keep, recv):
             send = block == 0
             outs = [((rows, channels), BF), *saved_shapes]
             outs += [((rows, part), BF)] * (2 * send)
@@ -545,36 +544,42 @@
                     act_shape,
                     pltpu.SemaphoreType.DMA((2, n_s)),
                 ],
-                rows * channels * 64,
-                4 * channels * hidden,
             )
 
-        d_last = flat(cotangent, back_order, False)[0]
         mine, near_w[0] = barrier((mine, near_w[0]))
         recv_a, (keep, give) = share(0, mine, give)
-        give, d_last = barrier((give, d_last))
         cross_w = [cross(near_w[0])]
+        near_s, keep, cotangent = barrier((near_s, keep, cotangent))
+        cross_s = swap(near_s, "dp")
+        own_s = jnp.concatenate([squeeze, excite], axis=0)
+        sides = [swap(side, "segment") for side in (squeeze, excite)]
+        s_other = [jnp.concatenate(sides, axis=0)]
+        s_other += [swap(near_s, "segment")]
+        recv, cross_s = barrier((meet(give), cross_s))
+        s_other += [swap(cross_s, "segment")]
+        s_own = [own_s, near_s, cross_s]
+        d_last = flat(cotangent, back_order, False)[0]
         keep, cross_w[0], near_w[1] = barrier((keep, cross_w[0], near_w[1]))
-        result = finish(0, h_first, keep, give)
+        result = finish(0, h_first, keep, recv)
         h_mid, saved_a = result[0], result[1:6]
         mid_mine, mid_give = result[6:]
         cross_w.append(cross(near_w[1]))
-        mid_mine, cross_w[1], near_w[2] = barrier((mid_mine, cross_w[1], near_w[2]))
+        mid_mine, cross_w[1], near_w[2], d_last = barrier((mid_mine, cross_w[1], near_w[2], d_last))
         recv_b, (keep, give) = share(1, mid_mine, mid_give)
-        late_weight, give = barrier((weight, give))
-        result = finish(1, h_mid, keep, give)
+        cross_w.append(cross(near_w[2]))
+        result = finish(1, h_mid, keep, meet(give))
         h_out, saved_b = result[0], result[1:6]
-        cross_w.append(cross(near_w[2]))
-        far_early = near_w + cross_w
+        h_in = move(h_out, ("segment",), lambda s: (s + 2,) if s < 2 else None)
+        late_weight, h_out = barrier((weight, h_out))
         far_late = [
             move(cut, ("segment", "fsdp"), lambda s, f: (s, 1 - f) if s == 1 else None)
             for cut in (late_weight[:half], late_weight[half:])
         ]
-        late_other = to_other_core(far_late, (1,))
+        h_in, cross_w[2] = barrier((h_in, cross_w[2]))
+        far_early = near_w + cross_w
         late_at = [mine_at, far_at, far_at + half]
         early = [weight, *far_early, *s_own]
         early += [w_swapped, *to_other_core(far_early, last_stage), *s_other]
-        late = [weight, *far_late, *s_own, w_swapped, *late_other, *s_other]
         first_units = [jnp.concatenate(pair, axis=0) for pair in ((mine, recv_a), (mid_mine, recv_b))]
     else:
         d_last = flat(cotangent, back_order, False)[0]
@@ -583,7 +588,7 @@
         early = late = [whole, *s_own, swap(whole, "segment"), *s_other]
         result = forward_pass(h_first, 0, early)
         h_mid, h_out, saved_a, saved_b = result[0], result[1], result[2:7], result[7:12]
-        first_units = None
+        h_in = move(h_out, ("segment",), lambda s: (s + 2,) if s < 2 else None)
     first = (saved_a, saved_b)
 
     final = stage == 1
@@ -595,16 +600,8 @@
         found = []
         for step in range(fsdp):
             cut = lax.dynamic_slice_in_dim(value, ((mesh_f - step) % fsdp) * part, part, 1)
-            if step and first_units is not None:
-                cut = move(
-                    cut,
-                    ("segment", "fsdp"),
-                    lambda s, f: (s, (f - step) % fsdp) if s > 1 else None,
-                )
-            elif step:
-                cut = rotate(cut, "fsdp", -step)
-            found.append(cut)
-        return found
+            found.append(rotate(cut, "fsdp", -step) if step else cut)
+        return jnp.concatenate(found, axis=0)
 
     def dp_slots(unit):
         found = [unit] + [swap(unit, "dp", step) for step in range(1, dp if dp != 4 else 3)]
@@ -627,42 +624,48 @@
     def both_cores(first, second):
         return jnp.concatenate(swap_blocks(first, second), axis=-2)
 
-    h_in = move(h_out, ("segment",), lambda s: (s + 2,) if s < 2 else None)
-    unit_a = fsdp_unit(h_in)
-    if first_units is not None:
-        h_in, far_late[0] = barrier((h_in, far_late[0]))
     result = forward_pass(h_in, 1, early)
     last = (result[2:7], result[7:12])
-    unit_b = fsdp_unit(result[0])
-    unit_a, mid = barrier((unit_a, result[0]))
-    if first_units is None:
-        theirs = [jnp.concatenate(fsdp_unit(h), axis=0) for h in (h_first, h_mid)]
+    if fast:
+        halves_mine, halves_give = result[12:]
+        halves_recv = move(
+            halves_give, ("segment", "fsdp"), lambda s, f: (s, 1 - f) if s > 1 else None
+        )
+
+    ended = backward_pass(d_last, last, 1, early, w_at, True)
+    d_out = move(ended[6], ("segment",), lambda s: (s - 2,) if s > 1 else None)
+    if fast:
+        ended = list(ended)
+        halves_recv, ended[1] = barrier((halves_recv, ended[1]))
+        units = [
+            of_stage(jnp.concatenate([halves_mine[b], halves_recv[b]], axis=0), first_units[b])
+            for b in range(2)
+        ]
+        late_other = to_other_core(far_late, (1,))
+        late = [weight, *far_late, *s_own, w_swapped, *late_other, *s_other]
     else:
-        theirs = first_units
-    slots_a = dp_slots(of_stage(jnp.concatenate(unit_a, axis=0), theirs[0]))
-
-    ended = backward_pass(d_last, last, 1, early, w_at, True)
-    unit_b, ended = barrier((unit_b, ended))
-    slots_b = dp_slots(of_stage(jnp.concatenate(unit_b, axis=0), theirs[1]))
-    pool = both_cores(*[of_stage(last[b][3], first[b][3]) for b in range(2)])
-    hid = both_cores(*[of_stage(last[b][4], first[b][4]) for b in range(2)])
-    pool, hid = small_exchange(pool, hid, mesh_f, mesh_z)
-
-    d_out = move(ended[6], ("segment",), lambda s: (s - 2,) if s > 1 else None)
-    if dp == 4:
-        d_out, slots_a[2] = barrier((d_out, slots_a[2]))
+        units = [
+            fsdp_unit(of_stage(ours, theirs)) for ours, theirs in ((h_in, h_first), (result[0], h_mid))
+        ]
+    keep, other = swap_blocks(*units)
+    cuts = []
+    for step in range(fsdp):
+        cuts += [side[step * rows : (step + 1) * rows] for side in (keep, other)]
+    h_all = dp_slots(jnp.concatenate(cuts, axis=0))
+
     begun = backward_pass(d_out, first, 0, late, late_at, False)
-    d_pre, d_sq, d_ex = [
-        both_cores(*[of_stage(ended[3 * b + i], begun[3 * b + i]) for b in range(2)])
-        for i in range(3)
+    h_all, begun = barrier((h_all, begun))
+    h_all = forwarded(h_all)
+    found = [
+        [of_stage(ended[3 * b + i], begun[3 * b + i]) for b in range(2)] for i in range(3)
     ]
-    h_all = []
-    for slot_a, slot_b in zip(forwarded(slots_a), forwarded(slots_b)):
-        keep, other = swap_blocks(slot_a, slot_b)
-        cuts = []
-        for step in range(fsdp):
-            cuts += [side[step * rows : (step + 1) * rows] for side in (keep, other)]
-        h_all.append(jnp.concatenate(cuts, axis=0))
+    d_pre = both_cores(*found[0])
+    small = []
+    for b in range(2):
+        pool, hid = [of_stage(last[b][i], first[b][i]) for i in (3, 4)]
+        small.append(jnp.concatenate([pool, found[2][b], hid, found[1][b]], axis=1).astype(BF))
+    small = both_cores(*small)
+    pool, d_ex, hid_sq = jnp.split(small, (channels, 2 * channels), axis=1)
 
     total = None
     for step in range(dp):
@@ -673,8 +676,10 @@
         term = tn(h_all[step], piece)
         total = term if total is None else total + term
     total = total.astype(BF)
-    d_ex, d_sq = small_exchange(d_ex, d_sq, mesh_f, mesh_z)
     own_rows = part // dp
+    wide, hid_sq = small_exchange([pool, d_ex], hid_sq, mesh_f, mesh_z)
+    grad_s = tn(wide[:, :own_rows], hid_sq[:, hidden:])
+    grad_e = tn(wide[:, own_rows:], hid_sq[:, :hidden])
     gathered = jnp.zeros((dp, own_rows, group), BF)
     for step in range(dp):
         block = lax.dynamic_slice_in_dim(total, (mesh_z ^ step) * own_rows, own_rows, 0)
@@ -682,7 +687,7 @@
             block = swap(block, "dp", step)
         gathered = lax.dynamic_update_index_in_dim(gathered, block, mesh_z ^ step, 0)
     grad_w = jnp.concatenate([gathered[i, :, :w] for i, (_, w) in enumerate(tiles)], axis=1)
-    return (grad_w.astype(F32)[None], tn(pool, d_sq)[None], tn(d_ex, hid)[None])
+    return (grad_w.astype(F32)[None], grad_s[None], grad_e[None])
 
 
 def solution(mesh):

time: 632 us -> 587 us (0.929)
  starting transfers between devices: 136 us -> 83 us
  Pallas kernels: 76.2 us -> 83.9 us
    ppermute x24 -> x23, starting transfers between devices: 90.9 us -> 52.4 us  [move(): return lax.ppermute(value, axes, pairs)]
    ppermute x6 -> x5, waiting for transfers between devices: 5.52 us -> 29.3 us  [rotate(): lax.ppermute(value, axis, [(i, (i + steps) % count) for i in range(count)])]
    ppermute x2 -> x1, waiting for transfers between devices: 21.9 us -> 0.01 us  [forwarded(): outer = lax.ppermute(slots[2], 'dp', [(2, 3), (1, 0)])]
    ppermute x31 -> x21, starting transfers between devices: 33.2 us -> 19.7 us  [swap(): return lax.ppermute(value, axis, [(i, i ^ stride) for i in range(count)])]
    slice x8 -> x2, local copies, waits for them, and re-layouts: 8.71 us -> 0.13 us  [on_device(): cuts += [side[step * rows:(step + 1) * rows] for side in (keep, other)]]
    pallas_call x9, Pallas kernels: 76.2 us -> 83.9 us  [call(): pl.pallas_call(kernel, out_shape=[jax.ShapeDtypeStruct(shape, dtype) for...]
    ppermute x2 -> x1, waiting for transfers between devices: 33.3 us -> 39.4 us  [dp_slots(): inner = lax.ppermute(unit, 'dp', [(1, 2), (2, 1)])]
    ppermute x24 -> x23, waiting for transfers between devices: 74.5 us -> 71.5 us  [move(): return lax.ppermute(value, axes, pairs)]
  transfers between devices with their start and end apart: 65 -> 51, of which waited for: 20 -> 20; matrix products, arithmetic and copies ran while one was open for 11% -> 11% of each run, Pallas kernels for 12% -> 14%
where the time goes in v4:
time: 587 us; the launch traced here: 577 us
  waiting for transfers between devices  335 us (57%)
  Pallas kernels  83.9 us (14%)
  starting transfers between devices  83 us (14%)
  local copies, waits for them, and re-layouts  41.7 us (7%)
  matrix products  16.1 us (3%)
  other arithmetic  14.8 us (3%)
    ppermute x21, waiting for transfers between devices, swap(): return lax.ppermute(value, axis, [(i, i ^ stride) for i in range(count)])  195 us
    pallas_call x9, Pallas kernels, call(): pl.pallas_call(kernel, out_shape=[jax.ShapeDtypeStruct(shape, dtype) for...  83.9 us
    ppermute x23, waiting for transfers between devices, move(): return lax.ppermute(value, axes, pairs)  71.5 us
    ppermute x23, starting transfers between devices, move(): return lax.ppermute(value, axes, pairs)  52.4 us
    ppermute x1, waiting for transfers between devices, dp_slots(): inner = lax.ppermute(unit, 'dp', [(1, 2), (2, 1)])  39.4 us
    ppermute x5, waiting for transfers between devices, rotate(): lax.ppermute(value, axis, [(i, (i + steps) % count) for i in range(count)])  29.3 us
    ppermute x21, starting transfers between devices, swap(): return lax.ppermute(value, axis, [(i, i ^ stride) for i in range(count)])  19.7 us
    dot_general x6, matrix products, tn(): lax.dot_general(left, right, (((0,), (0,)), ((), ())), preferred_element_...  16.1 us
  transfers between devices with their start and end apart: 51, of which 20 were waited for; matrix products, arithmetic and copies ran while one was open for 11% of the time, Pallas kernels for 14%

profile of v4, /device:TPU:10, one launch (start us, length us, event | category | flops | bytes accessed | tf_op | source)
XLA Modules:
  0.0 577.1 jit_solution(10799228088058634208)
XLA Ops:
  4.1 4.8 reshape.72.all_ref
  10.1 3.6 shard_map.85
  13.6 4.1 constant_dynamic-slice_fusion.3
  17.8 3.4 collective-permute-start.1
  22.5 3.4 collective-permute-start.5
  25.9 27.6 %collective-permute-done.1.refs_1_.refs_7_ = bf16[240,2880]{1,0:T(8,128)(2,1)} collective-permute-done((bf16[240,2880]{1,0:T(8,128)(2,1)S(1)}, bf16[240,2880]{1,0:T(8,128)(2,1)}, u32[]{:S(2)}, u32[]{:S(2)}) %collective-permute-start.1) | collective-permute-done | bytes 1382432 | tf_op jit(solution)/shard_map/ppermute | solution.py:339
  53.5 2.4 collective-permute-start.4
  57.3 2.8 shard_map.86
  60.8 16.3 %collective-permute-done.refs_1_.refs_8_.refs_14_.refs_10_ = bf16[1440,360]{1,0:T(8,128)(2,1)S(1)} collective-permute-done((bf16[1440,360]{1,0:T(8,128)(2,1)}, bf16[1440,360]{1,0:T(8,128)(2,1)S(1)}, u32[]{:S(2)}, u32[]{:S(2)}) %collective-permute-start) | collective-permute-done | bytes 1036832 | tf_op jit(solution)/shard_map/ppermute | solution.py:344
  78.6 32.9 %collective-permute-done.7.refs_2_.refs_9_.refs_15_.refs_11_ = bf16[1440,360]{1,0:T(8,128)(2,1)S(1)} collective-permute-done((bf16[1440,360]{1,0:T(8,128)(2,1)S(1)}, bf16[1440,360]{1,0:T(8,128)(2,1)S(1)}, u32[]{:S(2)}, u32[]{:S(2)}) %collective-permute-start.7) | collective-permute-done | bytes 1036832 | tf_op jit(solution)/shard_map/ppermute | solution.py:344
  112.0 3.4 collective-permute-start.13
  115.4 2.4 collective-permute-start.12
  117.8 3.2 pad_maximum_fusion.refs_0_.refs_7_.refs_13_.refs_9_
  125.2 4.1 shard_map.87
  130.6 4.8 reshape.73.all_ref
  135.5 3.1 shard_map.88.up_ref
  138.6 8.6 %collective-permute-done.13.refs_3_.refs_9_ = bf16[240,2880]{1,0:T(8,128)(2,1)} collective-permute-done((bf16[240,2880]{1,0:T(8,128)(2,1)}, bf16[240,2880]{1,0:T(8,128)(2,1)}, u32[]{:S(2)}, u32[]{:S(2)}) %collective-permute-start.13) | collective-permute-done | bytes 1382432 | tf_op jit(solution)/shard_map/ppermute | solution.py:339
  147.1 3.2 collective-permute-done.12.refs_5_.refs_11_
  151.1 3.1 shard_map.89
  155.8 2.3 collective-permute-start.17
  158.1 3.8 shard_map.90
  163.2 6.0 %fusion.42 = (bf16[720,2880]{1,0:T(8,128)(2,1)}, bf16[720,2880]{1,0:T(8,128)(2,1)}) fusion(bf16[1440,2880]{1,0:T(8,128)(2,1)} %bitcast.74), kind=kLoop, calls=%fused_computation.112 | loop fusion | bytes 16588800 | tf_op jit(solution)/shard_map/slice | solution.py:576
  169.2 2.7 collective-permute-start.30
  171.9 2.7 collective-permute-start.31
  176.5 13.1 %collective-permute-done.17.refs_6_.refs_12_ = bf16[240,2880]{1,0:T(8,128)(2,1)S(1)} collective-permute-done((bf16[240,2880]{1,0:T(8,128)(2,1)}, bf16[240,2880]{1,0:T(8,128)(2,1)S(1)}, u32[]{:S(2)}, u32[]{:S(2)}) %collective-permute-start.17) | collective-permute-done | bytes 1382432 | tf_op jit(solution)/shard_map/ppermute | solution.py:339
  191.6 2.8 collective-permute-done.16.h_ref
  194.4 1.9 collective-permute-start.21
  196.3 2.4 collective-permute-start.20
  198.7 1.9 collective-permute-start.22
  201.9 2.4 collective-permute-start.23
  204.9 2.3 collective-permute-done.23.refs_16_.refs_22_
  207.2 32.9 %shard_map.91 = (bf16[160,2880]{1,0:T(8,128)(2,1)}, bf16[160,2880]{1,0:T(8,128)(2,1)}, f32[160,2880]{1,0:T(8,128)}, f32[8,2880]{1,0:T(8,128)}, f32[8,360]{1,0:T(...) custom-call(s32[13]{0:T(128)} %stack.126.meta, ...), custom_call_target="tpu_custom_call" | custom-call | flops 1024 | bytes 1024 | tf_op jit(solution)/shard_map/pallas_call | solution.py:316
  240.1 2.4 collective-permute-start.24
  242.5 26.7 %shard_map.92 = (bf16[4,160,768]{2,1,0:T(8,128)(2,1)}, f32[8,360]{1,0:T(8,128)}, f32[8,2880]{1,0:T(8,128)}, bf16[4,160,768]{2,1,0:T(8,128)(2,1)}, f32[8,360]{1,0...) custom-call(s32[13]{0:T(128)} %stack.126.meta, bf16[160,2880]{1,0:T(8,128)(2,1)} %shard_map.88.up_ref, ...), custom_call_target="tpu_custom_call" | custom-call | flops 1024 | bytes 1024 | tf_op jit(solution)/shard_map/pallas_call | solution.py:316
  270.6 2.6 collective-permute-start.32
  273.2 2.6 collective-permute-start.33
  278.3 4.5 collective-permute-start.29
  283.2 2.2 copy.21
  285.9 2.6 collective-permute-start.27
  288.5 14.0 %collective-permute-done.29.up_ref = bf16[160,2880]{1,0:T(8,128)(2,1)} collective-permute-done((bf16[160,2880]{1,0:T(8,128)(2,1)S(1)}, bf16[160,2880]{1,0:T(8,128)(2,1)}, u32[]{:S(2)}, u32[]{:S(2)}) %collective-permute-start.29) | collective-permute-done | bytes 921632 | tf_op jit(solution)/shard_map/ppermute | solution.py:339
  302.5 3.5 collective-permute-start.28
  307.4 4.0 shard_map.93
  311.4 53.6 %collective-permute-done.26 = bf16[640,1440]{0,1:T(8,128)(2,1)} collective-permute-done((bf16[640,1440]{0,1:T(8,128)(2,1)}, bf16[640,1440]{0,1:T(8,128)(2,1)}, u32[]{:S(2)}, u32[]{:S(2)}) %collective-permute-start.26) | collective-permute-done | bytes 1843232 | tf_op jit(solution)/shard_map/ppermute | solution.py:344
  365.0 3.9 collective-permute-done.27
  368.9 39.4 %collective-permute-done.28 = bf16[640,1440]{0,1:T(8,128)(2,1)} collective-permute-done((bf16[640,1440]{0,1:T(8,128)(2,1)}, bf16[640,1440]{0,1:T(8,128)(2,1)}, u32[]{:S(2)}, u32[]{:S(2)}) %collective-permute-start.28) | collective-permute-done | bytes 1843232 | tf_op jit(solution)/shard_map/ppermute | solution.py:609
  408.4 2.8 broadcast_select_fusion.2
  412.2 2.7 collective-permute-start.40
  416.7 2.5 fusion.24
  424.8 13.4 %collective-permute-done.47 = bf16[4,16,1440]{2,1,0:T(8,128)(2,1)S(1)} collective-permute-done((bf16[4,16,1440]{2,1,0:T(8,128)(2,1)}, bf16[4,16,1440]{2,1,0:T(8,128)(2,1)S(1)}, u32[]{:S(2)}, u32[]{:S(2)}) %collective-permute-start.47) | collective-permute-done | bytes 184352 | tf_op jit(solution)/shard_map/ppermute | solution.py:349
  438.2 2.7 collective-permute-start.38
  440.9 44.4 %collective-permute-done.36 = bf16[320,768]{1,0:T(8,128)(2,1)} collective-permute-done((bf16[320,768]{1,0:T(8,128)(2,1)}, bf16[320,768]{1,0:T(8,128)(2,1)}, u32[]{:S(2)}, u32[]{:S(2)}) %collective-permute-start.36) | collective-permute-done | bytes 491552 | tf_op jit(solution)/shard_map/ppermute | solution.py:344
  485.9 2.5 collective-permute-start.48
  490.0 3.0 fusion.3
  494.1 5.6 collective-permute-done.37
  500.2 3.5 fusion.7
  505.3 4.9 collective-permute-done.42
  510.2 3.6 fusion
  513.8 5.5 collective-permute-done.39
  519.3 3.8 add_convert_fusion
  523.2 2.5 collective-permute-start.43
  529.9 16.9 %collective-permute-done.43 = bf16[360,768]{1,0:T(8,128)(2,1)S(1)} collective-permute-done((bf16[360,768]{1,0:T(8,128)(2,1)S(1)}, bf16[360,768]{1,0:T(8,128)(2,1)S(1)}, u32[]{:S(2)}, u32[]{:S(2)}) %collective-permute-start.43) | collective-permute-done | bytes 552992 | tf_op jit(solution)/shard_map/ppermute | solution.py:344
  546.9 16.7 %collective-permute-done.44 = bf16[360,768]{1,0:T(8,128)(2,1)S(1)} collective-permute-done((bf16[360,768]{1,0:T(8,128)(2,1)S(1)}, bf16[360,768]{1,0:T(8,128)(2,1)S(1)}, u32[]{:S(2)}, u32[]{:S(2)}) %collective-permute-start.44) | collective-permute-done | bytes 552992 | tf_op jit(solution)/shard_map/ppermute | solution.py:344
  563.7 10.5 %collective-permute-done.45 = bf16[360,768]{1,0:T(8,128)(2,1)S(1)} collective-permute-done((bf16[360,768]{1,0:T(8,128)(2,1)S(1)}, bf16[360,768]{1,0:T(8,128)(2,1)S(1)}, u32[]{:S(2)}, u32[]{:S(2)}) %collective-permute-start.45) | collective-permute-done | bytes 552992 | tf_op jit(solution)/shard_map/ppermute | solution.py:344
  574.3 2.3 maximum_convert_fusion
  (183 shorter events, 48.9 us)
Async XLA Ops:
  0.6 55.9 %collective-permute-start.3 = (bf16[1440,2880]{1,0:T(8,128)(2,1)}, bf16[1440,2880]{1,0:T(8,128)(2,1)}, u32[]{:S(2)}, u32[]{:S(2)}) collective-permute-start(bf16[1440,2880]{1,0:T(8,128)(2,1)} %bitcast.70), channel_id=1, source_target_pairs={{0,8},{8,0},{16,24},{24,16},{1,9},{9,1},{17,25},{25,17},{2,10},{10... | collective-permute-start | bytes 24883208 | tf_op jit(solution)/shard_map/ppermute | solution.py:344
  13.6 8.1 %copy-start.37 = (bf16[160,1440]{1,0:T(8,128)(2,1)S(1)}, bf16[160,1440]{1,0:T(8,128)(2,1)}, u32[]{:S(2)}) copy-start(bf16[160,1440]{1,0:T(8,128)(2,1)} %get-tuple-element.89) | copy-start | bytes 1382404
  17.8 35.8 %collective-permute-start.1 = (bf16[240,2880]{1,0:T(8,128)(2,1)S(1)}, bf16[240,2880]{1,0:T(8,128)(2,1)}, u32[]{:S(2)}, u32[]{:S(2)}) collective-permute-start(bf16[240,2880]{1,0:T(8,128)(2,1)S(1)} %get-tuple-element.165), channel_id=1, source_target_pairs={{16,20},{20,16},{24,28},{28,24},{17,21},{21,17},{25,29},{29,25},{1... | collective-permute-start | bytes 4147208 | tf_op jit(solution)/shard_map/ppermute | solution.py:339
  21.2 55.9 %collective-permute-start = (bf16[1440,360]{1,0:T(8,128)(2,1)}, bf16[1440,360]{1,0:T(8,128)(2,1)S(1)}, u32[]{:S(2)}, u32[]{:S(2)}) collective-permute-start(bf16[1440,360]{1,0:T(8,128)(2,1)} %pad_maximum_fusion.2), channel_id=1, source_target_pairs={{0,4},{4,0},{1,5},{5,1},{2,6},{6,2},{3,7},{7,3},{8,12},{12,8},{9,1... | collective-permute-start | bytes 3110408 | tf_op jit(solution)/shard_map/ppermute | solution.py:344
  21.8 34.7 %collective-permute-start.2 = (bf16[160,1440]{1,0:T(8,128)(2,1)S(1)}, bf16[160,1440]{1,0:T(8,128)(2,1)S(1)}, u32[]{:S(2)}, u32[]{:S(2)}) collective-permute-start(bf16[160,1440]{1,0:T(8,128)(2,1)S(1)} %copy-done.37), channel_id=1, source_target_pairs={{0,4},{4,0},{8,12},{12,8},{1,5},{5,1},{9,13},{13,9},{2,6},{6,2},{1... | collective-permute-start | bytes 1382408 | tf_op jit(solution)/shard_map/ppermute | solution.py:339
  22.5 89.0 %collective-permute-start.5 = (bf16[240,2880]{1,0:T(8,128)(2,1)}, bf16[240,2880]{1,0:T(8,128)(2,1)}, u32[]{:S(2)}, u32[]{:S(2)}) collective-permute-start(bf16[240,2880]{1,0:T(8,128)(2,1)} %get-tuple-element.164), channel_id=1, source_target_pairs={{16,20},{20,16},{24,28},{28,24},{17,21},{21,17},{25,29},{29,25},{1... | collective-permute-start | bytes 4147208 | tf_op jit(solution)/shard_map/ppermute | solution.py:339
  53.5 58.4 %collective-permute-start.4 = (bf16[240,2880]{1,0:T(8,128)(2,1)}, bf16[240,2880]{1,0:T(8,128)(2,1)}, u32[]{:S(2)}, u32[]{:S(2)}) collective-permute-start(bf16[240,2880]{1,0:T(8,128)(2,1)} %collective-permute-done.1.refs_1_.refs_7_), channel_id=1, source_target_pairs={{16,17},{17,16},{18,19},{19,18},{24,25},{25,24},{26,27},{27,26},{2... | collective-permute-start | bytes 4147208 | tf_op jit(solution)/shard_map/ppermute | solution.py:339
  60.1 17.5 %collective-permute-start.6 = (bf16[160,2880]{1,0:T(8,128)(2,1)}, bf16[160,2880]{1,0:T(8,128)(2,1)S(1)}, u32[]{:S(2)}, u32[]{:S(2)}) collective-permute-start(bf16[160,2880]{1,0:T(8,128)(2,1)} %get-tuple-element.94), channel_id=1, source_target_pairs={{0,4},{4,0},{8,12},{12,8},{1,5},{5,1},{9,13},{13,9},{2,6},{6,2},{1... | collective-permute-start | bytes 2764808 | tf_op jit(solution)/shard_map/ppermute | solution.py:339
  77.1 43.8 %copy-start = (bf16[1440,360]{1,0:T(8,128)(2,1)}, bf16[1440,360]{1,0:T(8,128)(2,1)S(1)}, u32[]{:S(2)}) copy-start(bf16[1440,360]{1,0:T(8,128)(2,1)S(1)} %collective-permute-done.refs_1_.refs_8_.refs_14_.refs_10_) | copy-start | bytes 3110404
  77.1 34.3 %collective-permute-start.7 = (bf16[1440,360]{1,0:T(8,128)(2,1)S(1)}, bf16[1440,360]{1,0:T(8,128)(2,1)S(1)}, u32[]{:S(2)}, u32[]{:S(2)}) collective-permute-start(bf16[1440,360]{1,0:T(8,128)(2,1)S(1)} %collective-permute-done.refs_1_.refs_8_.refs_14_.refs_10_), channel_id=1, source_target_pairs={{0,1},{1,0},{2,3},{3,2},{4,5},{5,4},{6,7},{7,6},{8,9},{9,8},{10,11... | collective-permute-start | bytes 3110408 | tf_op jit(solution)/shard_map/ppermute | solution.py:344
  77.6 37.8 %collective-permute-start.8 = (bf16[1440,360]{1,0:T(8,128)(2,1)}, bf16[1440,360]{1,0:T(8,128)(2,1)S(1)}, u32[]{:S(2)}, u32[]{:S(2)}) collective-permute-start(bf16[1440,360]{1,0:T(8,128)(2,1)} %bitcast.78), channel_id=1, source_target_pairs={{0,8},{8,0},{16,24},{24,16},{1,9},{9,1},{17,25},{25,17},{2,10},{10... | collective-permute-start | bytes 3110408 | tf_op jit(solution)/shard_map/ppermute | solution.py:344
  77.6 44.5 %collective-permute-start.9 = (bf16[1440,360]{1,0:T(8,128)(2,1)}, bf16[1440,360]{1,0:T(8,128)(2,1)S(1)}, u32[]{:S(2)}, u32[]{:S(2)}) collective-permute-start(bf16[1440,360]{1,0:T(8,128)(2,1)} %bitcast.80), channel_id=1, source_target_pairs={{0,8},{8,0},{16,24},{24,16},{1,9},{9,1},{17,25},{25,17},{2,10},{10... | collective-permute-start | bytes 3110408 | tf_op jit(solution)/shard_map/ppermute | solution.py:344
  111.5 9.5 %copy-start.1 = (bf16[1440,360]{1,0:T(8,128)(2,1)}, bf16[1440,360]{1,0:T(8,128)(2,1)S(1)}, u32[]{:S(2)}) copy-start(bf16[1440,360]{1,0:T(8,128)(2,1)S(1)} %collective-permute-done.7.refs_2_.refs_9_.refs_15_.refs_11_) | copy-start | bytes 3110404
  111.5 11.7 %collective-permute-start.10 = (bf16[1440,360]{1,0:T(8,128)(2,1)S(1)}, bf16[1440,360]{1,0:T(8,128)(2,1)S(1)}, u32[]{:S(2)}, u32[]{:S(2)}) collective-permute-start(bf16[1440,360]{1,0:T(8,128)(2,1)S(1)} %collective-permute-done.refs_1_.refs_8_.refs_14_.refs_10_), channel_id=1, source_target_pairs={{0,8},{8,0},{16,24},{24,16},{1,9},{9,1},{17,25},{25,17},{2,10},{10... | collective-permute-start | bytes 3110408 | tf_op jit(solution)/shard_map/ppermute | solution.py:344
  111.5 11.7 %collective-permute-start.11 = (bf16[1440,360]{1,0:T(8,128)(2,1)S(1)}, bf16[1440,360]{1,0:T(8,128)(2,1)S(1)}, u32[]{:S(2)}, u32[]{:S(2)}) collective-permute-start(bf16[1440,360]{1,0:T(8,128)(2,1)S(1)} %collective-permute-done.7.refs_2_.refs_9_.refs_15_.refs_11_), channel_id=1, source_target_pairs={{0,8},{8,0},{16,24},{24,16},{1,9},{9,1},{17,25},{25,17},{2,10},{10... | collective-permute-start | bytes 3110408 | tf_op jit(solution)/shard_map/ppermute | solution.py:344
  112.0 35.1 %collective-permute-start.13 = (bf16[240,2880]{1,0:T(8,128)(2,1)}, bf16[240,2880]{1,0:T(8,128)(2,1)}, u32[]{:S(2)}, u32[]{:S(2)}) collective-permute-start(bf16[240,2880]{1,0:T(8,128)(2,1)} %get-tuple-element.163), channel_id=1, source_target_pairs={{16,20},{20,16},{24,28},{28,24},{17,21},{21,17},{25,29},{29,25},{1... | collective-permute-start | bytes 4147208 | tf_op jit(solution)/shard_map/ppermute | solution.py:339
  115.4 34.9 %collective-permute-start.12 = (bf16[240,2880]{1,0:T(8,128)(2,1)}, bf16[240,2880]{1,0:T(8,128)(2,1)}, u32[]{:S(2)}, u32[]{:S(2)}) collective-permute-start(bf16[240,2880]{1,0:T(8,128)(2,1)} %collective-permute-done.5.refs_2_.refs_8_), channel_id=1, source_target_pairs={{16,17},{17,16},{18,19},{19,18},{24,25},{25,24},{26,27},{27,26},{2... | collective-permute-start | bytes 4147208 | tf_op jit(solution)/shard_map/ppermute | solution.py:339
  129.3 21.0 %collective-permute-start.14 = (bf16[160,1440]{1,0:T(8,128)(2,1)}, bf16[160,1440]{1,0:T(8,128)(2,1)S(1)}, u32[]{:S(2)}, u32[]{:S(2)}) collective-permute-start(bf16[160,1440]{1,0:T(8,128)(2,1)} %get-tuple-element.103), channel_id=1, source_target_pairs={{0,4},{4,0},{8,12},{12,8},{1,5},{5,1},{9,13},{13,9},{2,6},{6,2},{1... | collective-permute-start | bytes 1382408 | tf_op jit(solution)/shard_map/ppermute | solution.py:339
  154.2 4.0 collective-permute-start.15
  155.8 33.9 %collective-permute-start.17 = (bf16[240,2880]{1,0:T(8,128)(2,1)}, bf16[240,2880]{1,0:T(8,128)(2,1)S(1)}, u32[]{:S(2)}, u32[]{:S(2)}) collective-permute-start(bf16[240,2880]{1,0:T(8,128)(2,1)} %collective-permute-done.13.refs_3_.refs_9_), channel_id=1, source_target_pairs={{16,17},{17,16},{18,19},{19,18},{24,25},{25,24},{26,27},{27,26},{2... | collective-permute-start | bytes 4147208 | tf_op jit(solution)/shard_map/ppermute | solution.py:339
  161.9 32.5 %collective-permute-start.16 = (bf16[160,2880]{1,0:T(8,128)(2,1)}, bf16[160,2880]{1,0:T(8,128)(2,1)S(1)}, u32[]{:S(2)}, u32[]{:S(2)}) collective-permute-start(bf16[160,2880]{1,0:T(8,128)(2,1)} %get-tuple-element.106), channel_id=1, source_target_pairs={{0,16},{8,24},{1,17},{9,25},{2,18},{10,26},{3,19},{11,27},{4,20},{... | collective-permute-start | bytes 2764808 | tf_op jit(solution)/shard_map/ppermute | solution.py:339
  169.2 101.4 %collective-permute-start.30 = (bf16[720,2880]{1,0:T(8,128)(2,1)}, bf16[720,2880]{1,0:T(8,128)(2,1)}, u32[]{:S(2)}, u32[]{:S(2)}) collective-permute-start(bf16[720,2880]{1,0:T(8,128)(2,1)} %get-tuple-element.162), channel_id=1, source_target_pairs={{8,12},{12,8},{9,13},{13,9},{10,14},{14,10},{11,15},{15,11}} | collective-permute-start | bytes 12441608 | tf_op jit(solution)/shard_map/ppermute | solution.py:339
  171.9 101.3 %collective-permute-start.31 = (bf16[720,2880]{1,0:T(8,128)(2,1)}, bf16[720,2880]{1,0:T(8,128)(2,1)}, u32[]{:S(2)}, u32[]{:S(2)}) collective-permute-start(bf16[720,2880]{1,0:T(8,128)(2,1)} %get-tuple-element.161), channel_id=1, source_target_pairs={{8,12},{12,8},{9,13},{13,9},{10,14},{14,10},{11,15},{15,11}} | collective-permute-start | bytes 12441608 | tf_op jit(solution)/shard_map/ppermute | solution.py:339
  174.6 21.7 %collective-permute-start.18 = (bf16[240,2880]{1,0:T(8,128)(2,1)}, bf16[240,2880]{1,0:T(8,128)(2,1)S(1)}, u32[]{:S(2)}, u32[]{:S(2)}) collective-permute-start(bf16[240,2880]{1,0:T(8,128)(2,1)} %collective-permute-done.1.refs_1_.refs_7_), channel_id=1, source_target_pairs={{16,24},{24,16},{17,25},{25,17},{18,26},{26,18},{19,27},{27,19},{2... | collective-permute-start | bytes 4147208 | tf_op jit(solution)/shard_map/ppermute | solution.py:339
  189.6 17.5 %copy-start.4 = (bf16[240,2880]{1,0:T(8,128)(2,1)}, bf16[240,2880]{1,0:T(8,128)(2,1)S(1)}, u32[]{:S(2)}) copy-start(bf16[240,2880]{1,0:T(8,128)(2,1)S(1)} %collective-permute-done.17.refs_6_.refs_12_) | copy-start | bytes 4147204
  189.7 9.1 %collective-permute-start.19 = (bf16[240,2880]{1,0:T(8,128)(2,1)}, bf16[240,2880]{1,0:T(8,128)(2,1)S(1)}, u32[]{:S(2)}, u32[]{:S(2)}) collective-permute-start(bf16[240,2880]{1,0:T(8,128)(2,1)} %collective-permute-done.5.refs_2_.refs_8_), channel_id=1, source_target_pairs={{16,24},{24,16},{17,25},{25,17},{18,26},{26,18},{19,27},{27,19},{2... | collective-permute-start | bytes 4147208 | tf_op jit(solution)/shard_map/ppermute | solution.py:339
  194.4 6.3 %collective-permute-start.21 = (bf16[240,2880]{1,0:T(8,128)(2,1)}, bf16[240,2880]{1,0:T(8,128)(2,1)S(1)}, u32[]{:S(2)}, u32[]{:S(2)}) collective-permute-start(bf16[240,2880]{1,0:T(8,128)(2,1)} %collective-permute-done.4.refs_4_.refs_10_), channel_id=1, source_target_pairs={{16,24},{24,16},{17,25},{25,17},{18,26},{26,18},{19,27},{27,19},{2... | collective-permute-start | bytes 4147208 | tf_op jit(solution)/shard_map/ppermute | solution.py:339
  196.3 8.6 %collective-permute-start.20 = (bf16[240,2880]{1,0:T(8,128)(2,1)}, bf16[240,2880]{1,0:T(8,128)(2,1)}, u32[]{:S(2)}, u32[]{:S(2)}) collective-permute-start(bf16[240,2880]{1,0:T(8,128)(2,1)} %collective-permute-done.13.refs_3_.refs_9_), channel_id=1, source_target_pairs={{16,24},{24,16},{17,25},{25,17},{18,26},{26,18},{19,27},{27,19},{2... | collective-permute-start | bytes 4147208 | tf_op jit(solution)/shard_map/ppermute | solution.py:339
  198.7 6.2 %collective-permute-start.22 = (bf16[240,2880]{1,0:T(8,128)(2,1)}, bf16[240,2880]{1,0:T(8,128)(2,1)}, u32[]{:S(2)}, u32[]{:S(2)}) collective-permute-start(bf16[240,2880]{1,0:T(8,128)(2,1)} %collective-permute-done.12.refs_5_.refs_11_), channel_id=1, source_target_pairs={{16,24},{24,16},{17,25},{25,17},{18,26},{26,18},{19,27},{27,19},{2... | collective-permute-start | bytes 4147208 | tf_op jit(solution)/shard_map/ppermute | solution.py:339
  201.9 5.3 collective-permute-start.23
  240.1 30.5 %collective-permute-start.24 = (bf16[2,160,1440]{2,1,0:T(8,128)(2,1)}, bf16[2,160,1440]{2,1,0:T(8,128)(2,1)}, u32[]{:S(2)}, u32[]{:S(2)}) collective-permute-start(bf16[2,160,1440]{2,1,0:T(8,128)(2,1)} %get-tuple-element.113), channel_id=1, source_target_pairs={{16,20},{20,16},{24,28},{28,24},{17,21},{21,17},{25,29},{29,25},{1... | collective-permute-start | bytes 2764808 | tf_op jit(solution)/shard_map/ppermute | solution.py:339
  270.6 36.8 %collective-permute-start.32 = (bf16[720,2880]{1,0:T(8,128)(2,1)}, bf16[720,2880]{1,0:T(8,128)(2,1)}, u32[]{:S(2)}, u32[]{:S(2)}) collective-permute-start(bf16[720,2880]{1,0:T(8,128)(2,1)} %collective-permute-done.30.refs_7_), channel_id=1, source_target_pairs={{8,0},{9,1},{10,2},{11,3},{12,4},{13,5},{14,6},{15,7}} | collective-permute-start | bytes 12441608 | tf_op jit(solution)/shard_map/ppermute | solution.py:339
  273.2 34.2 %collective-permute-start.33 = (bf16[720,2880]{1,0:T(8,128)(2,1)}, bf16[720,2880]{1,0:T(8,128)(2,1)}, u32[]{:S(2)}, u32[]{:S(2)}) collective-permute-start(bf16[720,2880]{1,0:T(8,128)(2,1)} %collective-permute-done.31.refs_8_), channel_id=1, source_target_pairs={{8,0},{9,1},{10,2},{11,3},{12,4},{13,5},{14,6},{15,7}} | collective-permute-start | bytes 12441608 | tf_op jit(solution)/shard_map/ppermute | solution.py:339
  277.7 5.2 collective-permute-start.25
  278.3 24.2 %collective-permute-start.29 = (bf16[160,2880]{1,0:T(8,128)(2,1)S(1)}, bf16[160,2880]{1,0:T(8,128)(2,1)}, u32[]{:S(2)}, u32[]{:S(2)}) collective-permute-start(bf16[160,2880]{1,0:T(8,128)(2,1)S(1)} %copy-done.36), channel_id=1, source_target_pairs={{16,0},{24,8},{17,1},{25,9},{18,2},{26,10},{19,3},{27,11},{20,4},{... | collective-permute-start | bytes 2764808 | tf_op jit(solution)/shard_map/ppermute | solution.py:339
  283.2 23.5 %copy-start.28 = (f32[8,360]{1,0:T(8,128)S(1)}, f32[8,360]{1,0:T(8,128)}, u32[]{:S(2)}) copy-start(f32[8,360]{1,0:T(8,128)} %get-tuple-element.150) | copy-start | bytes 34564
  283.2 23.5 %copy-start.29 = (f32[8,360]{1,0:T(8,128)S(1)}, f32[8,360]{1,0:T(8,128)}, u32[]{:S(2)}) copy-start(f32[8,360]{1,0:T(8,128)} %get-tuple-element.158) | copy-start | bytes 34564
  283.2 23.5 %copy-start.32 = (f32[8,360]{1,0:T(8,128)S(1)}, f32[8,360]{1,0:T(8,128)}, u32[]{:S(2)}) copy-start(f32[8,360]{1,0:T(8,128)} %get-tuple-element.149) | copy-start | bytes 34564
  283.2 23.5 %copy-start.33 = (f32[8,360]{1,0:T(8,128)S(1)}, f32[8,360]{1,0:T(8,128)}, u32[]{:S(2)}) copy-start(f32[8,360]{1,0:T(8,128)} %get-tuple-element.157) | copy-start | bytes 34564
  283.2 23.5 %copy-start.20 = (f32[8,2880]{1,0:T(8,128)S(1)}, f32[8,2880]{1,0:T(8,128)}, u32[]{:S(2)}) copy-start(f32[8,2880]{1,0:T(8,128)} %get-tuple-element.146) | copy-start | bytes 276484
  283.2 23.5 %copy-start.21 = (f32[8,2880]{1,0:T(8,128)S(1)}, f32[8,2880]{1,0:T(8,128)}, u32[]{:S(2)}) copy-start(f32[8,2880]{1,0:T(8,128)} %get-tuple-element.154) | copy-start | bytes 276484
  283.2 23.5 %copy-start.24 = (f32[8,2880]{1,0:T(8,128)S(1)}, f32[8,2880]{1,0:T(8,128)}, u32[]{:S(2)}) copy-start(f32[8,2880]{1,0:T(8,128)} %get-tuple-element.145) | copy-start | bytes 276484
  283.2 23.5 %copy-start.25 = (f32[8,2880]{1,0:T(8,128)S(1)}, f32[8,2880]{1,0:T(8,128)}, u32[]{:S(2)}) copy-start(f32[8,2880]{1,0:T(8,128)} %get-tuple-element.153) | copy-start | bytes 276484
  285.5 79.6 %collective-permute-start.26 = (bf16[640,1440]{0,1:T(8,128)(2,1)}, bf16[640,1440]{0,1:T(8,128)(2,1)}, u32[]{:S(2)}, u32[]{:S(2)}) collective-permute-start(bf16[640,1440]{0,1:T(8,128)(2,1)} %copy.21), channel_id=1, source_target_pairs={{0,1},{1,0},{2,3},{3,2},{4,5},{5,4},{6,7},{7,6},{8,9},{9,8},{10,11... | collective-permute-start | bytes 5529608 | tf_op jit(solution)/shard_map/ppermute | solution.py:344
  285.9 83.0 %collective-permute-start.27 = (bf16[640,1440]{0,1:T(8,128)(2,1)}, bf16[640,1440]{0,1:T(8,128)(2,1)}, u32[]{:S(2)}, u32[]{:S(2)}) collective-permute-start(bf16[640,1440]{0,1:T(8,128)(2,1)} %copy.21), channel_id=1, source_target_pairs={{0,2},{1,3},{2,0},{3,1},{4,6},{5,7},{6,4},{7,5},{8,10},{9,11},{10,... | collective-permute-start | bytes 5529608 | tf_op jit(solution)/shard_map/ppermute | solution.py:344
  302.5 105.9 %collective-permute-start.28 = (bf16[640,1440]{0,1:T(8,128)(2,1)}, bf16[640,1440]{0,1:T(8,128)(2,1)}, u32[]{:S(2)}, u32[]{:S(2)}) collective-permute-start(bf16[640,1440]{0,1:T(8,128)(2,1)} %copy.21), channel_id=1, source_target_pairs={{1,2},{2,1},{5,6},{6,5},{9,10},{10,9},{13,14},{14,13},{17,18},{18,... | collective-permute-start | bytes 5529608 | tf_op jit(solution)/shard_map/ppermute | solution.py:609
  411.2 5.5 collective-permute-start.34
  411.6 3.3 collective-permute-start.46
  412.2 91.5 %collective-permute-start.40 = (bf16[640,1440]{0,1:T(8,128)(2,1)}, bf16[640,1440]{0,1:T(8,128)(2,1)}, u32[]{:S(2)}, u32[]{:S(2)}) collective-permute-start(bf16[640,1440]{0,1:T(8,128)(2,1)} %collective-permute-done.27), channel_id=1, source_target_pairs={{2,3},{1,0},{6,7},{5,4},{10,11},{9,8},{14,15},{13,12},{18,19},{17,... | collective-permute-start | bytes 5529608 | tf_op jit(solution)/shard_map/ppermute | solution.py:616
  419.2 66.1 %collective-permute-start.36 = (bf16[320,768]{1,0:T(8,128)(2,1)}, bf16[320,768]{1,0:T(8,128)(2,1)}, u32[]{:S(2)}, u32[]{:S(2)}) collective-permute-start(bf16[320,768]{1,0:T(8,128)(2,1)} %get-tuple-element.178), channel_id=1, source_target_pairs={{0,1},{1,0},{2,3},{3,2},{4,5},{5,4},{6,7},{7,6},{8,9},{9,8},{10,11... | collective-permute-start | bytes 1474568 | tf_op jit(solution)/shard_map/ppermute | solution.py:344
  419.2 70.7 %copy-start.16 = (bf16[320,768]{1,0:T(8,128)(2,1)S(1)}, bf16[320,768]{1,0:T(8,128)(2,1)}, u32[]{:S(2)}) copy-start(bf16[320,768]{1,0:T(8,128)(2,1)} %get-tuple-element.177) | copy-start | bytes 1474564
  420.5 65.4 %collective-permute-start.35 = (bf16[320,768]{1,0:T(8,128)(2,1)}, bf16[320,768]{1,0:T(8,128)(2,1)}, u32[]{:S(2)}, u32[]{:S(2)}) collective-permute-start(bf16[320,768]{1,0:T(8,128)(2,1)} %get-tuple-element.177), channel_id=1, source_target_pairs={{0,4},{4,0},{1,5},{5,1},{2,6},{6,2},{3,7},{7,3},{8,12},{12,8},{9,1... | collective-permute-start | bytes 1474568 | tf_op jit(solution)/shard_map/ppermute | solution.py:349
  421.1 67.4 %collective-permute-start.41 = (bf16[320,768]{1,0:T(8,128)(2,1)}, bf16[320,768]{1,0:T(8,128)(2,1)}, u32[]{:S(2)}, u32[]{:S(2)}) collective-permute-start(bf16[320,768]{1,0:T(8,128)(2,1)} %get-tuple-element.179), channel_id=1, source_target_pairs={{0,3},{1,2},{2,1},{3,0},{4,7},{5,6},{6,5},{7,4},{8,11},{9,10},{10,... | collective-permute-start | bytes 1474568 | tf_op jit(solution)/shard_map/ppermute | solution.py:344
  423.3 14.9 %collective-permute-start.47 = (bf16[4,16,1440]{2,1,0:T(8,128)(2,1)}, bf16[4,16,1440]{2,1,0:T(8,128)(2,1)S(1)}, u32[]{:S(2)}, u32[]{:S(2)}) collective-permute-start(bf16[4,16,1440]{2,1,0:T(8,128)(2,1)} %get-tuple-element.192), channel_id=1, source_target_pairs={{0,4},{4,0},{1,5},{5,1},{2,6},{6,2},{3,7},{7,3},{8,12},{12,8},{9,1... | collective-permute-start | bytes 552968 | tf_op jit(solution)/shard_map/ppermute | solution.py:349
  438.2 54.7 %collective-permute-start.38 = (bf16[320,768]{1,0:T(8,128)(2,1)S(1)}, bf16[320,768]{1,0:T(8,128)(2,1)S(1)}, u32[]{:S(2)}, u32[]{:S(2)}) collective-permute-start(bf16[320,768]{1,0:T(8,128)(2,1)S(1)} %get-tuple-element.176), channel_id=1, source_target_pairs={{0,2},{1,3},{2,0},{3,1},{4,6},{5,7},{6,4},{7,5},{8,10},{9,11},{10,... | collective-permute-start | bytes 1474568 | tf_op jit(solution)/shard_map/ppermute | solution.py:344
  485.3 14.4 %collective-permute-start.37 = (bf16[320,768]{1,0:T(8,128)(2,1)}, bf16[320,768]{1,0:T(8,128)(2,1)S(1)}, u32[]{:S(2)}, u32[]{:S(2)}) collective-permute-start(bf16[320,768]{1,0:T(8,128)(2,1)} %collective-permute-done.36), channel_id=1, source_target_pairs={{0,4},{4,0},{1,5},{5,1},{2,6},{6,2},{3,7},{7,3},{8,12},{12,8},{9,1... | collective-permute-start | bytes 1474568 | tf_op jit(solution)/shard_map/ppermute | solution.py:349
  485.9 39.9 %collective-permute-start.48 = (bf16[2,16,1440]{2,1,0:T(8,128)(2,1)S(1)}, bf16[2,16,1440]{2,1,0:T(8,128)(2,1)S(1)}, u32[]{:S(2)}, u32[]{:S(2)}) collective-permute-start(bf16[2,16,1440]{2,1,0:T(8,128)(2,1)S(1)} %get-tuple-element.189), channel_id=1, source_target_pairs={{0,1},{1,0},{2,3},{3,2},{4,5},{5,4},{6,7},{7,6},{8,9},{9,8},{10,11... | collective-permute-start | bytes 276488 | tf_op jit(solution)/shard_map/ppermute | solution.py:344
  488.4 21.8 %collective-permute-start.42 = (bf16[320,768]{1,0:T(8,128)(2,1)}, bf16[320,768]{1,0:T(8,128)(2,1)S(1)}, u32[]{:S(2)}, u32[]{:S(2)}) collective-permute-start(bf16[320,768]{1,0:T(8,128)(2,1)} %collective-permute-done.41), channel_id=1, source_target_pairs={{0,4},{4,0},{1,5},{5,1},{2,6},{6,2},{3,7},{7,3},{8,12},{12,8},{9,1... | collective-permute-start | bytes 1474568 | tf_op jit(solution)/shard_map/ppermute | solution.py:349
  492.9 32.8 %collective-permute-start.49 = (bf16[2,16,1440]{2,1,0:T(8,128)(2,1)S(1)}, bf16[2,16,1440]{2,1,0:T(8,128)(2,1)S(1)}, u32[]{:S(2)}, u32[]{:S(2)}) collective-permute-start(bf16[2,16,1440]{2,1,0:T(8,128)(2,1)S(1)} %get-tuple-element.190), channel_id=1, source_target_pairs={{0,2},{1,3},{2,0},{3,1},{4,6},{5,7},{6,4},{7,5},{8,10},{9,11},{10,... | collective-permute-start | bytes 276488 | tf_op jit(solution)/shard_map/ppermute | solution.py:344
  499.7 19.6 %collective-permute-start.39 = (bf16[320,768]{1,0:T(8,128)(2,1)S(1)}, bf16[320,768]{1,0:T(8,128)(2,1)S(1)}, u32[]{:S(2)}, u32[]{:S(2)}) collective-permute-start(bf16[320,768]{1,0:T(8,128)(2,1)S(1)} %collective-permute-done.38), channel_id=1, source_target_pairs={{0,4},{4,0},{1,5},{5,1},{2,6},{6,2},{3,7},{7,3},{8,12},{12,8},{9,1... | collective-permute-start | bytes 1474568 | tf_op jit(solution)/shard_map/ppermute | solution.py:349
  503.7 22.1 %collective-permute-start.50 = (bf16[2,16,1440]{2,1,0:T(8,128)(2,1)S(1)}, bf16[2,16,1440]{2,1,0:T(8,128)(2,1)S(1)}, u32[]{:S(2)}, u32[]{:S(2)}) collective-permute-start(bf16[2,16,1440]{2,1,0:T(8,128)(2,1)S(1)} %get-tuple-element.191), channel_id=1, source_target_pairs={{0,3},{1,2},{2,1},{3,0},{4,7},{5,6},{6,5},{7,4},{8,11},{9,10},{10,... | collective-permute-start | bytes 276488 | tf_op jit(solution)/shard_map/ppermute | solution.py:344
  523.2 23.7 %collective-permute-start.43 = (bf16[360,768]{1,0:T(8,128)(2,1)S(1)}, bf16[360,768]{1,0:T(8,128)(2,1)S(1)}, u32[]{:S(2)}, u32[]{:S(2)}) collective-permute-start(bf16[360,768]{1,0:T(8,128)(2,1)S(1)} %get-tuple-element.175), channel_id=1, source_target_pairs={{0,1},{1,0},{2,3},{3,2},{4,5},{5,4},{6,7},{7,6},{8,9},{9,8},{10,11... | collective-permute-start | bytes 1658888 | tf_op jit(solution)/shard_map/ppermute | solution.py:344
  525.8 37.8 %collective-permute-start.44 = (bf16[360,768]{1,0:T(8,128)(2,1)S(1)}, bf16[360,768]{1,0:T(8,128)(2,1)S(1)}, u32[]{:S(2)}, u32[]{:S(2)}) collective-permute-start(bf16[360,768]{1,0:T(8,128)(2,1)S(1)} %get-tuple-element.174), channel_id=1, source_target_pairs={{0,2},{1,3},{2,0},{3,1},{4,6},{5,7},{6,4},{7,5},{8,10},{9,11},{10,... | collective-permute-start | bytes 1658888 | tf_op jit(solution)/shard_map/ppermute | solution.py:344
  529.2 44.9 %collective-permute-start.45 = (bf16[360,768]{1,0:T(8,128)(2,1)S(1)}, bf16[360,768]{1,0:T(8,128)(2,1)S(1)}, u32[]{:S(2)}, u32[]{:S(2)}) collective-permute-start(bf16[360,768]{1,0:T(8,128)(2,1)S(1)} %get-tuple-element.173), channel_id=1, source_target_pairs={{0,3},{1,2},{2,1},{3,0},{4,7},{5,6},{6,5},{7,4},{8,11},{9,10},{10,... | collective-permute-start | bytes 1658888 | tf_op jit(solution)/shard_map/ppermute | solution.py:344
  (26 other events, 86.4 us)

commit v5 on v4

--- a/solution.py
+++ b/solution.py
@@ -12,6 +12,7 @@
 F32 = jnp.float32
 SUB = 8
 PIECES = 3
+PASS_FLOPS = 30 * 10**9
 VMEM_LIMIT = 62 * 1024 * 1024
 
 
@@ -245,8 +246,8 @@
                 act_ref,
                 outs[block],
             )
-            if send:
-                halves(src, sends[0].at[block], sends[1].at[block], meta[2])
+            if send and block == 0:
+                halves(dst, sends[0], sends[1], meta[2])
 
 
 def backward_kernel(cfg, meta, up_ref, *refs):
@@ -311,7 +312,7 @@
                 dst[:, cols] = (src[:, cols].astype(F32) + back).astype(BF)
 
 
-def call(kernel, smem, dense, pieces, outs, scratch):
+def call(kernel, smem, dense, pieces, outs, scratch, flops=1024):
     vmem = pl.BlockSpec(memory_space=pltpu.VMEM)
     return pl.pallas_call(
         kernel,
@@ -322,7 +323,7 @@
         out_specs=[vmem] * len(outs),
         scratch_shapes=scratch,
         compiler_params=pltpu.CompilerParams(vmem_limit_bytes=VMEM_LIMIT),
-        cost_estimate=pl.CostEstimate(flops=1024, bytes_accessed=1024, transcendentals=0),
+        cost_estimate=pl.CostEstimate(flops=flops, bytes_accessed=1024, transcendentals=0),
     )(*smem, *dense, *pieces)
 
 
@@ -411,8 +412,7 @@
         near_at = far_at + parity * half
         cross_at = far_at + (1 - parity) * half
         near_s = [parity_half(side, parity, 0, half) for side in (squeeze, excite)]
-        near_s, inputs = barrier((jnp.concatenate(near_s, axis=0), inputs))
-        near_s = swap(near_s, "fsdp")
+        near_cut, inputs = barrier((jnp.concatenate(near_s, axis=0), inputs))
         s_at = [mine_at, near_at, cross_at]
         step = half // PIECES
         w_at = [mine_at] + [near_at + i * step for i in range(PIECES)]
@@ -470,8 +470,9 @@
             pieces,
             [((rows, channels), BF)] * 2
             + saved_shapes * 2
-            + [((2, rows, part), BF)] * (2 * fast),
+            + [((rows, part), BF)] * (2 * fast),
             [*bufs, act_shape, *sems],
+            PASS_FLOPS,
         )
 
     def backward_pass(d_out, saved, where, pieces, at, through):
@@ -485,6 +486,7 @@
             pieces,
             outs,
             [*bufs, act_shape, act_shape, *sems],
+            PASS_FLOPS if through else 1024,
         )
 
     if fast:
@@ -502,12 +504,14 @@
 
         near_w = [near(index) for index in range(PIECES)]
 
-        def share(block, mine, give):
-            recv = move(
+        def meet(give):
+            return move(
                 give, ("segment", "fsdp"), lambda s, f: (s, 1 - f) if s in first_stage else None
             )
+
+        def share(block, mine, recv):
             shapes = [((rows, channels), F32), ((rows, channels), BF)]
-            return recv, call(
+            return call(
                 functools.partial(share_kernel, block),
                 [meta_s],
                 [mine, recv],
@@ -523,13 +527,8 @@
         def share_kernel(block, meta, mine_ref, recv_ref, own, other, *refs):
             partial_kernel((tiles,), block, meta, mine_ref, recv_ref, own, other, *refs)
 
-        def meet(give):
-            return move(
-                give, ("segment", "fsdp"), lambda s, f: (s, 1 - f) if s in first_stage else None
-            )
-
         def finish(block, h_row, keep, recv):
-            send = block == 0
+            send = True
             outs = [((rows, channels), BF), *saved_shapes]
             outs += [((rows, part), BF)] * (2 * send)
             return call(
@@ -546,30 +545,35 @@
                 ],
             )
 
-        mine, near_w[0] = barrier((mine, near_w[0]))
-        recv_a, (keep, give) = share(0, mine, give)
+        recv_a, near_cut = barrier((meet(give), near_cut))
+        near_s = swap(near_cut, "fsdp")
+        own_s = jnp.concatenate([squeeze, excite], axis=0)
+        other_s = jnp.concatenate([swap(side, "segment") for side in (squeeze, excite)], axis=0)
+        mine, near_w[0], own_s, other_s = barrier((mine, near_w[0], own_s, other_s))
+        keep, give = share(0, mine, recv_a)
         cross_w = [cross(near_w[0])]
         near_s, keep, cotangent = barrier((near_s, keep, cotangent))
         cross_s = swap(near_s, "dp")
-        own_s = jnp.concatenate([squeeze, excite], axis=0)
-        sides = [swap(side, "segment") for side in (squeeze, excite)]
-        s_other = [jnp.concatenate(sides, axis=0)]
-        s_other += [swap(near_s, "segment")]
         recv, cross_s = barrier((meet(give), cross_s))
-        s_other += [swap(cross_s, "segment")]
+        s_other = [other_s, swap(near_s, "segment"), swap(cross_s, "segment")]
         s_own = [own_s, near_s, cross_s]
         d_last = flat(cotangent, back_order, False)[0]
-        keep, cross_w[0], near_w[1] = barrier((keep, cross_w[0], near_w[1]))
+        keep, cross_w[0], *near_w[1:] = barrier((keep, cross_w[0], *near_w[1:]))
         result = finish(0, h_first, keep, recv)
         h_mid, saved_a = result[0], result[1:6]
         mid_mine, mid_give = result[6:]
         cross_w.append(cross(near_w[1]))
-        mid_mine, cross_w[1], near_w[2], d_last = barrier((mid_mine, cross_w[1], near_w[2], d_last))
-        recv_b, (keep, give) = share(1, mid_mine, mid_give)
         cross_w.append(cross(near_w[2]))
+        recv_b = meet(mid_give)
+        mid_mine, cross_w[1], d_last = barrier((mid_mine, cross_w[1], d_last))
+        keep, give = share(1, mid_mine, recv_b)
         result = finish(1, h_mid, keep, meet(give))
         h_out, saved_b = result[0], result[1:6]
+        out_mine, out_give = result[6:]
         h_in = move(h_out, ("segment",), lambda s: (s + 2,) if s < 2 else None)
+        in_recv = move(
+            out_give, ("segment", "fsdp"), lambda s, f: (s + 2, 1 - f) if s < 2 else None
+        )
         late_weight, h_out = barrier((weight, h_out))
         far_late = [
             move(cut, ("segment", "fsdp"), lambda s, f: (s, 1 - f) if s == 1 else None)
@@ -624,38 +628,44 @@
     def both_cores(first, second):
         return jnp.concatenate(swap_blocks(first, second), axis=-2)
 
+    if fast:
+        in_mine = jnp.where(mesh_f == 0, h_in[:, :part], h_in[:, part:])
+        unit = of_stage(jnp.concatenate([in_mine, in_recv], axis=0), first_units[0])
+    else:
+        unit = fsdp_unit(of_stage(h_in, h_first))
+    h_in, unit = barrier((h_in, unit))
+    slots_a = dp_slots(unit)
     result = forward_pass(h_in, 1, early)
+    result, slots_a, d_last = barrier((list(result), slots_a, d_last))
     last = (result[2:7], result[7:12])
     if fast:
-        halves_mine, halves_give = result[12:]
-        halves_recv = move(
-            halves_give, ("segment", "fsdp"), lambda s, f: (s, 1 - f) if s > 1 else None
+        mid_recv = move(
+            result[13], ("segment", "fsdp"), lambda s, f: (s, 1 - f) if s > 1 else None
         )
 
-    ended = backward_pass(d_last, last, 1, early, w_at, True)
+    ended = list(backward_pass(d_last, last, 1, early, w_at, True))
     d_out = move(ended[6], ("segment",), lambda s: (s - 2,) if s > 1 else None)
     if fast:
-        ended = list(ended)
-        halves_recv, ended[1] = barrier((halves_recv, ended[1]))
-        units = [
-            of_stage(jnp.concatenate([halves_mine[b], halves_recv[b]], axis=0), first_units[b])
-            for b in range(2)
-        ]
+        mid_recv, far_late, ended[1] = barrier((mid_recv, far_late, ended[1]))
+        ours = jnp.concatenate([result[12], mid_recv], axis=0)
+        unit = of_stage(ours, first_units[1])
         late_other = to_other_core(far_late, (1,))
         late = [weight, *far_late, *s_own, w_swapped, *late_other, *s_other]
     else:
-        units = [
-            fsdp_unit(of_stage(ours, theirs)) for ours, theirs in ((h_in, h_first), (result[0], h_mid))
-        ]
-    keep, other = swap_blocks(*units)
-    cuts = []
-    for step in range(fsdp):
-        cuts += [side[step * rows : (step + 1) * rows] for side in (keep, other)]
-    h_all = dp_slots(jnp.concatenate(cuts, axis=0))
+        unit = fsdp_unit(of_stage(result[0], h_mid))
+    slots_b = dp_slots(unit)
+    slots_a = forwarded(slots_a)
 
     begun = backward_pass(d_out, first, 0, late, late_at, False)
-    h_all, begun = barrier((h_all, begun))
-    h_all = forwarded(h_all)
+    slots_b, begun = barrier((slots_b, begun))
+    slots_b = forwarded(slots_b)
+    h_all = []
+    for slot_a, slot_b in zip(slots_a, slots_b):
+        keep, other = swap_blocks(slot_a, slot_b)
+        cuts = []
+        for step in range(fsdp):
+            cuts += [side[step * rows : (step + 1) * rows] for side in (keep, other)]
+        h_all.append(jnp.concatenate(cuts, axis=0))
     found = [
         [of_stage(ended[3 * b + i], begun[3 * b + i]) for b in range(2)] for i in range(3)
     ]

time: 587 us -> 578 us (0.985)
  waiting for transfers between devices: 335 us -> 319 us
  starting transfers between devices: 83 us -> 92.2 us
  other arithmetic: 14.8 us -> 24 us
    ppermute x21 -> x26, waiting for transfers between devices: 195 us -> 151 us  [swap(): return lax.ppermute(value, axis, [(i, i ^ stride) for i in range(count)])]
    ppermute x23 -> x24, waiting for transfers between devices: 71.5 us -> 101 us  [move(): return lax.ppermute(value, axes, pairs)]
    select_n x1 -> x4, other arithmetic: 0.6 us -> 8.12 us  [swap_blocks(): keep = jnp.where(core == 0, first, second)]
    ppermute x21 -> x26, starting transfers between devices: 19.7 us -> 24.6 us  [swap(): return lax.ppermute(value, axis, [(i, i ^ stride) for i in range(count)])]
    ppermute x23 -> x24, starting transfers between devices: 52.4 us -> 50.8 us  [move(): return lax.ppermute(value, axes, pairs)]
    ppermute x1 -> x2, waiting for transfers between devices: 39.4 us -> 39.4 us  [dp_slots(): inner = lax.ppermute(unit, 'dp', [(1, 2), (2, 1)])]
  transfers between devices with their start and end apart: 51 -> 59, of which waited for: 20 -> 24; matrix products, arithmetic and copies ran while one was open for 11% -> 11% of each run, Pallas kernels for 14% -> 14%
where the time goes in v5:
time: 578 us; the launch traced here: 569 us
  waiting for transfers between devices  319 us (55%)
  starting transfers between devices  92.2 us (16%)
  Pallas kernels  83.9 us (15%)
  local copies, waits for them, and re-layouts  36.5 us (6%)
  other arithmetic  24 us (4%)
  matrix products  10.9 us (2%)
    ppermute x26, waiting for transfers between devices, swap(): return lax.ppermute(value, axis, [(i, i ^ stride) for i in range(count)])  151 us
    ppermute x24, waiting for transfers between devices, move(): return lax.ppermute(value, axes, pairs)  101 us
    pallas_call x9, Pallas kernels, call(): pl.pallas_call(kernel, out_shape=[jax.ShapeDtypeStruct(shape, dtype) for...  83.9 us
    ppermute x24, starting transfers between devices, move(): return lax.ppermute(value, axes, pairs)  50.8 us
    ppermute x2, waiting for transfers between devices, dp_slots(): inner = lax.ppermute(unit, 'dp', [(1, 2), (2, 1)])  39.4 us
    ppermute x5, waiting for transfers between devices, rotate(): lax.ppermute(value, axis, [(i, (i + steps) % count) for i in range(count)])  26.9 us
    ppermute x26, starting transfers between devices, swap(): return lax.ppermute(value, axis, [(i, i ^ stride) for i in range(count)])  24.6 us
  transfers between devices with their start and end apart: 59, of which 24 were waited for; matrix products, arithmetic and copies ran while one was open for 11% of the time, Pallas kernels for 14%

profile of v5, /device:TPU:10, one launch (start us, length us, event | category | flops | bytes accessed | tf_op | source)
XLA Modules:
  0.0 569.0 jit_solution(5246876242253268719)
XLA Ops:
  4.8 3.7 reshape.72.all_ref
  9.7 3.6 shard_map.85
  13.3 4.3 constant_dynamic-slice_fusion.3
  17.5 3.4 collective-permute-start.2
  23.9 3.4 collective-permute-start.7
  27.3 2.4 collective-permute-start.8
  29.7 3.2 pad_maximum_fusion.1.refs_3_.refs_17_.refs_23_.refs_15_
  32.9 20.4 %collective-permute-done.2.refs_1_.refs_7_ = bf16[240,2880]{1,0:T(8,128)(2,1)} collective-permute-done((bf16[240,2880]{1,0:T(8,128)(2,1)S(1)}, bf16[240,2880]{1,0:T(8,128)(2,1)}, u32[]{:S(2)}, u32[]{:S(2)}) %collective-permute-start.2) | collective-permute-done | bytes 1382432 | tf_op jit(solution)/shard_map/ppermute | solution.py:340
  53.3 2.3 collective-permute-start.6
  56.3 2.8 shard_map.86
  59.1 17.7 %collective-permute-done.1.refs_1_.refs_8_.refs_14_.refs_10_ = bf16[1440,360]{1,0:T(8,128)(2,1)S(1)} collective-permute-done((bf16[1440,360]{1,0:T(8,128)(2,1)}, bf16[1440,360]{1,0:T(8,128)(2,1)S(1)}, u32[]{:S(2)}, u32[]{:S(2)}) %collective-permute-start.1) | collective-permute-done | bytes 1036832 | tf_op jit(solution)/shard_map/ppermute | solution.py:345
  79.0 32.2 %collective-permute-done.10.refs_2_.refs_9_.refs_15_.refs_11_ = bf16[1440,360]{1,0:T(8,128)(2,1)S(1)} collective-permute-done((bf16[1440,360]{1,0:T(8,128)(2,1)S(1)}, bf16[1440,360]{1,0:T(8,128)(2,1)S(1)}, u32[]{:S(2)}, u32[]{:S(2)}) %collective-permute-start.10) | collective-permute-done | bytes 1036832 | tf_op jit(solution)/shard_map/ppermute | solution.py:345
  111.2 25.9 %collective-permute-done.8.refs_3_.refs_9_ = bf16[240,2880]{1,0:T(8,128)(2,1)} collective-permute-done((bf16[240,2880]{1,0:T(8,128)(2,1)}, bf16[240,2880]{1,0:T(8,128)(2,1)}, u32[]{:S(2)}, u32[]{:S(2)}) %collective-permute-start.8) | collective-permute-done | bytes 1382432 | tf_op jit(solution)/shard_map/ppermute | solution.py:340
  137.1 2.3 collective-permute-start.13
  141.5 4.1 shard_map.87
  147.1 4.8 reshape.73.all_ref
  152.0 3.1 shard_map.88.up_ref
  155.1 16.8 %collective-permute-done.13.refs_5_.refs_11_ = bf16[240,2880]{1,0:T(8,128)(2,1)} collective-permute-done((bf16[240,2880]{1,0:T(8,128)(2,1)}, bf16[240,2880]{1,0:T(8,128)(2,1)}, u32[]{:S(2)}, u32[]{:S(2)}) %collective-permute-start.13) | collective-permute-done | bytes 1382432 | tf_op jit(solution)/shard_map/ppermute | solution.py:340
  172.6 2.8 shard_map.89
  176.2 2.3 collective-permute-start.17
  181.4 4.1 shard_map.90
  188.8 2.5 collective-permute-start.20
  191.3 18.7 %collective-permute-done.17.refs_6_.refs_12_ = bf16[240,2880]{1,0:T(8,128)(2,1)} collective-permute-done((bf16[240,2880]{1,0:T(8,128)(2,1)}, bf16[240,2880]{1,0:T(8,128)(2,1)}, u32[]{:S(2)}, u32[]{:S(2)}) %collective-permute-start.17) | collective-permute-done | bytes 1382432 | tf_op jit(solution)/shard_map/ppermute | solution.py:340
  211.9 2.4 collective-permute-start.22
  216.3 6.1 %collective-permute-done.18 = bf16[160,1440]{1,0:T(8,128)(2,1)S(1)} collective-permute-done((bf16[160,1440]{1,0:T(8,128)(2,1)}, bf16[160,1440]{1,0:T(8,128)(2,1)S(1)}, u32[]{:S(2)}, u32[]{:S(2)}) %collective-permute-start.18) | collective-permute-done | bytes 460832 | tf_op jit(solution)/shard_map/ppermute | solution.py:340
  224.3 5.9 %fusion.71 = (bf16[720,2880]{1,0:T(8,128)(2,1)}, bf16[720,2880]{1,0:T(8,128)(2,1)}) fusion(bf16[1440,2880]{1,0:T(8,128)(2,1)} %bitcast.63), kind=kLoop, calls=%fused_computation.142 | loop fusion | bytes 16588800 | tf_op jit(solution)/shard_map/slice | solution.py:580
  230.7 2.7 collective-permute-start.29
  233.4 2.6 collective-permute-start.30
  237.6 2.6 collective-permute-start.26
  243.3 32.5 %shard_map.91 = (bf16[160,2880]{1,0:T(8,128)(2,1)}, bf16[160,2880]{1,0:T(8,128)(2,1)}, f32[160,2880]{1,0:T(8,128)}, f32[8,2880]{1,0:T(8,128)}, f32[8,360]{1,0:T(...) custom-call(s32[13]{0:T(128)} %stack.126.meta, ...), custom_call_target="tpu_custom_call" | custom-call | flops 30000001024 | bytes 1024 | tf_op jit(solution)/shard_map/pallas_call | solution.py:317
  275.9 4.4 collective-permute-done.25
  280.3 3.3 collective-permute-done.26
  283.6 20.2 %collective-permute-done.27 = bf16[320,1440]{1,0:T(8,128)(2,1)S(1)} collective-permute-done((bf16[320,1440]{1,0:T(8,128)(2,1)S(1)}, bf16[320,1440]{1,0:T(8,128)(2,1)S(1)}, u32[]{:S(2)}, u32[]{:S(2)}) %collective-permute-start.27) | collective-permute-done | bytes 921632 | tf_op jit(solution)/shard_map/ppermute | solution.py:613
  303.7 2.4 collective-permute-start.28
  306.1 26.7 %shard_map.92 = (bf16[4,160,768]{2,1,0:T(8,128)(2,1)}, f32[8,360]{1,0:T(8,128)}, f32[8,2880]{1,0:T(8,128)}, bf16[4,160,768]{2,1,0:T(8,128)(2,1)}, f32[8,360]{1,0...) custom-call(s32[13]{0:T(128)} %stack.126.meta, bf16[160,2880]{1,0:T(8,128)(2,1)} %shard_map.88.up_ref, ...), custom_call_target="tpu_custom_call" | custom-call | flops 30000001024 | bytes 1024 | tf_op jit(solution)/shard_map/pallas_call | solution.py:317
  332.9 2.8 collective-permute-start.35
  335.7 2.6 collective-permute-start.36
  338.3 2.3 collective-permute-start.34
  342.4 3.9 collective-permute-start.32
  346.3 13.5 %collective-permute-done.34.up_ref = bf16[160,2880]{1,0:T(8,128)(2,1)} collective-permute-done((bf16[160,2880]{1,0:T(8,128)(2,1)}, bf16[160,2880]{1,0:T(8,128)(2,1)}, u32[]{:S(2)}, u32[]{:S(2)}) %collective-permute-start.34) | collective-permute-done | bytes 921632 | tf_op jit(solution)/shard_map/ppermute | solution.py:340
  359.8 4.4 collective-permute-start.33
  365.6 2.3 collective-permute-start.46
  367.9 4.3 shard_map.93
  372.1 12.9 %collective-permute-done.31 = bf16[320,1440]{1,0:T(8,128)(2,1)} collective-permute-done((bf16[320,1440]{1,0:T(8,128)(2,1)S(1)}, bf16[320,1440]{1,0:T(8,128)(2,1)}, u32[]{:S(2)}, u32[]{:S(2)}) %collective-permute-start.31) | collective-permute-done | bytes 921632 | tf_op jit(solution)/shard_map/ppermute | solution.py:345
  385.1 4.5 collective-permute-done.32
  389.6 19.2 %collective-permute-done.33 = bf16[320,1440]{1,0:T(8,128)(2,1)} collective-permute-done((bf16[320,1440]{1,0:T(8,128)(2,1)S(1)}, bf16[320,1440]{1,0:T(8,128)(2,1)}, u32[]{:S(2)}, u32[]{:S(2)}) %collective-permute-start.33) | collective-permute-done | bytes 921632 | tf_op jit(solution)/shard_map/ppermute | solution.py:613
  408.9 2.6 collective-permute-start.47
  411.5 2.9 broadcast_select_fusion.9
  414.9 2.7 broadcast_select_fusion.11
  429.3 5.2 collective-permute-done.55
  439.6 2.3 collective-permute-start.41
  445.5 9.7 %collective-permute-done.39 = bf16[320,768]{1,0:T(8,128)(2,1)S(1)} collective-permute-done((bf16[320,768]{1,0:T(8,128)(2,1)S(1)}, bf16[320,768]{1,0:T(8,128)(2,1)S(1)}, u32[]{:S(2)}, u32[]{:S(2)}) %collective-permute-start.39) | collective-permute-done | bytes 491552 | tf_op jit(solution)/shard_map/ppermute | solution.py:350
  455.2 2.3 collective-permute-start.57
  459.5 2.6 collective-permute-done.41
  462.6 17.6 %collective-permute-done.44 = bf16[320,768]{1,0:T(8,128)(2,1)S(1)} collective-permute-done((bf16[320,768]{1,0:T(8,128)(2,1)S(1)}, bf16[320,768]{1,0:T(8,128)(2,1)S(1)}, u32[]{:S(2)}, u32[]{:S(2)}) %collective-permute-start.44) | collective-permute-done | bytes 491552 | tf_op jit(solution)/shard_map/ppermute | solution.py:345
  482.3 12.9 %collective-permute-done.49 = bf16[320,768]{1,0:T(8,128)(2,1)S(1)} collective-permute-done((bf16[320,768]{1,0:T(8,128)(2,1)S(1)}, bf16[320,768]{1,0:T(8,128)(2,1)S(1)}, u32[]{:S(2)}, u32[]{:S(2)}) %collective-permute-start.49) | collective-permute-done | bytes 491552 | tf_op jit(solution)/shard_map/ppermute | solution.py:345
  499.2 5.7 %collective-permute-done.45 = bf16[320,768]{1,0:T(8,128)(2,1)S(1)} collective-permute-done((bf16[320,768]{1,0:T(8,128)(2,1)S(1)}, bf16[320,768]{1,0:T(8,128)(2,1)S(1)}, u32[]{:S(2)}, u32[]{:S(2)}) %collective-permute-start.45) | collective-permute-done | bytes 491552 | tf_op jit(solution)/shard_map/ppermute | solution.py:350
  506.9 6.2 %collective-permute-done.50 = bf16[320,768]{1,0:T(8,128)(2,1)S(1)} collective-permute-done((bf16[320,768]{1,0:T(8,128)(2,1)S(1)}, bf16[320,768]{1,0:T(8,128)(2,1)S(1)}, u32[]{:S(2)}, u32[]{:S(2)}) %collective-permute-start.50) | collective-permute-done | bytes 491552 | tf_op jit(solution)/shard_map/ppermute | solution.py:350
  513.1 2.8 add_convert_fusion
  516.0 2.5 collective-permute-start.51
  522.7 15.8 %collective-permute-done.51 = bf16[360,768]{1,0:T(8,128)(2,1)S(1)} collective-permute-done((bf16[360,768]{1,0:T(8,128)(2,1)S(1)}, bf16[360,768]{1,0:T(8,128)(2,1)S(1)}, u32[]{:S(2)}, u32[]{:S(2)}) %collective-permute-start.51) | collective-permute-done | bytes 552992 | tf_op jit(solution)/shard_map/ppermute | solution.py:345
  538.5 17.8 %collective-permute-done.52 = bf16[360,768]{1,0:T(8,128)(2,1)S(1)} collective-permute-done((bf16[360,768]{1,0:T(8,128)(2,1)S(1)}, bf16[360,768]{1,0:T(8,128)(2,1)S(1)}, u32[]{:S(2)}, u32[]{:S(2)}) %collective-permute-start.52) | collective-permute-done | bytes 552992 | tf_op jit(solution)/shard_map/ppermute | solution.py:345
  556.4 9.6 %collective-permute-done.53 = bf16[360,768]{1,0:T(8,128)(2,1)S(1)} collective-permute-done((bf16[360,768]{1,0:T(8,128)(2,1)S(1)}, bf16[360,768]{1,0:T(8,128)(2,1)S(1)}, u32[]{:S(2)}, u32[]{:S(2)}) %collective-permute-start.53) | collective-permute-done | bytes 552992 | tf_op jit(solution)/shard_map/ppermute | solution.py:345
  566.1 2.3 maximum_convert_fusion
  (232 shorter events, 71.8 us)
Async XLA Ops:
  0.6 55.7 %collective-permute-start.5 = (bf16[1440,2880]{1,0:T(8,128)(2,1)}, bf16[1440,2880]{1,0:T(8,128)(2,1)}, u32[]{:S(2)}, u32[]{:S(2)}) collective-permute-start(bf16[1440,2880]{1,0:T(8,128)(2,1)} %bitcast.59), channel_id=1, source_target_pairs={{0,8},{8,0},{16,24},{24,16},{1,9},{9,1},{17,25},{25,17},{2,10},{10... | collective-permute-start | bytes 24883208 | tf_op jit(solution)/shard_map/ppermute | solution.py:345
  0.7 23.2 %collective-permute-start.3 = (bf16[1440,360]{1,0:T(8,128)(2,1)}, bf16[1440,360]{1,0:T(8,128)(2,1)}, u32[]{:S(2)}, u32[]{:S(2)}) collective-permute-start(bf16[1440,360]{1,0:T(8,128)(2,1)} %bitcast.67), channel_id=1, source_target_pairs={{0,8},{8,0},{16,24},{24,16},{1,9},{9,1},{17,25},{25,17},{2,10},{10... | collective-permute-start | bytes 3110408 | tf_op jit(solution)/shard_map/ppermute | solution.py:345
  1.2 26.1 %collective-permute-start.4 = (bf16[1440,360]{1,0:T(8,128)(2,1)}, bf16[1440,360]{1,0:T(8,128)(2,1)}, u32[]{:S(2)}, u32[]{:S(2)}) collective-permute-start(bf16[1440,360]{1,0:T(8,128)(2,1)} %bitcast.69), channel_id=1, source_target_pairs={{0,8},{8,0},{16,24},{24,16},{1,9},{9,1},{17,25},{25,17},{2,10},{10... | collective-permute-start | bytes 3110408 | tf_op jit(solution)/shard_map/ppermute | solution.py:345
  17.5 35.8 %collective-permute-start.2 = (bf16[240,2880]{1,0:T(8,128)(2,1)S(1)}, bf16[240,2880]{1,0:T(8,128)(2,1)}, u32[]{:S(2)}, u32[]{:S(2)}) collective-permute-start(bf16[240,2880]{1,0:T(8,128)(2,1)S(1)} %get-tuple-element.217), channel_id=1, source_target_pairs={{16,20},{20,16},{24,28},{28,24},{17,21},{21,17},{25,29},{29,25},{1... | collective-permute-start | bytes 4147208 | tf_op jit(solution)/shard_map/ppermute | solution.py:340
  21.0 0.7 collective-permute-start
  21.7 55.2 %collective-permute-start.1 = (bf16[1440,360]{1,0:T(8,128)(2,1)}, bf16[1440,360]{1,0:T(8,128)(2,1)S(1)}, u32[]{:S(2)}, u32[]{:S(2)}) collective-permute-start(bf16[1440,360]{1,0:T(8,128)(2,1)} %pad_maximum_fusion.2), channel_id=1, source_target_pairs={{0,4},{4,0},{1,5},{5,1},{2,6},{6,2},{3,7},{7,3},{8,12},{12,8},{9,1... | collective-permute-start | bytes 3110408 | tf_op jit(solution)/shard_map/ppermute | solution.py:345
  23.9 87.3 %collective-permute-start.7 = (bf16[240,2880]{1,0:T(8,128)(2,1)}, bf16[240,2880]{1,0:T(8,128)(2,1)}, u32[]{:S(2)}, u32[]{:S(2)}) collective-permute-start(bf16[240,2880]{1,0:T(8,128)(2,1)} %get-tuple-element.216), channel_id=1, source_target_pairs={{16,20},{20,16},{24,28},{28,24},{17,21},{21,17},{25,29},{29,25},{1... | collective-permute-start | bytes 4147208 | tf_op jit(solution)/shard_map/ppermute | solution.py:340
  27.3 109.8 %collective-permute-start.8 = (bf16[240,2880]{1,0:T(8,128)(2,1)}, bf16[240,2880]{1,0:T(8,128)(2,1)}, u32[]{:S(2)}, u32[]{:S(2)}) collective-permute-start(bf16[240,2880]{1,0:T(8,128)(2,1)} %get-tuple-element.215), channel_id=1, source_target_pairs={{16,20},{20,16},{24,28},{28,24},{17,21},{21,17},{25,29},{29,25},{1... | collective-permute-start | bytes 4147208 | tf_op jit(solution)/shard_map/ppermute | solution.py:340
  53.3 83.8 %collective-permute-start.6 = (bf16[240,2880]{1,0:T(8,128)(2,1)}, bf16[240,2880]{1,0:T(8,128)(2,1)}, u32[]{:S(2)}, u32[]{:S(2)}) collective-permute-start(bf16[240,2880]{1,0:T(8,128)(2,1)} %collective-permute-done.2.refs_1_.refs_7_), channel_id=1, source_target_pairs={{16,17},{17,16},{18,19},{19,18},{24,25},{25,24},{26,27},{27,26},{2... | collective-permute-start | bytes 4147208 | tf_op jit(solution)/shard_map/ppermute | solution.py:340
  76.9 64.6 %copy-start = (bf16[1440,360]{1,0:T(8,128)(2,1)}, bf16[1440,360]{1,0:T(8,128)(2,1)S(1)}, u32[]{:S(2)}) copy-start(bf16[1440,360]{1,0:T(8,128)(2,1)S(1)} %collective-permute-done.1.refs_1_.refs_8_.refs_14_.refs_10_) | copy-start | bytes 3110404
  76.9 34.3 %collective-permute-start.10 = (bf16[1440,360]{1,0:T(8,128)(2,1)S(1)}, bf16[1440,360]{1,0:T(8,128)(2,1)S(1)}, u32[]{:S(2)}, u32[]{:S(2)}) collective-permute-start(bf16[1440,360]{1,0:T(8,128)(2,1)S(1)} %collective-permute-done.1.refs_1_.refs_8_.refs_14_.refs_10_), channel_id=1, source_target_pairs={{0,1},{1,0},{2,3},{3,2},{4,5},{5,4},{6,7},{7,6},{8,9},{9,8},{10,11... | collective-permute-start | bytes 3110408 | tf_op jit(solution)/shard_map/ppermute | solution.py:345
  77.3 1.6 collective-permute-start.9
  79.0 60.5 %collective-permute-start.11 = (bf16[1440,360]{1,0:T(8,128)(2,1)S(1)}, bf16[1440,360]{1,0:T(8,128)(2,1)S(1)}, u32[]{:S(2)}, u32[]{:S(2)}) collective-permute-start(bf16[1440,360]{1,0:T(8,128)(2,1)S(1)} %collective-permute-done.1.refs_1_.refs_8_.refs_14_.refs_10_), channel_id=1, source_target_pairs={{0,8},{8,0},{16,24},{24,16},{1,9},{9,1},{17,25},{25,17},{2,10},{10... | collective-permute-start | bytes 3110408 | tf_op jit(solution)/shard_map/ppermute | solution.py:345
  111.1 28.3 %collective-permute-start.12 = (bf16[1440,360]{1,0:T(8,128)(2,1)S(1)}, bf16[1440,360]{1,0:T(8,128)(2,1)S(1)}, u32[]{:S(2)}, u32[]{:S(2)}) collective-permute-start(bf16[1440,360]{1,0:T(8,128)(2,1)S(1)} %collective-permute-done.10.refs_2_.refs_9_.refs_15_.refs_11_), channel_id=1, source_target_pairs={{0,8},{8,0},{16,24},{24,16},{1,9},{9,1},{17,25},{25,17},{2,10},{10... | collective-permute-start | bytes 3110408 | tf_op jit(solution)/shard_map/ppermute | solution.py:345
  137.1 34.7 %collective-permute-start.13 = (bf16[240,2880]{1,0:T(8,128)(2,1)}, bf16[240,2880]{1,0:T(8,128)(2,1)}, u32[]{:S(2)}, u32[]{:S(2)}) collective-permute-start(bf16[240,2880]{1,0:T(8,128)(2,1)} %collective-permute-done.7.refs_2_.refs_8_), channel_id=1, source_target_pairs={{16,17},{17,16},{18,19},{19,18},{24,25},{25,24},{26,27},{27,26},{2... | collective-permute-start | bytes 4147208 | tf_op jit(solution)/shard_map/ppermute | solution.py:340
  145.6 26.2 %collective-permute-start.14 = (bf16[160,1440]{1,0:T(8,128)(2,1)}, bf16[160,1440]{1,0:T(8,128)(2,1)S(1)}, u32[]{:S(2)}, u32[]{:S(2)}) collective-permute-start(bf16[160,1440]{1,0:T(8,128)(2,1)} %get-tuple-element.133), channel_id=1, source_target_pairs={{0,4},{4,0},{8,12},{12,8},{1,5},{5,1},{9,13},{13,9},{2,6},{6,2},{1... | collective-permute-start | bytes 1382408 | tf_op jit(solution)/shard_map/ppermute | solution.py:340
  175.4 5.0 collective-permute-start.15
  176.2 33.8 %collective-permute-start.17 = (bf16[240,2880]{1,0:T(8,128)(2,1)}, bf16[240,2880]{1,0:T(8,128)(2,1)}, u32[]{:S(2)}, u32[]{:S(2)}) collective-permute-start(bf16[240,2880]{1,0:T(8,128)(2,1)} %collective-permute-done.8.refs_3_.refs_9_), channel_id=1, source_target_pairs={{16,17},{17,16},{18,19},{19,18},{24,25},{25,24},{26,27},{27,26},{2... | collective-permute-start | bytes 4147208 | tf_op jit(solution)/shard_map/ppermute | solution.py:340
  178.5 35.8 %collective-permute-start.19 = (bf16[240,2880]{1,0:T(8,128)(2,1)}, bf16[240,2880]{1,0:T(8,128)(2,1)}, u32[]{:S(2)}, u32[]{:S(2)}) collective-permute-start(bf16[240,2880]{1,0:T(8,128)(2,1)} %collective-permute-done.2.refs_1_.refs_7_), channel_id=1, source_target_pairs={{16,24},{24,16},{17,25},{25,17},{18,26},{26,18},{19,27},{27,19},{2... | collective-permute-start | bytes 4147208 | tf_op jit(solution)/shard_map/ppermute | solution.py:340
  185.5 26.4 %collective-permute-start.16 = (bf16[160,2880]{1,0:T(8,128)(2,1)}, bf16[160,2880]{1,0:T(8,128)(2,1)S(1)}, u32[]{:S(2)}, u32[]{:S(2)}) collective-permute-start(bf16[160,2880]{1,0:T(8,128)(2,1)} %get-tuple-element.136), channel_id=1, source_target_pairs={{0,16},{8,24},{1,17},{9,25},{2,18},{10,26},{3,19},{11,27},{4,20},{... | collective-permute-start | bytes 2764808 | tf_op jit(solution)/shard_map/ppermute | solution.py:340
  186.8 35.6 %collective-permute-start.18 = (bf16[160,1440]{1,0:T(8,128)(2,1)}, bf16[160,1440]{1,0:T(8,128)(2,1)S(1)}, u32[]{:S(2)}, u32[]{:S(2)}) collective-permute-start(bf16[160,1440]{1,0:T(8,128)(2,1)} %get-tuple-element.139), channel_id=1, source_target_pairs={{0,20},{4,16},{8,28},{12,24},{1,21},{5,17},{9,29},{13,25},{2,22},{... | collective-permute-start | bytes 1382408 | tf_op jit(solution)/shard_map/ppermute | solution.py:340
  188.8 41.6 %copy-start.7 = (bf16[160,1440]{1,0:T(8,128)(2,1)S(1)}, bf16[160,1440]{1,0:T(8,128)(2,1)}, u32[]{:S(2)}) copy-start(bf16[160,1440]{1,0:T(8,128)(2,1)} %get-tuple-element.116.mine_ref) | copy-start | bytes 1382404
  188.8 41.6 %copy-start.10 = (bf16[160,1440]{1,0:T(8,128)(2,1)S(1)}, bf16[160,1440]{1,0:T(8,128)(2,1)}, u32[]{:S(2)}) copy-start(bf16[160,1440]{1,0:T(8,128)(2,1)} %copy-done.9) | copy-start | bytes 1382404
  188.8 41.9 %collective-permute-start.20 = (bf16[240,2880]{1,0:T(8,128)(2,1)}, bf16[240,2880]{1,0:T(8,128)(2,1)S(1)}, u32[]{:S(2)}, u32[]{:S(2)}) collective-permute-start(bf16[240,2880]{1,0:T(8,128)(2,1)} %collective-permute-done.7.refs_2_.refs_8_), channel_id=1, source_target_pairs={{16,24},{24,16},{17,25},{25,17},{18,26},{26,18},{19,27},{27,19},{2... | collective-permute-start | bytes 4147208 | tf_op jit(solution)/shard_map/ppermute | solution.py:340
  210.0 23.4 %collective-permute-start.21 = (bf16[240,2880]{1,0:T(8,128)(2,1)}, bf16[240,2880]{1,0:T(8,128)(2,1)S(1)}, u32[]{:S(2)}, u32[]{:S(2)}) collective-permute-start(bf16[240,2880]{1,0:T(8,128)(2,1)} %collective-permute-done.8.refs_3_.refs_9_), channel_id=1, source_target_pairs={{16,24},{24,16},{17,25},{25,17},{18,26},{26,18},{19,27},{27,19},{2... | collective-permute-start | bytes 4147208 | tf_op jit(solution)/shard_map/ppermute | solution.py:340
  211.9 24.0 %collective-permute-start.22 = (bf16[240,2880]{1,0:T(8,128)(2,1)}, bf16[240,2880]{1,0:T(8,128)(2,1)S(1)}, u32[]{:S(2)}, u32[]{:S(2)}) collective-permute-start(bf16[240,2880]{1,0:T(8,128)(2,1)} %collective-permute-done.6.refs_4_.refs_10_), channel_id=1, source_target_pairs={{16,24},{24,16},{17,25},{25,17},{18,26},{26,18},{19,27},{27,19},{2... | collective-permute-start | bytes 4147208 | tf_op jit(solution)/shard_map/ppermute | solution.py:340
  214.4 23.2 %collective-permute-start.23 = (bf16[240,2880]{1,0:T(8,128)(2,1)}, bf16[240,2880]{1,0:T(8,128)(2,1)S(1)}, u32[]{:S(2)}, u32[]{:S(2)}) collective-permute-start(bf16[240,2880]{1,0:T(8,128)(2,1)} %collective-permute-done.13.refs_5_.refs_11_), channel_id=1, source_target_pairs={{16,24},{24,16},{17,25},{25,17},{18,26},{26,18},{19,27},{27,19},{2... | collective-permute-start | bytes 4147208 | tf_op jit(solution)/shard_map/ppermute | solution.py:340
  222.4 17.8 %collective-permute-start.24 = (bf16[240,2880]{1,0:T(8,128)(2,1)}, bf16[240,2880]{1,0:T(8,128)(2,1)S(1)}, u32[]{:S(2)}, u32[]{:S(2)}) collective-permute-start(bf16[240,2880]{1,0:T(8,128)(2,1)} %collective-permute-done.17.refs_6_.refs_12_), channel_id=1, source_target_pairs={{16,24},{24,16},{17,25},{25,17},{18,26},{26,18},{19,27},{27,19},{2... | collective-permute-start | bytes 4147208 | tf_op jit(solution)/shard_map/ppermute | solution.py:340
  230.7 102.2 %collective-permute-start.29 = (bf16[720,2880]{1,0:T(8,128)(2,1)}, bf16[720,2880]{1,0:T(8,128)(2,1)}, u32[]{:S(2)}, u32[]{:S(2)}) collective-permute-start(bf16[720,2880]{1,0:T(8,128)(2,1)} %get-tuple-element.214), channel_id=1, source_target_pairs={{8,12},{12,8},{9,13},{13,9},{10,14},{14,10},{11,15},{15,11}} | collective-permute-start | bytes 12441608 | tf_op jit(solution)/shard_map/ppermute | solution.py:340
  233.4 99.5 %collective-permute-start.30 = (bf16[720,2880]{1,0:T(8,128)(2,1)}, bf16[720,2880]{1,0:T(8,128)(2,1)}, u32[]{:S(2)}, u32[]{:S(2)}) collective-permute-start(bf16[720,2880]{1,0:T(8,128)(2,1)} %get-tuple-element.213), channel_id=1, source_target_pairs={{8,12},{12,8},{9,13},{13,9},{10,14},{14,10},{11,15},{15,11}} | collective-permute-start | bytes 12441608 | tf_op jit(solution)/shard_map/ppermute | solution.py:340
  236.0 44.3 %collective-permute-start.25 = (bf16[320,1440]{1,0:T(8,128)(2,1)S(1)}, bf16[320,1440]{1,0:T(8,128)(2,1)}, u32[]{:S(2)}, u32[]{:S(2)}) collective-permute-start(bf16[320,1440]{1,0:T(8,128)(2,1)S(1)} %maximum_select_fusion), channel_id=1, source_target_pairs={{0,1},{1,0},{2,3},{3,2},{4,5},{5,4},{6,7},{7,6},{8,9},{9,8},{10,11... | collective-permute-start | bytes 2764808 | tf_op jit(solution)/shard_map/ppermute | solution.py:345
  237.6 46.0 %collective-permute-start.26 = (bf16[320,1440]{1,0:T(8,128)(2,1)S(1)}, bf16[320,1440]{1,0:T(8,128)(2,1)}, u32[]{:S(2)}, u32[]{:S(2)}) collective-permute-start(bf16[320,1440]{1,0:T(8,128)(2,1)S(1)} %maximum_select_fusion), channel_id=1, source_target_pairs={{0,2},{1,3},{2,0},{3,1},{4,6},{5,7},{6,4},{7,5},{8,10},{9,11},{10,... | collective-permute-start | bytes 2764808 | tf_op jit(solution)/shard_map/ppermute | solution.py:345
  241.3 62.4 %collective-permute-start.27 = (bf16[320,1440]{1,0:T(8,128)(2,1)S(1)}, bf16[320,1440]{1,0:T(8,128)(2,1)S(1)}, u32[]{:S(2)}, u32[]{:S(2)}) collective-permute-start(bf16[320,1440]{1,0:T(8,128)(2,1)S(1)} %maximum_select_fusion), channel_id=1, source_target_pairs={{1,2},{2,1},{5,6},{6,5},{9,10},{10,9},{13,14},{14,13},{17,18},{18,... | collective-permute-start | bytes 2764808 | tf_op jit(solution)/shard_map/ppermute | solution.py:613
  303.7 29.2 %collective-permute-start.28 = (bf16[160,1440]{1,0:T(8,128)(2,1)}, bf16[160,1440]{1,0:T(8,128)(2,1)}, u32[]{:S(2)}, u32[]{:S(2)}) collective-permute-start(bf16[160,1440]{1,0:T(8,128)(2,1)} %get-tuple-element.160), channel_id=1, source_target_pairs={{16,20},{20,16},{24,28},{28,24},{17,21},{21,17},{25,29},{29,25},{1... | collective-permute-start | bytes 1382408 | tf_op jit(solution)/shard_map/ppermute | solution.py:340
  332.9 32.7 %collective-permute-start.35 = (bf16[720,2880]{1,0:T(8,128)(2,1)}, bf16[720,2880]{1,0:T(8,128)(2,1)}, u32[]{:S(2)}, u32[]{:S(2)}) collective-permute-start(bf16[720,2880]{1,0:T(8,128)(2,1)} %collective-permute-done.29.refs_7_), channel_id=1, source_target_pairs={{8,0},{9,1},{10,2},{11,3},{12,4},{13,5},{14,6},{15,7}} | collective-permute-start | bytes 12441608 | tf_op jit(solution)/shard_map/ppermute | solution.py:340
  335.7 32.1 %collective-permute-start.36 = (bf16[720,2880]{1,0:T(8,128)(2,1)}, bf16[720,2880]{1,0:T(8,128)(2,1)}, u32[]{:S(2)}, u32[]{:S(2)}) collective-permute-start(bf16[720,2880]{1,0:T(8,128)(2,1)} %collective-permute-done.30.refs_8_), channel_id=1, source_target_pairs={{8,0},{9,1},{10,2},{11,3},{12,4},{13,5},{14,6},{15,7}} | collective-permute-start | bytes 12441608 | tf_op jit(solution)/shard_map/ppermute | solution.py:340
  338.3 21.5 %collective-permute-start.34 = (bf16[160,2880]{1,0:T(8,128)(2,1)}, bf16[160,2880]{1,0:T(8,128)(2,1)}, u32[]{:S(2)}, u32[]{:S(2)}) collective-permute-start(bf16[160,2880]{1,0:T(8,128)(2,1)} %get-tuple-element.171), channel_id=1, source_target_pairs={{16,0},{24,8},{17,1},{25,9},{18,2},{26,10},{19,3},{27,11},{20,4},{... | collective-permute-start | bytes 2764808 | tf_op jit(solution)/shard_map/ppermute | solution.py:340
  342.3 42.7 %collective-permute-start.31 = (bf16[320,1440]{1,0:T(8,128)(2,1)S(1)}, bf16[320,1440]{1,0:T(8,128)(2,1)}, u32[]{:S(2)}, u32[]{:S(2)}) collective-permute-start(bf16[320,1440]{1,0:T(8,128)(2,1)S(1)} %maximum_select_fusion.1), channel_id=1, source_target_pairs={{0,1},{1,0},{2,3},{3,2},{4,5},{5,4},{6,7},{7,6},{8,9},{9,8},{10,11... | collective-permute-start | bytes 2764808 | tf_op jit(solution)/shard_map/ppermute | solution.py:345
  342.4 47.2 %collective-permute-start.32 = (bf16[320,1440]{1,0:T(8,128)(2,1)S(1)}, bf16[320,1440]{1,0:T(8,128)(2,1)}, u32[]{:S(2)}, u32[]{:S(2)}) collective-permute-start(bf16[320,1440]{1,0:T(8,128)(2,1)S(1)} %maximum_select_fusion.1), channel_id=1, source_target_pairs={{0,2},{1,3},{2,0},{3,1},{4,6},{5,7},{6,4},{7,5},{8,10},{9,11},{10,... | collective-permute-start | bytes 2764808 | tf_op jit(solution)/shard_map/ppermute | solution.py:345
  359.8 49.0 %collective-permute-start.33 = (bf16[320,1440]{1,0:T(8,128)(2,1)S(1)}, bf16[320,1440]{1,0:T(8,128)(2,1)}, u32[]{:S(2)}, u32[]{:S(2)}) collective-permute-start(bf16[320,1440]{1,0:T(8,128)(2,1)S(1)} %maximum_select_fusion.1), channel_id=1, source_target_pairs={{1,2},{2,1},{5,6},{6,5},{9,10},{10,9},{13,14},{14,13},{17,18},{18,... | collective-permute-start | bytes 2764808 | tf_op jit(solution)/shard_map/ppermute | solution.py:613
  365.6 68.9 %collective-permute-start.46 = (bf16[320,1440]{1,0:T(8,128)(2,1)}, bf16[320,1440]{1,0:T(8,128)(2,1)}, u32[]{:S(2)}, u32[]{:S(2)}) collective-permute-start(bf16[320,1440]{1,0:T(8,128)(2,1)} %collective-permute-done.26), channel_id=1, source_target_pairs={{2,3},{1,0},{6,7},{5,4},{10,11},{9,8},{14,15},{13,12},{18,19},{17,... | collective-permute-start | bytes 2764808 | tf_op jit(solution)/shard_map/ppermute | solution.py:620
  408.9 26.2 %collective-permute-start.47 = (bf16[320,1440]{1,0:T(8,128)(2,1)}, bf16[320,1440]{1,0:T(8,128)(2,1)}, u32[]{:S(2)}, u32[]{:S(2)}) collective-permute-start(bf16[320,1440]{1,0:T(8,128)(2,1)} %collective-permute-done.32), channel_id=1, source_target_pairs={{2,3},{1,0},{6,7},{5,4},{10,11},{9,8},{14,15},{13,12},{18,19},{17,... | collective-permute-start | bytes 2764808 | tf_op jit(solution)/shard_map/ppermute | solution.py:620
  414.8 8.4 %collective-permute-start.54 = (bf16[8,6480]{1,0:T(8,128)(2,1)S(1)}, bf16[8,6480]{1,0:T(8,128)(2,1)S(1)}, u32[]{:S(2)}, u32[]{:S(2)}) collective-permute-start(bf16[8,6480]{1,0:T(8,128)(2,1)S(1)} %get-tuple-element.262), channel_id=1, source_target_pairs={{0,8},{8,0},{16,24},{24,16},{1,9},{9,1},{17,25},{25,17},{2,10},{10... | collective-permute-start | bytes 311048 | tf_op jit(solution)/shard_map/ppermute | solution.py:345
  417.6 19.0 %collective-permute-start.40 = (bf16[320,1440]{1,0:T(8,128)(2,1)}, bf16[320,1440]{1,0:T(8,128)(2,1)}, u32[]{:S(2)}, u32[]{:S(2)}) collective-permute-start(bf16[320,1440]{1,0:T(8,128)(2,1)} %get-tuple-element.233), channel_id=1, source_target_pairs={{0,8},{8,0},{16,24},{24,16},{1,9},{9,1},{17,25},{25,17},{2,10},{10... | collective-permute-start | bytes 2764808 | tf_op jit(solution)/shard_map/ppermute | solution.py:345
  420.3 17.8 %collective-permute-start.38 = (bf16[4,160,768]{2,1,0:T(8,128)(2,1)}, bf16[4,160,768]{2,1,0:T(8,128)(2,1)}, u32[]{:S(2)}, u32[]{:S(2)}) collective-permute-start(bf16[4,160,768]{2,1,0:T(8,128)(2,1)} %get-tuple-element.220), channel_id=1, source_target_pairs={{0,8},{8,0},{16,24},{24,16},{1,9},{9,1},{17,25},{25,17},{2,10},{10... | collective-permute-start | bytes 2949128 | tf_op jit(solution)/shard_map/ppermute | solution.py:345
  427.6 6.9 %collective-permute-start.55 = (bf16[4,16,1440]{2,1,0:T(8,128)(2,1)S(1)}, bf16[4,16,1440]{2,1,0:T(8,128)(2,1)S(1)}, u32[]{:S(2)}, u32[]{:S(2)}) collective-permute-start(bf16[4,16,1440]{2,1,0:T(8,128)(2,1)S(1)} %get-tuple-element.258), channel_id=1, source_target_pairs={{0,4},{4,0},{1,5},{5,1},{2,6},{6,2},{3,7},{7,3},{8,12},{12,8},{9,1... | collective-permute-start | bytes 552968 | tf_op jit(solution)/shard_map/ppermute | solution.py:350
  434.5 3.6 collective-permute-start.37
  434.5 8.9 %collective-permute-start.43 = (bf16[320,1440]{1,0:T(8,128)(2,1)S(1)}, bf16[320,1440]{1,0:T(8,128)(2,1)S(1)}, u32[]{:S(2)}, u32[]{:S(2)}) collective-permute-start(bf16[320,1440]{1,0:T(8,128)(2,1)S(1)} %copy-done.19), channel_id=1, source_target_pairs={{0,8},{8,0},{16,24},{24,16},{1,9},{9,1},{17,25},{25,17},{2,10},{10... | collective-permute-start | bytes 2764808 | tf_op jit(solution)/shard_map/ppermute | solution.py:345
  435.1 83.4 %collective-permute-start.56 = (bf16[2,16,1440]{2,1,0:T(8,128)(2,1)S(1)}, bf16[2,16,1440]{2,1,0:T(8,128)(2,1)S(1)}, u32[]{:S(2)}, u32[]{:S(2)}) collective-permute-start(bf16[2,16,1440]{2,1,0:T(8,128)(2,1)S(1)} %get-tuple-element.255), channel_id=1, source_target_pairs={{0,1},{1,0},{2,3},{3,2},{4,5},{5,4},{6,7},{7,6},{8,9},{9,8},{10,11... | collective-permute-start | bytes 276488 | tf_op jit(solution)/shard_map/ppermute | solution.py:345
  436.6 44.1 %collective-permute-start.48 = (bf16[320,1440]{1,0:T(8,128)(2,1)S(1)}, bf16[320,1440]{1,0:T(8,128)(2,1)S(1)}, u32[]{:S(2)}, u32[]{:S(2)}) collective-permute-start(bf16[320,1440]{1,0:T(8,128)(2,1)S(1)} %get-tuple-element.219), channel_id=1, source_target_pairs={{0,8},{8,0},{16,24},{24,16},{1,9},{9,1},{17,25},{25,17},{2,10},{10... | collective-permute-start | bytes 2764808 | tf_op jit(solution)/shard_map/ppermute | solution.py:345
  439.6 22.5 %collective-permute-start.41 = (bf16[320,768]{1,0:T(8,128)(2,1)S(1)}, bf16[320,768]{1,0:T(8,128)(2,1)S(1)}, u32[]{:S(2)}, u32[]{:S(2)}) collective-permute-start(bf16[320,768]{1,0:T(8,128)(2,1)S(1)} %get-tuple-element.230), channel_id=1, source_target_pairs={{0,1},{1,0},{2,3},{3,2},{4,5},{5,4},{6,7},{7,6},{8,9},{9,8},{10,11... | collective-permute-start | bytes 1474568 | tf_op jit(solution)/shard_map/ppermute | solution.py:345
  441.9 13.3 %collective-permute-start.39 = (bf16[320,768]{1,0:T(8,128)(2,1)S(1)}, bf16[320,768]{1,0:T(8,128)(2,1)S(1)}, u32[]{:S(2)}, u32[]{:S(2)}) collective-permute-start(bf16[320,768]{1,0:T(8,128)(2,1)S(1)} %get-tuple-element.229), channel_id=1, source_target_pairs={{0,4},{4,0},{1,5},{5,1},{2,6},{6,2},{3,7},{7,3},{8,12},{12,8},{9,1... | collective-permute-start | bytes 1474568 | tf_op jit(solution)/shard_map/ppermute | solution.py:350
  443.4 36.8 %collective-permute-start.44 = (bf16[320,768]{1,0:T(8,128)(2,1)S(1)}, bf16[320,768]{1,0:T(8,128)(2,1)S(1)}, u32[]{:S(2)}, u32[]{:S(2)}) collective-permute-start(bf16[320,768]{1,0:T(8,128)(2,1)S(1)} %get-tuple-element.231), channel_id=1, source_target_pairs={{0,2},{1,3},{2,0},{3,1},{4,6},{5,7},{6,4},{7,5},{8,10},{9,11},{10,... | collective-permute-start | bytes 1474568 | tf_op jit(solution)/shard_map/ppermute | solution.py:345
  455.2 63.2 %collective-permute-start.57 = (bf16[2,16,1440]{2,1,0:T(8,128)(2,1)S(1)}, bf16[2,16,1440]{2,1,0:T(8,128)(2,1)S(1)}, u32[]{:S(2)}, u32[]{:S(2)}) collective-permute-start(bf16[2,16,1440]{2,1,0:T(8,128)(2,1)S(1)} %get-tuple-element.256), channel_id=1, source_target_pairs={{0,2},{1,3},{2,0},{3,1},{4,6},{5,7},{6,4},{7,5},{8,10},{9,11},{10,... | collective-permute-start | bytes 276488 | tf_op jit(solution)/shard_map/ppermute | solution.py:345
  459.5 37.8 %copy-start.23 = (bf16[160,1440]{1,0:T(8,128)(2,1)S(1)}, bf16[160,1440]{1,0:T(8,128)(2,1)}, u32[]{:S(2)}) copy-start(bf16[160,1440]{1,0:T(8,128)(2,1)} %get-tuple-element.242) | copy-start | bytes 1382404
  459.5 37.8 %copy-start.24 = (bf16[160,1440]{1,0:T(8,128)(2,1)S(1)}, bf16[160,1440]{1,0:T(8,128)(2,1)}, u32[]{:S(2)}) copy-start(bf16[160,1440]{1,0:T(8,128)(2,1)} %get-tuple-element.243) | copy-start | bytes 1382404
  462.1 33.1 %collective-permute-start.49 = (bf16[320,768]{1,0:T(8,128)(2,1)S(1)}, bf16[320,768]{1,0:T(8,128)(2,1)S(1)}, u32[]{:S(2)}, u32[]{:S(2)}) collective-permute-start(bf16[320,768]{1,0:T(8,128)(2,1)S(1)} %get-tuple-element.228), channel_id=1, source_target_pairs={{0,3},{1,2},{2,1},{3,0},{4,7},{5,6},{6,5},{7,4},{8,11},{9,10},{10,... | collective-permute-start | bytes 1474568 | tf_op jit(solution)/shard_map/ppermute | solution.py:345
  480.2 16.5 %collective-permute-start.42 = (bf16[320,768]{1,0:T(8,128)(2,1)S(1)}, bf16[320,768]{1,0:T(8,128)(2,1)S(1)}, u32[]{:S(2)}, u32[]{:S(2)}) collective-permute-start(bf16[320,768]{1,0:T(8,128)(2,1)S(1)} %collective-permute-done.41), channel_id=1, source_target_pairs={{0,4},{4,0},{1,5},{5,1},{2,6},{6,2},{3,7},{7,3},{8,12},{12,8},{9,1... | collective-permute-start | bytes 1474568 | tf_op jit(solution)/shard_map/ppermute | solution.py:350
  480.7 24.2 %collective-permute-start.45 = (bf16[320,768]{1,0:T(8,128)(2,1)S(1)}, bf16[320,768]{1,0:T(8,128)(2,1)S(1)}, u32[]{:S(2)}, u32[]{:S(2)}) collective-permute-start(bf16[320,768]{1,0:T(8,128)(2,1)S(1)} %collective-permute-done.44), channel_id=1, source_target_pairs={{0,4},{4,0},{1,5},{5,1},{2,6},{6,2},{3,7},{7,3},{8,12},{12,8},{9,1... | collective-permute-start | bytes 1474568 | tf_op jit(solution)/shard_map/ppermute | solution.py:350
  495.2 23.3 %collective-permute-start.58 = (bf16[2,16,1440]{2,1,0:T(8,128)(2,1)S(1)}, bf16[2,16,1440]{2,1,0:T(8,128)(2,1)S(1)}, u32[]{:S(2)}, u32[]{:S(2)}) collective-permute-start(bf16[2,16,1440]{2,1,0:T(8,128)(2,1)S(1)} %get-tuple-element.257), channel_id=1, source_target_pairs={{0,3},{1,2},{2,1},{3,0},{4,7},{5,6},{6,5},{7,4},{8,11},{9,10},{10,... | collective-permute-start | bytes 276488 | tf_op jit(solution)/shard_map/ppermute | solution.py:345
  496.7 16.4 %collective-permute-start.50 = (bf16[320,768]{1,0:T(8,128)(2,1)S(1)}, bf16[320,768]{1,0:T(8,128)(2,1)S(1)}, u32[]{:S(2)}, u32[]{:S(2)}) collective-permute-start(bf16[320,768]{1,0:T(8,128)(2,1)S(1)} %collective-permute-done.49), channel_id=1, source_target_pairs={{0,4},{4,0},{1,5},{5,1},{2,6},{6,2},{3,7},{7,3},{8,12},{12,8},{9,1... | collective-permute-start | bytes 1474568 | tf_op jit(solution)/shard_map/ppermute | solution.py:350
  516.0 22.5 %collective-permute-start.51 = (bf16[360,768]{1,0:T(8,128)(2,1)S(1)}, bf16[360,768]{1,0:T(8,128)(2,1)S(1)}, u32[]{:S(2)}, u32[]{:S(2)}) collective-permute-start(bf16[360,768]{1,0:T(8,128)(2,1)S(1)} %get-tuple-element.227), channel_id=1, source_target_pairs={{0,1},{1,0},{2,3},{3,2},{4,5},{5,4},{6,7},{7,6},{8,9},{9,8},{10,11... | collective-permute-start | bytes 1658888 | tf_op jit(solution)/shard_map/ppermute | solution.py:345
  518.6 37.8 %collective-permute-start.52 = (bf16[360,768]{1,0:T(8,128)(2,1)S(1)}, bf16[360,768]{1,0:T(8,128)(2,1)S(1)}, u32[]{:S(2)}, u32[]{:S(2)}) collective-permute-start(bf16[360,768]{1,0:T(8,128)(2,1)S(1)} %get-tuple-element.226), channel_id=1, source_target_pairs={{0,2},{1,3},{2,0},{3,1},{4,6},{5,7},{6,4},{7,5},{8,10},{9,11},{10,... | collective-permute-start | bytes 1658888 | tf_op jit(solution)/shard_map/ppermute | solution.py:345
  521.9 44.0 %collective-permute-start.53 = (bf16[360,768]{1,0:T(8,128)(2,1)S(1)}, bf16[360,768]{1,0:T(8,128)(2,1)S(1)}, u32[]{:S(2)}, u32[]{:S(2)}) collective-permute-start(bf16[360,768]{1,0:T(8,128)(2,1)S(1)} %get-tuple-element.225), channel_id=1, source_target_pairs={{0,3},{1,2},{2,1},{3,0},{4,7},{5,6},{6,5},{7,4},{8,11},{9,10},{10,... | collective-permute-start | bytes 1658888 | tf_op jit(solution)/shard_map/ppermute | solution.py:345
  (47 other events, 533.1 us)

commit v6 on v5

--- a/solution.py
+++ b/solution.py
@@ -11,7 +11,6 @@
 BF = jnp.bfloat16
 F32 = jnp.float32
 SUB = 8
-PIECES = 3
 PASS_FLOPS = 30 * 10**9
 VMEM_LIMIT = 62 * 1024 * 1024
 
@@ -399,8 +398,8 @@
     part = channels // fsdp
     tiles = [(low, min(group, channels - low)) for low in range(0, channels, group)]
     weight, squeeze, excite = weight[0], squeeze[0], excite[0]
-    assert PIECES == 3 and sections == 4 and dp & (dp - 1) == 0 and len(tiles) == dp
-    fast = fsdp == 2 and dp % 2 == 0 and part % (2 * 16 * PIECES) == 0
+    assert sections == 4 and dp & (dp - 1) == 0 and len(tiles) == dp
+    fast = fsdp == 2 and dp % 2 == 0 and part % 32 == 0
     first_stage, last_stage = (0, 1), (2, 3)
     barrier = lax.optimization_barrier
 
@@ -414,9 +413,9 @@
         near_s = [parity_half(side, parity, 0, half) for side in (squeeze, excite)]
         near_cut, inputs = barrier((jnp.concatenate(near_s, axis=0), inputs))
         s_at = [mine_at, near_at, cross_at]
-        step = half // PIECES
-        w_at = [mine_at] + [near_at + i * step for i in range(PIECES)]
-        w_at += [cross_at + i * step for i in range(PIECES)]
+        middle = half // 32 * 16
+        cut_at = ((0, middle), (middle, half - middle))
+        w_at = [mine_at, near_at, near_at + middle, cross_at, cross_at + middle]
     else:
         both = [lax.all_gather(side, "fsdp", axis=0, tiled=True) for side in (squeeze, excite)]
         s_own = [jnp.concatenate(both, axis=0)]
@@ -496,13 +495,13 @@
         later_weight, give = barrier((weight, give))
 
         def near(index):
-            cut = parity_half(later_weight, parity, index * step, step)
+            cut = parity_half(later_weight, parity, *cut_at[index])
             return move(cut, ("segment", "fsdp"), lambda s, f: (s, 1 - f) if s > 1 else None)
 
         def cross(cut):
             return move(cut, ("segment", "dp"), lambda s, z: (s, z ^ 1) if s > 1 else None)
 
-        near_w = [near(index) for index in range(PIECES)]
+        near_w = [near(index) for index in range(len(cut_at))]
 
         def meet(give):
             return move(
@@ -558,15 +557,15 @@
         s_other = [other_s, swap(near_s, "segment"), swap(cross_s, "segment")]
         s_own = [own_s, near_s, cross_s]
         d_last = flat(cotangent, back_order, False)[0]
-        keep, cross_w[0], *near_w[1:] = barrier((keep, cross_w[0], *near_w[1:]))
+        keep, cross_w[0], near_w[1] = barrier((keep, cross_w[0], near_w[1]))
         result = finish(0, h_first, keep, recv)
         h_mid, saved_a = result[0], result[1:6]
         mid_mine, mid_give = result[6:]
         cross_w.append(cross(near_w[1]))
-        cross_w.append(cross(near_w[2]))
         recv_b = meet(mid_give)
-        mid_mine, cross_w[1], d_last = barrier((mid_mine, cross_w[1], d_last))
+        mid_mine, d_last = barrier((mid_mine, d_last))
         keep, give = share(1, mid_mine, recv_b)
+        keep, cross_w[1] = barrier((keep, cross_w[1]))
         result = finish(1, h_mid, keep, meet(give))
         h_out, saved_b = result[0], result[1:6]
         out_mine, out_give = result[6:]
@@ -579,7 +578,6 @@
             move(cut, ("segment", "fsdp"), lambda s, f: (s, 1 - f) if s == 1 else None)
             for cut in (late_weight[:half], late_weight[half:])
         ]
-        h_in, cross_w[2] = barrier((h_in, cross_w[2]))
         far_early = near_w + cross_w
         late_at = [mine_at, far_at, far_at + half]
         early = [weight, *far_early, *s_own]
@@ -636,7 +634,7 @@
     h_in, unit = barrier((h_in, unit))
     slots_a = dp_slots(unit)
     result = forward_pass(h_in, 1, early)
-    result, slots_a, d_last = barrier((list(result), slots_a, d_last))
+    result, slots_a[:3], d_last = barrier((list(result), slots_a[:3], d_last))
     last = (result[2:7], result[7:12])
     if fast:
         mid_recv = move(

time: 578 us -> 594 us (1.028)
  waiting for transfers between devices: 319 us -> 329 us
    ppermute x26, waiting for transfers between devices: 151 us -> 184 us  [swap(): return lax.ppermute(value, axis, [(i, i ^ stride) for i in range(count)])]
    ppermute x2, waiting for transfers between devices: 39.4 us -> 22.4 us  [dp_slots(): inner = lax.ppermute(unit, 'dp', [(1, 2), (2, 1)])]
    ppermute x26, starting transfers between devices: 24.6 us -> 39.7 us  [swap(): return lax.ppermute(value, axis, [(i, i ^ stride) for i in range(count)])]
    ppermute x24 -> x20, starting transfers between devices: 50.8 us -> 42.2 us  [move(): return lax.ppermute(value, axes, pairs)]
    ppermute x24 -> x20, waiting for transfers between devices: 101 us -> 94.9 us  [move(): return lax.ppermute(value, axes, pairs)]
  transfers between devices with their start and end apart: 59 -> 55, of which waited for: 24 -> 22; matrix products, arithmetic and copies ran while one was open for 11% -> 11% of each run, Pallas kernels for 14% -> 14%
where the time goes in v6:
time: 594 us; the launch traced here: 585 us
  waiting for transfers between devices  329 us (55%)
  starting transfers between devices  97.2 us (16%)
  Pallas kernels  83.5 us (14%)
  local copies, waits for them, and re-layouts  40 us (7%)
  other arithmetic  21.7 us (4%)
  matrix products  10.9 us (2%)
    ppermute x26, waiting for transfers between devices, swap(): return lax.ppermute(value, axis, [(i, i ^ stride) for i in range(count)])  184 us
    ppermute x20, waiting for transfers between devices, move(): return lax.ppermute(value, axes, pairs)  94.9 us
    pallas_call x9, Pallas kernels, call(): pl.pallas_call(kernel, out_shape=[jax.ShapeDtypeStruct(shape, dtype) for...  83.5 us
    ppermute x20, starting transfers between devices, move(): return lax.ppermute(value, axes, pairs)  42.2 us
    ppermute x26, starting transfers between devices, swap(): return lax.ppermute(value, axis, [(i, i ^ stride) for i in range(count)])  39.7 us
    ppermute x5, waiting for transfers between devices, rotate(): lax.ppermute(value, axis, [(i, (i + steps) % count) for i in range(count)])  28.4 us
    ppermute x2, waiting for transfers between devices, dp_slots(): inner = lax.ppermute(unit, 'dp', [(1, 2), (2, 1)])  22.4 us
  transfers between devices with their start and end apart: 55, of which 22 were waited for; matrix products, arithmetic and copies ran while one was open for 11% of the time, Pallas kernels for 14%

profile of v6, /device:TPU:10, one launch (start us, length us, event | category | flops | bytes accessed | tf_op | source)
XLA Modules:
  0.0 584.8 jit_solution(9030350053494422225)
XLA Ops:
  4.2 3.7 reshape.72.all_ref
  9.1 3.6 shard_map.85
  12.7 3.2 constant_dynamic-slice_fusion.4
  15.9 3.4 collective-permute-start.2
  22.2 3.1 constant_dynamic-slice_fusion.3
  25.3 2.4 collective-permute-start.7
  27.7 3.2 pad_maximum_fusion.1.refs_3_.refs_13_.refs_19_.refs_15_
  30.9 35.1 %collective-permute-done.2.refs_1_.refs_7_ = bf16[352,2880]{1,0:T(8,128)(2,1)} collective-permute-done((bf16[352,2880]{1,0:T(8,128)(2,1)}, bf16[352,2880]{1,0:T(8,128)(2,1)}, u32[]{:S(2)}, u32[]{:S(2)}) %collective-permute-start.2) | collective-permute-done | bytes 2027552 | tf_op jit(solution)/shard_map/ppermute | solution.py:339
  66.0 2.4 collective-permute-start.6
  70.6 2.9 shard_map.86
  73.5 62.1 %collective-permute-done.1.refs_1_.refs_6_.refs_12_.refs_10_ = bf16[1440,360]{1,0:T(8,128)(2,1)S(1)} collective-permute-done((bf16[1440,360]{1,0:T(8,128)(2,1)}, bf16[1440,360]{1,0:T(8,128)(2,1)S(1)}, u32[]{:S(2)}, u32[]{:S(2)}) %collective-permute-start.1) | collective-permute-done | bytes 1036832 | tf_op jit(solution)/shard_map/ppermute | solution.py:344
  136.8 3.5 collective-permute-start.13
  141.3 21.6 %collective-permute-done.9.refs_2_.refs_7_.refs_13_.refs_11_ = bf16[1440,360]{1,0:T(8,128)(2,1)S(1)} collective-permute-done((bf16[1440,360]{1,0:T(8,128)(2,1)S(1)}, bf16[1440,360]{1,0:T(8,128)(2,1)S(1)}, u32[]{:S(2)}, u32[]{:S(2)}) %collective-permute-start.9) | collective-permute-done | bytes 1036832 | tf_op jit(solution)/shard_map/ppermute | solution.py:344
  166.6 4.1 shard_map.87
  172.3 4.8 reshape.73.all_ref
  177.1 3.1 shard_map.88.up_ref
  181.0 2.8 shard_map.89
  184.6 2.0 collective-permute-start.18
  186.6 21.5 %collective-permute-done.13.refs_4_.refs_10_ = bf16[368,2880]{1,0:T(8,128)(2,1)} collective-permute-done((bf16[368,2880]{1,0:T(8,128)(2,1)}, bf16[368,2880]{1,0:T(8,128)(2,1)}, u32[]{:S(2)}, u32[]{:S(2)}) %collective-permute-start.13) | collective-permute-done | bytes 2119712 | tf_op jit(solution)/shard_map/ppermute | solution.py:339
  208.1 1.9 collective-permute-start.20
  210.0 2.4 collective-permute-start.17
  212.4 1.9 collective-permute-start.19
  216.0 4.1 shard_map.90
  221.6 5.9 %fusion.71 = (bf16[720,2880]{1,0:T(8,128)(2,1)}, bf16[720,2880]{1,0:T(8,128)(2,1)}) fusion(bf16[1440,2880]{1,0:T(8,128)(2,1)} %bitcast.62), kind=kLoop, calls=%fused_computation.141 | loop fusion | bytes 16588800 | tf_op jit(solution)/shard_map/slice | solution.py:579
  227.5 18.2 %collective-permute-done.15.h_ref = bf16[160,2880]{1,0:T(8,128)(2,1)S(1)} collective-permute-done((bf16[160,2880]{1,0:T(8,128)(2,1)}, bf16[160,2880]{1,0:T(8,128)(2,1)S(1)}, u32[]{:S(2)}, u32[]{:S(2)}) %collective-permute-start.15) | collective-permute-done | bytes 921632 | tf_op jit(solution)/shard_map/ppermute | solution.py:339
  247.1 14.1 %collective-permute-done.16 = bf16[160,1440]{1,0:T(8,128)(2,1)S(1)} collective-permute-done((bf16[160,1440]{1,0:T(8,128)(2,1)S(1)}, bf16[160,1440]{1,0:T(8,128)(2,1)S(1)}, u32[]{:S(2)}, u32[]{:S(2)}) %collective-permute-start.16) | collective-permute-done | bytes 460832 | tf_op jit(solution)/shard_map/ppermute | solution.py:339
  261.3 2.7 collective-permute-start.24
  264.3 2.6 collective-permute-start.25
  267.4 2.6 collective-permute-start.22
  269.9 32.1 %shard_map.91 = (bf16[160,2880]{1,0:T(8,128)(2,1)}, bf16[160,2880]{1,0:T(8,128)(2,1)}, f32[160,2880]{1,0:T(8,128)}, f32[8,2880]{1,0:T(8,128)}, f32[8,360]{1,0:T(...) custom-call(s32[11]{0:T(128)} %stack.116.meta, ...), custom_call_target="tpu_custom_call" | custom-call | flops 30000001024 | bytes 1024 | tf_op jit(solution)/shard_map/pallas_call | solution.py:316
  302.1 6.2 %collective-permute-done.21 = bf16[320,1440]{1,0:T(8,128)(2,1)S(1)} collective-permute-done((bf16[320,1440]{1,0:T(8,128)(2,1)S(1)}, bf16[320,1440]{1,0:T(8,128)(2,1)S(1)}, u32[]{:S(2)}, u32[]{:S(2)}) %collective-permute-start.21) | collective-permute-done | bytes 921632 | tf_op jit(solution)/shard_map/ppermute | solution.py:344
  308.3 3.4 collective-permute-done.22
  311.7 3.4 collective-permute-start.23
  315.1 26.6 %shard_map.92 = (bf16[4,160,768]{2,1,0:T(8,128)(2,1)}, f32[8,360]{1,0:T(8,128)}, f32[8,2880]{1,0:T(8,128)}, bf16[4,160,768]{2,1,0:T(8,128)(2,1)}, f32[8,360]{1,0...) custom-call(s32[11]{0:T(128)} %stack.116.meta, bf16[160,2880]{1,0:T(8,128)(2,1)} %shard_map.88.up_ref, ...), custom_call_target="tpu_custom_call" | custom-call | flops 30000001024 | bytes 1024 | tf_op jit(solution)/shard_map/pallas_call | solution.py:316
  341.8 2.8 collective-permute-start.30
  344.6 2.7 collective-permute-start.31
  347.3 2.2 collective-permute-start.29
  354.0 6.1 %collective-permute-done.29.up_ref = bf16[160,2880]{1,0:T(8,128)(2,1)} collective-permute-done((bf16[160,2880]{1,0:T(8,128)(2,1)}, bf16[160,2880]{1,0:T(8,128)(2,1)}, u32[]{:S(2)}, u32[]{:S(2)}) %collective-permute-start.29) | collective-permute-done | bytes 921632 | tf_op jit(solution)/shard_map/ppermute | solution.py:339
  360.0 2.3 collective-permute-start.28
  363.8 3.5 collective-permute-start.41
  367.3 2.3 collective-permute-start.42
  369.5 4.2 shard_map.93
  373.8 13.6 %collective-permute-done.26 = bf16[320,1440]{1,0:T(8,128)(2,1)} collective-permute-done((bf16[320,1440]{1,0:T(8,128)(2,1)S(1)}, bf16[320,1440]{1,0:T(8,128)(2,1)}, u32[]{:S(2)}, u32[]{:S(2)}) %collective-permute-start.26) | collective-permute-done | bytes 921632 | tf_op jit(solution)/shard_map/ppermute | solution.py:344
  387.5 22.4 %collective-permute-done.28 = bf16[320,1440]{1,0:T(8,128)(2,1)} collective-permute-done((bf16[320,1440]{1,0:T(8,128)(2,1)S(1)}, bf16[320,1440]{1,0:T(8,128)(2,1)}, u32[]{:S(2)}, u32[]{:S(2)}) %collective-permute-start.28) | collective-permute-done | bytes 921632 | tf_op jit(solution)/shard_map/ppermute | solution.py:611
  409.9 2.6 collective-permute-start.43
  412.5 2.6 broadcast_select_fusion.9
  415.4 19.7 %collective-permute-start.50 = (bf16[8,6480]{1,0:T(8,128)(2,1)S(1)}, bf16[8,6480]{1,0:T(8,128)(2,1)S(1)}, u32[]{:S(2)}, u32[]{:S(2)}) collective-permute-start(bf16[8,6480]{1,0:T(8,128)(2,1)S(1)} %get-tuple-element.253), channel_id=1, source_target_pairs={{0,8},{8,0},{16,24},{24,16},{1,9},{9,1},{17,25},{25,17},{2,10},{10... | collective-permute-start | bytes 311048 | tf_op jit(solution)/shard_map/ppermute | solution.py:344
  435.1 2.7 broadcast_select_fusion.11
  447.9 6.6 %collective-permute-done.51 = bf16[4,16,1440]{2,1,0:T(8,128)(2,1)S(1)} collective-permute-done((bf16[4,16,1440]{2,1,0:T(8,128)(2,1)S(1)}, bf16[4,16,1440]{2,1,0:T(8,128)(2,1)S(1)}, u32[]{:S(2)}, u32[]{:S(2)}) %collective-permute-start.51) | collective-permute-done | bytes 184352 | tf_op jit(solution)/shard_map/ppermute | solution.py:349
  462.5 11.5 %collective-permute-done.34 = bf16[320,768]{1,0:T(8,128)(2,1)S(1)} collective-permute-done((bf16[320,768]{1,0:T(8,128)(2,1)S(1)}, bf16[320,768]{1,0:T(8,128)(2,1)S(1)}, u32[]{:S(2)}, u32[]{:S(2)}) %collective-permute-start.34) | collective-permute-done | bytes 491552 | tf_op jit(solution)/shard_map/ppermute | solution.py:349
  475.3 1.9 fusion
  477.3 4.6 collective-permute-done.36
  482.4 14.8 %collective-permute-done.39 = bf16[320,768]{1,0:T(8,128)(2,1)S(1)} collective-permute-done((bf16[320,768]{1,0:T(8,128)(2,1)S(1)}, bf16[320,768]{1,0:T(8,128)(2,1)S(1)}, u32[]{:S(2)}, u32[]{:S(2)}) %collective-permute-start.39) | collective-permute-done | bytes 491552 | tf_op jit(solution)/shard_map/ppermute | solution.py:344
  499.4 12.7 %collective-permute-done.45 = bf16[320,768]{1,0:T(8,128)(2,1)S(1)} collective-permute-done((bf16[320,768]{1,0:T(8,128)(2,1)S(1)}, bf16[320,768]{1,0:T(8,128)(2,1)S(1)}, u32[]{:S(2)}, u32[]{:S(2)}) %collective-permute-start.45) | collective-permute-done | bytes 491552 | tf_op jit(solution)/shard_map/ppermute | solution.py:344
  515.0 1.9 fusion.8
  517.0 5.0 collective-permute-done.40
  522.0 2.0 fusion.16
  523.9 5.4 collective-permute-done.46
  529.3 2.8 add_convert_fusion
  532.2 2.6 collective-permute-start.47
  538.9 16.0 %collective-permute-done.47 = bf16[360,768]{1,0:T(8,128)(2,1)S(1)} collective-permute-done((bf16[360,768]{1,0:T(8,128)(2,1)S(1)}, bf16[360,768]{1,0:T(8,128)(2,1)S(1)}, u32[]{:S(2)}, u32[]{:S(2)}) %collective-permute-start.47) | collective-permute-done | bytes 552992 | tf_op jit(solution)/shard_map/ppermute | solution.py:344
  554.9 17.6 %collective-permute-done.48 = bf16[360,768]{1,0:T(8,128)(2,1)S(1)} collective-permute-done((bf16[360,768]{1,0:T(8,128)(2,1)S(1)}, bf16[360,768]{1,0:T(8,128)(2,1)S(1)}, u32[]{:S(2)}, u32[]{:S(2)}) %collective-permute-start.48) | collective-permute-done | bytes 552992 | tf_op jit(solution)/shard_map/ppermute | solution.py:344
  572.6 9.2 %collective-permute-done.49 = bf16[360,768]{1,0:T(8,128)(2,1)S(1)} collective-permute-done((bf16[360,768]{1,0:T(8,128)(2,1)S(1)}, bf16[360,768]{1,0:T(8,128)(2,1)S(1)}, u32[]{:S(2)}, u32[]{:S(2)}) %collective-permute-start.49) | collective-permute-done | bytes 552992 | tf_op jit(solution)/shard_map/ppermute | solution.py:344
  582.0 2.3 maximum_convert_fusion
  (211 shorter events, 59.5 us)
Async XLA Ops:
  0.6 69.9 %collective-permute-start.5 = (bf16[1440,2880]{1,0:T(8,128)(2,1)}, bf16[1440,2880]{1,0:T(8,128)(2,1)}, u32[]{:S(2)}, u32[]{:S(2)}) collective-permute-start(bf16[1440,2880]{1,0:T(8,128)(2,1)} %bitcast.57), channel_id=1, source_target_pairs={{0,8},{8,0},{16,24},{24,16},{1,9},{9,1},{17,25},{25,17},{2,10},{10... | collective-permute-start | bytes 24883208 | tf_op jit(solution)/shard_map/ppermute | solution.py:344
  15.9 50.1 %collective-permute-start.2 = (bf16[352,2880]{1,0:T(8,128)(2,1)}, bf16[352,2880]{1,0:T(8,128)(2,1)}, u32[]{:S(2)}, u32[]{:S(2)}) collective-permute-start(bf16[352,2880]{1,0:T(8,128)(2,1)} %constant_dynamic-slice_fusion.4), channel_id=1, source_target_pairs={{16,20},{20,16},{24,28},{28,24},{17,21},{21,17},{25,29},{29,25},{1... | collective-permute-start | bytes 6082568 | tf_op jit(solution)/shard_map/ppermute | solution.py:339
  19.3 6.0 %collective-permute-start.3 = (bf16[1440,360]{1,0:T(8,128)(2,1)S(1)}, bf16[1440,360]{1,0:T(8,128)(2,1)}, u32[]{:S(2)}, u32[]{:S(2)}) collective-permute-start(bf16[1440,360]{1,0:T(8,128)(2,1)S(1)} %bitcast.66), channel_id=1, source_target_pairs={{0,8},{8,0},{16,24},{24,16},{1,9},{9,1},{17,25},{25,17},{2,10},{10... | collective-permute-start | bytes 3110408 | tf_op jit(solution)/shard_map/ppermute | solution.py:344
  19.6 8.1 %collective-permute-start.4 = (bf16[1440,360]{1,0:T(8,128)(2,1)S(1)}, bf16[1440,360]{1,0:T(8,128)(2,1)}, u32[]{:S(2)}, u32[]{:S(2)}) collective-permute-start(bf16[1440,360]{1,0:T(8,128)(2,1)S(1)} %bitcast.68), channel_id=1, source_target_pairs={{0,8},{8,0},{16,24},{24,16},{1,9},{9,1},{17,25},{25,17},{2,10},{10... | collective-permute-start | bytes 3110408 | tf_op jit(solution)/shard_map/ppermute | solution.py:344
  19.9 48.4 %collective-permute-start = (bf16[160,1440]{1,0:T(8,128)(2,1)}, bf16[160,1440]{1,0:T(8,128)(2,1)S(1)}, u32[]{:S(2)}, u32[]{:S(2)}) collective-permute-start(bf16[160,1440]{1,0:T(8,128)(2,1)} %get-tuple-element.108), channel_id=1, source_target_pairs={{0,4},{4,0},{8,12},{12,8},{1,5},{5,1},{9,13},{13,9},{2,6},{6,2},{1... | collective-permute-start | bytes 1382408 | tf_op jit(solution)/shard_map/ppermute | solution.py:339
  25.3 111.4 %collective-permute-start.7 = (bf16[368,2880]{1,0:T(8,128)(2,1)}, bf16[368,2880]{1,0:T(8,128)(2,1)}, u32[]{:S(2)}, u32[]{:S(2)}) collective-permute-start(bf16[368,2880]{1,0:T(8,128)(2,1)} %constant_dynamic-slice_fusion.3), channel_id=1, source_target_pairs={{16,20},{20,16},{24,28},{28,24},{17,21},{21,17},{25,29},{29,25},{1... | collective-permute-start | bytes 6359048 | tf_op jit(solution)/shard_map/ppermute | solution.py:339
  66.0 70.8 %collective-permute-start.6 = (bf16[352,2880]{1,0:T(8,128)(2,1)}, bf16[352,2880]{1,0:T(8,128)(2,1)}, u32[]{:S(2)}, u32[]{:S(2)}) collective-permute-start(bf16[352,2880]{1,0:T(8,128)(2,1)} %collective-permute-done.2.refs_1_.refs_7_), channel_id=1, source_target_pairs={{16,17},{17,16},{18,19},{19,18},{24,25},{25,24},{26,27},{27,26},{2... | collective-permute-start | bytes 6082568 | tf_op jit(solution)/shard_map/ppermute | solution.py:339
  68.4 67.2 %collective-permute-start.1 = (bf16[1440,360]{1,0:T(8,128)(2,1)}, bf16[1440,360]{1,0:T(8,128)(2,1)S(1)}, u32[]{:S(2)}, u32[]{:S(2)}) collective-permute-start(bf16[1440,360]{1,0:T(8,128)(2,1)} %pad_maximum_fusion.2), channel_id=1, source_target_pairs={{0,4},{4,0},{1,5},{5,1},{2,6},{6,2},{3,7},{7,3},{8,12},{12,8},{9,1... | collective-permute-start | bytes 3110408 | tf_op jit(solution)/shard_map/ppermute | solution.py:344
  135.6 27.3 %collective-permute-start.9 = (bf16[1440,360]{1,0:T(8,128)(2,1)S(1)}, bf16[1440,360]{1,0:T(8,128)(2,1)S(1)}, u32[]{:S(2)}, u32[]{:S(2)}) collective-permute-start(bf16[1440,360]{1,0:T(8,128)(2,1)S(1)} %collective-permute-done.1.refs_1_.refs_6_.refs_12_.refs_10_), channel_id=1, source_target_pairs={{0,1},{1,0},{2,3},{3,2},{4,5},{5,4},{6,7},{7,6},{8,9},{9,8},{10,11... | collective-permute-start | bytes 3110408 | tf_op jit(solution)/shard_map/ppermute | solution.py:344
  136.0 4.3 collective-permute-start.8
  136.8 71.3 %collective-permute-start.13 = (bf16[368,2880]{1,0:T(8,128)(2,1)}, bf16[368,2880]{1,0:T(8,128)(2,1)}, u32[]{:S(2)}, u32[]{:S(2)}) collective-permute-start(bf16[368,2880]{1,0:T(8,128)(2,1)} %collective-permute-done.7.refs_2_.refs_8_), channel_id=1, source_target_pairs={{16,17},{17,16},{18,19},{19,18},{24,25},{25,24},{26,27},{27,26},{2... | collective-permute-start | bytes 6359048 | tf_op jit(solution)/shard_map/ppermute | solution.py:339
  140.3 22.6 %collective-permute-start.10 = (bf16[1440,360]{1,0:T(8,128)(2,1)S(1)}, bf16[1440,360]{1,0:T(8,128)(2,1)S(1)}, u32[]{:S(2)}, u32[]{:S(2)}) collective-permute-start(bf16[1440,360]{1,0:T(8,128)(2,1)S(1)} %collective-permute-done.1.refs_1_.refs_6_.refs_12_.refs_10_), channel_id=1, source_target_pairs={{0,8},{8,0},{16,24},{24,16},{1,9},{9,1},{17,25},{25,17},{2,10},{10... | collective-permute-start | bytes 3110408 | tf_op jit(solution)/shard_map/ppermute | solution.py:344
  162.9 2.7 collective-permute-start.11
  170.7 9.6 %collective-permute-start.12 = (bf16[160,1440]{1,0:T(8,128)(2,1)}, bf16[160,1440]{1,0:T(8,128)(2,1)S(1)}, u32[]{:S(2)}, u32[]{:S(2)}) collective-permute-start(bf16[160,1440]{1,0:T(8,128)(2,1)} %get-tuple-element.129), channel_id=1, source_target_pairs={{0,4},{4,0},{8,12},{12,8},{1,5},{5,1},{9,13},{13,9},{2,6},{6,2},{1... | collective-permute-start | bytes 1382408 | tf_op jit(solution)/shard_map/ppermute | solution.py:339
  183.8 31.2 %collective-permute-start.14 = (bf16[160,2880]{1,0:T(8,128)(2,1)}, bf16[160,2880]{1,0:T(8,128)(2,1)S(1)}, u32[]{:S(2)}, u32[]{:S(2)}) collective-permute-start(bf16[160,2880]{1,0:T(8,128)(2,1)} %get-tuple-element.133), channel_id=1, source_target_pairs={{0,4},{4,0},{8,12},{12,8},{1,5},{5,1},{9,13},{13,9},{2,6},{6,2},{1... | collective-permute-start | bytes 2764808 | tf_op jit(solution)/shard_map/ppermute | solution.py:339
  184.6 82.8 %collective-permute-start.18 = (bf16[368,2880]{1,0:T(8,128)(2,1)}, bf16[368,2880]{1,0:T(8,128)(2,1)}, u32[]{:S(2)}, u32[]{:S(2)}) collective-permute-start(bf16[368,2880]{1,0:T(8,128)(2,1)} %collective-permute-done.7.refs_2_.refs_8_), channel_id=1, source_target_pairs={{16,24},{24,16},{17,25},{25,17},{18,26},{26,18},{19,27},{27,19},{2... | collective-permute-start | bytes 6359048 | tf_op jit(solution)/shard_map/ppermute | solution.py:339
  208.1 61.9 %collective-permute-start.20 = (bf16[368,2880]{1,0:T(8,128)(2,1)}, bf16[368,2880]{1,0:T(8,128)(2,1)}, u32[]{:S(2)}, u32[]{:S(2)}) collective-permute-start(bf16[368,2880]{1,0:T(8,128)(2,1)} %collective-permute-done.13.refs_4_.refs_10_), channel_id=1, source_target_pairs={{16,24},{24,16},{17,25},{25,17},{18,26},{26,18},{19,27},{27,19},{2... | collective-permute-start | bytes 6359048 | tf_op jit(solution)/shard_map/ppermute | solution.py:339
  210.0 54.2 %collective-permute-start.17 = (bf16[352,2880]{1,0:T(8,128)(2,1)}, bf16[352,2880]{1,0:T(8,128)(2,1)}, u32[]{:S(2)}, u32[]{:S(2)}) collective-permute-start(bf16[352,2880]{1,0:T(8,128)(2,1)} %collective-permute-done.2.refs_1_.refs_7_), channel_id=1, source_target_pairs={{16,24},{24,16},{17,25},{25,17},{18,26},{26,18},{19,27},{27,19},{2... | collective-permute-start | bytes 6082568 | tf_op jit(solution)/shard_map/ppermute | solution.py:339
  212.4 54.5 %collective-permute-start.19 = (bf16[352,2880]{1,0:T(8,128)(2,1)}, bf16[352,2880]{1,0:T(8,128)(2,1)}, u32[]{:S(2)}, u32[]{:S(2)}) collective-permute-start(bf16[352,2880]{1,0:T(8,128)(2,1)} %collective-permute-done.6.refs_3_.refs_9_), channel_id=1, source_target_pairs={{16,24},{24,16},{17,25},{25,17},{18,26},{26,18},{19,27},{27,19},{2... | collective-permute-start | bytes 6082568 | tf_op jit(solution)/shard_map/ppermute | solution.py:339
  220.1 43.9 %copy-start.6 = (bf16[160,1440]{1,0:T(8,128)(2,1)S(1)}, bf16[160,1440]{1,0:T(8,128)(2,1)}, u32[]{:S(2)}) copy-start(bf16[160,1440]{1,0:T(8,128)(2,1)} %get-tuple-element.113.mine_ref) | copy-start | bytes 1382404
  220.1 43.9 %copy-start.8 = (bf16[160,1440]{1,0:T(8,128)(2,1)S(1)}, bf16[160,1440]{1,0:T(8,128)(2,1)}, u32[]{:S(2)}) copy-start(bf16[160,1440]{1,0:T(8,128)(2,1)} %copy-done.7) | copy-start | bytes 1382404
  220.1 25.5 %collective-permute-start.15 = (bf16[160,2880]{1,0:T(8,128)(2,1)}, bf16[160,2880]{1,0:T(8,128)(2,1)S(1)}, u32[]{:S(2)}, u32[]{:S(2)}) collective-permute-start(bf16[160,2880]{1,0:T(8,128)(2,1)} %get-tuple-element.134), channel_id=1, source_target_pairs={{0,16},{8,24},{1,17},{9,25},{2,18},{10,26},{3,19},{11,27},{4,20},{... | collective-permute-start | bytes 2764808 | tf_op jit(solution)/shard_map/ppermute | solution.py:339
  245.6 15.6 %collective-permute-start.16 = (bf16[160,1440]{1,0:T(8,128)(2,1)S(1)}, bf16[160,1440]{1,0:T(8,128)(2,1)S(1)}, u32[]{:S(2)}, u32[]{:S(2)}) collective-permute-start(bf16[160,1440]{1,0:T(8,128)(2,1)S(1)} %copy-done.43), channel_id=1, source_target_pairs={{0,20},{4,16},{8,28},{12,24},{1,21},{5,17},{9,29},{13,25},{2,22},{... | collective-permute-start | bytes 1382408 | tf_op jit(solution)/shard_map/ppermute | solution.py:339
  261.3 80.5 %collective-permute-start.24 = (bf16[720,2880]{1,0:T(8,128)(2,1)}, bf16[720,2880]{1,0:T(8,128)(2,1)}, u32[]{:S(2)}, u32[]{:S(2)}) collective-permute-start(bf16[720,2880]{1,0:T(8,128)(2,1)} %get-tuple-element.208), channel_id=1, source_target_pairs={{8,12},{12,8},{9,13},{13,9},{10,14},{14,10},{11,15},{15,11}} | collective-permute-start | bytes 12441608 | tf_op jit(solution)/shard_map/ppermute | solution.py:339
  264.3 77.5 %collective-permute-start.25 = (bf16[720,2880]{1,0:T(8,128)(2,1)}, bf16[720,2880]{1,0:T(8,128)(2,1)}, u32[]{:S(2)}, u32[]{:S(2)}) collective-permute-start(bf16[720,2880]{1,0:T(8,128)(2,1)} %get-tuple-element.207), channel_id=1, source_target_pairs={{8,12},{12,8},{9,13},{13,9},{10,14},{14,10},{11,15},{15,11}} | collective-permute-start | bytes 12441608 | tf_op jit(solution)/shard_map/ppermute | solution.py:339
  266.9 41.4 %collective-permute-start.21 = (bf16[320,1440]{1,0:T(8,128)(2,1)S(1)}, bf16[320,1440]{1,0:T(8,128)(2,1)S(1)}, u32[]{:S(2)}, u32[]{:S(2)}) collective-permute-start(bf16[320,1440]{1,0:T(8,128)(2,1)S(1)} %maximum_select_fusion), channel_id=1, source_target_pairs={{0,1},{1,0},{2,3},{3,2},{4,5},{5,4},{6,7},{7,6},{8,9},{9,8},{10,11... | collective-permute-start | bytes 2764808 | tf_op jit(solution)/shard_map/ppermute | solution.py:344
  267.4 44.3 %collective-permute-start.22 = (bf16[320,1440]{1,0:T(8,128)(2,1)S(1)}, bf16[320,1440]{1,0:T(8,128)(2,1)}, u32[]{:S(2)}, u32[]{:S(2)}) collective-permute-start(bf16[320,1440]{1,0:T(8,128)(2,1)S(1)} %maximum_select_fusion), channel_id=1, source_target_pairs={{0,2},{1,3},{2,0},{3,1},{4,6},{5,7},{6,4},{7,5},{8,10},{9,11},{10,... | collective-permute-start | bytes 2764808 | tf_op jit(solution)/shard_map/ppermute | solution.py:344
  311.7 30.1 %collective-permute-start.23 = (bf16[160,1440]{1,0:T(8,128)(2,1)}, bf16[160,1440]{1,0:T(8,128)(2,1)}, u32[]{:S(2)}, u32[]{:S(2)}) collective-permute-start(bf16[160,1440]{1,0:T(8,128)(2,1)} %get-tuple-element.155), channel_id=1, source_target_pairs={{16,20},{20,16},{24,28},{28,24},{17,21},{21,17},{25,29},{29,25},{1... | collective-permute-start | bytes 1382408 | tf_op jit(solution)/shard_map/ppermute | solution.py:339
  341.8 22.0 %collective-permute-start.30 = (bf16[720,2880]{1,0:T(8,128)(2,1)}, bf16[720,2880]{1,0:T(8,128)(2,1)}, u32[]{:S(2)}, u32[]{:S(2)}) collective-permute-start(bf16[720,2880]{1,0:T(8,128)(2,1)} %collective-permute-done.24.refs_7_), channel_id=1, source_target_pairs={{8,0},{9,1},{10,2},{11,3},{12,4},{13,5},{14,6},{15,7}} | collective-permute-start | bytes 12441608 | tf_op jit(solution)/shard_map/ppermute | solution.py:339
  344.6 22.7 %collective-permute-start.31 = (bf16[720,2880]{1,0:T(8,128)(2,1)}, bf16[720,2880]{1,0:T(8,128)(2,1)}, u32[]{:S(2)}, u32[]{:S(2)}) collective-permute-start(bf16[720,2880]{1,0:T(8,128)(2,1)} %collective-permute-done.25.refs_8_), channel_id=1, source_target_pairs={{8,0},{9,1},{10,2},{11,3},{12,4},{13,5},{14,6},{15,7}} | collective-permute-start | bytes 12441608 | tf_op jit(solution)/shard_map/ppermute | solution.py:339
  347.3 12.8 %collective-permute-start.29 = (bf16[160,2880]{1,0:T(8,128)(2,1)}, bf16[160,2880]{1,0:T(8,128)(2,1)}, u32[]{:S(2)}, u32[]{:S(2)}) collective-permute-start(bf16[160,2880]{1,0:T(8,128)(2,1)} %get-tuple-element.166), channel_id=1, source_target_pairs={{16,0},{24,8},{17,1},{25,9},{18,2},{26,10},{19,3},{27,11},{20,4},{... | collective-permute-start | bytes 2764808 | tf_op jit(solution)/shard_map/ppermute | solution.py:339
  351.2 36.2 %collective-permute-start.26 = (bf16[320,1440]{1,0:T(8,128)(2,1)S(1)}, bf16[320,1440]{1,0:T(8,128)(2,1)}, u32[]{:S(2)}, u32[]{:S(2)}) collective-permute-start(bf16[320,1440]{1,0:T(8,128)(2,1)S(1)} %maximum_select_fusion.1), channel_id=1, source_target_pairs={{0,1},{1,0},{2,3},{3,2},{4,5},{5,4},{6,7},{7,6},{8,9},{9,8},{10,11... | collective-permute-start | bytes 2764808 | tf_op jit(solution)/shard_map/ppermute | solution.py:344
  352.9 34.6 %collective-permute-start.27 = (bf16[320,1440]{1,0:T(8,128)(2,1)S(1)}, bf16[320,1440]{1,0:T(8,128)(2,1)}, u32[]{:S(2)}, u32[]{:S(2)}) collective-permute-start(bf16[320,1440]{1,0:T(8,128)(2,1)S(1)} %maximum_select_fusion.1), channel_id=1, source_target_pairs={{0,2},{1,3},{2,0},{3,1},{4,6},{5,7},{6,4},{7,5},{8,10},{9,11},{10,... | collective-permute-start | bytes 2764808 | tf_op jit(solution)/shard_map/ppermute | solution.py:344
  360.0 49.9 %collective-permute-start.28 = (bf16[320,1440]{1,0:T(8,128)(2,1)S(1)}, bf16[320,1440]{1,0:T(8,128)(2,1)}, u32[]{:S(2)}, u32[]{:S(2)}) collective-permute-start(bf16[320,1440]{1,0:T(8,128)(2,1)S(1)} %maximum_select_fusion.1), channel_id=1, source_target_pairs={{1,2},{2,1},{5,6},{6,5},{9,10},{10,9},{13,14},{14,13},{17,18},{18,... | collective-permute-start | bytes 2764808 | tf_op jit(solution)/shard_map/ppermute | solution.py:611
  363.8 90.7 %collective-permute-start.41 = (bf16[320,1440]{1,0:T(8,128)(2,1)S(1)}, bf16[320,1440]{1,0:T(8,128)(2,1)}, u32[]{:S(2)}, u32[]{:S(2)}) collective-permute-start(bf16[320,1440]{1,0:T(8,128)(2,1)S(1)} %maximum_select_fusion), channel_id=1, source_target_pairs={{1,2},{2,1},{5,6},{6,5},{9,10},{10,9},{13,14},{14,13},{17,18},{18,... | collective-permute-start | bytes 2764808 | tf_op jit(solution)/shard_map/ppermute | solution.py:611
  367.3 87.8 %collective-permute-start.42 = (bf16[320,1440]{1,0:T(8,128)(2,1)}, bf16[320,1440]{1,0:T(8,128)(2,1)}, u32[]{:S(2)}, u32[]{:S(2)}) collective-permute-start(bf16[320,1440]{1,0:T(8,128)(2,1)} %collective-permute-done.22), channel_id=1, source_target_pairs={{2,3},{1,0},{6,7},{5,4},{10,11},{9,8},{14,15},{13,12},{18,19},{17,... | collective-permute-start | bytes 2764808 | tf_op jit(solution)/shard_map/ppermute | solution.py:618
  373.8 41.3 %copy-start.37 = (f32[8,360]{1,0:T(8,128)S(1)}, f32[8,360]{1,0:T(8,128)}, u32[]{:S(2)}) copy-start(f32[8,360]{1,0:T(8,128)} %get-tuple-element.197) | copy-start | bytes 34564
  373.8 41.3 %copy-start.38 = (f32[8,360]{1,0:T(8,128)S(1)}, f32[8,360]{1,0:T(8,128)}, u32[]{:S(2)}) copy-start(f32[8,360]{1,0:T(8,128)} %get-tuple-element.205) | copy-start | bytes 34564
  373.8 41.3 %copy-start.41 = (f32[8,360]{1,0:T(8,128)S(1)}, f32[8,360]{1,0:T(8,128)}, u32[]{:S(2)}) copy-start(f32[8,360]{1,0:T(8,128)} %get-tuple-element.198) | copy-start | bytes 34564
  373.8 41.3 %copy-start.29 = (f32[8,2880]{1,0:T(8,128)S(1)}, f32[8,2880]{1,0:T(8,128)}, u32[]{:S(2)}) copy-start(f32[8,2880]{1,0:T(8,128)} %get-tuple-element.193) | copy-start | bytes 276484
  373.8 41.3 %copy-start.30 = (f32[8,2880]{1,0:T(8,128)S(1)}, f32[8,2880]{1,0:T(8,128)}, u32[]{:S(2)}) copy-start(f32[8,2880]{1,0:T(8,128)} %get-tuple-element.201) | copy-start | bytes 276484
  373.8 41.3 %copy-start.33 = (f32[8,2880]{1,0:T(8,128)S(1)}, f32[8,2880]{1,0:T(8,128)}, u32[]{:S(2)}) copy-start(f32[8,2880]{1,0:T(8,128)} %get-tuple-element.194) | copy-start | bytes 276484
  373.8 41.3 %copy-start.34 = (f32[8,2880]{1,0:T(8,128)S(1)}, f32[8,2880]{1,0:T(8,128)}, u32[]{:S(2)}) copy-start(f32[8,2880]{1,0:T(8,128)} %get-tuple-element.202) | copy-start | bytes 276484
  409.9 45.3 %collective-permute-start.43 = (bf16[320,1440]{1,0:T(8,128)(2,1)}, bf16[320,1440]{1,0:T(8,128)(2,1)}, u32[]{:S(2)}, u32[]{:S(2)}) collective-permute-start(bf16[320,1440]{1,0:T(8,128)(2,1)} %collective-permute-done.27), channel_id=1, source_target_pairs={{2,3},{1,0},{6,7},{5,4},{10,11},{9,8},{14,15},{13,12},{18,19},{17,... | collective-permute-start | bytes 2764808 | tf_op jit(solution)/shard_map/ppermute | solution.py:618
  415.4 26.6 %collective-permute-start.50 = (bf16[8,6480]{1,0:T(8,128)(2,1)S(1)}, bf16[8,6480]{1,0:T(8,128)(2,1)S(1)}, u32[]{:S(2)}, u32[]{:S(2)}) collective-permute-start(bf16[8,6480]{1,0:T(8,128)(2,1)S(1)} %get-tuple-element.253), channel_id=1, source_target_pairs={{0,8},{8,0},{16,24},{24,16},{1,9},{9,1},{17,25},{25,17},{2,10},{10... | collective-permute-start | bytes 311048 | tf_op jit(solution)/shard_map/ppermute | solution.py:344
  437.8 19.2 %collective-permute-start.35 = (bf16[320,1440]{1,0:T(8,128)(2,1)}, bf16[320,1440]{1,0:T(8,128)(2,1)}, u32[]{:S(2)}, u32[]{:S(2)}) collective-permute-start(bf16[320,1440]{1,0:T(8,128)(2,1)} %get-tuple-element.224), channel_id=1, source_target_pairs={{0,8},{8,0},{16,24},{24,16},{1,9},{9,1},{17,25},{25,17},{2,10},{10... | collective-permute-start | bytes 2764808 | tf_op jit(solution)/shard_map/ppermute | solution.py:344
  447.1 7.4 %collective-permute-start.51 = (bf16[4,16,1440]{2,1,0:T(8,128)(2,1)S(1)}, bf16[4,16,1440]{2,1,0:T(8,128)(2,1)S(1)}, u32[]{:S(2)}, u32[]{:S(2)}) collective-permute-start(bf16[4,16,1440]{2,1,0:T(8,128)(2,1)S(1)} %get-tuple-element.249), channel_id=1, source_target_pairs={{0,4},{4,0},{1,5},{5,1},{2,6},{6,2},{3,7},{7,3},{8,12},{12,8},{9,1... | collective-permute-start | bytes 552968 | tf_op jit(solution)/shard_map/ppermute | solution.py:349
  454.5 4.4 collective-permute-start.33
  454.5 4.2 collective-permute-start.32
  455.1 6.2 %collective-permute-start.38 = (bf16[320,1440]{1,0:T(8,128)(2,1)S(1)}, bf16[320,1440]{1,0:T(8,128)(2,1)S(1)}, u32[]{:S(2)}, u32[]{:S(2)}) collective-permute-start(bf16[320,1440]{1,0:T(8,128)(2,1)S(1)} %copy-done.15), channel_id=1, source_target_pairs={{0,8},{8,0},{16,24},{24,16},{1,9},{9,1},{17,25},{25,17},{2,10},{10... | collective-permute-start | bytes 2764808 | tf_op jit(solution)/shard_map/ppermute | solution.py:344
  455.2 79.5 %collective-permute-start.52 = (bf16[2,16,1440]{2,1,0:T(8,128)(2,1)S(1)}, bf16[2,16,1440]{2,1,0:T(8,128)(2,1)S(1)}, u32[]{:S(2)}, u32[]{:S(2)}) collective-permute-start(bf16[2,16,1440]{2,1,0:T(8,128)(2,1)S(1)} %get-tuple-element.246), channel_id=1, source_target_pairs={{0,1},{1,0},{2,3},{3,2},{4,5},{5,4},{6,7},{7,6},{8,9},{9,8},{10,11... | collective-permute-start | bytes 276488 | tf_op jit(solution)/shard_map/ppermute | solution.py:344
  457.0 41.8 %collective-permute-start.44 = (bf16[320,1440]{1,0:T(8,128)(2,1)S(1)}, bf16[320,1440]{1,0:T(8,128)(2,1)S(1)}, u32[]{:S(2)}, u32[]{:S(2)}) collective-permute-start(bf16[320,1440]{1,0:T(8,128)(2,1)S(1)} %get-tuple-element.210), channel_id=1, source_target_pairs={{0,8},{8,0},{16,24},{24,16},{1,9},{9,1},{17,25},{25,17},{2,10},{10... | collective-permute-start | bytes 2764808 | tf_op jit(solution)/shard_map/ppermute | solution.py:344
  459.0 22.8 %collective-permute-start.36 = (bf16[320,768]{1,0:T(8,128)(2,1)S(1)}, bf16[320,768]{1,0:T(8,128)(2,1)S(1)}, u32[]{:S(2)}, u32[]{:S(2)}) collective-permute-start(bf16[320,768]{1,0:T(8,128)(2,1)S(1)} %get-tuple-element.221), channel_id=1, source_target_pairs={{0,1},{1,0},{2,3},{3,2},{4,5},{5,4},{6,7},{7,6},{8,9},{9,8},{10,11... | collective-permute-start | bytes 1474568 | tf_op jit(solution)/shard_map/ppermute | solution.py:344
  460.9 13.2 %collective-permute-start.34 = (bf16[320,768]{1,0:T(8,128)(2,1)S(1)}, bf16[320,768]{1,0:T(8,128)(2,1)S(1)}, u32[]{:S(2)}, u32[]{:S(2)}) collective-permute-start(bf16[320,768]{1,0:T(8,128)(2,1)S(1)} %get-tuple-element.220), channel_id=1, source_target_pairs={{0,4},{4,0},{1,5},{5,1},{2,6},{6,2},{3,7},{7,3},{8,12},{12,8},{9,1... | collective-permute-start | bytes 1474568 | tf_op jit(solution)/shard_map/ppermute | solution.py:349
  461.4 35.9 %collective-permute-start.39 = (bf16[320,768]{1,0:T(8,128)(2,1)S(1)}, bf16[320,768]{1,0:T(8,128)(2,1)S(1)}, u32[]{:S(2)}, u32[]{:S(2)}) collective-permute-start(bf16[320,768]{1,0:T(8,128)(2,1)S(1)} %get-tuple-element.222), channel_id=1, source_target_pairs={{0,2},{1,3},{2,0},{3,1},{4,6},{5,7},{6,4},{7,5},{8,10},{9,11},{10,... | collective-permute-start | bytes 1474568 | tf_op jit(solution)/shard_map/ppermute | solution.py:344
  474.0 60.7 %collective-permute-start.53 = (bf16[2,16,1440]{2,1,0:T(8,128)(2,1)S(1)}, bf16[2,16,1440]{2,1,0:T(8,128)(2,1)S(1)}, u32[]{:S(2)}, u32[]{:S(2)}) collective-permute-start(bf16[2,16,1440]{2,1,0:T(8,128)(2,1)S(1)} %get-tuple-element.247), channel_id=1, source_target_pairs={{0,2},{1,3},{2,0},{3,1},{4,6},{5,7},{6,4},{7,5},{8,10},{9,11},{10,... | collective-permute-start | bytes 276488 | tf_op jit(solution)/shard_map/ppermute | solution.py:344
  481.8 30.2 %collective-permute-start.45 = (bf16[320,768]{1,0:T(8,128)(2,1)S(1)}, bf16[320,768]{1,0:T(8,128)(2,1)S(1)}, u32[]{:S(2)}, u32[]{:S(2)}) collective-permute-start(bf16[320,768]{1,0:T(8,128)(2,1)S(1)} %get-tuple-element.219), channel_id=1, source_target_pairs={{0,3},{1,2},{2,1},{3,0},{4,7},{5,6},{6,5},{7,4},{8,11},{9,10},{10,... | collective-permute-start | bytes 1474568 | tf_op jit(solution)/shard_map/ppermute | solution.py:344
  497.3 16.2 %collective-permute-start.37 = (bf16[320,768]{1,0:T(8,128)(2,1)S(1)}, bf16[320,768]{1,0:T(8,128)(2,1)S(1)}, u32[]{:S(2)}, u32[]{:S(2)}) collective-permute-start(bf16[320,768]{1,0:T(8,128)(2,1)S(1)} %collective-permute-done.36), channel_id=1, source_target_pairs={{0,4},{4,0},{1,5},{5,1},{2,6},{6,2},{3,7},{7,3},{8,12},{12,8},{9,1... | collective-permute-start | bytes 1474568 | tf_op jit(solution)/shard_map/ppermute | solution.py:349
  498.8 23.1 %collective-permute-start.40 = (bf16[320,768]{1,0:T(8,128)(2,1)S(1)}, bf16[320,768]{1,0:T(8,128)(2,1)S(1)}, u32[]{:S(2)}, u32[]{:S(2)}) collective-permute-start(bf16[320,768]{1,0:T(8,128)(2,1)S(1)} %collective-permute-done.39), channel_id=1, source_target_pairs={{0,4},{4,0},{1,5},{5,1},{2,6},{6,2},{3,7},{7,3},{8,12},{12,8},{9,1... | collective-permute-start | bytes 1474568 | tf_op jit(solution)/shard_map/ppermute | solution.py:349
  512.0 22.7 %collective-permute-start.54 = (bf16[2,16,1440]{2,1,0:T(8,128)(2,1)S(1)}, bf16[2,16,1440]{2,1,0:T(8,128)(2,1)S(1)}, u32[]{:S(2)}, u32[]{:S(2)}) collective-permute-start(bf16[2,16,1440]{2,1,0:T(8,128)(2,1)S(1)} %get-tuple-element.248), channel_id=1, source_target_pairs={{0,3},{1,2},{2,1},{3,0},{4,7},{5,6},{6,5},{7,4},{8,11},{9,10},{10,... | collective-permute-start | bytes 276488 | tf_op jit(solution)/shard_map/ppermute | solution.py:344
  513.5 15.8 %collective-permute-start.46 = (bf16[320,768]{1,0:T(8,128)(2,1)S(1)}, bf16[320,768]{1,0:T(8,128)(2,1)S(1)}, u32[]{:S(2)}, u32[]{:S(2)}) collective-permute-start(bf16[320,768]{1,0:T(8,128)(2,1)S(1)} %collective-permute-done.45), channel_id=1, source_target_pairs={{0,4},{4,0},{1,5},{5,1},{2,6},{6,2},{3,7},{7,3},{8,12},{12,8},{9,1... | collective-permute-start | bytes 1474568 | tf_op jit(solution)/shard_map/ppermute | solution.py:349
  532.2 22.7 %collective-permute-start.47 = (bf16[360,768]{1,0:T(8,128)(2,1)S(1)}, bf16[360,768]{1,0:T(8,128)(2,1)S(1)}, u32[]{:S(2)}, u32[]{:S(2)}) collective-permute-start(bf16[360,768]{1,0:T(8,128)(2,1)S(1)} %get-tuple-element.218), channel_id=1, source_target_pairs={{0,1},{1,0},{2,3},{3,2},{4,5},{5,4},{6,7},{7,6},{8,9},{9,8},{10,11... | collective-permute-start | bytes 1658888 | tf_op jit(solution)/shard_map/ppermute | solution.py:344
  534.8 37.7 %collective-permute-start.48 = (bf16[360,768]{1,0:T(8,128)(2,1)S(1)}, bf16[360,768]{1,0:T(8,128)(2,1)S(1)}, u32[]{:S(2)}, u32[]{:S(2)}) collective-permute-start(bf16[360,768]{1,0:T(8,128)(2,1)S(1)} %get-tuple-element.217), channel_id=1, source_target_pairs={{0,2},{1,3},{2,0},{3,1},{4,6},{5,7},{6,4},{7,5},{8,10},{9,11},{10,... | collective-permute-start | bytes 1658888 | tf_op jit(solution)/shard_map/ppermute | solution.py:344
  538.1 43.7 %collective-permute-start.49 = (bf16[360,768]{1,0:T(8,128)(2,1)S(1)}, bf16[360,768]{1,0:T(8,128)(2,1)S(1)}, u32[]{:S(2)}, u32[]{:S(2)}) collective-permute-start(bf16[360,768]{1,0:T(8,128)(2,1)S(1)} %get-tuple-element.216), channel_id=1, source_target_pairs={{0,3},{1,2},{2,1},{3,0},{4,7},{5,6},{6,5},{7,4},{8,11},{9,10},{10,... | collective-permute-start | bytes 1658888 | tf_op jit(solution)/shard_map/ppermute | solution.py:344
  (36 other events, 510.1 us)
